TPU v7x, 32 devices: a whole 2x2x4 slice. The times are simulated.
32 devices in a mesh: ctx: 8 (over y, x, core), ch: 4 (over z).
Axes of the slice: x: 2, y: 2, z: 4, core: 2. Of those that a mesh axis runs over, the one named last changes fastest.
Arguments:
- tokens: float32 [1024, 3072], P('ctx', 'ch'), may hold values from -6 to 6
- gate_input: float32 [1024, 3072], P('ctx', 'ch'), may hold values from -6 to 6
- cotangent: float32 [1024, 3072], P('ctx', 'ch'), may hold values from -6 to 6
- conv_weight: float32 [2, 4, 3072], P(None, None, 'ch'), may hold values from -3 to 3
- conv_bias: float32 [2, 3072], P(None, 'ch'), may hold values from -3 to 3
- select_weight: float32 [2, 3072, 128], P(None, 'ch'), may hold values from -0.109375 to 0.109375
- step_weight: float32 [2, 96, 3072], P(None, None, 'ch'), may hold values from -0.625 to 0.625
- step_bias: float32 [2, 3072], P(None, 'ch'), may hold values from -6 to -2.5
- decay_log: float32 [2, 16, 3072], P(None, None, 'ch'), may hold values from -12 to 2.75
- skip_gain: float32 [2, 3072], P(None, 'ch'), may hold values from 0.5 to 1.5
Outputs:
- block_out: float32 [1024, 3072], P('ctx', 'ch')
- tokens_grad: float32 [1024, 3072], P('ctx', 'ch')
- gate_grad: float32 [1024, 3072], P('ctx', 'ch')
- select_grad: float32 [2, 3072, 128], P(None, 'ch')
- step_grad: float32 [2, 96, 3072], P(None, None, 'ch')
All inputs are finite; a program needn't handle non-finite values.
Results may differ from a plain program's by a relative error of at most 0.0003.
Values sent between devices are 32-bit elements; how exact they have to be, the bound alone decides.
No kernel may reach another device: no remote copies, remote signals or barrier semaphores. Data moves between devices by JAX's collectives and lax.ppermute only.
A program may use at most 64 MiB of HBM per device.

v0:
```python
import functools

import jax
import jax.numpy as jnp
from jax import lax
from jax.experimental import pallas as pl
from jax.experimental.pallas import tpu as pltpu
from jax.sharding import PartitionSpec as P

FULL_PRECISION = lax.Precision.HIGHEST
LANES = 128
CHAINS = 8
HALO = 8
MIB = 1024 * 1024


def params(mib):
    return pltpu.CompilerParams(vmem_limit_bytes=mib * MIB)


def shape_of(*dims):
    return jax.ShapeDtypeStruct(dims, jnp.float32)


def dot(a, b, contract):
    return lax.dot_general(
        a, b, ((contract[:1], contract[1:]), ((), ())), precision=FULL_PRECISION,
        preferred_element_type=jnp.float32,
    )


def silu_grad(values):
    sigmoid_values = jax.nn.sigmoid(values)
    return sigmoid_values * (1.0 + values * (1.0 - sigmoid_values))


def lane_tile(t):
    return slice(t * LANES, (t + 1) * LANES)


def full_width(ref, *lead):
    tiles = ref.shape[len(lead)]
    return jnp.concatenate([ref[(*lead, t)] for t in range(tiles)], axis=1)


def convolved(ext, at_row, side, lanes, rows, conv_weight, conv_bias):
    taps = conv_weight.shape[1]
    margin = taps - 1
    conv = jnp.broadcast_to(conv_bias[side : side + 1, lanes], (rows, LANES))
    for k in range(taps):
        at = at_row + (k - margin if side == 0 else margin - k)
        conv = conv + conv_weight[side, k : k + 1, lanes] * ext[at : at + rows, lanes]
    return conv


def copies_of(pairs, sems):
    copies = [pltpu.make_async_copy(a, b, sems.at[i]) for i, (a, b) in enumerate(pairs)]
    for copy in copies:
        copy.start()
    return copies


def finish_all(copies):
    for copy in copies:
        copy.wait()


def entry_kernel(
    before, after, tokens, conv_weight_in, conv_bias_in, select_in,
    partial, act_out, pre_out,
    ext, conv_weight, conv_bias, select, act, pre, sems,
):
    length, width = tokens.shape
    loads = copies_of(
        [
            (tokens, ext.at[pl.ds(HALO, length)]), (conv_weight_in, conv_weight),
            (conv_bias_in, conv_bias), (select_in, select),
        ],
        sems,
    )
    ext[:HALO] = before[...]
    ext[HALO + length :] = after[...]
    finish_all(loads[:3])
    for side in range(2):
        for t in range(width // LANES):
            conv = convolved(ext, HALO, side, lane_tile(t), length, conv_weight, conv_bias)
            pre[side, t] = conv
            act[side, t] = conv * jax.nn.sigmoid(conv)
    stores = copies_of([(pre, pre_out), (act, act_out)], sems.at[pl.ds(4, 2)])
    loads[3].wait()
    for side in range(2):
        partial[side] = dot(full_width(act, side), select[side], (1, 0))
    finish_all(stores)


def spread(projection, side, j, states, basis_b, basis_c):
    length = basis_b.shape[0]
    count = length // CHAINS
    rows = projection[side, pl.ds(j, CHAINS, stride=count), :]
    ranks = LANES - 2 * states
    at = pl.ds(pl.multiple_of(j * CHAINS, CHAINS), CHAINS)
    for n in range(states):
        b = rows[:, ranks + n : ranks + n + 1]
        c = rows[:, ranks + states + n : ranks + states + n + 1]
        basis_b[at, lane_tile(n)] = jnp.broadcast_to(b, (CHAINS, LANES))
        basis_c[at, lane_tile(n)] = jnp.broadcast_to(c, (CHAINS, LANES))


def fill_bases(projection, side, states, basis_b, basis_c):
    def body(j, carry):
        spread(projection, side, j, states, basis_b, basis_c)
        return carry

    lax.fori_loop(0, basis_b.shape[0] // CHAINS, body, 0)


def fill_rates(decay_log, rates):
    for side in range(rates.shape[0]):
        for t in range(rates.shape[1]):
            rates[side, t] = -jnp.exp(decay_log[side, :, lane_tile(t)])


def sublane():
    return lax.broadcasted_iota(jnp.int32, (CHAINS, LANES), 0)


def shifted(value, by, up):
    rolled = pltpu.roll(value, by if up else CHAINS - by, 0)
    place = sublane()
    keep = place >= by if up else place < CHAINS - by
    return jnp.where(keep, rolled, 0.0)


def over_chains(decays, ends, up):
    by = 1
    while by < CHAINS:
        ends = [d * shifted(f, by, up) + f for d, f in zip(decays, ends)]
        if 2 * by < CHAINS:
            turn = by if up else CHAINS - by
            decays = [d * pltpu.roll(d, turn, 0) for d in decays]
        by *= 2
    return ends


def order(i, count, up):
    return i if up else count - 1 - i


def tile_group(tiles):
    return 2 if tiles % 2 == 0 else 1


def unrolled(count, body, start):
    times = 2 if count % 2 == 0 else 1

    def several(i, state):
        for k in range(times):
            state = body(i * times + k, state)
        return state

    return lax.fori_loop(0, count // times, several, start)


def fill_rate_rows(rates, side, tiles, rate_rows):
    for g, t in enumerate(tiles):
        for n in range(rate_rows.shape[1]):
            rate_rows[g, n] = jnp.broadcast_to(rates[side, t, n : n + 1], (CHAINS, LANES))


def token_rows(j, count):
    return pl.ds(j, CHAINS, stride=count)


def cell_rows(j):
    return pl.ds(pl.multiple_of(j * CHAINS, CHAINS), CHAINS)


def local_kernel(
    own, first, second, third, step_weight_in, step_bias_in, decay_log_in, act_in, gate_in, cot_in,
    projection_out, step_out, step_pre_out, grad_gated_out, entering_out, carry,
    projection, act, step, step_pre, grad_gated, entering, step_weight, step_bias, decay_log,
    gate, cot, rates, basis_b, basis_c, rate_rows, decays, sems,
):
    sides, tiles, length, _ = act.shape
    states = decay_log.shape[1]
    ranks = step_weight.shape[1]
    count = length // CHAINS
    group = tile_group(tiles)
    loads = copies_of(
        [
            (step_weight_in, step_weight), (step_bias_in, step_bias), (decay_log_in, decay_log),
            (gate_in, gate), (cot_in, cot), (act_in, act),
        ],
        sems,
    )
    projection[...] = (own[...] + first[...]) + (second[...] + third[...])
    finish_all(loads)
    for t in range(tiles):
        lanes = lane_tile(t)
        values = gate[:, lanes]
        grad_gated[t] = cot[:, lanes] * values * jax.nn.sigmoid(values)
    fill_rates(decay_log, rates)
    for side in range(2):
        wide = dot(projection[side][:, :ranks], step_weight[side], (1, 0))
        wide = wide + step_bias[side : side + 1]
        for t in range(tiles):
            part = wide[:, lane_tile(t)]
            step_pre[side, t] = part
            step[side, t] = jnp.maximum(part, 0.0) + jnp.log1p(jnp.exp(-jnp.abs(part)))
    stores = copies_of(
        [
            (projection, projection_out), (step, step_out), (step_pre, step_pre_out),
            (grad_gated, grad_gated_out),
        ],
        sems,
    )
    zero = jnp.zeros((CHAINS, LANES), jnp.float32)
    carry[...] = jnp.zeros_like(carry)
    for side in range(2):
        up = side == 0
        fill_bases(projection, side, states, basis_b, basis_c)

        def some_tiles(first, keep):
            at_tiles = [first * group + g for g in range(group)]
            fill_rate_rows(rates, side, at_tiles, rate_rows)

            def forward(i, current):
                state, summed = current
                j = order(i, count, up)
                rows, at = token_rows(j, count), cell_rows(j)
                steps = [step[side, t, rows, :] for t in at_tiles]
                drives = [v * act[side, t, rows, :] for v, t in zip(steps, at_tiles)]
                new = []
                for n in range(states):
                    lanes = lane_tile(n)
                    b = basis_b[at, lanes]
                    for g in range(group):
                        decay = jnp.exp(steps[g] * rate_rows[g, n])
                        decays[g, at, lanes] = decay
                        new.append(decay * state[n * group + g] + b * drives[g])
                return (tuple(new), tuple(a + v for a, v in zip(summed, steps)))

            start = ((zero,) * (states * group), (zero,) * group)
            state, summed = unrolled(count, forward, start)

            def retreat(i, state):
                j = order(i, count, not up)
                rows, at = token_rows(j, count), cell_rows(j)
                grads = [grad_gated[t, rows, :] for t in at_tiles]
                new = []
                for n in range(states):
                    lanes = lane_tile(n)
                    c = basis_c[at, lanes]
                    for g in range(group):
                        adjoint = state[n * group + g] + c * grads[g]
                        new.append(decays[g, at, lanes] * adjoint)
                return tuple(new)

            sent = unrolled(count, retreat, (zero,) * (states * group))
            for g, t in enumerate(at_tiles):
                across = [jnp.exp(summed[g] * rate_rows[g, n]) for n in range(states)]
                for kind, ends, upward in ((0, state, up), (1, sent, not up)):
                    slot = 2 * side + kind
                    ends = over_chains(across, list(ends[g::group]), upward)
                    last = CHAINS - 1 if upward else 0
                    for n in range(states):
                        entering[slot, t, n] = shifted(ends[n], 1, upward)
                        at = side * states + n
                        carry[0 if upward else 1, t, at : at + 1] = ends[n][last : last + 1]
                whole = jnp.sum(summed[g], axis=0, keepdims=True)
                at = 2 * states + side
                for k in range(2):
                    carry[k, t, at : at + 1] = whole
            return keep

        lax.fori_loop(0, tiles // group, some_tiles, 0)
    stores = stores + copies_of([(entering, entering_out)], sems.at[pl.ds(4, 1)])
    finish_all(stores)


def fill_row_rates(decay_log, rates):
    for side in range(2):
        states = decay_log.shape[1]
        for t in range(rates.shape[0]):
            value = -jnp.exp(decay_log[side, :, lane_tile(t)])
            rates[t, side * states : (side + 1) * states] = value


def tile_decay(part, rates):
    rows = rates.shape[1]
    row = lax.broadcasted_iota(jnp.int32, rates.shape, 1)
    sums = jnp.where(row < rows // 2, part[:, rows : rows + 1], part[:, rows + 1 : rows + 2])
    return jnp.exp(rates * sums)


def pair_kernel(place, mine, other, decay_log, *refs):
    outs, (rates, total) = refs[:-2], refs[-2:]
    rows = rates.shape[1]
    fill_row_rates(decay_log, rates)
    core, chip = lax.rem(place[0], 2), lax.div(place[0], 2)
    low = jnp.where(core == 0, mine[...], other[...])
    high = jnp.where(core == 0, other[...], mine[...])
    spread_rates = rates[...]
    decay_low = tile_decay(low[0], spread_rates)
    decay_high = tile_decay(high[0], spread_rates)
    total[...] = low + high
    total[0, :, :rows] = decay_high * low[0][:, :rows] + high[0][:, :rows]
    total[1, :, :rows] = decay_low * high[1][:, :rows] + low[1][:, :rows]
    for s, out in enumerate(outs, 1):
        below = lax.convert_element_type((chip ^ s) < chip, jnp.int32)
        out[...] = total[below]


def chain_kernel(place, other, decay_log, *refs):
    gathered, (out, rates, parts) = refs[:-3], refs[-3:]
    rows = rates.shape[1]
    chips = parts.shape[0]
    fill_row_rates(decay_log, rates)
    core, chip = lax.rem(place[0], 2), lax.div(place[0], 2)
    parts[chip] = jnp.zeros(parts.shape[1:], jnp.float32)
    for s, part in enumerate(gathered, 1):
        parts[chip ^ s] = part[...]
    spread_rates = rates[...]
    for kind in range(2):
        state = jnp.zeros(rates.shape, jnp.float32)
        for k in range(chips) if kind == 0 else reversed(range(chips)):
            part = parts[k]
            new = tile_decay(part, spread_rates) * state + part[:, :rows]
            state = jnp.where(k < chip if kind == 0 else k > chip, new, state)
        part = other[kind]
        new = tile_decay(part, spread_rates) * state + part[:, :rows]
        out[kind] = jnp.where(core == 1 - kind, new, state)


def long_chain_kernel(place, gathered, decay_log, out, rates):
    rows = rates.shape[1]
    shards = gathered.shape[0]
    fill_row_rates(decay_log, rates)
    for kind in range(2):

        def turn(i, state):
            part = gathered[order(i, shards, kind == 0), kind]
            return tile_decay(part, rates[...]) * state + part[:, :rows]

        turns = place[0] if kind == 0 else shards - 1 - place[0]
        out[kind] = lax.fori_loop(0, turns, turn, jnp.zeros(rates.shape, jnp.float32))


def scan_kernel(
    incoming, projection_in, step_weight_in, decay_log_in, skip_gain_in, act_in, step_in,
    step_pre_in, grad_gated_in, entering_in,
    partial, grad_act_out, grad_pre_out, summed_outs,
    projection, step_weight, decay_log, skip_gain, act, step, step_pre, grad_gated, entering,
    grad_act, grad_pre, summed_out, rates, basis_b, basis_c, rate_rows, history,
    grad_in, grad_out, weights, packed, sems,
):
    sides, tiles, length, _ = act.shape
    states = decay_log.shape[1]
    ranks = step_weight.shape[1]
    count = length // CHAINS
    group = tile_group(tiles)
    loads = copies_of(
        [
            (projection_in, projection), (decay_log_in, decay_log), (step_in, step),
            (act_in, act), (grad_gated_in, grad_gated), (entering_in, entering),
            (skip_gain_in, skip_gain), (step_pre_in, step_pre), (step_weight_in, step_weight),
        ],
        sems,
    )
    stores = []
    finish_all(loads[:2])
    fill_rates(decay_log, rates)
    zero = jnp.zeros((CHAINS, LANES), jnp.float32)
    column = lax.broadcasted_iota(jnp.int32, (CHAINS, LANES), 1)
    for side in range(2):
        up = side == 0
        fill_bases(projection, side, states, basis_b, basis_c)
        grad_in[...] = jnp.zeros_like(grad_in)
        grad_out[...] = jnp.zeros_like(grad_out)
        if side == 0:
            finish_all(loads[2:])

        def some_tiles(first, keep):
            at_tiles = [first * group + g for g in range(group)]
            fill_rate_rows(rates, side, at_tiles, rate_rows)
            skips = [skip_gain[side, t] for t in at_tiles]
            sums = []
            for t in at_tiles:
                summed = step[side, t, token_rows(0, count), :]
                for j in range(1, count):
                    summed = summed + step[side, t, token_rows(j, count), :]
                sums.append(summed)

            def start(kind, upward):
                slot = 2 * side + kind
                spans = []
                for g in range(group):
                    span = shifted(sums[g], 1, upward)
                    by = 1
                    while by < CHAINS:
                        span = span + shifted(span, by, upward)
                        by *= 2
                    spans.append(span)
                first = []
                for n in range(states):
                    at = side * states + n
                    for g, t in enumerate(at_tiles):
                        decay = jnp.exp(spans[g] * rate_rows[g, n])
                        value = incoming[0 if upward else 1, t, at : at + 1, :]
                        first.append(entering[slot, t, n] + decay * value)
                return tuple(first)

            def forward(i, state):
                j = order(i, count, up)
                rows, at = token_rows(j, count), cell_rows(j)
                steps = [step[side, t, rows, :] for t in at_tiles]
                acts = [act[side, t, rows, :] for t in at_tiles]
                grads = [grad_gated[t, rows, :] for t in at_tiles]
                drives = [v * a for v, a in zip(steps, acts)]
                outs = [v * a for v, a in zip(skips, acts)]
                new = []
                for n in range(states):
                    lanes = lane_tile(n)
                    b, c = basis_b[at, lanes], basis_c[at, lanes]
                    read = grad_out[at, lanes]
                    for g in range(group):
                        before = state[n * group + g]
                        decay = jnp.exp(steps[g] * rate_rows[g, n])
                        history[g, at, lanes] = before
                        current = decay * before + b * drives[g]
                        outs[g] = outs[g] + c * current
                        read = read + current * grads[g]
                        new.append(current)
                    grad_out[at, lanes] = read
                for g, t in enumerate(at_tiles):
                    if side == 0:
                        summed_out[t, rows, :] = outs[g]
                    else:
                        summed_out[t, rows, :] = summed_out[t, rows, :] + outs[g]
                return tuple(new)

            unrolled(count, forward, start(0, up))

            def retreat(i, state):
                j = order(i, count, not up)
                rows, at = token_rows(j, count), cell_rows(j)
                steps = [step[side, t, rows, :] for t in at_tiles]
                acts = [act[side, t, rows, :] for t in at_tiles]
                grads = [grad_gated[t, rows, :] for t in at_tiles]
                drives = [v * a for v, a in zip(steps, acts)]
                step_terms = [zero] * group
                drive_grads = [zero] * group
                new = []
                for n in range(states):
                    lanes = lane_tile(n)
                    b, c = basis_b[at, lanes], basis_c[at, lanes]
                    put = grad_in[at, lanes]
                    for g in range(group):
                        adjoint = state[n * group + g] + c * grads[g]
                        rate = rate_rows[g, n]
                        carried = jnp.exp(steps[g] * rate) * adjoint
                        new.append(carried)
                        term = carried * history[g, at, lanes] * rate
                        step_terms[g] = step_terms[g] + term
                        drive_grads[g] = drive_grads[g] + adjoint * b
                        put = put + adjoint * drives[g]
                    grad_in[at, lanes] = put
                for g, t in enumerate(at_tiles):
                    grad_step = step_terms[g] + drive_grads[g] * acts[g]
                    grad_act[side, t, rows, :] = grads[g] * skips[g] + drive_grads[g] * steps[g]
                    pre = step_pre[side, t, rows, :]
                    grad_pre[side, t, rows, :] = grad_step * jax.nn.sigmoid(pre)
                return tuple(new)

            unrolled(count, retreat, start(1, not up))
            return keep

        lax.fori_loop(0, tiles // group, some_tiles, 0)
        pairs = [
            (grad_act.at[side], grad_act_out.at[side]), (grad_pre.at[side], grad_pre_out.at[side]),
        ]
        if side == 1:
            pairs.append((summed_out, summed_outs))
        stores = stores + copies_of(pairs, sems.at[pl.ds(2 * side, 3)])
        wide = full_width(grad_pre, side)
        weights[...] = jnp.zeros_like(weights)
        weights[:ranks] = step_weight[side]
        packed[...] = dot(wide, weights[...], (1, 1))

        def pack(j, keep):
            rows, at = token_rows(j, count), cell_rows(j)
            line = packed[rows, :]
            for values, start_at in ((grad_in, ranks), (grad_out, ranks + states)):
                for n in range(states):
                    total = jnp.sum(values[at, lane_tile(n)], axis=1, keepdims=True)
                    line = jnp.where(column == start_at + n, total, line)
            packed[rows, :] = line
            return keep

        lax.fori_loop(0, count, pack, 0)
        partial[side] = packed[...]
    finish_all(stores)


def outer_kernel(
    summed_in, gate_in, cot_in, grad_pre_in, projection_in, block_out, gate_grad, step_part,
    summed, gate, cot, grad_pre, projection, sems,
):
    tiles = summed.shape[0]
    ranks = step_part.shape[2]
    loads = copies_of(
        [
            (summed_in, summed), (gate_in, gate), (cot_in, cot), (grad_pre_in, grad_pre),
            (projection_in, projection),
        ],
        sems,
    )
    finish_all(loads)
    for t in range(tiles):
        lanes = lane_tile(t)
        values = gate[:, lanes]
        block_out[:, lanes] = summed[t] * values * jax.nn.sigmoid(values)
        gate_grad[:, lanes] = cot[:, lanes] * summed[t] * silu_grad(values)
    for side in range(2):
        wide = dot(projection[side], full_width(grad_pre, side), (0, 0))
        for t in range(tiles):
            step_part[side, t] = wide[:ranks, lane_tile(t)]


def weight_kernel(
    place, own, first, second, third, act_in, pre_in, grad_act_in, select_in, step_part,
    keep, send, conv_grad_out, head, tail,
    act, pre, grad_act, select, grad, both, conv_grad, sems,
):
    sides, tiles, length, _ = act.shape
    width = tiles * LANES
    half = both.shape[1]
    loads = copies_of(
        [
            (act_in, act), (select_in, select), (grad_act_in, grad_act), (pre_in, pre),
        ],
        sems,
    )
    grad[...] = (own[...] + first[...]) + (second[...] + third[...])
    loads[0].wait()
    place_rows(both, 2 * width, step_part[...].reshape(-1, LANES))
    for side in range(2):
        part = dot(full_width(act, side), grad[side], (0, 0))
        place_rows(both, side * width, part)
    core = lax.rem(place[0], 2)
    stores = copies_of(
        [(both.at[core], keep), (both.at[1 - core], send)], sems.at[pl.ds(4, 2)]
    )
    finish_all(loads[1:])
    for side in range(2):
        wide = dot(grad[side], select[side], (1, 1))
        for t in range(tiles):
            lanes = lane_tile(t)
            total = grad_act[side, t] + wide[:, lanes]
            conv_grad[side, :, lanes] = total * silu_grad(pre[side, t])
    head[...] = conv_grad[0, :HALO]
    tail[...] = conv_grad[1, length - HALO :]
    stores = stores + copies_of([(conv_grad, conv_grad_out)], sems.at[pl.ds(0, 1)])
    finish_all(stores)


def place_rows(both, first, value):
    half = both.shape[1]
    rows = value.shape[0]
    for k in range(2):
        low, high = max(first, k * half), min(first + rows, (k + 1) * half)
        if low < high:
            both[k, low - k * half : high - k * half] = value[low - first : high - first]


def halves_kernel(place, keep, got, mine, *refs):
    outs, (total,) = refs[:-1], refs[-1:]
    share = mine.shape[0]
    chips = len(outs) + 1
    for k in range(chips):
        at = slice(k * share, (k + 1) * share)
        total[k] = keep[at] + got[at]
    chip = lax.div(place[0], 2)
    mine[...] = total[chip]
    for s, out in enumerate(outs, 1):
        out[...] = total[chip ^ s]


def add_kernel(*refs):
    total = refs[0][...]
    for ref in refs[1:-1]:
        total = total + ref[...]
    refs[-1][...] = total


def join_kernel(place, mine, *refs):
    parts, out = refs[:-1], refs[-1]
    chip = lax.div(place[0], 2)
    out[chip] = mine[...]
    for s, part in enumerate(parts, 1):
        out[chip ^ s] = part[...]


def outputs_kernel(place, mine, other, select_grad, step_grad, both):
    sides, width, _ = select_grad.shape
    ranks = step_grad.shape[1]
    core = lax.rem(place[0], 2)
    half = both.shape[0] // 2
    size = mine.shape[1]
    for k in range(mine.shape[0]):
        low = jnp.where(core == 0, mine[k], other[k])
        high = jnp.where(core == 0, other[k], mine[k])
        both[k * size : (k + 1) * size] = low
        both[half + k * size : half + (k + 1) * size] = high
    for side in range(sides):
        select_grad[side] = both[side * width : (side + 1) * width]
        for t in range(width // LANES):
            at = 2 * width + (side * (width // LANES) + t) * ranks
            step_grad[side, :, lane_tile(t)] = both[at : at + ranks]


def exit_kernel(
    before, after, conv_grad, conv_weight_in, tokens_grad, up, down, conv_weight, sems
):
    _, length, width = conv_grad.shape
    taps = conv_weight.shape[1]
    margin = taps - 1
    loads = copies_of(
        [
            (conv_grad.at[0], up.at[pl.ds(0, length)]),
            (conv_grad.at[1], down.at[pl.ds(HALO, length)]),
            (conv_weight_in, conv_weight),
        ],
        sems,
    )
    up[length:] = after[...]
    down[:HALO] = before[...]
    finish_all(loads)
    for t in range(width // LANES):
        lanes = lane_tile(t)
        total = jnp.zeros((length, LANES), jnp.float32)
        for k in range(taps):
            at = margin - k
            total = total + conv_weight[0, k : k + 1, lanes] * up[at : at + length, lanes]
            at = HALO - margin + k
            total = total + conv_weight[1, k : k + 1, lanes] * down[at : at + length, lanes]
        tokens_grad[:, lanes] = total


def from_before(value, axis):
    count = lax.axis_size(axis)
    return lax.ppermute(value, axis, [(i, i + 1) for i in range(count - 1)])


def from_after(value, axis):
    count = lax.axis_size(axis)
    return lax.ppermute(value, axis, [(i + 1, i) for i in range(count - 1)])


def swapped(value, axis, by):
    count = lax.axis_size(axis)
    return lax.ppermute(value, axis, [(i, i ^ by) for i in range(count)])


def call(kernel, name, out_shape, scratch, mib, args, kinds, outs=None):
    spaces = {
        "v": pl.BlockSpec(memory_space=pltpu.VMEM),
        "h": pl.BlockSpec(memory_space=pltpu.HBM),
        "s": pl.BlockSpec(memory_space=pltpu.SMEM),
    }
    single = isinstance(out_shape, jax.ShapeDtypeStruct)
    outs = outs or "v" * (1 if single else len(out_shape))
    out_specs = [spaces[k] for k in outs]
    return pl.pallas_call(
        kernel,
        in_specs=[spaces[k] for k in kinds],
        out_specs=out_specs[0] if single else out_specs,
        out_shape=out_shape,
        scratch_shapes=scratch,
        compiler_params=params(mib),
        cost_estimate=pl.CostEstimate(flops=2**28, bytes_accessed=2**22, transcendentals=2**18),
        name=name,
    )(*args)


def summed_parts(partial):
    count = lax.axis_size("ch")
    if count == 4:
        return (partial, *(swapped(partial, "ch", s) for s in range(1, 4)))
    zero = jnp.zeros_like(partial)
    return (lax.psum(partial, "ch"), zero, zero, zero)


def on_device(
    tokens, gate_input, cotangent, conv_weight, conv_bias, select_weight, step_weight,
    step_bias, decay_log, skip_gain,
):
    length, width = tokens.shape
    tiles = width // LANES
    states = decay_log.shape[1]
    ranks = step_weight.shape[1]
    places = lax.axis_size("ctx")
    place = lax.axis_index("ctx").astype(jnp.int32).reshape(1)
    group = tile_group(tiles)
    chips = places // 2
    near = places == 8
    narrow = (2, length, LANES)
    one = (tiles, length, LANES)
    pair = (2, *one)
    chain_ends = (4, tiles, states, CHAINS, LANES)
    carry = (2, tiles, 2 * states + 8, LANES)
    vmem = functools.partial(pltpu.VMEM, dtype=jnp.float32)
    dma = lambda n: pltpu.SemaphoreType.DMA((n,))
    bases = vmem((length, states * LANES))
    grouped = vmem((group, length, states * LANES))
    rate_scratch = vmem((2, tiles, states, LANES))
    row_scratch = vmem((group, states, CHAINS, LANES))
    row_rates = vmem((tiles, 2 * states, LANES))
    skip = skip_gain.reshape(2, tiles, 1, LANES)

    before = from_before(tokens[length - HALO :], "ctx")
    after = from_after(tokens[:HALO], "ctx")
    partial, act, pre = call(
        entry_kernel, "entry", (shape_of(*narrow), shape_of(*pair), shape_of(*pair)),
        [
            vmem((length + 2 * HALO, width)), vmem(conv_weight.shape), vmem(conv_bias.shape),
            vmem(select_weight.shape), vmem(pair), vmem(pair), dma(6),
        ],
        12, (before, after, tokens, conv_weight, conv_bias, select_weight), "vvhhhh", "vhh",
    )
    projection, step, step_pre, grad_gated, entering, carried = call(
        local_kernel, "local",
        (
            shape_of(*narrow), shape_of(*pair), shape_of(*pair), shape_of(*one),
            shape_of(*chain_ends), shape_of(*carry),
        ),
        [
            vmem(narrow), vmem(pair), vmem(pair), vmem(pair), vmem(one), vmem(chain_ends),
            vmem(step_weight.shape), vmem(step_bias.shape), vmem(decay_log.shape),
            vmem((length, width)), vmem((length, width)),
            rate_scratch, bases, bases, row_scratch, grouped, dma(6),
        ],
        24,
        (*summed_parts(partial), step_weight, step_bias, decay_log, act, gate_input, cotangent),
        "vvvvhhhhhh", "hhhhhv",
    )
    if near:
        other = swapped(carried, "ctx", 1)
        sent = call(
            pair_kernel, "pair", (shape_of(*carry[1:]),) * (chips - 1),
            [row_rates, vmem(carry)], 8, (place, carried, other, decay_log), "svvv",
        )
        got = [swapped(part, "ctx", 2 * s) for s, part in enumerate(sent, 1)]
        incoming = call(
            chain_kernel, "chain", shape_of(2, tiles, 2 * states, LANES),
            [row_rates, vmem((chips, *carry[1:]))],
            8, (place, other, decay_log, *got), "svv" + "v" * len(got),
        )
    else:
        gathered = lax.all_gather(carried, "ctx")
        incoming = call(
            long_chain_kernel, "chain", shape_of(2, tiles, 2 * states, LANES), [row_rates],
            48, (place, gathered, decay_log), "svv",
        )
    partial_grad, grad_act, grad_pre, summed = call(
        scan_kernel, "scan",
        (shape_of(*narrow), shape_of(*pair), shape_of(*pair), shape_of(*one)),
        [
            vmem(narrow), vmem(step_weight.shape), vmem(decay_log.shape), vmem(skip.shape),
            vmem(pair), vmem(pair), vmem(pair), vmem(one), vmem(chain_ends),
            vmem(pair), vmem(pair), vmem(one), rate_scratch, bases, bases, row_scratch, grouped,
            bases, bases, vmem((LANES, width)), vmem((length, LANES)), dma(9),
        ],
        28,
        (
            incoming, projection, step_weight, decay_log, skip, act, step, step_pre, grad_gated,
            entering,
        ),
        "vhhhhhhhhh", "vhhh",
    )
    grad_parts = summed_parts(partial_grad)
    block_out, gate_grad, step_part = call(
        outer_kernel, "outer",
        (
            shape_of(length, width), shape_of(length, width),
            shape_of(2, tiles, ranks, LANES),
        ),
        [
            vmem(one), vmem((length, width)), vmem((length, width)), vmem(pair), vmem(narrow),
            dma(5),
        ],
        12, (summed, gate_input, cotangent, grad_pre, projection), "hhhhh",
    )
    half = width + tiles * ranks
    keep, send, conv_grad, head, tail = call(
        weight_kernel, "weights",
        (
            shape_of(half, LANES), shape_of(half, LANES), shape_of(2, length, width),
            shape_of(HALO, width), shape_of(HALO, width),
        ),
        [
            vmem(pair), vmem(pair), vmem(pair), vmem(select_weight.shape), vmem(narrow),
            vmem((2, half, LANES)), vmem((2, length, width)), dma(6),
        ],
        16,
        (place, *grad_parts, act, pre, grad_act, select_weight, step_part),
        "svvvvhhhhv", "hhhvv",
    )
    before = from_before(tail, "ctx")
    after = from_after(head, "ctx")
    if near:
        share = half // chips
        mine, *sent = call(
            halves_kernel, "halves", (shape_of(share, LANES),) * chips,
            [vmem((chips, share, LANES))],
            8, (place, keep, swapped(send, "ctx", 1)), "svv",
        )
        got = [swapped(part, "ctx", 2 * s) for s, part in enumerate(sent, 1)]
        mine = call(
            add_kernel, "share_sum", shape_of(share, LANES), [], 4, (mine, *got), "v" * chips
        )
        got = [swapped(mine, "ctx", 2 * s) for s in range(1, chips)]
        joined = call(
            join_kernel, "joined", shape_of(chips, share, LANES), [],
            8, (place, mine, *got), "s" + "v" * chips,
        )
        select_grad, step_grad = call(
            outputs_kernel, "weight_grads",
            (shape_of(2, width, LANES), shape_of(2, ranks, width)),
            [vmem((2 * half, LANES))],
            12, (place, joined, swapped(joined, "ctx", 1)), "svv",
        )
    else:
        core = lax.rem(place[0], 2) == 0
        both = jnp.where(core, jnp.stack([keep, send]), jnp.stack([send, keep]))
        both = lax.psum(both, "ctx").reshape(2 * half, LANES)
        select_grad = both[: 2 * width].reshape(2, width, LANES)
        step_grad = both[2 * width :].reshape(2, tiles, ranks, LANES)
        step_grad = step_grad.transpose(0, 2, 1, 3).reshape(2, ranks, width)
    tokens_grad = call(
        exit_kernel, "exit", shape_of(length, width),
        [
            vmem((length + HALO, width)), vmem((length + HALO, width)), vmem(conv_weight.shape),
            dma(3),
        ],
        8, (before, after, conv_grad, conv_weight), "vvhh",
    )
    return (block_out, tokens_grad, gate_grad, select_grad, step_grad)


def solution(mesh):
    return jax.shard_map(
        on_device,
        mesh=mesh,
        in_specs=(
            P("ctx", "ch"),
            P("ctx", "ch"),
            P("ctx", "ch"),
            P(None, None, "ch"),
            P(None, "ch"),
            P(None, "ch", None),
            P(None, None, "ch"),
            P(None, "ch"),
            P(None, None, "ch"),
            P(None, "ch"),
        ),
        out_specs=(
            P("ctx", "ch"),
            P("ctx", "ch"),
            P("ctx", "ch"),
            P(None, "ch", None),
            P(None, None, "ch"),
        ),
        check_vma=False,
    )
```

profile of v0, /device:TPU:3, one launch (start us, length us, event | category | flops | bytes accessed | tf_op | source)
XLA Modules:
  0.0 146.1 jit_solution(13071009182698599615)
XLA Ops:
  1.4 2.6 %collective-permute-start.1 = (f32[8,768]{1,0:T(8,128)S(1)}, f32[8,768]{1,0:T(8,128)S(1)}, u32[]{:S(2)}, u32[]{:S(2)}) collective-permute-start(f32[8,768]{1,0:T(8,128)S(1)} %get-tuple-element.65), channel_id=1, source_target_pairs={{4,0},{8,4},{12,8},{16,12},{20,16},{24,20},{28,24},{5,1},{9,5},{13... | collective-permute-start | bytes 73736 | tf_op jit(solution)/shard_map/ppermute | solution.py:657
  4.0 3.9 %collective-permute-start = (f32[8,768]{1,0:T(8,128)S(1)}, f32[8,768]{1,0:T(8,128)S(1)}, u32[]{:S(2)}, u32[]{:S(2)}) collective-permute-start(f32[8,768]{1,0:T(8,128)S(1)} %get-tuple-element.66), channel_id=1, source_target_pairs={{0,4},{4,8},{8,12},{12,16},{16,20},{20,24},{24,28},{1,5},{5,9},{9,... | collective-permute-start | bytes 73736 | tf_op jit(solution)/shard_map/ppermute | solution.py:652
  7.9 0.9 collective-permute-done.before
  8.8 1.1 copy-done
  9.9 1.0 copy-done.13
  12.3 1.7 %entry.1 = (f32[2,128,128]{2,1,0:T(8,128)S(1)}, f32[2,6,128,128]{3,2,1,0:T(8,128)S(1)}, f32[2,6,128,128]{3,2,1,0:T(8,128)S(1)}) custom-call(f32[8,768]{1,0:T(8,128)S(1)} %collective-permute-done.before, f32[8,768]{1,0:T(8,128)S(1)} %collective-permute-done.1.after, f32[128,768]{1,0:T(8,128)S(1)} %copy-done.13, f32[2,4,768]{2,1,0:T(4,128)S(1)} %copy-done.18, ...), custom_call_target="tpu_custom_call" | custom-call | flops 268435456 | bytes 4194304 | tf_op jit(solution)/shard_map/entry/pallas_call | solution.py:674
  14.9 3.3 %collective-permute-start.4 = (f32[2,128,128]{2,1,0:T(8,128)S(1)}, f32[2,128,128]{2,1,0:T(8,128)S(1)}, u32[]{:S(2)}, u32[]{:S(2)}) collective-permute-start(f32[2,128,128]{2,1,0:T(8,128)S(1)} %get-tuple-element.35.own), channel_id=1, source_target_pairs={{0,3},{1,2},{2,1},{3,0},{4,7},{5,6},{6,5},{7,4},{8,11},{9,10},{10,... | collective-permute-start | bytes 393224 | tf_op jit(solution)/shard_map/ppermute | solution.py:662
  18.5 3.1 %collective-permute-done.4.third = f32[2,128,128]{2,1,0:T(8,128)S(1)} collective-permute-done((f32[2,128,128]{2,1,0:T(8,128)S(1)}, f32[2,128,128]{2,1,0:T(8,128)S(1)}, u32[]{:S(2)}, u32[]{:S(2)}) %collective-permute-start.4) | collective-permute-done | bytes 131104 | tf_op jit(solution)/shard_map/ppermute | solution.py:662
  21.7 7.5 %collective-permute-done.3.second = f32[2,128,128]{2,1,0:T(8,128)S(1)} collective-permute-done((f32[2,128,128]{2,1,0:T(8,128)S(1)}, f32[2,128,128]{2,1,0:T(8,128)S(1)}, u32[]{:S(2)}, u32[]{:S(2)}) %collective-permute-start.3) | collective-permute-done | bytes 131104 | tf_op jit(solution)/shard_map/ppermute | solution.py:662
  29.1 1.0 copy-done.3
  30.1 1.0 copy-done.5
  32.7 14.5 %local.1 = (f32[2,128,128]{2,1,0:T(8,128)S(1)}, f32[2,6,128,128]{3,2,1,0:T(8,128)S(1)}, f32[2,6,128,128]{3,2,1,0:T(8,128)S(1)}, f32[6,128,128]{2,1,0:T(8,128)S(1...) custom-call(f32[2,128,128]{2,1,0:T(8,128)S(1)} %get-tuple-element.35.own, ...), custom_call_target="tpu_custom_call" | custom-call | flops 268435456 | bytes 4194304 | tf_op jit(solution)/shard_map/local/pallas_call | solution.py:674
  48.1 0.9 copy-done.11
  49.0 1.2 collective-permute-start.5
  50.1 1.5 %collective-permute-done.5.other = f32[2,6,40,128]{3,2,1,0:T(8,128)} collective-permute-done((f32[2,6,40,128]{3,2,1,0:T(8,128)}, f32[2,6,40,128]{3,2,1,0:T(8,128)}, u32[]{:S(2)}, u32[]{:S(2)}) %collective-permute-start.5) | collective-permute-done | bytes 245792 | tf_op jit(solution)/shard_map/ppermute | solution.py:662
  51.6 0.9 copy-done.15
  52.5 1.9 %pair.1 = (f32[6,40,128]{2,1,0:T(8,128)}, f32[6,40,128]{2,1,0:T(8,128)}, f32[6,40,128]{2,1,0:T(8,128)}) custom-call(s32[1]{0:T(128)} %bitcast.place, f32[2,6,40,128]{3,2,1,0:T(8,128)} %get-tuple-element.37.mine, f32[2,6,40,128]{3,2,1,0:T(8,128)} %collective-permute-done.5.other, f32[2,16,768]{2,1,0:T(8,128)S(1)} %copy-done.15), custom_call_target="tpu_custom_call" | custom-call | flops 268435456 | bytes 4194304 | tf_op jit(solution)/shard_map/pair/pallas_call | solution.py:674
  55.1 2.0 %collective-permute-start.8 = (f32[6,40,128]{2,1,0:T(8,128)}, f32[6,40,128]{2,1,0:T(8,128)}, u32[]{:S(2)}, u32[]{:S(2)}) collective-permute-start(f32[6,40,128]{2,1,0:T(8,128)} %get-tuple-element.40), channel_id=1, source_target_pairs={{0,24},{4,28},{8,16},{12,20},{16,8},{20,12},{24,0},{28,4},{1,25},{... | collective-permute-start | bytes 368648 | tf_op jit(solution)/shard_map/ppermute | solution.py:662
  57.1 2.2 %collective-permute-done.6.refs_0_ = f32[6,40,128]{2,1,0:T(8,128)} collective-permute-done((f32[6,40,128]{2,1,0:T(8,128)}, f32[6,40,128]{2,1,0:T(8,128)}, u32[]{:S(2)}, u32[]{:S(2)}) %collective-permute-start.6) | collective-permute-done | bytes 122912 | tf_op jit(solution)/shard_map/ppermute | solution.py:662
  59.5 1.4 collective-permute-done.8.refs_2_
  60.9 0.9 copy-done.16
  61.8 1.4 chain.1.incoming
  63.2 1.1 copy-done.10
  64.3 1.1 copy-done.12
  65.5 0.9 copy-done.17
  66.4 26.2 %scan.1 = (f32[2,128,128]{2,1,0:T(8,128)S(1)}, f32[2,6,128,128]{3,2,1,0:T(8,128)S(1)}, f32[2,6,128,128]{3,2,1,0:T(8,128)S(1)}, f32[6,128,128]{2,1,0:T(8,128)S(1)}) custom-call(f32[2,6,32,128]{3,2,1,0:T(8,128)S(1)} %chain.1.incoming, f32[2,128,128]{2,1,0:T(8,128)S(1)} %get-tuple-element.41.projection_in, f32[2,96,768]{2,1,0:T(8,128)S(1)} %copy-done.2, ...), custom_call_target="tpu_custom_call" | custom-call | flops 268435456 | bytes 4194304 | tf_op jit(solution)/shard_map/scan/pallas_call | solution.py:674
  92.6 2.3 %collective-permute-start.11 = (f32[2,128,128]{2,1,0:T(8,128)S(1)}, f32[2,128,128]{2,1,0:T(8,128)S(1)}, u32[]{:S(2)}, u32[]{:S(2)}) collective-permute-start(f32[2,128,128]{2,1,0:T(8,128)S(1)} %get-tuple-element.49.own), channel_id=1, source_target_pairs={{0,3},{1,2},{2,1},{3,0},{4,7},{5,6},{6,5},{7,4},{8,11},{9,10},{10,... | collective-permute-start | bytes 393224 | tf_op jit(solution)/shard_map/ppermute | solution.py:662
  94.9 1.4 collective-permute-start.9
  96.2 2.5 %outer.1 = (f32[128,768]{1,0:T(8,128)}, f32[128,768]{1,0:T(8,128)}, f32[2,6,96,128]{3,2,1,0:T(8,128)S(1)}) custom-call(f32[6,128,128]{2,1,0:T(8,128)S(1)} %get-tuple-element.46.summed_in, f32[128,768]{1,0:T(8,128)S(1)} %copy-done.4, f32[128,768]{1,0:T(8,128)S(1)} %copy-done.6, f32[2,6,128,128]{3,2,1,0:T(8,128)S(1)} %get-tuple-element.47.grad_pre_in, ...), custom_call_target="tpu_custom_call" | custom-call | flops 268435456 | bytes 4194304 | tf_op jit(solution)/shard_map/outer/pallas_call | solution.py:674
  98.8 6.9 %collective-permute-done.10.second = f32[2,128,128]{2,1,0:T(8,128)S(1)} collective-permute-done((f32[2,128,128]{2,1,0:T(8,128)S(1)}, f32[2,128,128]{2,1,0:T(8,128)S(1)}, u32[]{:S(2)}, u32[]{:S(2)}) %collective-permute-start.10) | collective-permute-done | bytes 131104 | tf_op jit(solution)/shard_map/ppermute | solution.py:662
  105.7 2.6 %weights.1 = (f32[1344,128]{1,0:T(8,128)S(1)}, f32[1344,128]{1,0:T(8,128)S(1)}, f32[2,128,768]{2,1,0:T(8,128)S(1)}, f32[8,768]{1,0:T(8,128)S(1)}, f32[8,768]{1,0:T(8,128)S(1)}) custom-call(s32[1]{0:T(128)} %bitcast.place, f32[2,128,128]{2,1,0:T(8,128)S(1)} %get-tuple-element.49.own, f32[2,128,128]{2,1,0:T(8,128)S(1)} %collective-permute-done.9.first, ...), custom_call_target="tpu_custom_call" | custom-call | flops 268435456 | bytes 4194304 | tf_op jit(solution)/shard_map/weights/pallas_call | solution.py:674
  108.3 1.8 %collective-permute-start.14 = (f32[1344,128]{1,0:T(8,128)S(1)}, f32[1344,128]{1,0:T(8,128)S(1)}, u32[]{:S(2)}, u32[]{:S(2)}) collective-permute-start(f32[1344,128]{1,0:T(8,128)S(1)} %get-tuple-element.58), channel_id=1, source_target_pairs={{0,4},{4,0},{8,12},{12,8},{16,20},{20,16},{24,28},{28,24},{1,5},{5... | collective-permute-start | bytes 2064392 | tf_op jit(solution)/shard_map/ppermute | solution.py:662
  110.1 1.8 %collective-permute-done.14.got = f32[1344,128]{1,0:T(8,128)S(1)} collective-permute-done((f32[1344,128]{1,0:T(8,128)S(1)}, f32[1344,128]{1,0:T(8,128)S(1)}, u32[]{:S(2)}, u32[]{:S(2)}) %collective-permute-start.14) | collective-permute-done | bytes 688160 | tf_op jit(solution)/shard_map/ppermute | solution.py:662
  112.0 1.7 %collective-permute-start.15 = (f32[336,128]{1,0:T(8,128)S(1)}, f32[336,128]{1,0:T(8,128)S(1)}, u32[]{:S(2)}, u32[]{:S(2)}) collective-permute-start(f32[336,128]{1,0:T(8,128)S(1)} %get-tuple-element.60), channel_id=1, source_target_pairs={{0,8},{4,12},{8,0},{12,4},{16,24},{20,28},{24,16},{28,20},{1,9},{5... | collective-permute-start | bytes 516104 | tf_op jit(solution)/shard_map/ppermute | solution.py:662
  113.7 1.3 collective-permute-start.17
  115.0 3.1 %collective-permute-done.15.refs_1_ = f32[336,128]{1,0:T(8,128)S(1)} collective-permute-done((f32[336,128]{1,0:T(8,128)S(1)}, f32[336,128]{1,0:T(8,128)S(1)}, u32[]{:S(2)}, u32[]{:S(2)}) %collective-permute-start.15) | collective-permute-done | bytes 172064 | tf_op jit(solution)/shard_map/ppermute | solution.py:662
  118.0 1.2 collective-permute-done.16.refs_2_
  119.2 3.3 %collective-permute-done.17.refs_3_ = f32[336,128]{1,0:T(8,128)S(1)} collective-permute-done((f32[336,128]{1,0:T(8,128)S(1)}, f32[336,128]{1,0:T(8,128)S(1)}, u32[]{:S(2)}, u32[]{:S(2)}) %collective-permute-start.17) | collective-permute-done | bytes 172064 | tf_op jit(solution)/shard_map/ppermute | solution.py:662
  122.5 1.5 %collective-permute-start.20 = (f32[336,128]{1,0:T(8,128)S(1)}, f32[336,128]{1,0:T(8,128)S(1)}, u32[]{:S(2)}, u32[]{:S(2)}) collective-permute-start(f32[336,128]{1,0:T(8,128)S(1)} %share_sum.1.mine), channel_id=1, source_target_pairs={{0,24},{4,28},{8,16},{12,20},{16,8},{20,12},{24,0},{28,4},{1,25},{... | collective-permute-start | bytes 516104 | tf_op jit(solution)/shard_map/ppermute | solution.py:662
  124.0 1.2 collective-permute-start.18
  125.2 2.6 %collective-permute-done.20.refs_2_ = f32[336,128]{1,0:T(8,128)S(1)} collective-permute-done((f32[336,128]{1,0:T(8,128)S(1)}, f32[336,128]{1,0:T(8,128)S(1)}, u32[]{:S(2)}, u32[]{:S(2)}) %collective-permute-start.20) | collective-permute-done | bytes 172064 | tf_op jit(solution)/shard_map/ppermute | solution.py:662
  127.9 5.1 %collective-permute-done.19.refs_1_ = f32[336,128]{1,0:T(8,128)S(1)} collective-permute-done((f32[336,128]{1,0:T(8,128)S(1)}, f32[336,128]{1,0:T(8,128)S(1)}, u32[]{:S(2)}, u32[]{:S(2)}) %collective-permute-start.19) | collective-permute-done | bytes 172064 | tf_op jit(solution)/shard_map/ppermute | solution.py:662
  133.1 1.0 collective-permute-start.21
  134.1 3.2 %collective-permute-start.12 = (f32[8,768]{1,0:T(8,128)S(1)}, f32[8,768]{1,0:T(8,128)S(1)}, u32[]{:S(2)}, u32[]{:S(2)}) collective-permute-start(f32[8,768]{1,0:T(8,128)S(1)} %get-tuple-element.53), channel_id=1, source_target_pairs={{0,4},{4,8},{8,12},{12,16},{16,20},{20,24},{24,28},{1,5},{5,9},{9,... | collective-permute-start | bytes 73736 | tf_op jit(solution)/shard_map/ppermute | solution.py:652
  137.3 1.9 %collective-permute-start.13 = (f32[8,768]{1,0:T(8,128)S(1)}, f32[8,768]{1,0:T(8,128)S(1)}, u32[]{:S(2)}, u32[]{:S(2)}) collective-permute-start(f32[8,768]{1,0:T(8,128)S(1)} %get-tuple-element.54), channel_id=1, source_target_pairs={{4,0},{8,4},{12,8},{16,12},{20,16},{24,20},{28,24},{5,1},{9,5},{13... | collective-permute-start | bytes 73736 | tf_op jit(solution)/shard_map/ppermute | solution.py:657
  139.2 4.1 %collective-permute-done.13.after = f32[8,768]{1,0:T(8,128)S(1)} collective-permute-done((f32[8,768]{1,0:T(8,128)S(1)}, f32[8,768]{1,0:T(8,128)S(1)}, u32[]{:S(2)}, u32[]{:S(2)}) %collective-permute-start.13) | collective-permute-done | bytes 24608 | tf_op jit(solution)/shard_map/ppermute | solution.py:657
  143.4 1.6 %exit.1 = f32[128,768]{1,0:T(8,128)} custom-call(f32[8,768]{1,0:T(8,128)S(1)} %collective-permute-done.12.before, f32[8,768]{1,0:T(8,128)S(1)} %collective-permute-done.13.after, f32[2,128,768]{2,1,0:T(8,128)S(1)} %get-tuple-element.55.conv_grad, f32[2,4,768]{2,1,0:T(4,128)S(1)} %copy-done.19), custom_call_target="tpu_custom_call" | custom-call | flops 268435456 | bytes 4194304 | tf_op jit(solution)/shard_map/exit/pallas_call | solution.py:674
  145.0 1.2 weight_grads.1
  (56 shorter events, 7.0 us)
Async XLA Ops:
  1.4 6.5 %collective-permute-start.1 = (f32[8,768]{1,0:T(8,128)S(1)}, f32[8,768]{1,0:T(8,128)S(1)}, u32[]{:S(2)}, u32[]{:S(2)}) collective-permute-start(f32[8,768]{1,0:T(8,128)S(1)} %get-tuple-element.65), channel_id=1, source_target_pairs={{4,0},{8,4},{12,8},{16,12},{20,16},{24,20},{28,24},{5,1},{9,5},{13... | collective-permute-start | bytes 73736 | tf_op jit(solution)/shard_map/ppermute | solution.py:657
  4.0 4.8 %collective-permute-start = (f32[8,768]{1,0:T(8,128)S(1)}, f32[8,768]{1,0:T(8,128)S(1)}, u32[]{:S(2)}, u32[]{:S(2)}) collective-permute-start(f32[8,768]{1,0:T(8,128)S(1)} %get-tuple-element.66), channel_id=1, source_target_pairs={{0,4},{4,8},{8,12},{12,16},{16,20},{20,24},{24,28},{1,5},{5,9},{9,... | collective-permute-start | bytes 73736 | tf_op jit(solution)/shard_map/ppermute | solution.py:652
  8.8 1.1 copy-start
  9.9 1.0 copy-start.13
  10.9 0.7 copy-start.18
  11.7 0.7 copy-start.20
  12.3 16.8 %copy-start.2 = (f32[2,96,768]{2,1,0:T(8,128)S(1)}, f32[2,96,768]{2,1,0:T(8,128)}, u32[]{:S(2)}) copy-start(f32[2,96,768]{2,1,0:T(8,128)} %step_weight_in.3) | copy-start | bytes 1769476
  14.0 0.9 copy-start.7
  14.9 6.7 %collective-permute-start.4 = (f32[2,128,128]{2,1,0:T(8,128)S(1)}, f32[2,128,128]{2,1,0:T(8,128)S(1)}, u32[]{:S(2)}, u32[]{:S(2)}) collective-permute-start(f32[2,128,128]{2,1,0:T(8,128)S(1)} %get-tuple-element.35.own), channel_id=1, source_target_pairs={{0,3},{1,2},{2,1},{3,0},{4,7},{5,6},{6,5},{7,4},{8,11},{9,10},{10,... | collective-permute-start | bytes 393224 | tf_op jit(solution)/shard_map/ppermute | solution.py:662
  18.3 10.8 %collective-permute-start.3 = (f32[2,128,128]{2,1,0:T(8,128)S(1)}, f32[2,128,128]{2,1,0:T(8,128)S(1)}, u32[]{:S(2)}, u32[]{:S(2)}) collective-permute-start(f32[2,128,128]{2,1,0:T(8,128)S(1)} %get-tuple-element.35.own), channel_id=1, source_target_pairs={{0,2},{1,3},{2,0},{3,1},{4,6},{5,7},{6,4},{7,5},{8,10},{9,11},{10,... | collective-permute-start | bytes 393224 | tf_op jit(solution)/shard_map/ppermute | solution.py:662
  18.3 10.8 %collective-permute-start.2 = (f32[2,128,128]{2,1,0:T(8,128)S(1)}, f32[2,128,128]{2,1,0:T(8,128)S(1)}, u32[]{:S(2)}, u32[]{:S(2)}) collective-permute-start(f32[2,128,128]{2,1,0:T(8,128)S(1)} %get-tuple-element.35.own), channel_id=1, source_target_pairs={{0,1},{1,0},{2,3},{3,2},{4,5},{5,4},{6,7},{7,6},{8,9},{9,8},{10,11... | collective-permute-start | bytes 393224 | tf_op jit(solution)/shard_map/ppermute | solution.py:662
  29.1 1.0 copy-start.3
  30.1 1.0 copy-start.5
  31.1 0.9 copy-start.14
  32.0 0.7 copy-start.21
  32.7 24.4 %copy-start.22 = (f32[2,768]{1,0:T(2,128)S(1)}, f32[2,768]{1,0:T(2,128)}, u32[]{:S(2)}) copy-start(f32[2,768]{1,0:T(2,128)} %param.19) | copy-start | bytes 18436
  47.2 0.9 copy-start.9
  48.1 0.9 copy-start.11
  49.0 2.7 %collective-permute-start.5 = (f32[2,6,40,128]{3,2,1,0:T(8,128)}, f32[2,6,40,128]{3,2,1,0:T(8,128)}, u32[]{:S(2)}, u32[]{:S(2)}) collective-permute-start(f32[2,6,40,128]{3,2,1,0:T(8,128)} %get-tuple-element.37.mine), channel_id=1, source_target_pairs={{0,4},{4,0},{8,12},{12,8},{16,20},{20,16},{24,28},{28,24},{1,5},{5... | collective-permute-start | bytes 737288 | tf_op jit(solution)/shard_map/ppermute | solution.py:662
  51.6 0.9 copy-start.15
  54.5 4.9 %collective-permute-start.6 = (f32[6,40,128]{2,1,0:T(8,128)}, f32[6,40,128]{2,1,0:T(8,128)}, u32[]{:S(2)}, u32[]{:S(2)}) collective-permute-start(f32[6,40,128]{2,1,0:T(8,128)} %get-tuple-element.38), channel_id=1, source_target_pairs={{0,8},{4,12},{8,0},{12,4},{16,24},{20,28},{24,16},{28,20},{1,9},{5... | collective-permute-start | bytes 368648 | tf_op jit(solution)/shard_map/ppermute | solution.py:662
  54.5 5.1 %collective-permute-start.7 = (f32[6,40,128]{2,1,0:T(8,128)}, f32[6,40,128]{2,1,0:T(8,128)}, u32[]{:S(2)}, u32[]{:S(2)}) collective-permute-start(f32[6,40,128]{2,1,0:T(8,128)} %get-tuple-element.39), channel_id=1, source_target_pairs={{0,16},{4,20},{8,24},{12,28},{16,0},{20,4},{24,8},{28,12},{1,17},{... | collective-permute-start | bytes 368648 | tf_op jit(solution)/shard_map/ppermute | solution.py:662
  55.1 5.8 %collective-permute-start.8 = (f32[6,40,128]{2,1,0:T(8,128)}, f32[6,40,128]{2,1,0:T(8,128)}, u32[]{:S(2)}, u32[]{:S(2)}) collective-permute-start(f32[6,40,128]{2,1,0:T(8,128)} %get-tuple-element.40), channel_id=1, source_target_pairs={{0,24},{4,28},{8,16},{12,20},{16,8},{20,12},{24,0},{28,4},{1,25},{... | collective-permute-start | bytes 368648 | tf_op jit(solution)/shard_map/ppermute | solution.py:662
  60.9 0.9 copy-start.16
  63.2 1.1 copy-start.10
  64.3 1.1 copy-start.12
  65.5 0.9 copy-start.17
  66.3 29.9 %copy-start.4 = (f32[128,768]{1,0:T(8,128)S(1)}, f32[128,768]{1,0:T(8,128)}, u32[]{:S(2)}) copy-start(f32[128,768]{1,0:T(8,128)} %gate_in.3) | copy-start | bytes 1179652
  66.4 29.9 %copy-start.6 = (f32[128,768]{1,0:T(8,128)S(1)}, f32[128,768]{1,0:T(8,128)}, u32[]{:S(2)}) copy-start(f32[128,768]{1,0:T(8,128)} %cot_in.3) | copy-start | bytes 1179652
  92.6 13.1 %copy-start.1 = (f32[2,768,128]{2,1,0:T(8,128)S(1)}, f32[2,768,128]{2,1,0:T(8,128)}, u32[]{:S(2)}) copy-start(f32[2,768,128]{2,1,0:T(8,128)} %select_in.3) | copy-start | bytes 2359300
  92.6 13.1 %copy-start.8 = (f32[2,6,128,128]{3,2,1,0:T(8,128)S(1)}, f32[2,6,128,128]{3,2,1,0:T(8,128)}, u32[]{:S(2)}) copy-start(f32[2,6,128,128]{3,2,1,0:T(8,128)} %copy-done.7) | copy-start | bytes 2359300
  92.6 6.2 %collective-permute-start.11 = (f32[2,128,128]{2,1,0:T(8,128)S(1)}, f32[2,128,128]{2,1,0:T(8,128)S(1)}, u32[]{:S(2)}, u32[]{:S(2)}) collective-permute-start(f32[2,128,128]{2,1,0:T(8,128)S(1)} %get-tuple-element.49.own), channel_id=1, source_target_pairs={{0,3},{1,2},{2,1},{3,0},{4,7},{5,6},{6,5},{7,4},{8,11},{9,10},{10,... | collective-permute-start | bytes 393224 | tf_op jit(solution)/shard_map/ppermute | solution.py:662
  94.9 10.8 %collective-permute-start.10 = (f32[2,128,128]{2,1,0:T(8,128)S(1)}, f32[2,128,128]{2,1,0:T(8,128)S(1)}, u32[]{:S(2)}, u32[]{:S(2)}) collective-permute-start(f32[2,128,128]{2,1,0:T(8,128)S(1)} %get-tuple-element.49.own), channel_id=1, source_target_pairs={{0,2},{1,3},{2,0},{3,1},{4,6},{5,7},{6,4},{7,5},{8,10},{9,11},{10,... | collective-permute-start | bytes 393224 | tf_op jit(solution)/shard_map/ppermute | solution.py:662
  94.9 10.8 %collective-permute-start.9 = (f32[2,128,128]{2,1,0:T(8,128)S(1)}, f32[2,128,128]{2,1,0:T(8,128)S(1)}, u32[]{:S(2)}, u32[]{:S(2)}) collective-permute-start(f32[2,128,128]{2,1,0:T(8,128)S(1)} %get-tuple-element.49.own), channel_id=1, source_target_pairs={{0,1},{1,0},{2,3},{3,2},{4,5},{5,4},{6,7},{7,6},{8,9},{9,8},{10,11... | collective-permute-start | bytes 393224 | tf_op jit(solution)/shard_map/ppermute | solution.py:662
  108.3 3.5 %collective-permute-start.14 = (f32[1344,128]{1,0:T(8,128)S(1)}, f32[1344,128]{1,0:T(8,128)S(1)}, u32[]{:S(2)}, u32[]{:S(2)}) collective-permute-start(f32[1344,128]{1,0:T(8,128)S(1)} %get-tuple-element.58), channel_id=1, source_target_pairs={{0,4},{4,0},{8,12},{12,8},{16,20},{20,16},{24,28},{28,24},{1,5},{5... | collective-permute-start | bytes 2064392 | tf_op jit(solution)/shard_map/ppermute | solution.py:662
  111.9 31.5 %copy-start.19 = (f32[2,4,768]{2,1,0:T(4,128)S(1)}, f32[2,4,768]{2,1,0:T(4,128)}, u32[]{:S(2)}) copy-start(f32[2,4,768]{2,1,0:T(4,128)} %conv_weight_in.3) | copy-start | bytes 73732
  112.0 6.0 %collective-permute-start.15 = (f32[336,128]{1,0:T(8,128)S(1)}, f32[336,128]{1,0:T(8,128)S(1)}, u32[]{:S(2)}, u32[]{:S(2)}) collective-permute-start(f32[336,128]{1,0:T(8,128)S(1)} %get-tuple-element.60), channel_id=1, source_target_pairs={{0,8},{4,12},{8,0},{12,4},{16,24},{20,28},{24,16},{28,20},{1,9},{5... | collective-permute-start | bytes 516104 | tf_op jit(solution)/shard_map/ppermute | solution.py:662
  113.7 5.5 %collective-permute-start.16 = (f32[336,128]{1,0:T(8,128)S(1)}, f32[336,128]{1,0:T(8,128)S(1)}, u32[]{:S(2)}, u32[]{:S(2)}) collective-permute-start(f32[336,128]{1,0:T(8,128)S(1)} %get-tuple-element.61), channel_id=1, source_target_pairs={{0,16},{4,20},{8,24},{12,28},{16,0},{20,4},{24,8},{28,12},{1,17},{... | collective-permute-start | bytes 516104 | tf_op jit(solution)/shard_map/ppermute | solution.py:662
  113.7 8.8 %collective-permute-start.17 = (f32[336,128]{1,0:T(8,128)S(1)}, f32[336,128]{1,0:T(8,128)S(1)}, u32[]{:S(2)}, u32[]{:S(2)}) collective-permute-start(f32[336,128]{1,0:T(8,128)S(1)} %get-tuple-element.62), channel_id=1, source_target_pairs={{0,24},{4,28},{8,16},{12,20},{16,8},{20,12},{24,0},{28,4},{1,25},{... | collective-permute-start | bytes 516104 | tf_op jit(solution)/shard_map/ppermute | solution.py:662
  122.5 5.3 %collective-permute-start.20 = (f32[336,128]{1,0:T(8,128)S(1)}, f32[336,128]{1,0:T(8,128)S(1)}, u32[]{:S(2)}, u32[]{:S(2)}) collective-permute-start(f32[336,128]{1,0:T(8,128)S(1)} %share_sum.1.mine), channel_id=1, source_target_pairs={{0,24},{4,28},{8,16},{12,20},{16,8},{20,12},{24,0},{28,4},{1,25},{... | collective-permute-start | bytes 516104 | tf_op jit(solution)/shard_map/ppermute | solution.py:662
  124.0 9.0 %collective-permute-start.19 = (f32[336,128]{1,0:T(8,128)S(1)}, f32[336,128]{1,0:T(8,128)S(1)}, u32[]{:S(2)}, u32[]{:S(2)}) collective-permute-start(f32[336,128]{1,0:T(8,128)S(1)} %share_sum.1.mine), channel_id=1, source_target_pairs={{0,16},{4,20},{8,24},{12,28},{16,0},{20,4},{24,8},{28,12},{1,17},{... | collective-permute-start | bytes 516104 | tf_op jit(solution)/shard_map/ppermute | solution.py:662
  124.0 9.0 %collective-permute-start.18 = (f32[336,128]{1,0:T(8,128)S(1)}, f32[336,128]{1,0:T(8,128)S(1)}, u32[]{:S(2)}, u32[]{:S(2)}) collective-permute-start(f32[336,128]{1,0:T(8,128)S(1)} %share_sum.1.mine), channel_id=1, source_target_pairs={{0,8},{4,12},{8,0},{12,4},{16,24},{20,28},{24,16},{28,20},{1,9},{5... | collective-permute-start | bytes 516104 | tf_op jit(solution)/shard_map/ppermute | solution.py:662
  133.1 11.9 %collective-permute-start.21 = (f32[4,336,128]{2,1,0:T(8,128)S(1)}, f32[4,336,128]{2,1,0:T(8,128)S(1)}, u32[]{:S(2)}, u32[]{:S(2)}) collective-permute-start(f32[4,336,128]{2,1,0:T(8,128)S(1)} %joined.1.mine), channel_id=1, source_target_pairs={{0,4},{4,0},{8,12},{12,8},{16,20},{20,16},{24,28},{28,24},{1,5},{5... | collective-permute-start | bytes 2064392 | tf_op jit(solution)/shard_map/ppermute | solution.py:662
  134.1 5.1 %collective-permute-start.12 = (f32[8,768]{1,0:T(8,128)S(1)}, f32[8,768]{1,0:T(8,128)S(1)}, u32[]{:S(2)}, u32[]{:S(2)}) collective-permute-start(f32[8,768]{1,0:T(8,128)S(1)} %get-tuple-element.53), channel_id=1, source_target_pairs={{0,4},{4,8},{8,12},{12,16},{16,20},{20,24},{24,28},{1,5},{5,9},{9,... | collective-permute-start | bytes 73736 | tf_op jit(solution)/shard_map/ppermute | solution.py:652
  137.3 6.0 %collective-permute-start.13 = (f32[8,768]{1,0:T(8,128)S(1)}, f32[8,768]{1,0:T(8,128)S(1)}, u32[]{:S(2)}, u32[]{:S(2)}) collective-permute-start(f32[8,768]{1,0:T(8,128)S(1)} %get-tuple-element.54), channel_id=1, source_target_pairs={{4,0},{8,4},{12,8},{16,12},{20,16},{24,20},{28,24},{5,1},{9,5},{13... | collective-permute-start | bytes 73736 | tf_op jit(solution)/shard_map/ppermute | solution.py:657
where the time goes:
time: 147 us; the launch traced here: 146 us
  Pallas kernels  53.8 us (37%)
  waiting for transfers between devices  44.8 us (30%)
  starting transfers between devices  31.1 us (21%)
  local copies, waits for them, and re-layouts  15.5 us (11%)
    pallas_call x12, Pallas kernels, call(): pl.pallas_call(kernel, in_specs=[spaces[k] for k in kinds], out_specs=out...  53.8 us
    ppermute x18, waiting for transfers between devices, swapped(): return lax.ppermute(value, axis, [(i, i ^ by) for i in range(count)])  39.8 us
    ppermute x18, starting transfers between devices, swapped(): return lax.ppermute(value, axis, [(i, i ^ by) for i in range(count)])  19.5 us
    unnamed x46, local copies, waits for them, and re-layouts  14.8 us
    ppermute x2, starting transfers between devices, from_before(): return lax.ppermute(value, axis, [(i, i + 1) for i in range(count - 1)])  7.08 us
    ppermute x2, starting transfers between devices, from_after(): return lax.ppermute(value, axis, [(i + 1, i) for i in range(count - 1)])  4.49 us
    ppermute x2, waiting for transfers between devices, from_after(): return lax.ppermute(value, axis, [(i + 1, i) for i in range(count - 1)])  4.11 us
  transfers between devices with their start and end apart: 22, of which 15 were waited for; matrix products, arithmetic and copies ran while one was open for 0% of the time, Pallas kernels for 3%

commit v1 on v0

--- a/solution.py
+++ b/solution.py
@@ -11,6 +11,8 @@
 LANES = 128
 CHAINS = 8
 HALO = 8
+LOG2E = 1.4426950408889634
+LN2 = 0.6931471805599453
 MIB = 1024 * 1024
 
 
@@ -66,10 +68,12 @@
 
 
 def entry_kernel(
-    before, after, tokens, conv_weight_in, conv_bias_in, select_in,
-    partial, act_out, pre_out,
-    ext, conv_weight, conv_bias, select, act, pre, sems,
+    place, before, after, tokens, conv_weight_in, conv_bias_in, select_in,
+    *refs,
 ):
+    outs, refs = refs[:-9], refs[-9:]
+    act_out, pre_out, ext, conv_weight, conv_bias, select, act, pre, sems = refs
+
     length, width = tokens.shape
     loads = copies_of(
         [
@@ -89,8 +93,26 @@
     stores = copies_of([(pre, pre_out), (act, act_out)], sems.at[pl.ds(4, 2)])
     loads[3].wait()
     for side in range(2):
-        partial[side] = dot(full_width(act, side), select[side], (1, 0))
+        deal(place, outs, side, dot(full_width(act, side), select[side], (1, 0)))
     finish_all(stores)
+
+
+def deal(place, outs, side, rows):
+    share = outs[0].shape[1]
+    for k in range(len(outs)):
+        for mine in range(len(outs)):
+
+            @pl.when(place[0] == mine)
+            def _():
+                at = (mine ^ k) * share
+                outs[k][side] = rows[at : at + share]
+
+
+def collect(place, parts, out):
+    share = parts[0].shape[1]
+    for k in range(len(parts)):
+        at = pl.multiple_of((place[0] ^ k) * share, share)
+        out[:, pl.ds(at, share), :] = parts[k][...]
 
 
 def spread(projection, side, j, states, basis_b, basis_c):
@@ -117,7 +139,7 @@
 def fill_rates(decay_log, rates):
     for side in range(rates.shape[0]):
         for t in range(rates.shape[1]):
-            rates[side, t] = -jnp.exp(decay_log[side, :, lane_tile(t)])
+            rates[side, t] = -LOG2E * jnp.exp(decay_log[side, :, lane_tile(t)])
 
 
 def sublane():
@@ -176,8 +198,9 @@
 
 
 def local_kernel(
-    own, first, second, third, step_weight_in, step_bias_in, decay_log_in, act_in, gate_in, cot_in,
-    projection_out, step_out, step_pre_out, grad_gated_out, entering_out, carry,
+    place, own, first, second, third,
+    step_weight_in, step_bias_in, decay_log_in, act_in, gate_in, cot_in,
+    projection_out, step_out, step_pre_out, grad_gated_out, entering_out, carry, row_rates,
     projection, act, step, step_pre, grad_gated, entering, step_weight, step_bias, decay_log,
     gate, cot, rates, basis_b, basis_c, rate_rows, decays, sems,
 ):
@@ -193,7 +216,7 @@
         ],
         sems,
     )
-    projection[...] = (own[...] + first[...]) + (second[...] + third[...])
+    collect(place, (own, first, second, third), projection)
     finish_all(loads)
     for t in range(tiles):
         lanes = lane_tile(t)
@@ -235,7 +258,7 @@
                     lanes = lane_tile(n)
                     b = basis_b[at, lanes]
                     for g in range(group):
-                        decay = jnp.exp(steps[g] * rate_rows[g, n])
+                        decay = jnp.exp2(steps[g] * rate_rows[g, n])
                         decays[g, at, lanes] = decay
                         new.append(decay * state[n * group + g] + b * drives[g])
                 return (tuple(new), tuple(a + v for a, v in zip(summed, steps)))
@@ -258,7 +281,7 @@
 
             sent = unrolled(count, retreat, (zero,) * (states * group))
             for g, t in enumerate(at_tiles):
-                across = [jnp.exp(summed[g] * rate_rows[g, n]) for n in range(states)]
+                across = [jnp.exp2(summed[g] * rate_rows[g, n]) for n in range(states)]
                 for kind, ends, upward in ((0, state, up), (1, sent, not up)):
                     slot = 2 * side + kind
                     ends = over_chains(across, list(ends[g::group]), upward)
@@ -275,28 +298,21 @@
 
         lax.fori_loop(0, tiles // group, some_tiles, 0)
     stores = stores + copies_of([(entering, entering_out)], sems.at[pl.ds(4, 1)])
+    for side in range(2):
+        row_rates[:, side * states : (side + 1) * states] = rates[side]
     finish_all(stores)
-
-
-def fill_row_rates(decay_log, rates):
-    for side in range(2):
-        states = decay_log.shape[1]
-        for t in range(rates.shape[0]):
-            value = -jnp.exp(decay_log[side, :, lane_tile(t)])
-            rates[t, side * states : (side + 1) * states] = value
 
 
 def tile_decay(part, rates):
     rows = rates.shape[1]
     row = lax.broadcasted_iota(jnp.int32, rates.shape, 1)
     sums = jnp.where(row < rows // 2, part[:, rows : rows + 1], part[:, rows + 1 : rows + 2])
-    return jnp.exp(rates * sums)
-
-
-def pair_kernel(place, mine, other, decay_log, *refs):
-    outs, (rates, total) = refs[:-2], refs[-2:]
+    return jnp.exp2(rates * sums)
+
+
+def pair_kernel(place, mine, other, rates, *refs):
+    outs, total = refs[:-1], refs[-1]
     rows = rates.shape[1]
-    fill_row_rates(decay_log, rates)
     core, chip = lax.rem(place[0], 2), lax.div(place[0], 2)
     low = jnp.where(core == 0, mine[...], other[...])
     high = jnp.where(core == 0, other[...], mine[...])
@@ -311,11 +327,10 @@
         out[...] = total[below]
 
 
-def chain_kernel(place, other, decay_log, *refs):
-    gathered, (out, rates, parts) = refs[:-3], refs[-3:]
+def chain_kernel(place, other, rates, *refs):
+    gathered, (out, parts) = refs[:-2], refs[-2:]
     rows = rates.shape[1]
     chips = parts.shape[0]
-    fill_row_rates(decay_log, rates)
     core, chip = lax.rem(place[0], 2), lax.div(place[0], 2)
     parts[chip] = jnp.zeros(parts.shape[1:], jnp.float32)
     for s, part in enumerate(gathered, 1):
@@ -332,10 +347,9 @@
         out[kind] = jnp.where(core == 1 - kind, new, state)
 
 
-def long_chain_kernel(place, gathered, decay_log, out, rates):
+def long_chain_kernel(place, gathered, rates, out):
     rows = rates.shape[1]
     shards = gathered.shape[0]
-    fill_row_rates(decay_log, rates)
     for kind in range(2):
 
         def turn(i, state):
@@ -347,12 +361,12 @@
 
 
 def scan_kernel(
-    incoming, projection_in, step_weight_in, decay_log_in, skip_gain_in, act_in, step_in,
+    place, incoming, projection_in, step_weight_in, decay_log_in, skip_gain_in, act_in, step_in,
     step_pre_in, grad_gated_in, entering_in,
-    partial, grad_act_out, grad_pre_out, summed_outs,
+    mine, first_out, second_out, third_out, grad_act_out, grad_pre_out, summed_outs,
     projection, step_weight, decay_log, skip_gain, act, step, step_pre, grad_gated, entering,
-    grad_act, grad_pre, summed_out, rates, basis_b, basis_c, rate_rows, history,
-    grad_in, grad_out, weights, packed, sems,
+    grad_act, grad_pre, summed_out, rates, basis_b, basis_c, rate_rows, decays, history,
+    grad_in, grad_out, weights, packed, skip_rows, sems,
 ):
     sides, tiles, length, _ = act.shape
     states = decay_log.shape[1]
@@ -379,11 +393,14 @@
         grad_out[...] = jnp.zeros_like(grad_out)
         if side == 0:
             finish_all(loads[2:])
+            for k in range(2):
+                for t in range(tiles):
+                    skip_rows[k, t] = skip_gain[k : k + 1, lane_tile(t)]
 
         def some_tiles(first, keep):
             at_tiles = [first * group + g for g in range(group)]
             fill_rate_rows(rates, side, at_tiles, rate_rows)
-            skips = [skip_gain[side, t] for t in at_tiles]
+            skips = [skip_rows[side, t] for t in at_tiles]
             sums = []
             for t in at_tiles:
                 summed = step[side, t, token_rows(0, count), :]
@@ -405,7 +422,7 @@
                 for n in range(states):
                     at = side * states + n
                     for g, t in enumerate(at_tiles):
-                        decay = jnp.exp(spans[g] * rate_rows[g, n])
+                        decay = jnp.exp2(spans[g] * rate_rows[g, n])
                         value = incoming[0 if upward else 1, t, at : at + 1, :]
                         first.append(entering[slot, t, n] + decay * value)
                 return tuple(first)
@@ -425,7 +442,8 @@
                     read = grad_out[at, lanes]
                     for g in range(group):
                         before = state[n * group + g]
-                        decay = jnp.exp(steps[g] * rate_rows[g, n])
+                        decay = jnp.exp2(steps[g] * rate_rows[g, n])
+                        decays[g, at, lanes] = decay
                         history[g, at, lanes] = before
                         current = decay * before + b * drives[g]
                         outs[g] = outs[g] + c * current
@@ -457,16 +475,15 @@
                     put = grad_in[at, lanes]
                     for g in range(group):
                         adjoint = state[n * group + g] + c * grads[g]
-                        rate = rate_rows[g, n]
-                        carried = jnp.exp(steps[g] * rate) * adjoint
+                        carried = decays[g, at, lanes] * adjoint
                         new.append(carried)
-                        term = carried * history[g, at, lanes] * rate
+                        term = carried * history[g, at, lanes] * rate_rows[g, n]
                         step_terms[g] = step_terms[g] + term
                         drive_grads[g] = drive_grads[g] + adjoint * b
                         put = put + adjoint * drives[g]
                     grad_in[at, lanes] = put
                 for g, t in enumerate(at_tiles):
-                    grad_step = step_terms[g] + drive_grads[g] * acts[g]
+                    grad_step = step_terms[g] * LN2 + drive_grads[g] * acts[g]
                     grad_act[side, t, rows, :] = grads[g] * skips[g] + drive_grads[g] * steps[g]
                     pre = step_pre[side, t, rows, :]
                     grad_pre[side, t, rows, :] = grad_step * jax.nn.sigmoid(pre)
@@ -498,16 +515,16 @@
             return keep
 
         lax.fori_loop(0, count, pack, 0)
-        partial[side] = packed[...]
+        deal(place, (mine, first_out, second_out, third_out), side, packed)
     finish_all(stores)
 
 
 def outer_kernel(
-    summed_in, gate_in, cot_in, grad_pre_in, projection_in, block_out, gate_grad, step_part,
+    place, summed_in, gate_in, cot_in, grad_pre_in, projection_in, block_out, gate_grad, keep, send,
     summed, gate, cot, grad_pre, projection, sems,
 ):
     tiles = summed.shape[0]
-    ranks = step_part.shape[2]
+    ranks = keep.shape[1]
     loads = copies_of(
         [
             (summed_in, summed), (gate_in, gate), (cot_in, cot), (grad_pre_in, grad_pre),
@@ -523,30 +540,30 @@
         gate_grad[:, lanes] = cot[:, lanes] * summed[t] * silu_grad(values)
     for side in range(2):
         wide = dot(projection[side], full_width(grad_pre, side), (0, 0))
-        for t in range(tiles):
-            step_part[side, t] = wide[:ranks, lane_tile(t)]
+        for out, core in ((keep, side), (send, 1 - side)):
+
+            @pl.when(lax.rem(place[0], 2) == core)
+            def _():
+                for t in range(tiles):
+                    out[t] = wide[:ranks, lane_tile(t)]
 
 
 def weight_kernel(
-    place, own, first, second, third, act_in, pre_in, grad_act_in, select_in, step_part,
+    place, column, own, first, second, third, act_in, pre_in, grad_act_in, select_in, after_this,
     keep, send, conv_grad_out, head, tail,
     act, pre, grad_act, select, grad, both, conv_grad, sems,
 ):
     sides, tiles, length, _ = act.shape
-    width = tiles * LANES
-    half = both.shape[1]
     loads = copies_of(
         [
             (act_in, act), (select_in, select), (grad_act_in, grad_act), (pre_in, pre),
         ],
         sems,
     )
-    grad[...] = (own[...] + first[...]) + (second[...] + third[...])
+    collect(column, (own, first, second, third), grad)
     loads[0].wait()
-    place_rows(both, 2 * width, step_part[...].reshape(-1, LANES))
     for side in range(2):
-        part = dot(full_width(act, side), grad[side], (0, 0))
-        place_rows(both, side * width, part)
+        both[side] = dot(full_width(act, side), grad[side], (0, 0))
     core = lax.rem(place[0], 2)
     stores = copies_of(
         [(both.at[core], keep), (both.at[1 - core], send)], sems.at[pl.ds(4, 2)]
@@ -564,15 +581,6 @@
     finish_all(stores)
 
 
-def place_rows(both, first, value):
-    half = both.shape[1]
-    rows = value.shape[0]
-    for k in range(2):
-        low, high = max(first, k * half), min(first + rows, (k + 1) * half)
-        if low < high:
-            both[k, low - k * half : high - k * half] = value[low - first : high - first]
-
-
 def halves_kernel(place, keep, got, mine, *refs):
     outs, (total,) = refs[:-1], refs[-1:]
     share = mine.shape[0]
@@ -593,7 +601,19 @@
     refs[-1][...] = total
 
 
-def join_kernel(place, mine, *refs):
+def add_both_kernel(*refs):
+    parts, out = refs[:-1], refs[-1]
+    count = len(parts) // 2
+    at = 0
+    for some in (parts[:count], parts[count:]):
+        total = some[0][...]
+        for ref in some[1:]:
+            total = total + ref[...]
+        out[at : at + total.shape[0]] = total
+        at += total.shape[0]
+
+
+def join_kernel(place, after_this, mine, *refs):
     parts, out = refs[:-1], refs[-1]
     chip = lax.div(place[0], 2)
     out[chip] = mine[...]
@@ -604,19 +624,17 @@
 def outputs_kernel(place, mine, other, select_grad, step_grad, both):
     sides, width, _ = select_grad.shape
     ranks = step_grad.shape[1]
+    chips = mine.shape[0]
     core = lax.rem(place[0], 2)
-    half = both.shape[0] // 2
-    size = mine.shape[1]
-    for k in range(mine.shape[0]):
-        low = jnp.where(core == 0, mine[k], other[k])
-        high = jnp.where(core == 0, other[k], mine[k])
-        both[k * size : (k + 1) * size] = low
-        both[half + k * size : half + (k + 1) * size] = high
-    for side in range(sides):
-        select_grad[side] = both[side * width : (side + 1) * width]
+    part = width // chips
+    flat = both.shape[1] // chips
+    for side in range(2):
+        for k in range(chips):
+            rows = jnp.where(core == side, mine[k], other[k])
+            select_grad[side, k * part : (k + 1) * part] = rows[:part]
+            both[side, k * flat : (k + 1) * flat] = rows[part:]
         for t in range(width // LANES):
-            at = 2 * width + (side * (width // LANES) + t) * ranks
-            step_grad[side, :, lane_tile(t)] = both[at : at + ranks]
+            step_grad[side, :, lane_tile(t)] = both[side, t * ranks : (t + 1) * ranks]
 
 
 def exit_kernel(
@@ -668,14 +686,20 @@
         "h": pl.BlockSpec(memory_space=pltpu.HBM),
         "s": pl.BlockSpec(memory_space=pltpu.SMEM),
     }
-    single = isinstance(out_shape, jax.ShapeDtypeStruct)
-    outs = outs or "v" * (1 if single else len(out_shape))
-    out_specs = [spaces[k] for k in outs]
+    outs = outs or "v" * len(out_shape)
+    args = [
+        pltpu.with_memory_space_constraint(a, pltpu.HBM) if k == "h" else a
+        for a, k in zip(args, kinds, strict=True)
+    ]
+    results = [
+        pltpu.HBM(shape, jnp.float32) if k == "h" else shape_of(*shape)
+        for shape, k in zip(out_shape, outs, strict=True)
+    ]
     return pl.pallas_call(
         kernel,
         in_specs=[spaces[k] for k in kinds],
-        out_specs=out_specs[0] if single else out_specs,
-        out_shape=out_shape,
+        out_specs=[spaces[k] for k in outs],
+        out_shape=results,
         scratch_shapes=scratch,
         compiler_params=params(mib),
         cost_estimate=pl.CostEstimate(flops=2**28, bytes_accessed=2**22, transcendentals=2**18),
@@ -683,12 +707,23 @@
     )(*args)
 
 
-def summed_parts(partial):
-    count = lax.axis_size("ch")
-    if count == 4:
-        return (partial, *(swapped(partial, "ch", s) for s in range(1, 4)))
-    zero = jnp.zeros_like(partial)
-    return (lax.psum(partial, "ch"), zero, zero, zero)
+def summed_shares(parts, name):
+    count = len(parts)
+    if count == 1:
+        return (lax.psum(parts[0], "ch"),)
+    got = [swapped(part, "ch", s) for s, part in enumerate(parts[1:], 1)]
+    (mine,) = call(add_kernel, name, (parts[0].shape,), [], 4, (parts[0], *got), "v" * count)
+    return (mine, *(swapped(mine, "ch", s) for s in range(1, count)))
+
+
+def halved(place, keep, send, rows, chips, name):
+    got = swapped(send, "ctx", 1)
+    share = rows // chips
+    mine, *sent = call(
+        halves_kernel, name, ((share, LANES),) * chips, [pltpu.VMEM((chips, share, LANES), jnp.float32)],
+        8, (place, keep.reshape(rows, LANES), got.reshape(rows, LANES)), "svv",
+    )
+    return (mine, *(swapped(part, "ctx", 2 * s) for s, part in enumerate(sent, 1)))
 
 
 def on_device(
@@ -700,151 +735,141 @@
     states = decay_log.shape[1]
     ranks = step_weight.shape[1]
     places = lax.axis_size("ctx")
+    columns = lax.axis_size("ch")
     place = lax.axis_index("ctx").astype(jnp.int32).reshape(1)
+    column = lax.axis_index("ch").astype(jnp.int32).reshape(1)
     group = tile_group(tiles)
     chips = places // 2
     near = places == 8
     narrow = (2, length, LANES)
+    shared = (2, length // columns, LANES)
     one = (tiles, length, LANES)
     pair = (2, *one)
+    flat = (length, width)
     chain_ends = (4, tiles, states, CHAINS, LANES)
     carry = (2, tiles, 2 * states + 8, LANES)
+    row_rates = (tiles, 2 * states, LANES)
     vmem = functools.partial(pltpu.VMEM, dtype=jnp.float32)
     dma = lambda n: pltpu.SemaphoreType.DMA((n,))
     bases = vmem((length, states * LANES))
     grouped = vmem((group, length, states * LANES))
     rate_scratch = vmem((2, tiles, states, LANES))
     row_scratch = vmem((group, states, CHAINS, LANES))
-    row_rates = vmem((tiles, 2 * states, LANES))
-    skip = skip_gain.reshape(2, tiles, 1, LANES)
 
     before = from_before(tokens[length - HALO :], "ctx")
     after = from_after(tokens[:HALO], "ctx")
-    partial, act, pre = call(
-        entry_kernel, "entry", (shape_of(*narrow), shape_of(*pair), shape_of(*pair)),
+    *parts, act, pre = call(
+        entry_kernel, "entry", (*(shared,) * columns, pair, pair),
         [
             vmem((length + 2 * HALO, width)), vmem(conv_weight.shape), vmem(conv_bias.shape),
             vmem(select_weight.shape), vmem(pair), vmem(pair), dma(6),
         ],
-        12, (before, after, tokens, conv_weight, conv_bias, select_weight), "vvhhhh", "vhh",
-    )
-    projection, step, step_pre, grad_gated, entering, carried = call(
-        local_kernel, "local",
-        (
-            shape_of(*narrow), shape_of(*pair), shape_of(*pair), shape_of(*one),
-            shape_of(*chain_ends), shape_of(*carry),
-        ),
+        12, (column, before, after, tokens, conv_weight, conv_bias, select_weight), "svvhhhh",
+        "v" * columns + "hh",
+    )
+    projection, step, step_pre, grad_gated, entering, carried, rates = call(
+        local_kernel, "local", (narrow, pair, pair, one, chain_ends, carry, row_rates),
         [
             vmem(narrow), vmem(pair), vmem(pair), vmem(pair), vmem(one), vmem(chain_ends),
             vmem(step_weight.shape), vmem(step_bias.shape), vmem(decay_log.shape),
-            vmem((length, width)), vmem((length, width)),
+            vmem(flat), vmem(flat),
             rate_scratch, bases, bases, row_scratch, grouped, dma(6),
         ],
         24,
-        (*summed_parts(partial), step_weight, step_bias, decay_log, act, gate_input, cotangent),
-        "vvvvhhhhhh", "hhhhhv",
+        (
+            column, *summed_shares(parts, "projection"), step_weight, step_bias, decay_log, act,
+            gate_input, cotangent,
+        ),
+        "svvvvhhhhhh", "hhhhhvv",
     )
     if near:
         other = swapped(carried, "ctx", 1)
         sent = call(
-            pair_kernel, "pair", (shape_of(*carry[1:]),) * (chips - 1),
-            [row_rates, vmem(carry)], 8, (place, carried, other, decay_log), "svvv",
+            pair_kernel, "pair", (carry[1:],) * (chips - 1),
+            [vmem(carry)], 8, (place, carried, other, rates), "svvv",
         )
         got = [swapped(part, "ctx", 2 * s) for s, part in enumerate(sent, 1)]
-        incoming = call(
-            chain_kernel, "chain", shape_of(2, tiles, 2 * states, LANES),
-            [row_rates, vmem((chips, *carry[1:]))],
-            8, (place, other, decay_log, *got), "svv" + "v" * len(got),
+        (incoming,) = call(
+            chain_kernel, "chain", ((2, *row_rates),), [vmem((chips, *carry[1:]))],
+            8, (place, other, rates, *got), "svv" + "v" * len(got),
         )
     else:
         gathered = lax.all_gather(carried, "ctx")
-        incoming = call(
-            long_chain_kernel, "chain", shape_of(2, tiles, 2 * states, LANES), [row_rates],
-            48, (place, gathered, decay_log), "svv",
+        (incoming,) = call(
+            long_chain_kernel, "chain", ((2, *row_rates),), [],
+            48, (place, gathered, rates), "svv",
         )
-    partial_grad, grad_act, grad_pre, summed = call(
-        scan_kernel, "scan",
-        (shape_of(*narrow), shape_of(*pair), shape_of(*pair), shape_of(*one)),
-        [
-            vmem(narrow), vmem(step_weight.shape), vmem(decay_log.shape), vmem(skip.shape),
+    *grad_parts, grad_act, grad_pre, summed = call(
+        scan_kernel, "scan", (*(shared,) * columns, pair, pair, one),
+        [
+            vmem(narrow), vmem(step_weight.shape), vmem(decay_log.shape), vmem(skip_gain.shape),
             vmem(pair), vmem(pair), vmem(pair), vmem(one), vmem(chain_ends),
             vmem(pair), vmem(pair), vmem(one), rate_scratch, bases, bases, row_scratch, grouped,
-            bases, bases, vmem((LANES, width)), vmem((length, LANES)), dma(9),
+            grouped, bases, bases, vmem((LANES, width)), vmem((length, LANES)),
+            vmem((2, tiles, 1, LANES)), dma(9),
         ],
         28,
         (
-            incoming, projection, step_weight, decay_log, skip, act, step, step_pre, grad_gated,
-            entering,
+            column, incoming, projection, step_weight, decay_log, skip_gain, act, step, step_pre,
+            grad_gated, entering,
         ),
-        "vhhhhhhhhh", "vhhh",
-    )
-    grad_parts = summed_parts(partial_grad)
-    block_out, gate_grad, step_part = call(
-        outer_kernel, "outer",
-        (
-            shape_of(length, width), shape_of(length, width),
-            shape_of(2, tiles, ranks, LANES),
-        ),
-        [
-            vmem(one), vmem((length, width)), vmem((length, width)), vmem(pair), vmem(narrow),
-            dma(5),
-        ],
-        12, (summed, gate_input, cotangent, grad_pre, projection), "hhhhh",
-    )
-    half = width + tiles * ranks
+        "svhhhhhhhhh", "v" * columns + "hhh",
+    )
+    grad_shares = summed_shares(grad_parts, "grad_projection")
+    block_out, gate_grad, step_keep, step_send = call(
+        outer_kernel, "outer", (flat, flat, (tiles, ranks, LANES), (tiles, ranks, LANES)),
+        [vmem(one), vmem(flat), vmem(flat), vmem(pair), vmem(narrow), dma(5)],
+        12, (place, summed, gate_input, cotangent, grad_pre, projection), "shhhhh",
+    )
+    if near:
+        step_shares = halved(place, step_keep, step_send, tiles * ranks, chips, "step_halves")
+        ahead = step_shares[0]
+    else:
+        ahead = step_keep
     keep, send, conv_grad, head, tail = call(
         weight_kernel, "weights",
-        (
-            shape_of(half, LANES), shape_of(half, LANES), shape_of(2, length, width),
-            shape_of(HALO, width), shape_of(HALO, width),
-        ),
+        ((width, LANES), (width, LANES), (2, *flat), (HALO, width), (HALO, width)),
         [
             vmem(pair), vmem(pair), vmem(pair), vmem(select_weight.shape), vmem(narrow),
-            vmem((2, half, LANES)), vmem((2, length, width)), dma(6),
+            vmem(select_weight.shape), vmem((2, *flat)), dma(6),
         ],
         16,
-        (place, *grad_parts, act, pre, grad_act, select_weight, step_part),
-        "svvvvhhhhv", "hhhvv",
+        (place, column, *grad_shares, act, pre, grad_act, select_weight, ahead),
+        "ssvvvvhhhhv", "vvhvv",
     )
     before = from_before(tail, "ctx")
     after = from_after(head, "ctx")
+    (tokens_grad,) = call(
+        exit_kernel, "exit", (flat,),
+        [
+            vmem((length + HALO, width)), vmem((length + HALO, width)), vmem(conv_weight.shape),
+            dma(3),
+        ],
+        8, (before, after, conv_grad, conv_weight), "vvhh",
+    )
     if near:
-        share = half // chips
-        mine, *sent = call(
-            halves_kernel, "halves", (shape_of(share, LANES),) * chips,
-            [vmem((chips, share, LANES))],
-            8, (place, keep, swapped(send, "ctx", 1)), "svv",
-        )
-        got = [swapped(part, "ctx", 2 * s) for s, part in enumerate(sent, 1)]
-        mine = call(
-            add_kernel, "share_sum", shape_of(share, LANES), [], 4, (mine, *got), "v" * chips
+        shares = halved(place, keep, send, width, chips, "select_halves")
+        rows = width // chips + tiles * ranks // chips
+        (mine,) = call(
+            add_both_kernel, "share_sum", ((rows, LANES),), [], 4, (*shares, *step_shares),
+            "v" * (2 * chips),
         )
         got = [swapped(mine, "ctx", 2 * s) for s in range(1, chips)]
-        joined = call(
-            join_kernel, "joined", shape_of(chips, share, LANES), [],
-            8, (place, mine, *got), "s" + "v" * chips,
+        (joined,) = call(
+            join_kernel, "joined", ((chips, rows, LANES),), [],
+            8, (place, tokens_grad, mine, *got), "sh" + "v" * chips,
         )
         select_grad, step_grad = call(
-            outputs_kernel, "weight_grads",
-            (shape_of(2, width, LANES), shape_of(2, ranks, width)),
-            [vmem((2 * half, LANES))],
+            outputs_kernel, "weight_grads", ((2, width, LANES), (2, ranks, width)),
+            [vmem((2, tiles * ranks, LANES))],
             12, (place, joined, swapped(joined, "ctx", 1)), "svv",
         )
     else:
-        core = lax.rem(place[0], 2) == 0
-        both = jnp.where(core, jnp.stack([keep, send]), jnp.stack([send, keep]))
-        both = lax.psum(both, "ctx").reshape(2 * half, LANES)
-        select_grad = both[: 2 * width].reshape(2, width, LANES)
-        step_grad = both[2 * width :].reshape(2, tiles, ranks, LANES)
-        step_grad = step_grad.transpose(0, 2, 1, 3).reshape(2, ranks, width)
-    tokens_grad = call(
-        exit_kernel, "exit", shape_of(length, width),
-        [
-            vmem((length + HALO, width)), vmem((length + HALO, width)), vmem(conv_weight.shape),
-            dma(3),
-        ],
-        8, (before, after, conv_grad, conv_weight), "vvhh",
-    )
+        first = lax.rem(place[0], 2) == 0
+        order_of = lambda a, b: jnp.where(first, jnp.stack([a, b]), jnp.stack([b, a]))
+        sums = lax.psum((order_of(keep, send), order_of(step_keep, step_send)), "ctx")
+        select_grad = sums[0]
+        step_grad = sums[1].transpose(0, 2, 1, 3).reshape(2, ranks, width)
     return (block_out, tokens_grad, gate_grad, select_grad, step_grad)
 
 

time: 147 us -> 135 us (0.918)
  the two profiles are of different devices: /device:TPU:3 before, /device:TPU:0 now
where the time goes in v1:
time: 135 us
  Pallas kernels  54.3 us (40%)
  starting transfers between devices  45.1 us (33%)
  waiting for transfers between devices  33.7 us (25%)
    pallas_call x15, Pallas kernels, call(): pl.pallas_call(kernel, in_specs=[spaces[k] for k in kinds], out_specs=[sp...  54.3 us
    ppermute x28, starting transfers between devices, swapped(): return lax.ppermute(value, axis, [(i, i ^ by) for i in range(count)])  38.3 us
    ppermute x28, waiting for transfers between devices, swapped(): return lax.ppermute(value, axis, [(i, i ^ by) for i in range(count)])  29.6 us
    ppermute x2, starting transfers between devices, from_before(): return lax.ppermute(value, axis, [(i, i + 1) for i in range(count - 1)])  4.31 us
    ppermute x2, waiting for transfers between devices, from_after(): return lax.ppermute(value, axis, [(i + 1, i) for i in range(count - 1)])  3.28 us
  transfers between devices with their start and end apart: 32, of which 18 were waited for; matrix products, arithmetic and copies ran while one was open for 0% of the time, Pallas kernels for 2%

profile of v1, /device:TPU:0, one launch (start us, length us, event | category | flops | bytes accessed | tf_op | source)
XLA Modules:
  0.0 134.7 jit_solution(3918939156020555877)
XLA Ops:
  0.6 0.8 fusion
  1.4 1.3 collective-permute-start.1
  2.7 3.0 %collective-permute-start = (f32[8,768]{1,0:T(8,128)S(1)}, f32[8,768]{1,0:T(8,128)S(1)}, u32[]{:S(2)}, u32[]{:S(2)}) collective-permute-start(f32[8,768]{1,0:T(8,128)S(1)} %get-tuple-element.90), channel_id=1, source_target_pairs={{0,4},{4,8},{8,12},{12,16},{16,20},{20,24},{24,28},{1,5},{5,9},{9,... | collective-permute-start | bytes 73736 | tf_op jit(solution)/shard_map/ppermute | solution.py:670
  5.7 0.8 collective-permute-done.before
  6.6 2.7 %entry.1 = (f32[2,32,128]{2,1,0:T(8,128)S(1)}, f32[2,32,128]{2,1,0:T(8,128)S(1)}, f32[2,32,128]{2,1,0:T(8,128)S(1)}, f32[2,32,128]{2,1,0:T(8,128)S(1)}, f32[2,6,...) custom-call(s32[1]{0:T(128)} %bitcast.1.place.column, f32[8,768]{1,0:T(8,128)S(1)} %collective-permute-done.before, ...), custom_call_target="tpu_custom_call" | custom-call | flops 268435456 | bytes 4194304 | tf_op jit(solution)/shard_map/entry/pallas_call | solution.py:698
  9.3 3.1 %collective-permute-start.2 = (f32[2,32,128]{2,1,0:T(8,128)S(1)}, f32[2,32,128]{2,1,0:T(8,128)S(1)}, u32[]{:S(2)}, u32[]{:S(2)}) collective-permute-start(f32[2,32,128]{2,1,0:T(8,128)S(1)} %get-tuple-element.48), channel_id=1, source_target_pairs={{0,1},{1,0},{2,3},{3,2},{4,5},{5,4},{6,7},{7,6},{8,9},{9,8},{10,11... | collective-permute-start | bytes 98312 | tf_op jit(solution)/shard_map/ppermute | solution.py:680
  12.4 2.6 %collective-permute-start.3 = (f32[2,32,128]{2,1,0:T(8,128)S(1)}, f32[2,32,128]{2,1,0:T(8,128)S(1)}, u32[]{:S(2)}, u32[]{:S(2)}) collective-permute-start(f32[2,32,128]{2,1,0:T(8,128)S(1)} %get-tuple-element.49), channel_id=1, source_target_pairs={{0,2},{1,3},{2,0},{3,1},{4,6},{5,7},{6,4},{7,5},{8,10},{9,11},{10,... | collective-permute-start | bytes 98312 | tf_op jit(solution)/shard_map/ppermute | solution.py:680
  15.0 3.3 %collective-permute-done.3.refs_2_ = f32[2,32,128]{2,1,0:T(8,128)S(1)} collective-permute-done((f32[2,32,128]{2,1,0:T(8,128)S(1)}, f32[2,32,128]{2,1,0:T(8,128)S(1)}, u32[]{:S(2)}, u32[]{:S(2)}) %collective-permute-start.3) | collective-permute-done | bytes 32800 | tf_op jit(solution)/shard_map/ppermute | solution.py:680
  18.2 2.5 %collective-permute-done.4.refs_3_ = f32[2,32,128]{2,1,0:T(8,128)S(1)} collective-permute-done((f32[2,32,128]{2,1,0:T(8,128)S(1)}, f32[2,32,128]{2,1,0:T(8,128)S(1)}, u32[]{:S(2)}, u32[]{:S(2)}) %collective-permute-start.4) | collective-permute-done | bytes 32800 | tf_op jit(solution)/shard_map/ppermute | solution.py:680
  20.7 1.2 collective-permute-start.7
  21.9 3.3 %collective-permute-start.5 = (f32[2,32,128]{2,1,0:T(8,128)S(1)}, f32[2,32,128]{2,1,0:T(8,128)S(1)}, u32[]{:S(2)}, u32[]{:S(2)}) collective-permute-start(f32[2,32,128]{2,1,0:T(8,128)S(1)} %projection.1.own), channel_id=1, source_target_pairs={{0,1},{1,0},{2,3},{3,2},{4,5},{5,4},{6,7},{7,6},{8,9},{9,8},{10,11... | collective-permute-start | bytes 98312 | tf_op jit(solution)/shard_map/ppermute | solution.py:680
  25.2 1.5 %collective-permute-done.7.third = f32[2,32,128]{2,1,0:T(8,128)S(1)} collective-permute-done((f32[2,32,128]{2,1,0:T(8,128)S(1)}, f32[2,32,128]{2,1,0:T(8,128)S(1)}, u32[]{:S(2)}, u32[]{:S(2)}) %collective-permute-start.7) | collective-permute-done | bytes 32800 | tf_op jit(solution)/shard_map/ppermute | solution.py:680
  27.2 14.8 %local.1 = (f32[2,128,128]{2,1,0:T(8,128)}, f32[2,6,128,128]{3,2,1,0:T(8,128)}, f32[2,6,128,128]{3,2,1,0:T(8,128)}, f32[6,128,128]{2,1,0:T(8,128)}, f32[4,6,16,8...) custom-call(s32[1]{0:T(128)} %bitcast.1.place.column, ...), custom_call_target="tpu_custom_call" | custom-call | flops 268435456 | bytes 4194304 | tf_op jit(solution)/shard_map/local/pallas_call | solution.py:698
  42.1 1.5 %collective-permute-done.8.other = f32[2,6,40,128]{3,2,1,0:T(8,128)S(1)} collective-permute-done((f32[2,6,40,128]{3,2,1,0:T(8,128)S(1)}, f32[2,6,40,128]{3,2,1,0:T(8,128)S(1)}, u32[]{:S(2)}, u32[]{:S(2)}) %collective-permute-start.8) | collective-permute-done | bytes 245792 | tf_op jit(solution)/shard_map/ppermute | solution.py:680
  43.7 3.4 %collective-permute-start.9 = (f32[6,40,128]{2,1,0:T(8,128)S(1)}, f32[6,40,128]{2,1,0:T(8,128)S(1)}, u32[]{:S(2)}, u32[]{:S(2)}) collective-permute-start(f32[6,40,128]{2,1,0:T(8,128)S(1)} %get-tuple-element.54), channel_id=1, source_target_pairs={{0,8},{4,12},{8,0},{12,4},{16,24},{20,28},{24,16},{28,20},{1,9},{5... | collective-permute-start | bytes 368648 | tf_op jit(solution)/shard_map/ppermute | solution.py:680
  47.1 1.8 %collective-permute-start.10 = (f32[6,40,128]{2,1,0:T(8,128)S(1)}, f32[6,40,128]{2,1,0:T(8,128)S(1)}, u32[]{:S(2)}, u32[]{:S(2)}) collective-permute-start(f32[6,40,128]{2,1,0:T(8,128)S(1)} %get-tuple-element.55), channel_id=1, source_target_pairs={{0,16},{4,20},{8,24},{12,28},{16,0},{20,4},{24,8},{28,12},{1,17},{... | collective-permute-start | bytes 368648 | tf_op jit(solution)/shard_map/ppermute | solution.py:680
  48.9 1.4 %collective-permute-start.11 = (f32[6,40,128]{2,1,0:T(8,128)S(1)}, f32[6,40,128]{2,1,0:T(8,128)S(1)}, u32[]{:S(2)}, u32[]{:S(2)}) collective-permute-start(f32[6,40,128]{2,1,0:T(8,128)S(1)} %get-tuple-element.56), channel_id=1, source_target_pairs={{0,24},{4,28},{8,16},{12,20},{16,8},{20,12},{24,0},{28,4},{1,25},{... | collective-permute-start | bytes 368648 | tf_op jit(solution)/shard_map/ppermute | solution.py:680
  50.7 3.7 %collective-permute-done.10.refs_1_ = f32[6,40,128]{2,1,0:T(8,128)S(1)} collective-permute-done((f32[6,40,128]{2,1,0:T(8,128)S(1)}, f32[6,40,128]{2,1,0:T(8,128)S(1)}, u32[]{:S(2)}, u32[]{:S(2)}) %collective-permute-start.10) | collective-permute-done | bytes 122912 | tf_op jit(solution)/shard_map/ppermute | solution.py:680
  54.4 1.8 %collective-permute-done.11.refs_2_ = f32[6,40,128]{2,1,0:T(8,128)S(1)} collective-permute-done((f32[6,40,128]{2,1,0:T(8,128)S(1)}, f32[6,40,128]{2,1,0:T(8,128)S(1)}, u32[]{:S(2)}, u32[]{:S(2)}) %collective-permute-start.11) | collective-permute-done | bytes 122912 | tf_op jit(solution)/shard_map/ppermute | solution.py:680
  56.5 24.7 %scan.1 = (f32[2,32,128]{2,1,0:T(8,128)S(1)}, f32[2,32,128]{2,1,0:T(8,128)S(1)}, f32[2,32,128]{2,1,0:T(8,128)S(1)}, f32[2,32,128]{2,1,0:T(8,128)S(1)}, f32[2,6,1...) custom-call(s32[1]{0:T(128)} %bitcast.1.place.column, f32[2,6,32,128]{3,2,1,0:T(8,128)S(1)} %chain.1.incoming, ...), custom_call_target="tpu_custom_call" | custom-call | flops 268435456 | bytes 4194304 | tf_op jit(solution)/shard_map/scan/pallas_call | solution.py:698
  81.1 3.8 %outer.1 = (f32[128,768]{1,0:T(8,128)}, f32[128,768]{1,0:T(8,128)}, f32[6,96,128]{2,1,0:T(8,128)S(1)}, f32[6,96,128]{2,1,0:T(8,128)S(1)}) custom-call(s32[1]{0:T(128)} %bitcast.place, f32[6,128,128]{2,1,0:T(8,128)} %get-tuple-element.62.summed_in, f32[128,768]{1,0:T(8,128)} %gate_in.3, f32[128,768]{1,0:T(8,128)} %cot_in.3, ...), custom_call_target="tpu_custom_call" | custom-call | flops 268435456 | bytes 4194304 | tf_op jit(solution)/shard_map/outer/pallas_call | solution.py:698
  85.0 2.1 %collective-permute-start.12 = (f32[2,32,128]{2,1,0:T(8,128)S(1)}, f32[2,32,128]{2,1,0:T(8,128)S(1)}, u32[]{:S(2)}, u32[]{:S(2)}) collective-permute-start(f32[2,32,128]{2,1,0:T(8,128)S(1)} %get-tuple-element.66), channel_id=1, source_target_pairs={{0,1},{1,0},{2,3},{3,2},{4,5},{5,4},{6,7},{7,6},{8,9},{9,8},{10,11... | collective-permute-start | bytes 98312 | tf_op jit(solution)/shard_map/ppermute | solution.py:680
  87.1 0.9 collective-permute-start.13
  88.0 1.5 %collective-permute-start.14 = (f32[2,32,128]{2,1,0:T(8,128)S(1)}, f32[2,32,128]{2,1,0:T(8,128)S(1)}, u32[]{:S(2)}, u32[]{:S(2)}) collective-permute-start(f32[2,32,128]{2,1,0:T(8,128)S(1)} %get-tuple-element.68), channel_id=1, source_target_pairs={{0,3},{1,2},{2,1},{3,0},{4,7},{5,6},{6,5},{7,4},{8,11},{9,10},{10,... | collective-permute-start | bytes 98312 | tf_op jit(solution)/shard_map/ppermute | solution.py:680
  89.5 2.7 %collective-permute-done.13.refs_2_ = f32[2,32,128]{2,1,0:T(8,128)S(1)} collective-permute-done((f32[2,32,128]{2,1,0:T(8,128)S(1)}, f32[2,32,128]{2,1,0:T(8,128)S(1)}, u32[]{:S(2)}, u32[]{:S(2)}) %collective-permute-start.13) | collective-permute-done | bytes 32800 | tf_op jit(solution)/shard_map/ppermute | solution.py:680
  92.2 1.5 %collective-permute-done.14.refs_3_ = f32[2,32,128]{2,1,0:T(8,128)S(1)} collective-permute-done((f32[2,32,128]{2,1,0:T(8,128)S(1)}, f32[2,32,128]{2,1,0:T(8,128)S(1)}, u32[]{:S(2)}, u32[]{:S(2)}) %collective-permute-start.14) | collective-permute-done | bytes 32800 | tf_op jit(solution)/shard_map/ppermute | solution.py:680
  93.7 1.6 %collective-permute-start.17 = (f32[2,32,128]{2,1,0:T(8,128)S(1)}, f32[2,32,128]{2,1,0:T(8,128)S(1)}, u32[]{:S(2)}, u32[]{:S(2)}) collective-permute-start(f32[2,32,128]{2,1,0:T(8,128)S(1)} %grad_projection.1.own), channel_id=1, source_target_pairs={{0,3},{1,2},{2,1},{3,0},{4,7},{5,6},{6,5},{7,4},{8,11},{9,10},{10,... | collective-permute-start | bytes 98312 | tf_op jit(solution)/shard_map/ppermute | solution.py:680
  95.3 2.8 %collective-permute-start.15 = (f32[2,32,128]{2,1,0:T(8,128)S(1)}, f32[2,32,128]{2,1,0:T(8,128)S(1)}, u32[]{:S(2)}, u32[]{:S(2)}) collective-permute-start(f32[2,32,128]{2,1,0:T(8,128)S(1)} %grad_projection.1.own), channel_id=1, source_target_pairs={{0,1},{1,0},{2,3},{3,2},{4,5},{5,4},{6,7},{7,6},{8,9},{9,8},{10,11... | collective-permute-start | bytes 98312 | tf_op jit(solution)/shard_map/ppermute | solution.py:680
  98.2 1.3 collective-permute-done.17.third
  99.5 0.8 collective-permute-done.16.second
  100.4 4.2 %weights.1 = (f32[768,128]{1,0:T(8,128)S(1)}, f32[768,128]{1,0:T(8,128)S(1)}, f32[2,128,768]{2,1,0:T(8,128)}, f32[8,768]{1,0:T(8,128)S(1)}, f32[8,768]{1,0:T(8,128)S(1)}) custom-call(s32[1]{0:T(128)} %bitcast.place, s32[1]{0:T(128)} %bitcast.1.place.column, f32[2,32,128]{2,1,0:T(8,128)S(1)} %grad_projection.1.own, ...), custom_call_target="tpu_custom_call" | custom-call | flops 268435456 | bytes 4194304 | tf_op jit(solution)/shard_map/weights/pallas_call | solution.py:698
  104.7 0.6 collective-permute-start.25
  105.3 1.1 collective-permute-done.21.got
  107.1 1.7 %collective-permute-start.23 = (f32[192,128]{1,0:T(8,128)S(1)}, f32[192,128]{1,0:T(8,128)S(1)}, u32[]{:S(2)}, u32[]{:S(2)}) collective-permute-start(f32[192,128]{1,0:T(8,128)S(1)} %get-tuple-element.82), channel_id=1, source_target_pairs={{0,16},{4,20},{8,24},{12,28},{16,0},{20,4},{24,8},{28,12},{1,17},{... | collective-permute-start | bytes 294920 | tf_op jit(solution)/shard_map/ppermute | solution.py:680
  108.8 1.2 collective-permute-start.24
  110.0 0.7 collective-permute-start.26
  110.7 1.4 %collective-permute-start.27 = (f32[144,128]{1,0:T(8,128)S(1)}, f32[144,128]{1,0:T(8,128)S(1)}, u32[]{:S(2)}, u32[]{:S(2)}) collective-permute-start(f32[144,128]{1,0:T(8,128)S(1)} %get-tuple-element.86), channel_id=1, source_target_pairs={{0,24},{4,28},{8,16},{12,20},{16,8},{20,12},{24,0},{28,4},{1,25},{... | collective-permute-start | bytes 221192 | tf_op jit(solution)/shard_map/ppermute | solution.py:680
  112.1 5.1 %collective-permute-done.26.refs_6_ = f32[144,128]{1,0:T(8,128)S(1)} collective-permute-done((f32[144,128]{1,0:T(8,128)S(1)}, f32[144,128]{1,0:T(8,128)S(1)}, u32[]{:S(2)}, u32[]{:S(2)}) %collective-permute-start.26) | collective-permute-done | bytes 73760 | tf_op jit(solution)/shard_map/ppermute | solution.py:680
  117.3 1.4 %collective-permute-start.30 = (f32[336,128]{1,0:T(8,128)S(1)}, f32[336,128]{1,0:T(8,128)S(1)}, u32[]{:S(2)}, u32[]{:S(2)}) collective-permute-start(f32[336,128]{1,0:T(8,128)S(1)} %share_sum.1.mine), channel_id=1, source_target_pairs={{0,24},{4,28},{8,16},{12,20},{16,8},{20,12},{24,0},{28,4},{1,25},{... | collective-permute-start | bytes 516104 | tf_op jit(solution)/shard_map/ppermute | solution.py:680
  118.7 1.3 %collective-permute-start.29 = (f32[336,128]{1,0:T(8,128)S(1)}, f32[336,128]{1,0:T(8,128)S(1)}, u32[]{:S(2)}, u32[]{:S(2)}) collective-permute-start(f32[336,128]{1,0:T(8,128)S(1)} %share_sum.1.mine), channel_id=1, source_target_pairs={{0,16},{4,20},{8,24},{12,28},{16,0},{20,4},{24,8},{28,12},{1,17},{... | collective-permute-start | bytes 516104 | tf_op jit(solution)/shard_map/ppermute | solution.py:680
  120.1 0.8 collective-permute-start.28
  120.8 1.3 collective-permute-start.19
  122.1 1.3 collective-permute-start.20
  123.4 3.3 %collective-permute-done.20.after = f32[8,768]{1,0:T(8,128)S(1)} collective-permute-done((f32[8,768]{1,0:T(8,128)S(1)}, f32[8,768]{1,0:T(8,128)S(1)}, u32[]{:S(2)}, u32[]{:S(2)}) %collective-permute-start.20) | collective-permute-done | bytes 24608 | tf_op jit(solution)/shard_map/ppermute | solution.py:675
  126.7 2.3 %exit.1.after_this = f32[128,768]{1,0:T(8,128)} custom-call(f32[8,768]{1,0:T(8,128)S(1)} %collective-permute-done.19.before, f32[8,768]{1,0:T(8,128)S(1)} %collective-permute-done.20.after, f32[2,128,768]{2,1,0:T(8,128)} %get-tuple-element.76.conv_grad, f32[2,4,768]{2,1,0:T(4,128)} %conv_weight_in.3), custom_call_target="tpu_custom_call" | custom-call | flops 268435456 | bytes 4194304 | tf_op jit(solution)/shard_map/exit/pallas_call | solution.py:698
  129.1 2.6 %collective-permute-start.31 = (f32[4,336,128]{2,1,0:T(8,128)S(1)}, f32[4,336,128]{2,1,0:T(8,128)S(1)}, u32[]{:S(2)}, u32[]{:S(2)}) collective-permute-start(f32[4,336,128]{2,1,0:T(8,128)S(1)} %joined.1.mine), channel_id=1, source_target_pairs={{0,4},{4,0},{8,12},{12,8},{16,20},{20,16},{24,28},{28,24},{1,5},{5... | collective-permute-start | bytes 2064392 | tf_op jit(solution)/shard_map/ppermute | solution.py:680
  131.7 1.8 %collective-permute-done.31.other = f32[4,336,128]{2,1,0:T(8,128)S(1)} collective-permute-done((f32[4,336,128]{2,1,0:T(8,128)S(1)}, f32[4,336,128]{2,1,0:T(8,128)S(1)}, u32[]{:S(2)}, u32[]{:S(2)}) %collective-permute-start.31) | collective-permute-done | bytes 688160 | tf_op jit(solution)/shard_map/ppermute | solution.py:680
  133.5 1.2 weight_grads.1
  (32 shorter events, 2.6 us)
Async XLA Ops:
  1.4 4.3 %collective-permute-start.1 = (f32[8,768]{1,0:T(8,128)S(1)}, f32[8,768]{1,0:T(8,128)S(1)}, u32[]{:S(2)}, u32[]{:S(2)}) collective-permute-start(f32[8,768]{1,0:T(8,128)S(1)} %get-tuple-element.89), channel_id=1, source_target_pairs={{4,0},{8,4},{12,8},{16,12},{20,16},{24,20},{28,24},{5,1},{9,5},{13... | collective-permute-start | bytes 73736 | tf_op jit(solution)/shard_map/ppermute | solution.py:675
  2.7 3.9 %collective-permute-start = (f32[8,768]{1,0:T(8,128)S(1)}, f32[8,768]{1,0:T(8,128)S(1)}, u32[]{:S(2)}, u32[]{:S(2)}) collective-permute-start(f32[8,768]{1,0:T(8,128)S(1)} %get-tuple-element.90), channel_id=1, source_target_pairs={{0,4},{4,8},{8,12},{12,16},{16,20},{20,24},{24,28},{1,5},{5,9},{9,... | collective-permute-start | bytes 73736 | tf_op jit(solution)/shard_map/ppermute | solution.py:670
  9.3 5.7 %collective-permute-start.2 = (f32[2,32,128]{2,1,0:T(8,128)S(1)}, f32[2,32,128]{2,1,0:T(8,128)S(1)}, u32[]{:S(2)}, u32[]{:S(2)}) collective-permute-start(f32[2,32,128]{2,1,0:T(8,128)S(1)} %get-tuple-element.48), channel_id=1, source_target_pairs={{0,1},{1,0},{2,3},{3,2},{4,5},{5,4},{6,7},{7,6},{8,9},{9,8},{10,11... | collective-permute-start | bytes 98312 | tf_op jit(solution)/shard_map/ppermute | solution.py:680
  12.4 5.9 %collective-permute-start.3 = (f32[2,32,128]{2,1,0:T(8,128)S(1)}, f32[2,32,128]{2,1,0:T(8,128)S(1)}, u32[]{:S(2)}, u32[]{:S(2)}) collective-permute-start(f32[2,32,128]{2,1,0:T(8,128)S(1)} %get-tuple-element.49), channel_id=1, source_target_pairs={{0,2},{1,3},{2,0},{3,1},{4,6},{5,7},{6,4},{7,5},{8,10},{9,11},{10,... | collective-permute-start | bytes 98312 | tf_op jit(solution)/shard_map/ppermute | solution.py:680
  15.0 5.7 %collective-permute-start.4 = (f32[2,32,128]{2,1,0:T(8,128)S(1)}, f32[2,32,128]{2,1,0:T(8,128)S(1)}, u32[]{:S(2)}, u32[]{:S(2)}) collective-permute-start(f32[2,32,128]{2,1,0:T(8,128)S(1)} %get-tuple-element.50), channel_id=1, source_target_pairs={{0,3},{1,2},{2,1},{3,0},{4,7},{5,6},{6,5},{7,4},{8,11},{9,10},{10,... | collective-permute-start | bytes 98312 | tf_op jit(solution)/shard_map/ppermute | solution.py:680
  20.7 6.0 %collective-permute-start.7 = (f32[2,32,128]{2,1,0:T(8,128)S(1)}, f32[2,32,128]{2,1,0:T(8,128)S(1)}, u32[]{:S(2)}, u32[]{:S(2)}) collective-permute-start(f32[2,32,128]{2,1,0:T(8,128)S(1)} %projection.1.own), channel_id=1, source_target_pairs={{0,3},{1,2},{2,1},{3,0},{4,7},{5,6},{6,5},{7,4},{8,11},{9,10},{10,... | collective-permute-start | bytes 98312 | tf_op jit(solution)/shard_map/ppermute | solution.py:680
  21.9 5.4 %collective-permute-start.6 = (f32[2,32,128]{2,1,0:T(8,128)S(1)}, f32[2,32,128]{2,1,0:T(8,128)S(1)}, u32[]{:S(2)}, u32[]{:S(2)}) collective-permute-start(f32[2,32,128]{2,1,0:T(8,128)S(1)} %projection.1.own), channel_id=1, source_target_pairs={{0,2},{1,3},{2,0},{3,1},{4,6},{5,7},{6,4},{7,5},{8,10},{9,11},{10,... | collective-permute-start | bytes 98312 | tf_op jit(solution)/shard_map/ppermute | solution.py:680
  21.9 5.4 %collective-permute-start.5 = (f32[2,32,128]{2,1,0:T(8,128)S(1)}, f32[2,32,128]{2,1,0:T(8,128)S(1)}, u32[]{:S(2)}, u32[]{:S(2)}) collective-permute-start(f32[2,32,128]{2,1,0:T(8,128)S(1)} %projection.1.own), channel_id=1, source_target_pairs={{0,1},{1,0},{2,3},{3,2},{4,5},{5,4},{6,7},{7,6},{8,9},{9,8},{10,11... | collective-permute-start | bytes 98312 | tf_op jit(solution)/shard_map/ppermute | solution.py:680
  42.0 1.6 %collective-permute-start.8 = (f32[2,6,40,128]{3,2,1,0:T(8,128)S(1)}, f32[2,6,40,128]{3,2,1,0:T(8,128)S(1)}, u32[]{:S(2)}, u32[]{:S(2)}) collective-permute-start(f32[2,6,40,128]{3,2,1,0:T(8,128)S(1)} %get-tuple-element.52.mine), channel_id=1, source_target_pairs={{0,4},{4,0},{8,12},{12,8},{16,20},{20,16},{24,28},{28,24},{1,5},{5... | collective-permute-start | bytes 737288 | tf_op jit(solution)/shard_map/ppermute | solution.py:680
  43.7 7.0 %collective-permute-start.9 = (f32[6,40,128]{2,1,0:T(8,128)S(1)}, f32[6,40,128]{2,1,0:T(8,128)S(1)}, u32[]{:S(2)}, u32[]{:S(2)}) collective-permute-start(f32[6,40,128]{2,1,0:T(8,128)S(1)} %get-tuple-element.54), channel_id=1, source_target_pairs={{0,8},{4,12},{8,0},{12,4},{16,24},{20,28},{24,16},{28,20},{1,9},{5... | collective-permute-start | bytes 368648 | tf_op jit(solution)/shard_map/ppermute | solution.py:680
  47.1 7.3 %collective-permute-start.10 = (f32[6,40,128]{2,1,0:T(8,128)S(1)}, f32[6,40,128]{2,1,0:T(8,128)S(1)}, u32[]{:S(2)}, u32[]{:S(2)}) collective-permute-start(f32[6,40,128]{2,1,0:T(8,128)S(1)} %get-tuple-element.55), channel_id=1, source_target_pairs={{0,16},{4,20},{8,24},{12,28},{16,0},{20,4},{24,8},{28,12},{1,17},{... | collective-permute-start | bytes 368648 | tf_op jit(solution)/shard_map/ppermute | solution.py:680
  48.9 7.4 %collective-permute-start.11 = (f32[6,40,128]{2,1,0:T(8,128)S(1)}, f32[6,40,128]{2,1,0:T(8,128)S(1)}, u32[]{:S(2)}, u32[]{:S(2)}) collective-permute-start(f32[6,40,128]{2,1,0:T(8,128)S(1)} %get-tuple-element.56), channel_id=1, source_target_pairs={{0,24},{4,28},{8,16},{12,20},{16,8},{20,12},{24,0},{28,4},{1,25},{... | collective-permute-start | bytes 368648 | tf_op jit(solution)/shard_map/ppermute | solution.py:680
  84.9 13.2 %collective-permute-start.18 = (f32[6,96,128]{2,1,0:T(8,128)S(1)}, f32[6,96,128]{2,1,0:T(8,128)S(1)}, u32[]{:S(2)}, u32[]{:S(2)}) collective-permute-start(f32[6,96,128]{2,1,0:T(8,128)S(1)} %get-tuple-element.72), channel_id=1, source_target_pairs={{0,4},{4,0},{8,12},{12,8},{16,20},{20,16},{24,28},{28,24},{1,5},{5... | collective-permute-start | bytes 884744 | tf_op jit(solution)/shard_map/ppermute | solution.py:680
  85.0 4.5 %collective-permute-start.12 = (f32[2,32,128]{2,1,0:T(8,128)S(1)}, f32[2,32,128]{2,1,0:T(8,128)S(1)}, u32[]{:S(2)}, u32[]{:S(2)}) collective-permute-start(f32[2,32,128]{2,1,0:T(8,128)S(1)} %get-tuple-element.66), channel_id=1, source_target_pairs={{0,1},{1,0},{2,3},{3,2},{4,5},{5,4},{6,7},{7,6},{8,9},{9,8},{10,11... | collective-permute-start | bytes 98312 | tf_op jit(solution)/shard_map/ppermute | solution.py:680
  87.1 5.1 %collective-permute-start.13 = (f32[2,32,128]{2,1,0:T(8,128)S(1)}, f32[2,32,128]{2,1,0:T(8,128)S(1)}, u32[]{:S(2)}, u32[]{:S(2)}) collective-permute-start(f32[2,32,128]{2,1,0:T(8,128)S(1)} %get-tuple-element.67), channel_id=1, source_target_pairs={{0,2},{1,3},{2,0},{3,1},{4,6},{5,7},{6,4},{7,5},{8,10},{9,11},{10,... | collective-permute-start | bytes 98312 | tf_op jit(solution)/shard_map/ppermute | solution.py:680
  88.0 5.7 %collective-permute-start.14 = (f32[2,32,128]{2,1,0:T(8,128)S(1)}, f32[2,32,128]{2,1,0:T(8,128)S(1)}, u32[]{:S(2)}, u32[]{:S(2)}) collective-permute-start(f32[2,32,128]{2,1,0:T(8,128)S(1)} %get-tuple-element.68), channel_id=1, source_target_pairs={{0,3},{1,2},{2,1},{3,0},{4,7},{5,6},{6,5},{7,4},{8,11},{9,10},{10,... | collective-permute-start | bytes 98312 | tf_op jit(solution)/shard_map/ppermute | solution.py:680
  93.7 5.8 %collective-permute-start.17 = (f32[2,32,128]{2,1,0:T(8,128)S(1)}, f32[2,32,128]{2,1,0:T(8,128)S(1)}, u32[]{:S(2)}, u32[]{:S(2)}) collective-permute-start(f32[2,32,128]{2,1,0:T(8,128)S(1)} %grad_projection.1.own), channel_id=1, source_target_pairs={{0,3},{1,2},{2,1},{3,0},{4,7},{5,6},{6,5},{7,4},{8,11},{9,10},{10,... | collective-permute-start | bytes 98312 | tf_op jit(solution)/shard_map/ppermute | solution.py:680
  95.3 5.0 %collective-permute-start.16 = (f32[2,32,128]{2,1,0:T(8,128)S(1)}, f32[2,32,128]{2,1,0:T(8,128)S(1)}, u32[]{:S(2)}, u32[]{:S(2)}) collective-permute-start(f32[2,32,128]{2,1,0:T(8,128)S(1)} %grad_projection.1.own), channel_id=1, source_target_pairs={{0,2},{1,3},{2,0},{3,1},{4,6},{5,7},{6,4},{7,5},{8,10},{9,11},{10,... | collective-permute-start | bytes 98312 | tf_op jit(solution)/shard_map/ppermute | solution.py:680
  95.3 5.1 %collective-permute-start.15 = (f32[2,32,128]{2,1,0:T(8,128)S(1)}, f32[2,32,128]{2,1,0:T(8,128)S(1)}, u32[]{:S(2)}, u32[]{:S(2)}) collective-permute-start(f32[2,32,128]{2,1,0:T(8,128)S(1)} %grad_projection.1.own), channel_id=1, source_target_pairs={{0,1},{1,0},{2,3},{3,2},{4,5},{5,4},{6,7},{7,6},{8,9},{9,8},{10,11... | collective-permute-start | bytes 98312 | tf_op jit(solution)/shard_map/ppermute | solution.py:680
  104.6 1.8 %collective-permute-start.21 = (f32[768,128]{1,0:T(8,128)S(1)}, f32[768,128]{1,0:T(8,128)S(1)}, u32[]{:S(2)}, u32[]{:S(2)}) collective-permute-start(f32[768,128]{1,0:T(8,128)S(1)} %get-tuple-element.79), channel_id=1, source_target_pairs={{0,4},{4,0},{8,12},{12,8},{16,20},{20,16},{24,28},{28,24},{1,5},{5... | collective-permute-start | bytes 1179656 | tf_op jit(solution)/shard_map/ppermute | solution.py:680
  104.7 6.0 %collective-permute-start.25 = (f32[144,128]{1,0:T(8,128)S(1)}, f32[144,128]{1,0:T(8,128)S(1)}, u32[]{:S(2)}, u32[]{:S(2)}) collective-permute-start(f32[144,128]{1,0:T(8,128)S(1)} %get-tuple-element.84), channel_id=1, source_target_pairs={{0,8},{4,12},{8,0},{12,4},{16,24},{20,28},{24,16},{28,20},{1,9},{5... | collective-permute-start | bytes 221192 | tf_op jit(solution)/shard_map/ppermute | solution.py:680
  106.5 10.7 %collective-permute-start.22 = (f32[192,128]{1,0:T(8,128)S(1)}, f32[192,128]{1,0:T(8,128)S(1)}, u32[]{:S(2)}, u32[]{:S(2)}) collective-permute-start(f32[192,128]{1,0:T(8,128)S(1)} %get-tuple-element.81), channel_id=1, source_target_pairs={{0,8},{4,12},{8,0},{12,4},{16,24},{20,28},{24,16},{28,20},{1,9},{5... | collective-permute-start | bytes 294920 | tf_op jit(solution)/shard_map/ppermute | solution.py:680
  107.1 10.1 %collective-permute-start.23 = (f32[192,128]{1,0:T(8,128)S(1)}, f32[192,128]{1,0:T(8,128)S(1)}, u32[]{:S(2)}, u32[]{:S(2)}) collective-permute-start(f32[192,128]{1,0:T(8,128)S(1)} %get-tuple-element.82), channel_id=1, source_target_pairs={{0,16},{4,20},{8,24},{12,28},{16,0},{20,4},{24,8},{28,12},{1,17},{... | collective-permute-start | bytes 294920 | tf_op jit(solution)/shard_map/ppermute | solution.py:680
  108.8 8.3 %collective-permute-start.24 = (f32[192,128]{1,0:T(8,128)S(1)}, f32[192,128]{1,0:T(8,128)S(1)}, u32[]{:S(2)}, u32[]{:S(2)}) collective-permute-start(f32[192,128]{1,0:T(8,128)S(1)} %get-tuple-element.83), channel_id=1, source_target_pairs={{0,24},{4,28},{8,16},{12,20},{16,8},{20,12},{24,0},{28,4},{1,25},{... | collective-permute-start | bytes 294920 | tf_op jit(solution)/shard_map/ppermute | solution.py:680
  110.0 7.2 %collective-permute-start.26 = (f32[144,128]{1,0:T(8,128)S(1)}, f32[144,128]{1,0:T(8,128)S(1)}, u32[]{:S(2)}, u32[]{:S(2)}) collective-permute-start(f32[144,128]{1,0:T(8,128)S(1)} %get-tuple-element.85), channel_id=1, source_target_pairs={{0,16},{4,20},{8,24},{12,28},{16,0},{20,4},{24,8},{28,12},{1,17},{... | collective-permute-start | bytes 221192 | tf_op jit(solution)/shard_map/ppermute | solution.py:680
  110.7 6.5 %collective-permute-start.27 = (f32[144,128]{1,0:T(8,128)S(1)}, f32[144,128]{1,0:T(8,128)S(1)}, u32[]{:S(2)}, u32[]{:S(2)}) collective-permute-start(f32[144,128]{1,0:T(8,128)S(1)} %get-tuple-element.86), channel_id=1, source_target_pairs={{0,24},{4,28},{8,16},{12,20},{16,8},{20,12},{24,0},{28,4},{1,25},{... | collective-permute-start | bytes 221192 | tf_op jit(solution)/shard_map/ppermute | solution.py:680
  117.3 11.7 %collective-permute-start.30 = (f32[336,128]{1,0:T(8,128)S(1)}, f32[336,128]{1,0:T(8,128)S(1)}, u32[]{:S(2)}, u32[]{:S(2)}) collective-permute-start(f32[336,128]{1,0:T(8,128)S(1)} %share_sum.1.mine), channel_id=1, source_target_pairs={{0,24},{4,28},{8,16},{12,20},{16,8},{20,12},{24,0},{28,4},{1,25},{... | collective-permute-start | bytes 516104 | tf_op jit(solution)/shard_map/ppermute | solution.py:680
  118.7 10.3 %collective-permute-start.29 = (f32[336,128]{1,0:T(8,128)S(1)}, f32[336,128]{1,0:T(8,128)S(1)}, u32[]{:S(2)}, u32[]{:S(2)}) collective-permute-start(f32[336,128]{1,0:T(8,128)S(1)} %share_sum.1.mine), channel_id=1, source_target_pairs={{0,16},{4,20},{8,24},{12,28},{16,0},{20,4},{24,8},{28,12},{1,17},{... | collective-permute-start | bytes 516104 | tf_op jit(solution)/shard_map/ppermute | solution.py:680
  120.1 9.0 %collective-permute-start.28 = (f32[336,128]{1,0:T(8,128)S(1)}, f32[336,128]{1,0:T(8,128)S(1)}, u32[]{:S(2)}, u32[]{:S(2)}) collective-permute-start(f32[336,128]{1,0:T(8,128)S(1)} %share_sum.1.mine), channel_id=1, source_target_pairs={{0,8},{4,12},{8,0},{12,4},{16,24},{20,28},{24,16},{28,20},{1,9},{5... | collective-permute-start | bytes 516104 | tf_op jit(solution)/shard_map/ppermute | solution.py:680
  120.8 2.6 %collective-permute-start.19 = (f32[8,768]{1,0:T(8,128)S(1)}, f32[8,768]{1,0:T(8,128)S(1)}, u32[]{:S(2)}, u32[]{:S(2)}) collective-permute-start(f32[8,768]{1,0:T(8,128)S(1)} %get-tuple-element.74), channel_id=1, source_target_pairs={{0,4},{4,8},{8,12},{12,16},{16,20},{20,24},{24,28},{1,5},{5,9},{9,... | collective-permute-start | bytes 73736 | tf_op jit(solution)/shard_map/ppermute | solution.py:670
  122.1 4.6 %collective-permute-start.20 = (f32[8,768]{1,0:T(8,128)S(1)}, f32[8,768]{1,0:T(8,128)S(1)}, u32[]{:S(2)}, u32[]{:S(2)}) collective-permute-start(f32[8,768]{1,0:T(8,128)S(1)} %get-tuple-element.75), channel_id=1, source_target_pairs={{4,0},{8,4},{12,8},{16,12},{20,16},{24,20},{28,24},{5,1},{9,5},{13... | collective-permute-start | bytes 73736 | tf_op jit(solution)/shard_map/ppermute | solution.py:675
  129.1 4.4 %collective-permute-start.31 = (f32[4,336,128]{2,1,0:T(8,128)S(1)}, f32[4,336,128]{2,1,0:T(8,128)S(1)}, u32[]{:S(2)}, u32[]{:S(2)}) collective-permute-start(f32[4,336,128]{2,1,0:T(8,128)S(1)} %joined.1.mine), channel_id=1, source_target_pairs={{0,4},{4,0},{8,12},{12,8},{16,20},{20,16},{24,28},{28,24},{1,5},{5... | collective-permute-start | bytes 2064392 | tf_op jit(solution)/shard_map/ppermute | solution.py:680

commit v2 on v1

--- a/solution.py
+++ b/solution.py
@@ -62,6 +62,18 @@
     return copies
 
 
+def to_cells(tokens, cells):
+    count = tokens.shape[0] // CHAINS
+    for j in range(count):
+        cells[j * CHAINS : (j + 1) * CHAINS] = tokens[pl.ds(j, CHAINS, stride=count), :]
+
+
+def to_tokens(cells, tokens):
+    count = tokens.shape[0] // CHAINS
+    for j in range(count):
+        tokens[pl.ds(j, CHAINS, stride=count), :] = cells[j * CHAINS : (j + 1) * CHAINS]
+
+
 def finish_all(copies):
     for copy in copies:
         copy.wait()
@@ -71,8 +83,8 @@
     place, before, after, tokens, conv_weight_in, conv_bias_in, select_in,
     *refs,
 ):
-    outs, refs = refs[:-9], refs[-9:]
-    act_out, pre_out, ext, conv_weight, conv_bias, select, act, pre, sems = refs
+    outs, refs = refs[:-10], refs[-10:]
+    act_out, pre_out, ext, conv_weight, conv_bias, select, act, pre, plain, sems = refs
 
     length, width = tokens.shape
     loads = copies_of(
@@ -89,7 +101,8 @@
         for t in range(width // LANES):
             conv = convolved(ext, HALO, side, lane_tile(t), length, conv_weight, conv_bias)
             pre[side, t] = conv
-            act[side, t] = conv * jax.nn.sigmoid(conv)
+            plain[...] = conv * jax.nn.sigmoid(conv)
+            to_cells(plain, act.at[side, t])
     stores = copies_of([(pre, pre_out), (act, act_out)], sems.at[pl.ds(4, 2)])
     loads[3].wait()
     for side in range(2):
@@ -116,11 +129,9 @@
 
 
 def spread(projection, side, j, states, basis_b, basis_c):
-    length = basis_b.shape[0]
-    count = length // CHAINS
-    rows = projection[side, pl.ds(j, CHAINS, stride=count), :]
     ranks = LANES - 2 * states
     at = pl.ds(pl.multiple_of(j * CHAINS, CHAINS), CHAINS)
+    rows = projection[side, at, :]
     for n in range(states):
         b = rows[:, ranks + n : ranks + n + 1]
         c = rows[:, ranks + states + n : ranks + states + n + 1]
@@ -172,8 +183,8 @@
     return 2 if tiles % 2 == 0 else 1
 
 
-def unrolled(count, body, start):
-    times = 2 if count % 2 == 0 else 1
+def unrolled(count, times, body, start):
+    times = times if count % times == 0 else 1
 
     def several(i, state):
         for k in range(times):
@@ -187,10 +198,6 @@
     for g, t in enumerate(tiles):
         for n in range(rate_rows.shape[1]):
             rate_rows[g, n] = jnp.broadcast_to(rates[side, t, n : n + 1], (CHAINS, LANES))
-
-
-def token_rows(j, count):
-    return pl.ds(j, CHAINS, stride=count)
 
 
 def cell_rows(j):
@@ -202,7 +209,7 @@
     step_weight_in, step_bias_in, decay_log_in, act_in, gate_in, cot_in,
     projection_out, step_out, step_pre_out, grad_gated_out, entering_out, carry, row_rates,
     projection, act, step, step_pre, grad_gated, entering, step_weight, step_bias, decay_log,
-    gate, cot, rates, basis_b, basis_c, rate_rows, decays, sems,
+    gate, cot, plain, rates, basis_b, basis_c, rate_rows, decays, sems,
 ):
     sides, tiles, length, _ = act.shape
     states = decay_log.shape[1]
@@ -221,7 +228,8 @@
     for t in range(tiles):
         lanes = lane_tile(t)
         values = gate[:, lanes]
-        grad_gated[t] = cot[:, lanes] * values * jax.nn.sigmoid(values)
+        plain[...] = cot[:, lanes] * values * jax.nn.sigmoid(values)
+        to_cells(plain, grad_gated.at[t])
     fill_rates(decay_log, rates)
     for side in range(2):
         wide = dot(projection[side][:, :ranks], step_weight[side], (1, 0))
@@ -250,9 +258,9 @@
             def forward(i, current):
                 state, summed = current
                 j = order(i, count, up)
-                rows, at = token_rows(j, count), cell_rows(j)
-                steps = [step[side, t, rows, :] for t in at_tiles]
-                drives = [v * act[side, t, rows, :] for v, t in zip(steps, at_tiles)]
+                at = cell_rows(j)
+                steps = [step[side, t, at, :] for t in at_tiles]
+                drives = [v * act[side, t, at, :] for v, t in zip(steps, at_tiles)]
                 new = []
                 for n in range(states):
                     lanes = lane_tile(n)
@@ -264,12 +272,12 @@
                 return (tuple(new), tuple(a + v for a, v in zip(summed, steps)))
 
             start = ((zero,) * (states * group), (zero,) * group)
-            state, summed = unrolled(count, forward, start)
+            state, summed = unrolled(count, 4, forward, start)
 
             def retreat(i, state):
                 j = order(i, count, not up)
-                rows, at = token_rows(j, count), cell_rows(j)
-                grads = [grad_gated[t, rows, :] for t in at_tiles]
+                at = cell_rows(j)
+                grads = [grad_gated[t, at, :] for t in at_tiles]
                 new = []
                 for n in range(states):
                     lanes = lane_tile(n)
@@ -279,7 +287,7 @@
                         new.append(decays[g, at, lanes] * adjoint)
                 return tuple(new)
 
-            sent = unrolled(count, retreat, (zero,) * (states * group))
+            sent = unrolled(count, 4, retreat, (zero,) * (states * group))
             for g, t in enumerate(at_tiles):
                 across = [jnp.exp2(summed[g] * rate_rows[g, n]) for n in range(states)]
                 for kind, ends, upward in ((0, state, up), (1, sent, not up)):
@@ -403,9 +411,9 @@
             skips = [skip_rows[side, t] for t in at_tiles]
             sums = []
             for t in at_tiles:
-                summed = step[side, t, token_rows(0, count), :]
+                summed = step[side, t, cell_rows(0), :]
                 for j in range(1, count):
-                    summed = summed + step[side, t, token_rows(j, count), :]
+                    summed = summed + step[side, t, cell_rows(j), :]
                 sums.append(summed)
 
             def start(kind, upward):
@@ -429,10 +437,10 @@
 
             def forward(i, state):
                 j = order(i, count, up)
-                rows, at = token_rows(j, count), cell_rows(j)
-                steps = [step[side, t, rows, :] for t in at_tiles]
-                acts = [act[side, t, rows, :] for t in at_tiles]
-                grads = [grad_gated[t, rows, :] for t in at_tiles]
+                at = cell_rows(j)
+                steps = [step[side, t, at, :] for t in at_tiles]
+                acts = [act[side, t, at, :] for t in at_tiles]
+                grads = [grad_gated[t, at, :] for t in at_tiles]
                 drives = [v * a for v, a in zip(steps, acts)]
                 outs = [v * a for v, a in zip(skips, acts)]
                 new = []
@@ -452,19 +460,19 @@
                     grad_out[at, lanes] = read
                 for g, t in enumerate(at_tiles):
                     if side == 0:
-                        summed_out[t, rows, :] = outs[g]
+                        summed_out[t, at, :] = outs[g]
                     else:
-                        summed_out[t, rows, :] = summed_out[t, rows, :] + outs[g]
+                        summed_out[t, at, :] = summed_out[t, at, :] + outs[g]
                 return tuple(new)
 
-            unrolled(count, forward, start(0, up))
+            unrolled(count, 2, forward, start(0, up))
 
             def retreat(i, state):
                 j = order(i, count, not up)
-                rows, at = token_rows(j, count), cell_rows(j)
-                steps = [step[side, t, rows, :] for t in at_tiles]
-                acts = [act[side, t, rows, :] for t in at_tiles]
-                grads = [grad_gated[t, rows, :] for t in at_tiles]
+                at = cell_rows(j)
+                steps = [step[side, t, at, :] for t in at_tiles]
+                acts = [act[side, t, at, :] for t in at_tiles]
+                grads = [grad_gated[t, at, :] for t in at_tiles]
                 drives = [v * a for v, a in zip(steps, acts)]
                 step_terms = [zero] * group
                 drive_grads = [zero] * group
@@ -484,12 +492,12 @@
                     grad_in[at, lanes] = put
                 for g, t in enumerate(at_tiles):
                     grad_step = step_terms[g] * LN2 + drive_grads[g] * acts[g]
-                    grad_act[side, t, rows, :] = grads[g] * skips[g] + drive_grads[g] * steps[g]
-                    pre = step_pre[side, t, rows, :]
-                    grad_pre[side, t, rows, :] = grad_step * jax.nn.sigmoid(pre)
+                    grad_act[side, t, at, :] = grads[g] * skips[g] + drive_grads[g] * steps[g]
+                    pre = step_pre[side, t, at, :]
+                    grad_pre[side, t, at, :] = grad_step * jax.nn.sigmoid(pre)
                 return tuple(new)
 
-            unrolled(count, retreat, start(1, not up))
+            unrolled(count, 2, retreat, start(1, not up))
             return keep
 
         lax.fori_loop(0, tiles // group, some_tiles, 0)
@@ -505,13 +513,13 @@
         packed[...] = dot(wide, weights[...], (1, 1))
 
         def pack(j, keep):
-            rows, at = token_rows(j, count), cell_rows(j)
-            line = packed[rows, :]
+            at = cell_rows(j)
+            line = packed[at, :]
             for values, start_at in ((grad_in, ranks), (grad_out, ranks + states)):
                 for n in range(states):
                     total = jnp.sum(values[at, lane_tile(n)], axis=1, keepdims=True)
                     line = jnp.where(column == start_at + n, total, line)
-            packed[rows, :] = line
+            packed[at, :] = line
             return keep
 
         lax.fori_loop(0, count, pack, 0)
@@ -519,39 +527,32 @@
     finish_all(stores)
 
 
-def outer_kernel(
-    place, summed_in, gate_in, cot_in, grad_pre_in, projection_in, block_out, gate_grad, keep, send,
-    summed, gate, cot, grad_pre, projection, sems,
+def step_kernel(grad_pre_in, projection_in, after_this, step_part, grad_pre, projection, sems):
+    _, tiles, ranks, _ = step_part.shape
+    finish_all(copies_of([(grad_pre_in, grad_pre), (projection_in, projection)], sems))
+    for side in range(2):
+        wide = dot(projection[side], full_width(grad_pre, side), (0, 0))
+        for t in range(tiles):
+            step_part[side, t] = wide[:ranks, lane_tile(t)]
+
+
+def gate_kernel(
+    summed_in, gate_in, cot_in, after_this, block_out, gate_grad, summed, gate, cot, plain, sems
 ):
-    tiles = summed.shape[0]
-    ranks = keep.shape[1]
-    loads = copies_of(
-        [
-            (summed_in, summed), (gate_in, gate), (cot_in, cot), (grad_pre_in, grad_pre),
-            (projection_in, projection),
-        ],
-        sems,
-    )
-    finish_all(loads)
-    for t in range(tiles):
+    finish_all(copies_of([(summed_in, summed), (gate_in, gate), (cot_in, cot)], sems))
+    for t in range(summed.shape[0]):
         lanes = lane_tile(t)
         values = gate[:, lanes]
-        block_out[:, lanes] = summed[t] * values * jax.nn.sigmoid(values)
-        gate_grad[:, lanes] = cot[:, lanes] * summed[t] * silu_grad(values)
-    for side in range(2):
-        wide = dot(projection[side], full_width(grad_pre, side), (0, 0))
-        for out, core in ((keep, side), (send, 1 - side)):
-
-            @pl.when(lax.rem(place[0], 2) == core)
-            def _():
-                for t in range(tiles):
-                    out[t] = wide[:ranks, lane_tile(t)]
+        to_tokens(summed.at[t], plain)
+        both = plain[...]
+        block_out[:, lanes] = both * values * jax.nn.sigmoid(values)
+        gate_grad[:, lanes] = cot[:, lanes] * both * silu_grad(values)
 
 
 def weight_kernel(
-    place, column, own, first, second, third, act_in, pre_in, grad_act_in, select_in, after_this,
+    place, column, own, first, second, third, act_in, pre_in, grad_act_in, select_in, step_part,
     keep, send, conv_grad_out, head, tail,
-    act, pre, grad_act, select, grad, both, conv_grad, sems,
+    act, pre, grad_act, select, grad, both, conv_grad, plain, sems,
 ):
     sides, tiles, length, _ = act.shape
     loads = copies_of(
@@ -563,7 +564,8 @@
     collect(column, (own, first, second, third), grad)
     loads[0].wait()
     for side in range(2):
-        both[side] = dot(full_width(act, side), grad[side], (0, 0))
+        both[side, : tiles * LANES] = dot(full_width(act, side), grad[side], (0, 0))
+        both[side, tiles * LANES :] = step_part[side].reshape(-1, LANES)
     core = lax.rem(place[0], 2)
     stores = copies_of(
         [(both.at[core], keep), (both.at[1 - core], send)], sems.at[pl.ds(4, 2)]
@@ -573,8 +575,9 @@
         wide = dot(grad[side], select[side], (1, 1))
         for t in range(tiles):
             lanes = lane_tile(t)
-            total = grad_act[side, t] + wide[:, lanes]
-            conv_grad[side, :, lanes] = total * silu_grad(pre[side, t])
+            grad_act[side, t] = grad_act[side, t] + wide[:, lanes]
+            to_tokens(grad_act.at[side, t], plain)
+            conv_grad[side, :, lanes] = plain[...] * silu_grad(pre[side, t])
     head[...] = conv_grad[0, :HALO]
     tail[...] = conv_grad[1, length - HALO :]
     stores = stores + copies_of([(conv_grad, conv_grad_out)], sems.at[pl.ds(0, 1)])
@@ -594,23 +597,15 @@
         out[...] = total[chip ^ s]
 
 
+def add_after_kernel(after_this, *refs):
+    add_kernel(*refs)
+
+
 def add_kernel(*refs):
     total = refs[0][...]
     for ref in refs[1:-1]:
         total = total + ref[...]
     refs[-1][...] = total
-
-
-def add_both_kernel(*refs):
-    parts, out = refs[:-1], refs[-1]
-    count = len(parts) // 2
-    at = 0
-    for some in (parts[:count], parts[count:]):
-        total = some[0][...]
-        for ref in some[1:]:
-            total = total + ref[...]
-        out[at : at + total.shape[0]] = total
-        at += total.shape[0]
 
 
 def join_kernel(place, after_this, mine, *refs):
@@ -626,19 +621,18 @@
     ranks = step_grad.shape[1]
     chips = mine.shape[0]
     core = lax.rem(place[0], 2)
-    part = width // chips
-    flat = both.shape[1] // chips
+    size = mine.shape[1]
     for side in range(2):
         for k in range(chips):
-            rows = jnp.where(core == side, mine[k], other[k])
-            select_grad[side, k * part : (k + 1) * part] = rows[:part]
-            both[side, k * flat : (k + 1) * flat] = rows[part:]
+            both[side, k * size : (k + 1) * size] = jnp.where(core == side, mine[k], other[k])
+        select_grad[side] = both[side, :width]
         for t in range(width // LANES):
-            step_grad[side, :, lane_tile(t)] = both[side, t * ranks : (t + 1) * ranks]
+            at = width + t * ranks
+            step_grad[side, :, lane_tile(t)] = both[side, at : at + ranks]
 
 
 def exit_kernel(
-    before, after, conv_grad, conv_weight_in, tokens_grad, up, down, conv_weight, sems
+    before, after, conv_grad, conv_weight_in, after_this, tokens_grad, up, down, conv_weight, sems
 ):
     _, length, width = conv_grad.shape
     taps = conv_weight.shape[1]
@@ -710,10 +704,10 @@
 def summed_shares(parts, name):
     count = len(parts)
     if count == 1:
-        return (lax.psum(parts[0], "ch"),)
+        return (lax.psum(parts[0], "ch"),), parts[0]
     got = [swapped(part, "ch", s) for s, part in enumerate(parts[1:], 1)]
     (mine,) = call(add_kernel, name, (parts[0].shape,), [], 4, (parts[0], *got), "v" * count)
-    return (mine, *(swapped(mine, "ch", s) for s in range(1, count)))
+    return (mine, *(swapped(mine, "ch", s) for s in range(1, count))), got[0]
 
 
 def halved(place, keep, send, rows, chips, name):
@@ -721,7 +715,7 @@
     share = rows // chips
     mine, *sent = call(
         halves_kernel, name, ((share, LANES),) * chips, [pltpu.VMEM((chips, share, LANES), jnp.float32)],
-        8, (place, keep.reshape(rows, LANES), got.reshape(rows, LANES)), "svv",
+        8, (place, keep, got), "svv",
     )
     return (mine, *(swapped(part, "ctx", 2 * s) for s, part in enumerate(sent, 1)))
 
@@ -762,7 +756,7 @@
         entry_kernel, "entry", (*(shared,) * columns, pair, pair),
         [
             vmem((length + 2 * HALO, width)), vmem(conv_weight.shape), vmem(conv_bias.shape),
-            vmem(select_weight.shape), vmem(pair), vmem(pair), dma(6),
+            vmem(select_weight.shape), vmem(pair), vmem(pair), vmem(one[1:]), dma(6),
         ],
         12, (column, before, after, tokens, conv_weight, conv_bias, select_weight), "svvhhhh",
         "v" * columns + "hh",
@@ -772,12 +766,12 @@
         [
             vmem(narrow), vmem(pair), vmem(pair), vmem(pair), vmem(one), vmem(chain_ends),
             vmem(step_weight.shape), vmem(step_bias.shape), vmem(decay_log.shape),
-            vmem(flat), vmem(flat),
+            vmem(flat), vmem(flat), vmem(one[1:]),
             rate_scratch, bases, bases, row_scratch, grouped, dma(6),
         ],
         24,
         (
-            column, *summed_shares(parts, "projection"), step_weight, step_bias, decay_log, act,
+            column, *summed_shares(parts, "projection")[0], step_weight, step_bias, decay_log, act,
             gate_input, cotangent,
         ),
         "svvvvhhhhhh", "hhhhhvv",
@@ -815,61 +809,68 @@
         ),
         "svhhhhhhhhh", "v" * columns + "hhh",
     )
-    grad_shares = summed_shares(grad_parts, "grad_projection")
-    block_out, gate_grad, step_keep, step_send = call(
-        outer_kernel, "outer", (flat, flat, (tiles, ranks, LANES), (tiles, ranks, LANES)),
-        [vmem(one), vmem(flat), vmem(flat), vmem(pair), vmem(narrow), dma(5)],
-        12, (place, summed, gate_input, cotangent, grad_pre, projection), "shhhhh",
-    )
-    if near:
-        step_shares = halved(place, step_keep, step_send, tiles * ranks, chips, "step_halves")
-        ahead = step_shares[0]
-    else:
-        ahead = step_keep
+    grad_shares, arrived = summed_shares(grad_parts, "grad_projection")
+    (step_part,) = call(
+        step_kernel, "step_grad", ((2, tiles, ranks, LANES),), [vmem(pair), vmem(narrow), dma(2)],
+        8, (grad_pre, projection, arrived), "hhv",
+    )
+    half = width + tiles * ranks
     keep, send, conv_grad, head, tail = call(
         weight_kernel, "weights",
-        ((width, LANES), (width, LANES), (2, *flat), (HALO, width), (HALO, width)),
+        ((half, LANES), (half, LANES), (2, *flat), (HALO, width), (HALO, width)),
         [
             vmem(pair), vmem(pair), vmem(pair), vmem(select_weight.shape), vmem(narrow),
-            vmem(select_weight.shape), vmem((2, *flat)), dma(6),
+            vmem((2, half, LANES)), vmem((2, *flat)), vmem(one[1:]), dma(6),
         ],
         16,
-        (place, column, *grad_shares, act, pre, grad_act, select_weight, ahead),
+        (place, column, *grad_shares, act, pre, grad_act, select_weight, step_part),
         "ssvvvvhhhhv", "vvhvv",
     )
     before = from_before(tail, "ctx")
     after = from_after(head, "ctx")
+    if near:
+        shares = halved(place, keep, send, half, chips, "halves")
+        ahead = shares[0]
+    else:
+        ahead = head
     (tokens_grad,) = call(
         exit_kernel, "exit", (flat,),
         [
             vmem((length + HALO, width)), vmem((length + HALO, width)), vmem(conv_weight.shape),
             dma(3),
         ],
-        8, (before, after, conv_grad, conv_weight), "vvhh",
+        8, (before, after, conv_grad, conv_weight, ahead), "vvhhv",
     )
     if near:
-        shares = halved(place, keep, send, width, chips, "select_halves")
-        rows = width // chips + tiles * ranks // chips
+        rows = half // chips
         (mine,) = call(
-            add_both_kernel, "share_sum", ((rows, LANES),), [], 4, (*shares, *step_shares),
-            "v" * (2 * chips),
+            add_after_kernel, "share_sum", ((rows, LANES),), [], 4, (tokens_grad, *shares),
+            "h" + "v" * chips,
         )
+        ahead = mine
+    block_out, gate_grad = call(
+        gate_kernel, "gate", (flat, flat),
+        [vmem(one), vmem(flat), vmem(flat), vmem(one[1:]), dma(3)],
+        8, (summed, gate_input, cotangent, ahead), "hhhv",
+    )
+    if near:
         got = [swapped(mine, "ctx", 2 * s) for s in range(1, chips)]
         (joined,) = call(
             join_kernel, "joined", ((chips, rows, LANES),), [],
-            8, (place, tokens_grad, mine, *got), "sh" + "v" * chips,
+            8, (place, block_out, mine, *got), "sh" + "v" * chips,
         )
         select_grad, step_grad = call(
             outputs_kernel, "weight_grads", ((2, width, LANES), (2, ranks, width)),
-            [vmem((2, tiles * ranks, LANES))],
+            [vmem((2, half, LANES))],
             12, (place, joined, swapped(joined, "ctx", 1)), "svv",
         )
     else:
         first = lax.rem(place[0], 2) == 0
-        order_of = lambda a, b: jnp.where(first, jnp.stack([a, b]), jnp.stack([b, a]))
-        sums = lax.psum((order_of(keep, send), order_of(step_keep, step_send)), "ctx")
-        select_grad = sums[0]
-        step_grad = sums[1].transpose(0, 2, 1, 3).reshape(2, ranks, width)
+        both = jnp.where(first, jnp.stack([keep, send]), jnp.stack([send, keep]))
+        both = lax.psum(both, "ctx")
+        select_grad = both[:, :width]
+        step_grad = both[:, width:].reshape(2, tiles, ranks, LANES)
+        step_grad = step_grad.transpose(0, 2, 1, 3).reshape(2, ranks, width)
     return (block_out, tokens_grad, gate_grad, select_grad, step_grad)
 
 

time: 135 us -> 129 us (0.956)
  starting transfers between devices: 45.1 us -> 41.4 us
  Pallas kernels: 54.3 us -> 51.6 us
    ppermute x28 -> x24, starting transfers between devices: 38.3 us -> 34.5 us  [swapped(): return lax.ppermute(value, axis, [(i, i ^ by) for i in range(count)])]
    pallas_call x15, Pallas kernels: 54.3 us -> 51.6 us  [call(): pl.pallas_call(kernel, in_specs=[spaces[k] for k in kinds], out_specs=[sp...]
    ppermute x28 -> x24, waiting for transfers between devices: 29.6 us -> 30.5 us  [swapped(): return lax.ppermute(value, axis, [(i, i ^ by) for i in range(count)])]
  transfers between devices with their start and end apart: 32 -> 28, of which waited for: 18 -> 19; matrix products, arithmetic and copies ran while one was open for 0% -> 0% of each run, Pallas kernels for 2% -> 5%
where the time goes in v2:
time: 129 us; the launch traced here: 128 us
  Pallas kernels  51.6 us (40%)
  starting transfers between devices  41.4 us (32%)
  waiting for transfers between devices  33.8 us (26%)
    pallas_call x15, Pallas kernels, call(): pl.pallas_call(kernel, in_specs=[spaces[k] for k in kinds], out_specs=[sp...  51.6 us
    ppermute x24, starting transfers between devices, swapped(): return lax.ppermute(value, axis, [(i, i ^ by) for i in range(count)])  34.5 us
    ppermute x24, waiting for transfers between devices, swapped(): return lax.ppermute(value, axis, [(i, i ^ by) for i in range(count)])  30.5 us
    ppermute x2, starting transfers between devices, from_before(): return lax.ppermute(value, axis, [(i, i + 1) for i in range(count - 1)])  4.31 us
  transfers between devices with their start and end apart: 28, of which 19 were waited for; matrix products, arithmetic and copies ran while one was open for 0% of the time, Pallas kernels for 5%

profile of v2, /device:TPU:0, one launch (start us, length us, event | category | flops | bytes accessed | tf_op | source)
XLA Modules:
  0.0 128.4 jit_solution(11705355371472585596)
XLA Ops:
  0.6 0.8 fusion
  1.4 1.3 collective-permute-start.1
  2.7 3.0 %collective-permute-start = (f32[8,768]{1,0:T(8,128)S(1)}, f32[8,768]{1,0:T(8,128)S(1)}, u32[]{:S(2)}, u32[]{:S(2)}) collective-permute-start(f32[8,768]{1,0:T(8,128)S(1)} %get-tuple-element.78), channel_id=1, source_target_pairs={{0,4},{4,8},{8,12},{12,16},{16,20},{20,24},{24,28},{1,5},{5,9},{9,... | collective-permute-start | bytes 73736 | tf_op jit(solution)/shard_map/ppermute | solution.py:664
  5.7 0.8 collective-permute-done.before
  6.6 2.9 %entry.1 = (f32[2,32,128]{2,1,0:T(8,128)S(1)}, f32[2,32,128]{2,1,0:T(8,128)S(1)}, f32[2,32,128]{2,1,0:T(8,128)S(1)}, f32[2,32,128]{2,1,0:T(8,128)S(1)}, f32[2,6,...) custom-call(s32[1]{0:T(128)} %bitcast.place.column, f32[8,768]{1,0:T(8,128)S(1)} %collective-permute-done.before, ...), custom_call_target="tpu_custom_call" | custom-call | flops 268435456 | bytes 4194304 | tf_op jit(solution)/shard_map/entry/pallas_call | solution.py:692
  9.5 3.1 %collective-permute-start.2 = (f32[2,32,128]{2,1,0:T(8,128)S(1)}, f32[2,32,128]{2,1,0:T(8,128)S(1)}, u32[]{:S(2)}, u32[]{:S(2)}) collective-permute-start(f32[2,32,128]{2,1,0:T(8,128)S(1)} %get-tuple-element.42), channel_id=1, source_target_pairs={{0,1},{1,0},{2,3},{3,2},{4,5},{5,4},{6,7},{7,6},{8,9},{9,8},{10,11... | collective-permute-start | bytes 98312 | tf_op jit(solution)/shard_map/ppermute | solution.py:674
  12.6 2.6 %collective-permute-start.3 = (f32[2,32,128]{2,1,0:T(8,128)S(1)}, f32[2,32,128]{2,1,0:T(8,128)S(1)}, u32[]{:S(2)}, u32[]{:S(2)}) collective-permute-start(f32[2,32,128]{2,1,0:T(8,128)S(1)} %get-tuple-element.43), channel_id=1, source_target_pairs={{0,2},{1,3},{2,0},{3,1},{4,6},{5,7},{6,4},{7,5},{8,10},{9,11},{10,... | collective-permute-start | bytes 98312 | tf_op jit(solution)/shard_map/ppermute | solution.py:674
  15.2 3.3 %collective-permute-done.3.refs_2_ = f32[2,32,128]{2,1,0:T(8,128)S(1)} collective-permute-done((f32[2,32,128]{2,1,0:T(8,128)S(1)}, f32[2,32,128]{2,1,0:T(8,128)S(1)}, u32[]{:S(2)}, u32[]{:S(2)}) %collective-permute-start.3) | collective-permute-done | bytes 32800 | tf_op jit(solution)/shard_map/ppermute | solution.py:674
  18.4 2.5 %collective-permute-done.4.refs_3_ = f32[2,32,128]{2,1,0:T(8,128)S(1)} collective-permute-done((f32[2,32,128]{2,1,0:T(8,128)S(1)}, f32[2,32,128]{2,1,0:T(8,128)S(1)}, u32[]{:S(2)}, u32[]{:S(2)}) %collective-permute-start.4) | collective-permute-done | bytes 32800 | tf_op jit(solution)/shard_map/ppermute | solution.py:674
  20.9 1.2 collective-permute-start.7
  22.1 3.3 %collective-permute-start.5 = (f32[2,32,128]{2,1,0:T(8,128)S(1)}, f32[2,32,128]{2,1,0:T(8,128)S(1)}, u32[]{:S(2)}, u32[]{:S(2)}) collective-permute-start(f32[2,32,128]{2,1,0:T(8,128)S(1)} %projection.1.own), channel_id=1, source_target_pairs={{0,1},{1,0},{2,3},{3,2},{4,5},{5,4},{6,7},{7,6},{8,9},{9,8},{10,11... | collective-permute-start | bytes 98312 | tf_op jit(solution)/shard_map/ppermute | solution.py:674
  25.4 1.5 %collective-permute-done.7.third = f32[2,32,128]{2,1,0:T(8,128)S(1)} collective-permute-done((f32[2,32,128]{2,1,0:T(8,128)S(1)}, f32[2,32,128]{2,1,0:T(8,128)S(1)}, u32[]{:S(2)}, u32[]{:S(2)}) %collective-permute-start.7) | collective-permute-done | bytes 32800 | tf_op jit(solution)/shard_map/ppermute | solution.py:674
  26.9 0.5 collective-permute-done.6.second
  27.4 13.8 %local.1 = (f32[2,128,128]{2,1,0:T(8,128)}, f32[2,6,128,128]{3,2,1,0:T(8,128)}, f32[2,6,128,128]{3,2,1,0:T(8,128)}, f32[6,128,128]{2,1,0:T(8,128)}, f32[4,6,16,8...) custom-call(s32[1]{0:T(128)} %bitcast.place.column, f32[2,32,128]{2,1,0:T(8,128)S(1)} %projection.1.own, ...), custom_call_target="tpu_custom_call" | custom-call | flops 268435456 | bytes 4194304 | tf_op jit(solution)/shard_map/local/pallas_call | solution.py:692
  41.3 1.5 %collective-permute-done.8.other = f32[2,6,40,128]{3,2,1,0:T(8,128)S(1)} collective-permute-done((f32[2,6,40,128]{3,2,1,0:T(8,128)S(1)}, f32[2,6,40,128]{3,2,1,0:T(8,128)S(1)}, u32[]{:S(2)}, u32[]{:S(2)}) %collective-permute-start.8) | collective-permute-done | bytes 245792 | tf_op jit(solution)/shard_map/ppermute | solution.py:674
  42.9 3.4 %collective-permute-start.9 = (f32[6,40,128]{2,1,0:T(8,128)S(1)}, f32[6,40,128]{2,1,0:T(8,128)S(1)}, u32[]{:S(2)}, u32[]{:S(2)}) collective-permute-start(f32[6,40,128]{2,1,0:T(8,128)S(1)} %get-tuple-element.48), channel_id=1, source_target_pairs={{0,8},{4,12},{8,0},{12,4},{16,24},{20,28},{24,16},{28,20},{1,9},{5... | collective-permute-start | bytes 368648 | tf_op jit(solution)/shard_map/ppermute | solution.py:674
  46.3 1.8 %collective-permute-start.10 = (f32[6,40,128]{2,1,0:T(8,128)S(1)}, f32[6,40,128]{2,1,0:T(8,128)S(1)}, u32[]{:S(2)}, u32[]{:S(2)}) collective-permute-start(f32[6,40,128]{2,1,0:T(8,128)S(1)} %get-tuple-element.49), channel_id=1, source_target_pairs={{0,16},{4,20},{8,24},{12,28},{16,0},{20,4},{24,8},{28,12},{1,17},{... | collective-permute-start | bytes 368648 | tf_op jit(solution)/shard_map/ppermute | solution.py:674
  48.1 1.4 %collective-permute-start.11 = (f32[6,40,128]{2,1,0:T(8,128)S(1)}, f32[6,40,128]{2,1,0:T(8,128)S(1)}, u32[]{:S(2)}, u32[]{:S(2)}) collective-permute-start(f32[6,40,128]{2,1,0:T(8,128)S(1)} %get-tuple-element.50), channel_id=1, source_target_pairs={{0,24},{4,28},{8,16},{12,20},{16,8},{20,12},{24,0},{28,4},{1,25},{... | collective-permute-start | bytes 368648 | tf_op jit(solution)/shard_map/ppermute | solution.py:674
  49.5 0.5 collective-permute-done.9.refs_0_
  49.9 3.7 %collective-permute-done.10.refs_1_ = f32[6,40,128]{2,1,0:T(8,128)S(1)} collective-permute-done((f32[6,40,128]{2,1,0:T(8,128)S(1)}, f32[6,40,128]{2,1,0:T(8,128)S(1)}, u32[]{:S(2)}, u32[]{:S(2)}) %collective-permute-start.10) | collective-permute-done | bytes 122912 | tf_op jit(solution)/shard_map/ppermute | solution.py:674
  53.6 1.8 %collective-permute-done.11.refs_2_ = f32[6,40,128]{2,1,0:T(8,128)S(1)} collective-permute-done((f32[6,40,128]{2,1,0:T(8,128)S(1)}, f32[6,40,128]{2,1,0:T(8,128)S(1)}, u32[]{:S(2)}, u32[]{:S(2)}) %collective-permute-start.11) | collective-permute-done | bytes 122912 | tf_op jit(solution)/shard_map/ppermute | solution.py:674
  55.4 0.2 chain.1.incoming
  55.7 21.8 %scan.1 = (f32[2,32,128]{2,1,0:T(8,128)S(1)}, f32[2,32,128]{2,1,0:T(8,128)S(1)}, f32[2,32,128]{2,1,0:T(8,128)S(1)}, f32[2,32,128]{2,1,0:T(8,128)S(1)}, f32[2,6,1...) custom-call(s32[1]{0:T(128)} %bitcast.place.column, f32[2,6,32,128]{3,2,1,0:T(8,128)S(1)} %chain.1.incoming, ...), custom_call_target="tpu_custom_call" | custom-call | flops 268435456 | bytes 4194304 | tf_op jit(solution)/shard_map/scan/pallas_call | solution.py:692
  77.5 2.1 %collective-permute-start.12 = (f32[2,32,128]{2,1,0:T(8,128)S(1)}, f32[2,32,128]{2,1,0:T(8,128)S(1)}, u32[]{:S(2)}, u32[]{:S(2)}) collective-permute-start(f32[2,32,128]{2,1,0:T(8,128)S(1)} %get-tuple-element.58), channel_id=1, source_target_pairs={{0,1},{1,0},{2,3},{3,2},{4,5},{5,4},{6,7},{7,6},{8,9},{9,8},{10,11... | collective-permute-start | bytes 98312 | tf_op jit(solution)/shard_map/ppermute | solution.py:674
  79.6 0.9 collective-permute-start.13
  80.5 1.5 %collective-permute-start.14 = (f32[2,32,128]{2,1,0:T(8,128)S(1)}, f32[2,32,128]{2,1,0:T(8,128)S(1)}, u32[]{:S(2)}, u32[]{:S(2)}) collective-permute-start(f32[2,32,128]{2,1,0:T(8,128)S(1)} %get-tuple-element.60), channel_id=1, source_target_pairs={{0,3},{1,2},{2,1},{3,0},{4,7},{5,6},{6,5},{7,4},{8,11},{9,10},{10,... | collective-permute-start | bytes 98312 | tf_op jit(solution)/shard_map/ppermute | solution.py:674
  82.0 2.6 %collective-permute-done.13.refs_2_ = f32[2,32,128]{2,1,0:T(8,128)S(1)} collective-permute-done((f32[2,32,128]{2,1,0:T(8,128)S(1)}, f32[2,32,128]{2,1,0:T(8,128)S(1)}, u32[]{:S(2)}, u32[]{:S(2)}) %collective-permute-start.13) | collective-permute-done | bytes 32800 | tf_op jit(solution)/shard_map/ppermute | solution.py:674
  84.6 1.7 %collective-permute-done.14.refs_3_ = f32[2,32,128]{2,1,0:T(8,128)S(1)} collective-permute-done((f32[2,32,128]{2,1,0:T(8,128)S(1)}, f32[2,32,128]{2,1,0:T(8,128)S(1)}, u32[]{:S(2)}, u32[]{:S(2)}) %collective-permute-start.14) | collective-permute-done | bytes 32800 | tf_op jit(solution)/shard_map/ppermute | solution.py:674
  86.3 1.5 %collective-permute-start.17 = (f32[2,32,128]{2,1,0:T(8,128)S(1)}, f32[2,32,128]{2,1,0:T(8,128)S(1)}, u32[]{:S(2)}, u32[]{:S(2)}) collective-permute-start(f32[2,32,128]{2,1,0:T(8,128)S(1)} %grad_projection.1.own), channel_id=1, source_target_pairs={{0,3},{1,2},{2,1},{3,0},{4,7},{5,6},{6,5},{7,4},{8,11},{9,10},{10,... | collective-permute-start | bytes 98312 | tf_op jit(solution)/shard_map/ppermute | solution.py:674
  87.8 2.9 %collective-permute-start.15 = (f32[2,32,128]{2,1,0:T(8,128)S(1)}, f32[2,32,128]{2,1,0:T(8,128)S(1)}, u32[]{:S(2)}, u32[]{:S(2)}) collective-permute-start(f32[2,32,128]{2,1,0:T(8,128)S(1)} %grad_projection.1.own), channel_id=1, source_target_pairs={{0,1},{1,0},{2,3},{3,2},{4,5},{5,4},{6,7},{7,6},{8,9},{9,8},{10,11... | collective-permute-start | bytes 98312 | tf_op jit(solution)/shard_map/ppermute | solution.py:674
  90.7 2.0 %step_grad.1.step_part = f32[2,6,96,128]{3,2,1,0:T(8,128)S(1)} custom-call(f32[2,6,128,128]{3,2,1,0:T(8,128)} %get-tuple-element.63.grad_pre_in, f32[2,128,128]{2,1,0:T(8,128)} %get-tuple-element.51.projection_in, f32[2,32,128]{2,1,0:T(8,128)S(1)} %collective-permute-done.12.refs_1_.after_this), custom_call_target="tpu_custom_call" | custom-call | flops 268435456 | bytes 4194304 | tf_op jit(solution)/shard_map/step_grad/pallas_call | solution.py:692
  93.0 4.6 %weights.1 = (f32[1344,128]{1,0:T(8,128)S(1)}, f32[1344,128]{1,0:T(8,128)S(1)}, f32[2,128,768]{2,1,0:T(8,128)}, f32[8,768]{1,0:T(8,128)S(1)}, f32[8,768]{1,0:T(8,128)S(1)}) custom-call(s32[1]{0:T(128)} %bitcast.1.place, s32[1]{0:T(128)} %bitcast.place.column, f32[2,32,128]{2,1,0:T(8,128)S(1)} %grad_projection.1.own, ...), custom_call_target="tpu_custom_call" | custom-call | flops 268435456 | bytes 4194304 | tf_op jit(solution)/shard_map/weights/pallas_call | solution.py:692
  97.7 2.1 %collective-permute-done.20.got = f32[1344,128]{1,0:T(8,128)S(1)} collective-permute-done((f32[1344,128]{1,0:T(8,128)S(1)}, f32[1344,128]{1,0:T(8,128)S(1)}, u32[]{:S(2)}, u32[]{:S(2)}) %collective-permute-start.20) | collective-permute-done | bytes 688160 | tf_op jit(solution)/shard_map/ppermute | solution.py:674
  99.9 0.5 collective-permute-start.21
  100.5 1.9 %collective-permute-start.22 = (f32[336,128]{1,0:T(8,128)S(1)}, f32[336,128]{1,0:T(8,128)S(1)}, u32[]{:S(2)}, u32[]{:S(2)}) collective-permute-start(f32[336,128]{1,0:T(8,128)S(1)} %get-tuple-element.71), channel_id=1, source_target_pairs={{0,16},{4,20},{8,24},{12,28},{16,0},{20,4},{24,8},{28,12},{1,17},{... | collective-permute-start | bytes 516104 | tf_op jit(solution)/shard_map/ppermute | solution.py:674
  102.3 1.2 collective-permute-start.23
  103.5 1.3 collective-permute-start.18
  104.8 1.3 %collective-permute-start.19 = (f32[8,768]{1,0:T(8,128)S(1)}, f32[8,768]{1,0:T(8,128)S(1)}, u32[]{:S(2)}, u32[]{:S(2)}) collective-permute-start(f32[8,768]{1,0:T(8,128)S(1)} %get-tuple-element.65), channel_id=1, source_target_pairs={{4,0},{8,4},{12,8},{16,12},{20,16},{24,20},{28,24},{5,1},{9,5},{13... | collective-permute-start | bytes 73736 | tf_op jit(solution)/shard_map/ppermute | solution.py:669
  106.1 2.5 %collective-permute-done.19.after = f32[8,768]{1,0:T(8,128)S(1)} collective-permute-done((f32[8,768]{1,0:T(8,128)S(1)}, f32[8,768]{1,0:T(8,128)S(1)}, u32[]{:S(2)}, u32[]{:S(2)}) %collective-permute-start.19) | collective-permute-done | bytes 24608 | tf_op jit(solution)/shard_map/ppermute | solution.py:669
  108.6 2.3 %exit.1.after_this = f32[128,768]{1,0:T(8,128)} custom-call(f32[8,768]{1,0:T(8,128)S(1)} %collective-permute-done.18.before, f32[8,768]{1,0:T(8,128)S(1)} %collective-permute-done.19.after, f32[2,128,768]{2,1,0:T(8,128)} %get-tuple-element.66.conv_grad, f32[2,4,768]{2,1,0:T(4,128)} %conv_weight_in.3, f32[336,128]{1,0:T(8,128)S(1)} %get-tuple-element.69.after_this.refs_0_), custom_call_target="tpu_custom_call" | custom-call | flops 268435456 | bytes 4194304 | tf_op jit(solution)/shard_map/exit/pallas_call | solution.py:692
  111.0 3.8 %collective-permute-start.26 = (f32[336,128]{1,0:T(8,128)S(1)}, f32[336,128]{1,0:T(8,128)S(1)}, u32[]{:S(2)}, u32[]{:S(2)}) collective-permute-start(f32[336,128]{1,0:T(8,128)S(1)} %share_sum.1.after_this.mine), channel_id=1, source_target_pairs={{0,24},{4,28},{8,16},{12,20},{16,8},{20,12},{24,0},{28,4},{1,25},{... | collective-permute-start | bytes 516104 | tf_op jit(solution)/shard_map/ppermute | solution.py:674
  114.9 1.1 collective-permute-start.24
  116.0 2.4 %gate.1 = (f32[128,768]{1,0:T(8,128)}, f32[128,768]{1,0:T(8,128)}) custom-call(f32[6,128,128]{2,1,0:T(8,128)} %get-tuple-element.56.summed_in, f32[128,768]{1,0:T(8,128)} %gate_in.3, f32[128,768]{1,0:T(8,128)} %cot_in.3, f32[336,128]{1,0:T(8,128)S(1)} %share_sum.1.after_this.mine), custom_call_target="tpu_custom_call" | custom-call | flops 268435456 | bytes 4194304 | tf_op jit(solution)/shard_map/gate/pallas_call | solution.py:692
  118.4 1.0 collective-permute-done.26.refs_2_
  119.4 4.3 %collective-permute-done.25.refs_1_ = f32[336,128]{1,0:T(8,128)S(1)} collective-permute-done((f32[336,128]{1,0:T(8,128)S(1)}, f32[336,128]{1,0:T(8,128)S(1)}, u32[]{:S(2)}, u32[]{:S(2)}) %collective-permute-start.25) | collective-permute-done | bytes 172064 | tf_op jit(solution)/shard_map/ppermute | solution.py:674
  123.7 1.2 collective-permute-done.24.refs_0_
  125.0 2.1 %collective-permute-done.27.other = f32[4,336,128]{2,1,0:T(8,128)S(1)} collective-permute-done((f32[4,336,128]{2,1,0:T(8,128)S(1)}, f32[4,336,128]{2,1,0:T(8,128)S(1)}, u32[]{:S(2)}, u32[]{:S(2)}) %collective-permute-start.27) | collective-permute-done | bytes 688160 | tf_op jit(solution)/shard_map/ppermute | solution.py:674
  127.1 1.2 weight_grads.1
  (24 shorter events, 1.0 us)
Async XLA Ops:
  1.4 4.3 %collective-permute-start.1 = (f32[8,768]{1,0:T(8,128)S(1)}, f32[8,768]{1,0:T(8,128)S(1)}, u32[]{:S(2)}, u32[]{:S(2)}) collective-permute-start(f32[8,768]{1,0:T(8,128)S(1)} %get-tuple-element.77), channel_id=1, source_target_pairs={{4,0},{8,4},{12,8},{16,12},{20,16},{24,20},{28,24},{5,1},{9,5},{13... | collective-permute-start | bytes 73736 | tf_op jit(solution)/shard_map/ppermute | solution.py:669
  2.7 3.9 %collective-permute-start = (f32[8,768]{1,0:T(8,128)S(1)}, f32[8,768]{1,0:T(8,128)S(1)}, u32[]{:S(2)}, u32[]{:S(2)}) collective-permute-start(f32[8,768]{1,0:T(8,128)S(1)} %get-tuple-element.78), channel_id=1, source_target_pairs={{0,4},{4,8},{8,12},{12,16},{16,20},{20,24},{24,28},{1,5},{5,9},{9,... | collective-permute-start | bytes 73736 | tf_op jit(solution)/shard_map/ppermute | solution.py:664
  9.5 5.7 %collective-permute-start.2 = (f32[2,32,128]{2,1,0:T(8,128)S(1)}, f32[2,32,128]{2,1,0:T(8,128)S(1)}, u32[]{:S(2)}, u32[]{:S(2)}) collective-permute-start(f32[2,32,128]{2,1,0:T(8,128)S(1)} %get-tuple-element.42), channel_id=1, source_target_pairs={{0,1},{1,0},{2,3},{3,2},{4,5},{5,4},{6,7},{7,6},{8,9},{9,8},{10,11... | collective-permute-start | bytes 98312 | tf_op jit(solution)/shard_map/ppermute | solution.py:674
  12.6 5.9 %collective-permute-start.3 = (f32[2,32,128]{2,1,0:T(8,128)S(1)}, f32[2,32,128]{2,1,0:T(8,128)S(1)}, u32[]{:S(2)}, u32[]{:S(2)}) collective-permute-start(f32[2,32,128]{2,1,0:T(8,128)S(1)} %get-tuple-element.43), channel_id=1, source_target_pairs={{0,2},{1,3},{2,0},{3,1},{4,6},{5,7},{6,4},{7,5},{8,10},{9,11},{10,... | collective-permute-start | bytes 98312 | tf_op jit(solution)/shard_map/ppermute | solution.py:674
  15.2 5.7 %collective-permute-start.4 = (f32[2,32,128]{2,1,0:T(8,128)S(1)}, f32[2,32,128]{2,1,0:T(8,128)S(1)}, u32[]{:S(2)}, u32[]{:S(2)}) collective-permute-start(f32[2,32,128]{2,1,0:T(8,128)S(1)} %get-tuple-element.44), channel_id=1, source_target_pairs={{0,3},{1,2},{2,1},{3,0},{4,7},{5,6},{6,5},{7,4},{8,11},{9,10},{10,... | collective-permute-start | bytes 98312 | tf_op jit(solution)/shard_map/ppermute | solution.py:674
  20.9 6.0 %collective-permute-start.7 = (f32[2,32,128]{2,1,0:T(8,128)S(1)}, f32[2,32,128]{2,1,0:T(8,128)S(1)}, u32[]{:S(2)}, u32[]{:S(2)}) collective-permute-start(f32[2,32,128]{2,1,0:T(8,128)S(1)} %projection.1.own), channel_id=1, source_target_pairs={{0,3},{1,2},{2,1},{3,0},{4,7},{5,6},{6,5},{7,4},{8,11},{9,10},{10,... | collective-permute-start | bytes 98312 | tf_op jit(solution)/shard_map/ppermute | solution.py:674
  22.1 5.4 %collective-permute-start.6 = (f32[2,32,128]{2,1,0:T(8,128)S(1)}, f32[2,32,128]{2,1,0:T(8,128)S(1)}, u32[]{:S(2)}, u32[]{:S(2)}) collective-permute-start(f32[2,32,128]{2,1,0:T(8,128)S(1)} %projection.1.own), channel_id=1, source_target_pairs={{0,2},{1,3},{2,0},{3,1},{4,6},{5,7},{6,4},{7,5},{8,10},{9,11},{10,... | collective-permute-start | bytes 98312 | tf_op jit(solution)/shard_map/ppermute | solution.py:674
  22.1 5.4 %collective-permute-start.5 = (f32[2,32,128]{2,1,0:T(8,128)S(1)}, f32[2,32,128]{2,1,0:T(8,128)S(1)}, u32[]{:S(2)}, u32[]{:S(2)}) collective-permute-start(f32[2,32,128]{2,1,0:T(8,128)S(1)} %projection.1.own), channel_id=1, source_target_pairs={{0,1},{1,0},{2,3},{3,2},{4,5},{5,4},{6,7},{7,6},{8,9},{9,8},{10,11... | collective-permute-start | bytes 98312 | tf_op jit(solution)/shard_map/ppermute | solution.py:674
  41.2 1.6 %collective-permute-start.8 = (f32[2,6,40,128]{3,2,1,0:T(8,128)S(1)}, f32[2,6,40,128]{3,2,1,0:T(8,128)S(1)}, u32[]{:S(2)}, u32[]{:S(2)}) collective-permute-start(f32[2,6,40,128]{3,2,1,0:T(8,128)S(1)} %get-tuple-element.46.mine), channel_id=1, source_target_pairs={{0,4},{4,0},{8,12},{12,8},{16,20},{20,16},{24,28},{28,24},{1,5},{5... | collective-permute-start | bytes 737288 | tf_op jit(solution)/shard_map/ppermute | solution.py:674
  42.9 7.0 %collective-permute-start.9 = (f32[6,40,128]{2,1,0:T(8,128)S(1)}, f32[6,40,128]{2,1,0:T(8,128)S(1)}, u32[]{:S(2)}, u32[]{:S(2)}) collective-permute-start(f32[6,40,128]{2,1,0:T(8,128)S(1)} %get-tuple-element.48), channel_id=1, source_target_pairs={{0,8},{4,12},{8,0},{12,4},{16,24},{20,28},{24,16},{28,20},{1,9},{5... | collective-permute-start | bytes 368648 | tf_op jit(solution)/shard_map/ppermute | solution.py:674
  46.3 7.3 %collective-permute-start.10 = (f32[6,40,128]{2,1,0:T(8,128)S(1)}, f32[6,40,128]{2,1,0:T(8,128)S(1)}, u32[]{:S(2)}, u32[]{:S(2)}) collective-permute-start(f32[6,40,128]{2,1,0:T(8,128)S(1)} %get-tuple-element.49), channel_id=1, source_target_pairs={{0,16},{4,20},{8,24},{12,28},{16,0},{20,4},{24,8},{28,12},{1,17},{... | collective-permute-start | bytes 368648 | tf_op jit(solution)/shard_map/ppermute | solution.py:674
  48.1 7.4 %collective-permute-start.11 = (f32[6,40,128]{2,1,0:T(8,128)S(1)}, f32[6,40,128]{2,1,0:T(8,128)S(1)}, u32[]{:S(2)}, u32[]{:S(2)}) collective-permute-start(f32[6,40,128]{2,1,0:T(8,128)S(1)} %get-tuple-element.50), channel_id=1, source_target_pairs={{0,24},{4,28},{8,16},{12,20},{16,8},{20,12},{24,0},{28,4},{1,25},{... | collective-permute-start | bytes 368648 | tf_op jit(solution)/shard_map/ppermute | solution.py:674
  77.5 4.5 %collective-permute-start.12 = (f32[2,32,128]{2,1,0:T(8,128)S(1)}, f32[2,32,128]{2,1,0:T(8,128)S(1)}, u32[]{:S(2)}, u32[]{:S(2)}) collective-permute-start(f32[2,32,128]{2,1,0:T(8,128)S(1)} %get-tuple-element.58), channel_id=1, source_target_pairs={{0,1},{1,0},{2,3},{3,2},{4,5},{5,4},{6,7},{7,6},{8,9},{9,8},{10,11... | collective-permute-start | bytes 98312 | tf_op jit(solution)/shard_map/ppermute | solution.py:674
  79.6 5.0 %collective-permute-start.13 = (f32[2,32,128]{2,1,0:T(8,128)S(1)}, f32[2,32,128]{2,1,0:T(8,128)S(1)}, u32[]{:S(2)}, u32[]{:S(2)}) collective-permute-start(f32[2,32,128]{2,1,0:T(8,128)S(1)} %get-tuple-element.59), channel_id=1, source_target_pairs={{0,2},{1,3},{2,0},{3,1},{4,6},{5,7},{6,4},{7,5},{8,10},{9,11},{10,... | collective-permute-start | bytes 98312 | tf_op jit(solution)/shard_map/ppermute | solution.py:674
  80.5 5.8 %collective-permute-start.14 = (f32[2,32,128]{2,1,0:T(8,128)S(1)}, f32[2,32,128]{2,1,0:T(8,128)S(1)}, u32[]{:S(2)}, u32[]{:S(2)}) collective-permute-start(f32[2,32,128]{2,1,0:T(8,128)S(1)} %get-tuple-element.60), channel_id=1, source_target_pairs={{0,3},{1,2},{2,1},{3,0},{4,7},{5,6},{6,5},{7,4},{8,11},{9,10},{10,... | collective-permute-start | bytes 98312 | tf_op jit(solution)/shard_map/ppermute | solution.py:674
  86.3 6.4 %collective-permute-start.17 = (f32[2,32,128]{2,1,0:T(8,128)S(1)}, f32[2,32,128]{2,1,0:T(8,128)S(1)}, u32[]{:S(2)}, u32[]{:S(2)}) collective-permute-start(f32[2,32,128]{2,1,0:T(8,128)S(1)} %grad_projection.1.own), channel_id=1, source_target_pairs={{0,3},{1,2},{2,1},{3,0},{4,7},{5,6},{6,5},{7,4},{8,11},{9,10},{10,... | collective-permute-start | bytes 98312 | tf_op jit(solution)/shard_map/ppermute | solution.py:674
  87.8 5.1 %collective-permute-start.16 = (f32[2,32,128]{2,1,0:T(8,128)S(1)}, f32[2,32,128]{2,1,0:T(8,128)S(1)}, u32[]{:S(2)}, u32[]{:S(2)}) collective-permute-start(f32[2,32,128]{2,1,0:T(8,128)S(1)} %grad_projection.1.own), channel_id=1, source_target_pairs={{0,2},{1,3},{2,0},{3,1},{4,6},{5,7},{6,4},{7,5},{8,10},{9,11},{10,... | collective-permute-start | bytes 98312 | tf_op jit(solution)/shard_map/ppermute | solution.py:674
  87.8 5.2 %collective-permute-start.15 = (f32[2,32,128]{2,1,0:T(8,128)S(1)}, f32[2,32,128]{2,1,0:T(8,128)S(1)}, u32[]{:S(2)}, u32[]{:S(2)}) collective-permute-start(f32[2,32,128]{2,1,0:T(8,128)S(1)} %grad_projection.1.own), channel_id=1, source_target_pairs={{0,1},{1,0},{2,3},{3,2},{4,5},{5,4},{6,7},{7,6},{8,9},{9,8},{10,11... | collective-permute-start | bytes 98312 | tf_op jit(solution)/shard_map/ppermute | solution.py:674
  97.6 2.2 %collective-permute-start.20 = (f32[1344,128]{1,0:T(8,128)S(1)}, f32[1344,128]{1,0:T(8,128)S(1)}, u32[]{:S(2)}, u32[]{:S(2)}) collective-permute-start(f32[1344,128]{1,0:T(8,128)S(1)} %get-tuple-element.68), channel_id=1, source_target_pairs={{0,4},{4,0},{8,12},{12,8},{16,20},{20,16},{24,28},{28,24},{1,5},{5... | collective-permute-start | bytes 2064392 | tf_op jit(solution)/shard_map/ppermute | solution.py:674
  99.9 10.9 %collective-permute-start.21 = (f32[336,128]{1,0:T(8,128)S(1)}, f32[336,128]{1,0:T(8,128)S(1)}, u32[]{:S(2)}, u32[]{:S(2)}) collective-permute-start(f32[336,128]{1,0:T(8,128)S(1)} %get-tuple-element.70), channel_id=1, source_target_pairs={{0,8},{4,12},{8,0},{12,4},{16,24},{20,28},{24,16},{28,20},{1,9},{5... | collective-permute-start | bytes 516104 | tf_op jit(solution)/shard_map/ppermute | solution.py:674
  100.5 10.4 %collective-permute-start.22 = (f32[336,128]{1,0:T(8,128)S(1)}, f32[336,128]{1,0:T(8,128)S(1)}, u32[]{:S(2)}, u32[]{:S(2)}) collective-permute-start(f32[336,128]{1,0:T(8,128)S(1)} %get-tuple-element.71), channel_id=1, source_target_pairs={{0,16},{4,20},{8,24},{12,28},{16,0},{20,4},{24,8},{28,12},{1,17},{... | collective-permute-start | bytes 516104 | tf_op jit(solution)/shard_map/ppermute | solution.py:674
  102.3 8.6 %collective-permute-start.23 = (f32[336,128]{1,0:T(8,128)S(1)}, f32[336,128]{1,0:T(8,128)S(1)}, u32[]{:S(2)}, u32[]{:S(2)}) collective-permute-start(f32[336,128]{1,0:T(8,128)S(1)} %get-tuple-element.72), channel_id=1, source_target_pairs={{0,24},{4,28},{8,16},{12,20},{16,8},{20,12},{24,0},{28,4},{1,25},{... | collective-permute-start | bytes 516104 | tf_op jit(solution)/shard_map/ppermute | solution.py:674
  103.5 2.6 %collective-permute-start.18 = (f32[8,768]{1,0:T(8,128)S(1)}, f32[8,768]{1,0:T(8,128)S(1)}, u32[]{:S(2)}, u32[]{:S(2)}) collective-permute-start(f32[8,768]{1,0:T(8,128)S(1)} %get-tuple-element.64), channel_id=1, source_target_pairs={{0,4},{4,8},{8,12},{12,16},{16,20},{20,24},{24,28},{1,5},{5,9},{9,... | collective-permute-start | bytes 73736 | tf_op jit(solution)/shard_map/ppermute | solution.py:664
  104.8 3.8 %collective-permute-start.19 = (f32[8,768]{1,0:T(8,128)S(1)}, f32[8,768]{1,0:T(8,128)S(1)}, u32[]{:S(2)}, u32[]{:S(2)}) collective-permute-start(f32[8,768]{1,0:T(8,128)S(1)} %get-tuple-element.65), channel_id=1, source_target_pairs={{4,0},{8,4},{12,8},{16,12},{20,16},{24,20},{28,24},{5,1},{9,5},{13... | collective-permute-start | bytes 73736 | tf_op jit(solution)/shard_map/ppermute | solution.py:669
  111.0 8.4 %collective-permute-start.26 = (f32[336,128]{1,0:T(8,128)S(1)}, f32[336,128]{1,0:T(8,128)S(1)}, u32[]{:S(2)}, u32[]{:S(2)}) collective-permute-start(f32[336,128]{1,0:T(8,128)S(1)} %share_sum.1.after_this.mine), channel_id=1, source_target_pairs={{0,24},{4,28},{8,16},{12,20},{16,8},{20,12},{24,0},{28,4},{1,25},{... | collective-permute-start | bytes 516104 | tf_op jit(solution)/shard_map/ppermute | solution.py:674
  114.8 8.9 %collective-permute-start.25 = (f32[336,128]{1,0:T(8,128)S(1)}, f32[336,128]{1,0:T(8,128)S(1)}, u32[]{:S(2)}, u32[]{:S(2)}) collective-permute-start(f32[336,128]{1,0:T(8,128)S(1)} %share_sum.1.after_this.mine), channel_id=1, source_target_pairs={{0,16},{4,20},{8,24},{12,28},{16,0},{20,4},{24,8},{28,12},{1,17},{... | collective-permute-start | bytes 516104 | tf_op jit(solution)/shard_map/ppermute | solution.py:674
  114.9 9.9 %collective-permute-start.24 = (f32[336,128]{1,0:T(8,128)S(1)}, f32[336,128]{1,0:T(8,128)S(1)}, u32[]{:S(2)}, u32[]{:S(2)}) collective-permute-start(f32[336,128]{1,0:T(8,128)S(1)} %share_sum.1.after_this.mine), channel_id=1, source_target_pairs={{0,8},{4,12},{8,0},{12,4},{16,24},{20,28},{24,16},{28,20},{1,9},{5... | collective-permute-start | bytes 516104 | tf_op jit(solution)/shard_map/ppermute | solution.py:674
  124.9 2.2 %collective-permute-start.27 = (f32[4,336,128]{2,1,0:T(8,128)S(1)}, f32[4,336,128]{2,1,0:T(8,128)S(1)}, u32[]{:S(2)}, u32[]{:S(2)}) collective-permute-start(f32[4,336,128]{2,1,0:T(8,128)S(1)} %joined.1.mine), channel_id=1, source_target_pairs={{0,4},{4,0},{8,12},{12,8},{16,20},{20,16},{24,28},{28,24},{1,5},{5... | collective-permute-start | bytes 2064392 | tf_op jit(solution)/shard_map/ppermute | solution.py:674

commit v3 on v2

--- a/solution.py
+++ b/solution.py
@@ -83,8 +83,8 @@
     place, before, after, tokens, conv_weight_in, conv_bias_in, select_in,
     *refs,
 ):
-    outs, refs = refs[:-10], refs[-10:]
-    act_out, pre_out, ext, conv_weight, conv_bias, select, act, pre, plain, sems = refs
+    outs, refs = refs[:-11], refs[-11:]
+    act_out, pre_out, ext, conv_weight, conv_bias, select, act, pre, plain, rows, sems = refs
 
     length, width = tokens.shape
     loads = copies_of(
@@ -106,25 +106,28 @@
     stores = copies_of([(pre, pre_out), (act, act_out)], sems.at[pl.ds(4, 2)])
     loads[3].wait()
     for side in range(2):
-        deal(place, outs, side, dot(full_width(act, side), select[side], (1, 0)))
+        rows[...] = dot(full_width(act, side), select[side], (1, 0))
+        deal(place, outs, side, rows)
     finish_all(stores)
+
+
+def turned(k, by, count):
+    return lax.rem(k - 1 + by, count - 1) + 1
 
 
 def deal(place, outs, side, rows):
     share = outs[0].shape[1]
     for k in range(len(outs)):
-        for mine in range(len(outs)):
-
-            @pl.when(place[0] == mine)
-            def _():
-                at = (mine ^ k) * share
-                outs[k][side] = rows[at : at + share]
+        to = place[1] ^ turned(k, place[0], len(outs)) if k else place[1]
+        at = pl.multiple_of(to * share, share)
+        outs[k][side] = rows[pl.ds(at, share), :]
 
 
 def collect(place, parts, out):
     share = parts[0].shape[1]
     for k in range(len(parts)):
-        at = pl.multiple_of((place[0] ^ k) * share, share)
+        source = place[1] ^ turned(k, place[0], len(parts)) if k else place[1]
+        at = pl.multiple_of(source * share, share)
         out[:, pl.ds(at, share), :] = parts[k][...]
 
 
@@ -192,6 +195,10 @@
         return state
 
     return lax.fori_loop(0, count // times, several, start)
+
+
+def plus(total, term):
+    return term if total is None else total + term
 
 
 def fill_rate_rows(rates, side, tiles, rate_rows):
@@ -272,7 +279,7 @@
                 return (tuple(new), tuple(a + v for a, v in zip(summed, steps)))
 
             start = ((zero,) * (states * group), (zero,) * group)
-            state, summed = unrolled(count, 4, forward, start)
+            state, summed = unrolled(count, 8, forward, start)
 
             def retreat(i, state):
                 j = order(i, count, not up)
@@ -287,7 +294,7 @@
                         new.append(decays[g, at, lanes] * adjoint)
                 return tuple(new)
 
-            sent = unrolled(count, 4, retreat, (zero,) * (states * group))
+            sent = unrolled(count, 8, retreat, (zero,) * (states * group))
             for g, t in enumerate(at_tiles):
                 across = [jnp.exp2(summed[g] * rate_rows[g, n]) for n in range(states)]
                 for kind, ends, upward in ((0, state, up), (1, sent, not up)):
@@ -318,6 +325,30 @@
     return jnp.exp2(rates * sums)
 
 
+def prep_kernel(
+    projection_in, act_in, pre_in, after_this, bases_out, turned_act_out, slope_out, done,
+    projection, act, pre, bases, turned_act, sems,
+):
+    sides, tiles, length, _ = act.shape
+    states = bases.shape[3] // LANES
+    loads = copies_of([(projection_in, projection), (act_in, act), (pre_in, pre)], sems)
+    loads[0].wait()
+    stores = []
+    for side in range(sides):
+        fill_bases(projection, side, states, bases.at[side, 0], bases.at[side, 1])
+        stores += copies_of([(bases.at[side], bases_out.at[side])], sems.at[pl.ds(3 + side, 1)])
+    finish_all(loads[1:])
+    for side in range(sides):
+        for t in range(tiles):
+            turned_act[side, lane_tile(t)] = act[side, t].T
+            pre[side, t] = silu_grad(pre[side, t])
+    stores += copies_of(
+        [(turned_act, turned_act_out), (pre, slope_out)], sems.at[pl.ds(5, 2)]
+    )
+    done[...] = jnp.zeros_like(done)
+    finish_all(stores)
+
+
 def pair_kernel(place, mine, other, rates, *refs):
     outs, total = refs[:-1], refs[-1]
     rows = rates.shape[1]
@@ -330,19 +361,31 @@
     total[...] = low + high
     total[0, :, :rows] = decay_high * low[0][:, :rows] + high[0][:, :rows]
     total[1, :, :rows] = decay_low * high[1][:, :rows] + low[1][:, :rows]
-    for s, out in enumerate(outs, 1):
-        below = lax.convert_element_type((chip ^ s) < chip, jnp.int32)
-        out[...] = total[below]
-
-
-def chain_kernel(place, other, rates, *refs):
+    tiles = rates.shape[0]
+    for k, out in enumerate(outs, 1):
+        to = chip ^ turned(k, core, len(outs) + 1)
+        below = lax.convert_element_type(to < chip, jnp.int32)
+        for t in range(tiles):
+            out[t * rows : (t + 1) * rows] = total[below, t, :rows]
+            for side in range(2):
+                at = tiles * rows + side * tiles + t
+                out[at : at + 1] = total[0, t, rows + side : rows + side + 1]
+
+
+def chain_kernel(place, other, rates, after_this, *refs):
     gathered, (out, parts) = refs[:-2], refs[-2:]
     rows = rates.shape[1]
     chips = parts.shape[0]
     core, chip = lax.rem(place[0], 2), lax.div(place[0], 2)
     parts[chip] = jnp.zeros(parts.shape[1:], jnp.float32)
-    for s, part in enumerate(gathered, 1):
-        parts[chip ^ s] = part[...]
+    tiles = rates.shape[0]
+    for k, part in enumerate(gathered, 1):
+        source = chip ^ turned(k, core, chips)
+        for t in range(tiles):
+            parts[source, t, :rows] = part[t * rows : (t + 1) * rows]
+            for side in range(2):
+                at = tiles * rows + side * tiles + t
+                parts[source, t, rows + side : rows + side + 1] = part[at : at + 1]
     spread_rates = rates[...]
     for kind in range(2):
         state = jnp.zeros(rates.shape, jnp.float32)
@@ -369,11 +412,11 @@
 
 
 def scan_kernel(
-    place, incoming, projection_in, step_weight_in, decay_log_in, skip_gain_in, act_in, step_in,
+    place, incoming, bases_in, step_weight_in, decay_log_in, skip_gain_in, act_in, step_in,
     step_pre_in, grad_gated_in, entering_in,
     mine, first_out, second_out, third_out, grad_act_out, grad_pre_out, summed_outs,
-    projection, step_weight, decay_log, skip_gain, act, step, step_pre, grad_gated, entering,
-    grad_act, grad_pre, summed_out, rates, basis_b, basis_c, rate_rows, decays, history,
+    bases, step_weight, decay_log, skip_gain, act, step, step_pre, grad_gated, entering,
+    grad_act, grad_pre, summed_out, rates, rate_rows, decays, history,
     grad_in, grad_out, weights, packed, skip_rows, sems,
 ):
     sides, tiles, length, _ = act.shape
@@ -383,27 +426,29 @@
     group = tile_group(tiles)
     loads = copies_of(
         [
-            (projection_in, projection), (decay_log_in, decay_log), (step_in, step),
-            (act_in, act), (grad_gated_in, grad_gated), (entering_in, entering),
-            (skip_gain_in, skip_gain), (step_pre_in, step_pre), (step_weight_in, step_weight),
+            (decay_log_in, decay_log), (skip_gain_in, skip_gain), (step_in, step),
+            (act_in, act), (bases_in.at[0], bases.at[0]), (grad_gated_in, grad_gated),
+            (entering_in, entering), (step_pre_in, step_pre), (bases_in.at[1], bases.at[1]),
+            (step_weight_in, step_weight),
         ],
         sems,
     )
     stores = []
     finish_all(loads[:2])
     fill_rates(decay_log, rates)
-    zero = jnp.zeros((CHAINS, LANES), jnp.float32)
     column = lax.broadcasted_iota(jnp.int32, (CHAINS, LANES), 1)
     for side in range(2):
         up = side == 0
-        fill_bases(projection, side, states, basis_b, basis_c)
+        basis_b, basis_c = bases.at[side, 0], bases.at[side, 1]
         grad_in[...] = jnp.zeros_like(grad_in)
         grad_out[...] = jnp.zeros_like(grad_out)
         if side == 0:
-            finish_all(loads[2:])
             for k in range(2):
                 for t in range(tiles):
                     skip_rows[k, t] = skip_gain[k : k + 1, lane_tile(t)]
+            finish_all(loads[2:-2])
+        else:
+            loads[-2].wait()
 
         def some_tiles(first, keep):
             at_tiles = [first * group + g for g in range(group)]
@@ -442,7 +487,7 @@
                 acts = [act[side, t, at, :] for t in at_tiles]
                 grads = [grad_gated[t, at, :] for t in at_tiles]
                 drives = [v * a for v, a in zip(steps, acts)]
-                outs = [v * a for v, a in zip(skips, acts)]
+                outs = [[v * a, None] for v, a in zip(skips, acts)]
                 new = []
                 for n in range(states):
                     lanes = lane_tile(n)
@@ -454,18 +499,19 @@
                         decays[g, at, lanes] = decay
                         history[g, at, lanes] = before
                         current = decay * before + b * drives[g]
-                        outs[g] = outs[g] + c * current
+                        outs[g][n % 2] = plus(outs[g][n % 2], c * current)
                         read = read + current * grads[g]
                         new.append(current)
                     grad_out[at, lanes] = read
                 for g, t in enumerate(at_tiles):
+                    out = outs[g][0] + outs[g][1]
                     if side == 0:
-                        summed_out[t, at, :] = outs[g]
+                        summed_out[t, at, :] = out
                     else:
-                        summed_out[t, at, :] = summed_out[t, at, :] + outs[g]
+                        summed_out[t, at, :] = summed_out[t, at, :] + out
                 return tuple(new)
 
-            unrolled(count, 2, forward, start(0, up))
+            unrolled(count, 4, forward, start(0, up))
 
             def retreat(i, state):
                 j = order(i, count, not up)
@@ -474,8 +520,8 @@
                 acts = [act[side, t, at, :] for t in at_tiles]
                 grads = [grad_gated[t, at, :] for t in at_tiles]
                 drives = [v * a for v, a in zip(steps, acts)]
-                step_terms = [zero] * group
-                drive_grads = [zero] * group
+                step_terms = [[None, None] for _ in range(group)]
+                drive_grads = [[None, None] for _ in range(group)]
                 new = []
                 for n in range(states):
                     lanes = lane_tile(n)
@@ -486,18 +532,20 @@
                         carried = decays[g, at, lanes] * adjoint
                         new.append(carried)
                         term = carried * history[g, at, lanes] * rate_rows[g, n]
-                        step_terms[g] = step_terms[g] + term
-                        drive_grads[g] = drive_grads[g] + adjoint * b
+                        step_terms[g][n % 2] = plus(step_terms[g][n % 2], term)
+                        drive_grads[g][n % 2] = plus(drive_grads[g][n % 2], adjoint * b)
                         put = put + adjoint * drives[g]
                     grad_in[at, lanes] = put
                 for g, t in enumerate(at_tiles):
-                    grad_step = step_terms[g] * LN2 + drive_grads[g] * acts[g]
-                    grad_act[side, t, at, :] = grads[g] * skips[g] + drive_grads[g] * steps[g]
+                    drive_grad = drive_grads[g][0] + drive_grads[g][1]
+                    step_term = step_terms[g][0] + step_terms[g][1]
+                    grad_step = step_term * LN2 + drive_grad * acts[g]
+                    grad_act[side, t, at, :] = grads[g] * skips[g] + drive_grad * steps[g]
                     pre = step_pre[side, t, at, :]
                     grad_pre[side, t, at, :] = grad_step * jax.nn.sigmoid(pre)
                 return tuple(new)
 
-            unrolled(count, 2, retreat, start(1, not up))
+            unrolled(count, 4, retreat, start(1, not up))
             return keep
 
         lax.fori_loop(0, tiles // group, some_tiles, 0)
@@ -509,6 +557,8 @@
         stores = stores + copies_of(pairs, sems.at[pl.ds(2 * side, 3)])
         wide = full_width(grad_pre, side)
         weights[...] = jnp.zeros_like(weights)
+        if side == 0:
+            loads[-1].wait()
         weights[:ranks] = step_weight[side]
         packed[...] = dot(wide, weights[...], (1, 1))
 
@@ -550,26 +600,28 @@
 
 
 def weight_kernel(
-    place, column, own, first, second, third, act_in, pre_in, grad_act_in, select_in, step_part,
+    place, own, first, second, third, turned_act_in, slope_in, grad_act_in, select_in, step_part,
     keep, send, conv_grad_out, head, tail,
-    act, pre, grad_act, select, grad, both, conv_grad, plain, sems,
+    turned_act, slope, grad_act, select, grad, conv_grad, plain, sems,
 ):
-    sides, tiles, length, _ = act.shape
+    sides, tiles, length, _ = slope.shape
     loads = copies_of(
         [
-            (act_in, act), (select_in, select), (grad_act_in, grad_act), (pre_in, pre),
+            (turned_act_in, turned_act), (select_in, select), (grad_act_in, grad_act),
+            (slope_in, slope),
         ],
         sems,
     )
-    collect(column, (own, first, second, third), grad)
+    collect(place, (own, first, second, third), grad)
     loads[0].wait()
     for side in range(2):
-        both[side, : tiles * LANES] = dot(full_width(act, side), grad[side], (0, 0))
-        both[side, tiles * LANES :] = step_part[side].reshape(-1, LANES)
-    core = lax.rem(place[0], 2)
-    stores = copies_of(
-        [(both.at[core], keep), (both.at[1 - core], send)], sems.at[pl.ds(4, 2)]
-    )
+        part = dot(turned_act[side], grad[side], (1, 0))
+        for out, core in ((keep, side), (send, 1 - side)):
+
+            @pl.when(lax.rem(place[0], 2) == core)
+            def _():
+                out[: tiles * LANES] = part
+                out[tiles * LANES :] = step_part[side].reshape(-1, LANES)
     finish_all(loads[1:])
     for side in range(2):
         wide = dot(grad[side], select[side], (1, 1))
@@ -577,10 +629,10 @@
             lanes = lane_tile(t)
             grad_act[side, t] = grad_act[side, t] + wide[:, lanes]
             to_tokens(grad_act.at[side, t], plain)
-            conv_grad[side, :, lanes] = plain[...] * silu_grad(pre[side, t])
+            conv_grad[side, :, lanes] = plain[...] * slope[side, t]
     head[...] = conv_grad[0, :HALO]
     tail[...] = conv_grad[1, length - HALO :]
-    stores = stores + copies_of([(conv_grad, conv_grad_out)], sems.at[pl.ds(0, 1)])
+    stores = copies_of([(conv_grad, conv_grad_out)], sems.at[pl.ds(4, 1)])
     finish_all(stores)
 
 
@@ -591,10 +643,10 @@
     for k in range(chips):
         at = slice(k * share, (k + 1) * share)
         total[k] = keep[at] + got[at]
-    chip = lax.div(place[0], 2)
+    core, chip = lax.rem(place[0], 2), lax.div(place[0], 2)
     mine[...] = total[chip]
-    for s, out in enumerate(outs, 1):
-        out[...] = total[chip ^ s]
+    for k, out in enumerate(outs, 1):
+        out[...] = total[chip ^ turned(k, core, chips)]
 
 
 def add_after_kernel(after_this, *refs):
@@ -610,10 +662,10 @@
 
 def join_kernel(place, after_this, mine, *refs):
     parts, out = refs[:-1], refs[-1]
-    chip = lax.div(place[0], 2)
+    core, chip = lax.rem(place[0], 2), lax.div(place[0], 2)
     out[chip] = mine[...]
-    for s, part in enumerate(parts, 1):
-        out[chip ^ s] = part[...]
+    for k, part in enumerate(parts, 1):
+        out[chip ^ turned(k, core, len(parts) + 1)] = part[...]
 
 
 def outputs_kernel(place, mine, other, select_grad, step_grad, both):
@@ -672,6 +724,23 @@
 def swapped(value, axis, by):
     count = lax.axis_size(axis)
     return lax.ppermute(value, axis, [(i, i ^ by) for i in range(count)])
+
+
+def swapped_shares(value, k):
+    places, columns = lax.axis_size("ctx"), lax.axis_size("ch")
+    pairs = [
+        (i * columns + j, i * columns + (j ^ ((k - 1 + i) % (columns - 1) + 1)))
+        for i in range(places)
+        for j in range(columns)
+    ]
+    return lax.ppermute(value, ("ctx", "ch"), pairs)
+
+
+def swapped_chips(value, k):
+    places = lax.axis_size("ctx")
+    chips = places // 2
+    pairs = [(i, i ^ (2 * ((k - 1 + i % 2) % (chips - 1) + 1))) for i in range(places)]
+    return lax.ppermute(value, "ctx", pairs)
 
 
 def call(kernel, name, out_shape, scratch, mib, args, kinds, outs=None):
@@ -705,9 +774,9 @@
     count = len(parts)
     if count == 1:
         return (lax.psum(parts[0], "ch"),), parts[0]
-    got = [swapped(part, "ch", s) for s, part in enumerate(parts[1:], 1)]
+    got = [swapped_shares(part, k) for k, part in enumerate(parts[1:], 1)]
     (mine,) = call(add_kernel, name, (parts[0].shape,), [], 4, (parts[0], *got), "v" * count)
-    return (mine, *(swapped(mine, "ch", s) for s in range(1, count))), got[0]
+    return (mine, *(swapped_shares(mine, k) for k in range(1, count))), got[0]
 
 
 def halved(place, keep, send, rows, chips, name):
@@ -717,7 +786,7 @@
         halves_kernel, name, ((share, LANES),) * chips, [pltpu.VMEM((chips, share, LANES), jnp.float32)],
         8, (place, keep, got), "svv",
     )
-    return (mine, *(swapped(part, "ctx", 2 * s) for s, part in enumerate(sent, 1)))
+    return (mine, *(swapped_chips(part, k) for k, part in enumerate(sent, 1)))
 
 
 def on_device(
@@ -730,8 +799,7 @@
     ranks = step_weight.shape[1]
     places = lax.axis_size("ctx")
     columns = lax.axis_size("ch")
-    place = lax.axis_index("ctx").astype(jnp.int32).reshape(1)
-    column = lax.axis_index("ch").astype(jnp.int32).reshape(1)
+    place = jnp.stack([lax.axis_index("ctx"), lax.axis_index("ch")]).astype(jnp.int32)
     group = tile_group(tiles)
     chips = places // 2
     near = places == 8
@@ -743,6 +811,7 @@
     chain_ends = (4, tiles, states, CHAINS, LANES)
     carry = (2, tiles, 2 * states + 8, LANES)
     row_rates = (tiles, 2 * states, LANES)
+    packed = (tiles * 2 * states + -(-2 * tiles // 8) * 8, LANES)
     vmem = functools.partial(pltpu.VMEM, dtype=jnp.float32)
     dma = lambda n: pltpu.SemaphoreType.DMA((n,))
     bases = vmem((length, states * LANES))
@@ -756,9 +825,9 @@
         entry_kernel, "entry", (*(shared,) * columns, pair, pair),
         [
             vmem((length + 2 * HALO, width)), vmem(conv_weight.shape), vmem(conv_bias.shape),
-            vmem(select_weight.shape), vmem(pair), vmem(pair), vmem(one[1:]), dma(6),
-        ],
-        12, (column, before, after, tokens, conv_weight, conv_bias, select_weight), "svvhhhh",
+            vmem(select_weight.shape), vmem(pair), vmem(pair), vmem(one[1:]), vmem(one[1:]), dma(6),
+        ],
+        12, (place, before, after, tokens, conv_weight, conv_bias, select_weight), "svvhhhh",
         "v" * columns + "hh",
     )
     projection, step, step_pre, grad_gated, entering, carried, rates = call(
@@ -771,7 +840,7 @@
         ],
         24,
         (
-            column, *summed_shares(parts, "projection")[0], step_weight, step_bias, decay_log, act,
+            place, *summed_shares(parts, "projection")[0], step_weight, step_bias, decay_log, act,
             gate_input, cotangent,
         ),
         "svvvvhhhhhh", "hhhhhvv",
@@ -779,16 +848,29 @@
     if near:
         other = swapped(carried, "ctx", 1)
         sent = call(
-            pair_kernel, "pair", (carry[1:],) * (chips - 1),
+            pair_kernel, "pair", (packed,) * (chips - 1),
             [vmem(carry)], 8, (place, carried, other, rates), "svvv",
         )
-        got = [swapped(part, "ctx", 2 * s) for s, part in enumerate(sent, 1)]
+        got = [swapped_chips(part, k) for k, part in enumerate(sent, 1)]
+        ahead = sent[0]
+    else:
+        gathered = lax.all_gather(carried, "ctx")
+        ahead = rates
+    spread_bases, turned_act, slope, done = call(
+        prep_kernel, "prep",
+        ((2, 2, length, states * LANES), (2, width, length), pair, (HALO, LANES)),
+        [
+            vmem(narrow), vmem(pair), vmem(pair), vmem((2, 2, length, states * LANES)),
+            vmem((2, width, length)), dma(7),
+        ],
+        14, (projection, act, pre, ahead), "hhhv", "hhhv",
+    )
+    if near:
         (incoming,) = call(
             chain_kernel, "chain", ((2, *row_rates),), [vmem((chips, *carry[1:]))],
-            8, (place, other, rates, *got), "svv" + "v" * len(got),
+            8, (place, other, rates, done, *got), "svvv" + "v" * len(got),
         )
     else:
-        gathered = lax.all_gather(carried, "ctx")
         (incoming,) = call(
             long_chain_kernel, "chain", ((2, *row_rates),), [],
             48, (place, gathered, rates), "svv",
@@ -796,15 +878,16 @@
     *grad_parts, grad_act, grad_pre, summed = call(
         scan_kernel, "scan", (*(shared,) * columns, pair, pair, one),
         [
-            vmem(narrow), vmem(step_weight.shape), vmem(decay_log.shape), vmem(skip_gain.shape),
+            vmem(spread_bases.shape), vmem(step_weight.shape), vmem(decay_log.shape),
+            vmem(skip_gain.shape),
             vmem(pair), vmem(pair), vmem(pair), vmem(one), vmem(chain_ends),
-            vmem(pair), vmem(pair), vmem(one), rate_scratch, bases, bases, row_scratch, grouped,
+            vmem(pair), vmem(pair), vmem(one), rate_scratch, row_scratch, grouped,
             grouped, bases, bases, vmem((LANES, width)), vmem((length, LANES)),
-            vmem((2, tiles, 1, LANES)), dma(9),
+            vmem((2, tiles, 1, LANES)), dma(10),
         ],
         28,
         (
-            column, incoming, projection, step_weight, decay_log, skip_gain, act, step, step_pre,
+            place, incoming, spread_bases, step_weight, decay_log, skip_gain, act, step, step_pre,
             grad_gated, entering,
         ),
         "svhhhhhhhhh", "v" * columns + "hhh",
@@ -819,12 +902,12 @@
         weight_kernel, "weights",
         ((half, LANES), (half, LANES), (2, *flat), (HALO, width), (HALO, width)),
         [
-            vmem(pair), vmem(pair), vmem(pair), vmem(select_weight.shape), vmem(narrow),
-            vmem((2, half, LANES)), vmem((2, *flat)), vmem(one[1:]), dma(6),
+            vmem((2, width, length)), vmem(pair), vmem(pair), vmem(select_weight.shape),
+            vmem(narrow), vmem((2, *flat)), vmem(one[1:]), dma(5),
         ],
         16,
-        (place, column, *grad_shares, act, pre, grad_act, select_weight, step_part),
-        "ssvvvvhhhhv", "vvhvv",
+        (place, *grad_shares, turned_act, slope, grad_act, select_weight, step_part),
+        "svvvvhhhhv", "vvhvv",
     )
     before = from_before(tail, "ctx")
     after = from_after(head, "ctx")
@@ -854,7 +937,7 @@
         8, (summed, gate_input, cotangent, ahead), "hhhv",
     )
     if near:
-        got = [swapped(mine, "ctx", 2 * s) for s in range(1, chips)]
+        got = [swapped_chips(mine, k) for k in range(1, chips)]
         (joined,) = call(
             join_kernel, "joined", ((chips, rows, LANES),), [],
             8, (place, block_out, mine, *got), "sh" + "v" * chips,

time: 129 us -> 133 us (1.031)
  Pallas kernels: 51.6 us -> 61.9 us
  waiting for transfers between devices: 33.8 us -> 27.2 us
    ppermute x0 -> x21, starting transfers between devices: none -> 34.4 us  [the longest x12 19 us: swapped_shares(): return lax.ppermute(value, ('ctx', 'ch'), pairs)]
    ppermute x24 -> x3, starting transfers between devices: 34.5 us -> 0.3 us  [swapped(): return lax.ppermute(value, axis, [(i, i ^ by) for i in range(count)])]
    ppermute x24 -> x3, waiting for transfers between devices: 30.5 us -> 5.68 us  [swapped(): return lax.ppermute(value, axis, [(i, i ^ by) for i in range(count)])]
    ppermute x0 -> x21, waiting for transfers between devices: none -> 17.9 us  [the longest x12 12.1 us: swapped_shares(): return lax.ppermute(value, ('ctx', 'ch'), pairs)]
    pallas_call x15 -> x16, Pallas kernels: 51.6 us -> 61.9 us  [call(): pl.pallas_call(kernel, in_specs=[spaces[k] for k in kinds], out_specs=[sp...]
  transfers between devices with their start and end apart: 28 -> 28, of which waited for: 19 -> 15; matrix products, arithmetic and copies ran while one was open for 0% -> 0% of each run, Pallas kernels for 5% -> 10%
where the time goes in v3:
time: 133 us; the launch traced here: 132 us
  Pallas kernels  61.9 us (47%)
  starting transfers between devices  41.6 us (31%)
  waiting for transfers between devices  27.2 us (20%)
    pallas_call x16, Pallas kernels, call(): pl.pallas_call(kernel, in_specs=[spaces[k] for k in kinds], out_specs=[sp...  61.9 us
    ppermute x12, starting transfers between devices, swapped_shares(): return lax.ppermute(value, ('ctx', 'ch'), pairs)  19 us
    ppermute x9, starting transfers between devices, swapped_chips(): return lax.ppermute(value, 'ctx', pairs)  15.3 us
    ppermute x12, waiting for transfers between devices, swapped_shares(): return lax.ppermute(value, ('ctx', 'ch'), pairs)  12.1 us
    ppermute x9, waiting for transfers between devices, swapped_chips(): return lax.ppermute(value, 'ctx', pairs)  5.83 us
    ppermute x3, waiting for transfers between devices, swapped(): return lax.ppermute(value, axis, [(i, i ^ by) for i in range(count)])  5.68 us
    ppermute x2, starting transfers between devices, from_before(): return lax.ppermute(value, axis, [(i, i + 1) for i in range(count - 1)])  4.31 us
    ppermute x2, waiting for transfers between devices, from_after(): return lax.ppermute(value, axis, [(i + 1, i) for i in range(count - 1)])  2.83 us
  transfers between devices with their start and end apart: 28, of which 15 were waited for; matrix products, arithmetic and copies ran while one was open for 0% of the time, Pallas kernels for 10%

profile of v3, /device:TPU:0, one launch (start us, length us, event | category | flops | bytes accessed | tf_op | source)
XLA Modules:
  0.0 132.3 jit_solution(17493503264927034010)
XLA Ops:
  0.6 0.8 fusion
  1.4 1.3 collective-permute-start.1
  2.7 3.0 %collective-permute-start = (f32[8,768]{1,0:T(8,128)S(1)}, f32[8,768]{1,0:T(8,128)S(1)}, u32[]{:S(2)}, u32[]{:S(2)}) collective-permute-start(f32[8,768]{1,0:T(8,128)S(1)} %get-tuple-element.86), channel_id=1, source_target_pairs={{0,4},{4,8},{8,12},{12,16},{16,20},{20,24},{24,28},{1,5},{5,9},{9,... | collective-permute-start | bytes 73736 | tf_op jit(solution)/shard_map/ppermute | solution.py:716
  5.8 0.7 collective-permute-done.before
  6.6 3.4 %entry.1 = (f32[2,32,128]{2,1,0:T(8,128)S(1)}, f32[2,32,128]{2,1,0:T(8,128)S(1)}, f32[2,32,128]{2,1,0:T(8,128)S(1)}, f32[2,32,128]{2,1,0:T(8,128)S(1)}, f32[2,6,...) custom-call(s32[2]{0:T(128)S(1)} %pad_add_fusion.place, f32[8,768]{1,0:T(8,128)S(1)} %collective-permute-done.before, ...), custom_call_target="tpu_custom_call" | custom-call | flops 268435456 | bytes 4194304 | tf_op jit(solution)/shard_map/entry/pallas_call | solution.py:761
  9.9 3.1 %collective-permute-start.2 = (f32[2,32,128]{2,1,0:T(8,128)S(1)}, f32[2,32,128]{2,1,0:T(8,128)S(1)}, u32[]{:S(2)}, u32[]{:S(2)}) collective-permute-start(f32[2,32,128]{2,1,0:T(8,128)S(1)} %get-tuple-element.46), channel_id=1, source_target_pairs={{0,1},{1,0},{2,3},{3,2},{4,6},{5,7},{6,4},{7,5},{8,11},{9,10},{10,... | collective-permute-start | bytes 98312 | tf_op jit(solution)/shard_map/ppermute | solution.py:736
  13.0 2.6 %collective-permute-start.3 = (f32[2,32,128]{2,1,0:T(8,128)S(1)}, f32[2,32,128]{2,1,0:T(8,128)S(1)}, u32[]{:S(2)}, u32[]{:S(2)}) collective-permute-start(f32[2,32,128]{2,1,0:T(8,128)S(1)} %get-tuple-element.47), channel_id=1, source_target_pairs={{0,2},{1,3},{2,0},{3,1},{4,7},{5,6},{6,5},{7,4},{8,9},{9,8},{10,11... | collective-permute-start | bytes 98312 | tf_op jit(solution)/shard_map/ppermute | solution.py:736
  15.6 2.8 %collective-permute-done.3.refs_2_ = f32[2,32,128]{2,1,0:T(8,128)S(1)} collective-permute-done((f32[2,32,128]{2,1,0:T(8,128)S(1)}, f32[2,32,128]{2,1,0:T(8,128)S(1)}, u32[]{:S(2)}, u32[]{:S(2)}) %collective-permute-start.3) | collective-permute-done | bytes 32800 | tf_op jit(solution)/shard_map/ppermute | solution.py:736
  18.4 3.0 %collective-permute-done.4.refs_3_ = f32[2,32,128]{2,1,0:T(8,128)S(1)} collective-permute-done((f32[2,32,128]{2,1,0:T(8,128)S(1)}, f32[2,32,128]{2,1,0:T(8,128)S(1)}, u32[]{:S(2)}, u32[]{:S(2)}) %collective-permute-start.4) | collective-permute-done | bytes 32800 | tf_op jit(solution)/shard_map/ppermute | solution.py:736
  21.4 0.9 collective-permute-start.7
  22.3 3.6 %collective-permute-start.5 = (f32[2,32,128]{2,1,0:T(8,128)S(1)}, f32[2,32,128]{2,1,0:T(8,128)S(1)}, u32[]{:S(2)}, u32[]{:S(2)}) collective-permute-start(f32[2,32,128]{2,1,0:T(8,128)S(1)} %projection.1.own), channel_id=1, source_target_pairs={{0,1},{1,0},{2,3},{3,2},{4,6},{5,7},{6,4},{7,5},{8,11},{9,10},{10,... | collective-permute-start | bytes 98312 | tf_op jit(solution)/shard_map/ppermute | solution.py:736
  25.8 1.4 %collective-permute-done.7.third = f32[2,32,128]{2,1,0:T(8,128)S(1)} collective-permute-done((f32[2,32,128]{2,1,0:T(8,128)S(1)}, f32[2,32,128]{2,1,0:T(8,128)S(1)}, u32[]{:S(2)}, u32[]{:S(2)}) %collective-permute-start.7) | collective-permute-done | bytes 32800 | tf_op jit(solution)/shard_map/ppermute | solution.py:736
  27.2 0.7 collective-permute-done.6.second
  27.9 14.6 %local.1 = (f32[2,128,128]{2,1,0:T(8,128)}, f32[2,6,128,128]{3,2,1,0:T(8,128)}, f32[2,6,128,128]{3,2,1,0:T(8,128)}, f32[6,128,128]{2,1,0:T(8,128)}, f32[4,6,16,8...) custom-call(s32[2]{0:T(128)S(1)} %pad_add_fusion.place, ...), custom_call_target="tpu_custom_call" | custom-call | flops 268435456 | bytes 4194304 | tf_op jit(solution)/shard_map/local/pallas_call | solution.py:761
  42.6 1.5 %collective-permute-done.8.other = f32[2,6,40,128]{3,2,1,0:T(8,128)S(1)} collective-permute-done((f32[2,6,40,128]{3,2,1,0:T(8,128)S(1)}, f32[2,6,40,128]{3,2,1,0:T(8,128)S(1)}, u32[]{:S(2)}, u32[]{:S(2)}) %collective-permute-start.8) | collective-permute-done | bytes 245792 | tf_op jit(solution)/shard_map/ppermute | solution.py:726
  44.1 0.7 pair.1
  44.7 5.0 %collective-permute-start.10 = (f32[208,128]{1,0:T(8,128)S(1)}, f32[208,128]{1,0:T(8,128)S(1)}, u32[]{:S(2)}, u32[]{:S(2)}) collective-permute-start(f32[208,128]{1,0:T(8,128)S(1)} %get-tuple-element.56), channel_id=1, source_target_pairs={{0,16},{4,28},{8,24},{12,20},{16,0},{20,12},{24,8},{28,4},{1,17},{... | collective-permute-start | bytes 319496 | tf_op jit(solution)/shard_map/ppermute | solution.py:743
  49.7 1.5 %collective-permute-start.9 = (f32[208,128]{1,0:T(8,128)S(1)}, f32[208,128]{1,0:T(8,128)S(1)}, u32[]{:S(2)}, u32[]{:S(2)}) collective-permute-start(f32[208,128]{1,0:T(8,128)S(1)} %get-tuple-element.54.after_this), channel_id=1, source_target_pairs={{0,8},{4,20},{8,0},{12,28},{16,24},{20,4},{24,16},{28,12},{1,9},{5... | collective-permute-start | bytes 319496 | tf_op jit(solution)/shard_map/ppermute | solution.py:743
  51.2 6.6 %prep.1 = (f32[2,2,128,2048]{3,2,1,0:T(8,128)}, f32[2,768,128]{2,1,0:T(8,128)}, f32[2,6,128,128]{3,2,1,0:T(8,128)}, f32[8,128]{1,0:T(8,128)S(1)}) custom-call(f32[2,128,128]{2,1,0:T(8,128)} %get-tuple-element.52.projection_in, f32[2,6,128,128]{3,2,1,0:T(8,128)} %get-tuple-element.49.act_in, f32[2,6,128,128]{3,2,1,0:T(8,128)} %get-tuple-element.53.pre_in, ...), custom_call_target="tpu_custom_call" | custom-call | flops 268435456 | bytes 4194304 | tf_op jit(solution)/shard_map/prep/pallas_call | solution.py:761
  57.9 0.8 chain.1.incoming
  58.7 20.7 %scan.1 = (f32[2,32,128]{2,1,0:T(8,128)S(1)}, f32[2,32,128]{2,1,0:T(8,128)S(1)}, f32[2,32,128]{2,1,0:T(8,128)S(1)}, f32[2,32,128]{2,1,0:T(8,128)S(1)}, f32[2,6,1...) custom-call(s32[2]{0:T(128)S(1)} %pad_add_fusion.place, ...), custom_call_target="tpu_custom_call" | custom-call | flops 268435456 | bytes 4194304 | tf_op jit(solution)/shard_map/scan/pallas_call | solution.py:761
  79.8 1.3 collective-permute-start.13
  81.1 2.8 %collective-permute-start.14 = (f32[2,32,128]{2,1,0:T(8,128)S(1)}, f32[2,32,128]{2,1,0:T(8,128)S(1)}, u32[]{:S(2)}, u32[]{:S(2)}) collective-permute-start(f32[2,32,128]{2,1,0:T(8,128)S(1)} %get-tuple-element.67), channel_id=1, source_target_pairs={{0,3},{1,2},{2,1},{3,0},{4,5},{5,4},{6,7},{7,6},{8,10},{9,11},{10,... | collective-permute-start | bytes 98312 | tf_op jit(solution)/shard_map/ppermute | solution.py:736
  83.9 0.8 collective-permute-done.13.refs_2_
  84.7 2.2 %collective-permute-done.14.refs_3_ = f32[2,32,128]{2,1,0:T(8,128)S(1)} collective-permute-done((f32[2,32,128]{2,1,0:T(8,128)S(1)}, f32[2,32,128]{2,1,0:T(8,128)S(1)}, u32[]{:S(2)}, u32[]{:S(2)}) %collective-permute-start.14) | collective-permute-done | bytes 32800 | tf_op jit(solution)/shard_map/ppermute | solution.py:736
  86.9 2.9 %collective-permute-start.17 = (f32[2,32,128]{2,1,0:T(8,128)S(1)}, f32[2,32,128]{2,1,0:T(8,128)S(1)}, u32[]{:S(2)}, u32[]{:S(2)}) collective-permute-start(f32[2,32,128]{2,1,0:T(8,128)S(1)} %grad_projection.1.own), channel_id=1, source_target_pairs={{0,3},{1,2},{2,1},{3,0},{4,5},{5,4},{6,7},{7,6},{8,10},{9,11},{10,... | collective-permute-start | bytes 98312 | tf_op jit(solution)/shard_map/ppermute | solution.py:736
  89.8 1.5 %collective-permute-start.15 = (f32[2,32,128]{2,1,0:T(8,128)S(1)}, f32[2,32,128]{2,1,0:T(8,128)S(1)}, u32[]{:S(2)}, u32[]{:S(2)}) collective-permute-start(f32[2,32,128]{2,1,0:T(8,128)S(1)} %grad_projection.1.own), channel_id=1, source_target_pairs={{0,1},{1,0},{2,3},{3,2},{4,6},{5,7},{6,4},{7,5},{8,11},{9,10},{10,... | collective-permute-start | bytes 98312 | tf_op jit(solution)/shard_map/ppermute | solution.py:736
  91.3 2.0 %step_grad.1.step_part = f32[2,6,96,128]{3,2,1,0:T(8,128)S(1)} custom-call(f32[2,6,128,128]{3,2,1,0:T(8,128)} %get-tuple-element.71.grad_pre_in, f32[2,128,128]{2,1,0:T(8,128)} %get-tuple-element.52.projection_in, f32[2,32,128]{2,1,0:T(8,128)S(1)} %collective-permute-done.12.refs_1_.after_this), custom_call_target="tpu_custom_call" | custom-call | flops 268435456 | bytes 4194304 | tf_op jit(solution)/shard_map/step_grad/pallas_call | solution.py:761
  93.3 1.3 collective-permute-done.16.second
  94.6 5.4 %weights.1 = (f32[1344,128]{1,0:T(8,128)S(1)}, f32[1344,128]{1,0:T(8,128)S(1)}, f32[2,128,768]{2,1,0:T(8,128)}, f32[8,768]{1,0:T(8,128)S(1)}, f32[8,768]{1,0:T(8,128)S(1)}) custom-call(s32[2]{0:T(128)S(1)} %pad_add_fusion.place, f32[2,32,128]{2,1,0:T(8,128)S(1)} %grad_projection.1.own, f32[2,32,128]{2,1,0:T(8,128)S(1)} %collective-permute-done.15.first, ...), custom_call_target="tpu_custom_call" | custom-call | flops 268435456 | bytes 4194304 | tf_op jit(solution)/shard_map/weights/pallas_call | solution.py:761
  100.1 2.1 %collective-permute-done.20.got = f32[1344,128]{1,0:T(8,128)S(1)} collective-permute-done((f32[1344,128]{1,0:T(8,128)S(1)}, f32[1344,128]{1,0:T(8,128)S(1)}, u32[]{:S(2)}, u32[]{:S(2)}) %collective-permute-start.20) | collective-permute-done | bytes 688160 | tf_op jit(solution)/shard_map/ppermute | solution.py:726
  102.2 0.7 halves.1
  102.9 0.9 collective-permute-start.21
  103.8 1.2 collective-permute-start.22
  105.0 1.5 %collective-permute-start.23 = (f32[336,128]{1,0:T(8,128)S(1)}, f32[336,128]{1,0:T(8,128)S(1)}, u32[]{:S(2)}, u32[]{:S(2)}) collective-permute-start(f32[336,128]{1,0:T(8,128)S(1)} %get-tuple-element.80), channel_id=1, source_target_pairs={{0,24},{4,12},{8,16},{12,4},{16,8},{20,28},{24,0},{28,20},{1,25},{... | collective-permute-start | bytes 516104 | tf_op jit(solution)/shard_map/ppermute | solution.py:743
  106.4 1.3 collective-permute-start.18
  107.7 1.3 collective-permute-start.19
  109.0 2.8 %collective-permute-done.19.after = f32[8,768]{1,0:T(8,128)S(1)} collective-permute-done((f32[8,768]{1,0:T(8,128)S(1)}, f32[8,768]{1,0:T(8,128)S(1)}, u32[]{:S(2)}, u32[]{:S(2)}) %collective-permute-start.19) | collective-permute-done | bytes 24608 | tf_op jit(solution)/shard_map/ppermute | solution.py:721
  111.9 2.3 %exit.1.after_this = f32[128,768]{1,0:T(8,128)} custom-call(f32[8,768]{1,0:T(8,128)S(1)} %collective-permute-done.18.before, f32[8,768]{1,0:T(8,128)S(1)} %collective-permute-done.19.after, f32[2,128,768]{2,1,0:T(8,128)} %get-tuple-element.74.conv_grad, f32[2,4,768]{2,1,0:T(4,128)} %conv_weight_in.3, f32[336,128]{1,0:T(8,128)S(1)} %get-tuple-element.77.after_this.refs_0_), custom_call_target="tpu_custom_call" | custom-call | flops 268435456 | bytes 4194304 | tf_op jit(solution)/shard_map/exit/pallas_call | solution.py:761
  114.2 3.8 %collective-permute-start.26 = (f32[336,128]{1,0:T(8,128)S(1)}, f32[336,128]{1,0:T(8,128)S(1)}, u32[]{:S(2)}, u32[]{:S(2)}) collective-permute-start(f32[336,128]{1,0:T(8,128)S(1)} %share_sum.1.after_this.mine), channel_id=1, source_target_pairs={{0,24},{4,12},{8,16},{12,4},{16,8},{20,28},{24,0},{28,20},{1,25},{... | collective-permute-start | bytes 516104 | tf_op jit(solution)/shard_map/ppermute | solution.py:743
  118.1 0.8 collective-permute-start.25
  118.9 0.7 collective-permute-start.24
  119.5 2.4 %gate.1 = (f32[128,768]{1,0:T(8,128)}, f32[128,768]{1,0:T(8,128)}) custom-call(f32[6,128,128]{2,1,0:T(8,128)} %get-tuple-element.63.summed_in, f32[128,768]{1,0:T(8,128)} %gate_in.3, f32[128,768]{1,0:T(8,128)} %cot_in.3, f32[336,128]{1,0:T(8,128)S(1)} %share_sum.1.after_this.mine), custom_call_target="tpu_custom_call" | custom-call | flops 268435456 | bytes 4194304 | tf_op jit(solution)/shard_map/gate/pallas_call | solution.py:761
  121.9 0.8 collective-permute-done.26.refs_2_
  122.7 4.9 %collective-permute-done.25.refs_1_ = f32[336,128]{1,0:T(8,128)S(1)} collective-permute-done((f32[336,128]{1,0:T(8,128)S(1)}, f32[336,128]{1,0:T(8,128)S(1)}, u32[]{:S(2)}, u32[]{:S(2)}) %collective-permute-start.25) | collective-permute-done | bytes 172064 | tf_op jit(solution)/shard_map/ppermute | solution.py:743
  127.7 0.6 joined.1.mine
  128.5 2.0 %collective-permute-done.27.other = f32[4,336,128]{2,1,0:T(8,128)S(1)} collective-permute-done((f32[4,336,128]{2,1,0:T(8,128)S(1)}, f32[4,336,128]{2,1,0:T(8,128)S(1)}, u32[]{:S(2)}, u32[]{:S(2)}) %collective-permute-start.27) | collective-permute-done | bytes 688160 | tf_op jit(solution)/shard_map/ppermute | solution.py:726
  130.5 1.8 %weight_grads.1 = (f32[2,768,128]{2,1,0:T(8,128)}, f32[2,96,768]{2,1,0:T(8,128)}) custom-call(s32[2]{0:T(128)S(1)} %pad_add_fusion.place, f32[4,336,128]{2,1,0:T(8,128)S(1)} %joined.1.mine, f32[4,336,128]{2,1,0:T(8,128)S(1)} %collective-permute-done.27.other), custom_call_target="tpu_custom_call" | custom-call | flops 268435456 | bytes 4194304 | tf_op jit(solution)/shard_map/weight_grads/pallas_call | solution.py:761
  (26 shorter events, 1.0 us)
Async XLA Ops:
  1.4 4.4 %collective-permute-start.1 = (f32[8,768]{1,0:T(8,128)S(1)}, f32[8,768]{1,0:T(8,128)S(1)}, u32[]{:S(2)}, u32[]{:S(2)}) collective-permute-start(f32[8,768]{1,0:T(8,128)S(1)} %get-tuple-element.85), channel_id=1, source_target_pairs={{4,0},{8,4},{12,8},{16,12},{20,16},{24,20},{28,24},{5,1},{9,5},{13... | collective-permute-start | bytes 73736 | tf_op jit(solution)/shard_map/ppermute | solution.py:721
  2.7 3.9 %collective-permute-start = (f32[8,768]{1,0:T(8,128)S(1)}, f32[8,768]{1,0:T(8,128)S(1)}, u32[]{:S(2)}, u32[]{:S(2)}) collective-permute-start(f32[8,768]{1,0:T(8,128)S(1)} %get-tuple-element.86), channel_id=1, source_target_pairs={{0,4},{4,8},{8,12},{12,16},{16,20},{20,24},{24,28},{1,5},{5,9},{9,... | collective-permute-start | bytes 73736 | tf_op jit(solution)/shard_map/ppermute | solution.py:716
  9.9 5.7 %collective-permute-start.2 = (f32[2,32,128]{2,1,0:T(8,128)S(1)}, f32[2,32,128]{2,1,0:T(8,128)S(1)}, u32[]{:S(2)}, u32[]{:S(2)}) collective-permute-start(f32[2,32,128]{2,1,0:T(8,128)S(1)} %get-tuple-element.46), channel_id=1, source_target_pairs={{0,1},{1,0},{2,3},{3,2},{4,6},{5,7},{6,4},{7,5},{8,11},{9,10},{10,... | collective-permute-start | bytes 98312 | tf_op jit(solution)/shard_map/ppermute | solution.py:736
  13.0 5.4 %collective-permute-start.3 = (f32[2,32,128]{2,1,0:T(8,128)S(1)}, f32[2,32,128]{2,1,0:T(8,128)S(1)}, u32[]{:S(2)}, u32[]{:S(2)}) collective-permute-start(f32[2,32,128]{2,1,0:T(8,128)S(1)} %get-tuple-element.47), channel_id=1, source_target_pairs={{0,2},{1,3},{2,0},{3,1},{4,7},{5,6},{6,5},{7,4},{8,9},{9,8},{10,11... | collective-permute-start | bytes 98312 | tf_op jit(solution)/shard_map/ppermute | solution.py:736
  15.6 5.7 %collective-permute-start.4 = (f32[2,32,128]{2,1,0:T(8,128)S(1)}, f32[2,32,128]{2,1,0:T(8,128)S(1)}, u32[]{:S(2)}, u32[]{:S(2)}) collective-permute-start(f32[2,32,128]{2,1,0:T(8,128)S(1)} %get-tuple-element.48), channel_id=1, source_target_pairs={{0,3},{1,2},{2,1},{3,0},{4,5},{5,4},{6,7},{7,6},{8,10},{9,11},{10,... | collective-permute-start | bytes 98312 | tf_op jit(solution)/shard_map/ppermute | solution.py:736
  21.4 5.9 %collective-permute-start.7 = (f32[2,32,128]{2,1,0:T(8,128)S(1)}, f32[2,32,128]{2,1,0:T(8,128)S(1)}, u32[]{:S(2)}, u32[]{:S(2)}) collective-permute-start(f32[2,32,128]{2,1,0:T(8,128)S(1)} %projection.1.own), channel_id=1, source_target_pairs={{0,3},{1,2},{2,1},{3,0},{4,5},{5,4},{6,7},{7,6},{8,10},{9,11},{10,... | collective-permute-start | bytes 98312 | tf_op jit(solution)/shard_map/ppermute | solution.py:736
  22.2 5.7 %collective-permute-start.6 = (f32[2,32,128]{2,1,0:T(8,128)S(1)}, f32[2,32,128]{2,1,0:T(8,128)S(1)}, u32[]{:S(2)}, u32[]{:S(2)}) collective-permute-start(f32[2,32,128]{2,1,0:T(8,128)S(1)} %projection.1.own), channel_id=1, source_target_pairs={{0,2},{1,3},{2,0},{3,1},{4,7},{5,6},{6,5},{7,4},{8,9},{9,8},{10,11... | collective-permute-start | bytes 98312 | tf_op jit(solution)/shard_map/ppermute | solution.py:736
  22.3 5.7 %collective-permute-start.5 = (f32[2,32,128]{2,1,0:T(8,128)S(1)}, f32[2,32,128]{2,1,0:T(8,128)S(1)}, u32[]{:S(2)}, u32[]{:S(2)}) collective-permute-start(f32[2,32,128]{2,1,0:T(8,128)S(1)} %projection.1.own), channel_id=1, source_target_pairs={{0,1},{1,0},{2,3},{3,2},{4,6},{5,7},{6,4},{7,5},{8,11},{9,10},{10,... | collective-permute-start | bytes 98312 | tf_op jit(solution)/shard_map/ppermute | solution.py:736
  42.5 1.6 %collective-permute-start.8 = (f32[2,6,40,128]{3,2,1,0:T(8,128)S(1)}, f32[2,6,40,128]{3,2,1,0:T(8,128)S(1)}, u32[]{:S(2)}, u32[]{:S(2)}) collective-permute-start(f32[2,6,40,128]{3,2,1,0:T(8,128)S(1)} %get-tuple-element.50.mine), channel_id=1, source_target_pairs={{0,4},{4,0},{8,12},{12,8},{16,20},{20,16},{24,28},{28,24},{1,5},{5... | collective-permute-start | bytes 737288 | tf_op jit(solution)/shard_map/ppermute | solution.py:726
  44.7 13.2 %collective-permute-start.10 = (f32[208,128]{1,0:T(8,128)S(1)}, f32[208,128]{1,0:T(8,128)S(1)}, u32[]{:S(2)}, u32[]{:S(2)}) collective-permute-start(f32[208,128]{1,0:T(8,128)S(1)} %get-tuple-element.56), channel_id=1, source_target_pairs={{0,16},{4,28},{8,24},{12,20},{16,0},{20,12},{24,8},{28,4},{1,17},{... | collective-permute-start | bytes 319496 | tf_op jit(solution)/shard_map/ppermute | solution.py:743
  49.7 8.2 %collective-permute-start.11 = (f32[208,128]{1,0:T(8,128)S(1)}, f32[208,128]{1,0:T(8,128)S(1)}, u32[]{:S(2)}, u32[]{:S(2)}) collective-permute-start(f32[208,128]{1,0:T(8,128)S(1)} %get-tuple-element.57), channel_id=1, source_target_pairs={{0,24},{4,12},{8,16},{12,4},{16,8},{20,28},{24,0},{28,20},{1,25},{... | collective-permute-start | bytes 319496 | tf_op jit(solution)/shard_map/ppermute | solution.py:743
  49.7 8.2 %collective-permute-start.9 = (f32[208,128]{1,0:T(8,128)S(1)}, f32[208,128]{1,0:T(8,128)S(1)}, u32[]{:S(2)}, u32[]{:S(2)}) collective-permute-start(f32[208,128]{1,0:T(8,128)S(1)} %get-tuple-element.54.after_this), channel_id=1, source_target_pairs={{0,8},{4,20},{8,0},{12,28},{16,24},{20,4},{24,16},{28,12},{1,9},{5... | collective-permute-start | bytes 319496 | tf_op jit(solution)/shard_map/ppermute | solution.py:743
  79.4 4.5 %collective-permute-start.12 = (f32[2,32,128]{2,1,0:T(8,128)S(1)}, f32[2,32,128]{2,1,0:T(8,128)S(1)}, u32[]{:S(2)}, u32[]{:S(2)}) collective-permute-start(f32[2,32,128]{2,1,0:T(8,128)S(1)} %get-tuple-element.65), channel_id=1, source_target_pairs={{0,1},{1,0},{2,3},{3,2},{4,6},{5,7},{6,4},{7,5},{8,11},{9,10},{10,... | collective-permute-start | bytes 98312 | tf_op jit(solution)/shard_map/ppermute | solution.py:736
  79.8 4.9 %collective-permute-start.13 = (f32[2,32,128]{2,1,0:T(8,128)S(1)}, f32[2,32,128]{2,1,0:T(8,128)S(1)}, u32[]{:S(2)}, u32[]{:S(2)}) collective-permute-start(f32[2,32,128]{2,1,0:T(8,128)S(1)} %get-tuple-element.66), channel_id=1, source_target_pairs={{0,2},{1,3},{2,0},{3,1},{4,7},{5,6},{6,5},{7,4},{8,9},{9,8},{10,11... | collective-permute-start | bytes 98312 | tf_op jit(solution)/shard_map/ppermute | solution.py:736
  81.1 5.7 %collective-permute-start.14 = (f32[2,32,128]{2,1,0:T(8,128)S(1)}, f32[2,32,128]{2,1,0:T(8,128)S(1)}, u32[]{:S(2)}, u32[]{:S(2)}) collective-permute-start(f32[2,32,128]{2,1,0:T(8,128)S(1)} %get-tuple-element.67), channel_id=1, source_target_pairs={{0,3},{1,2},{2,1},{3,0},{4,5},{5,4},{6,7},{7,6},{8,10},{9,11},{10,... | collective-permute-start | bytes 98312 | tf_op jit(solution)/shard_map/ppermute | solution.py:736
  86.9 6.4 %collective-permute-start.17 = (f32[2,32,128]{2,1,0:T(8,128)S(1)}, f32[2,32,128]{2,1,0:T(8,128)S(1)}, u32[]{:S(2)}, u32[]{:S(2)}) collective-permute-start(f32[2,32,128]{2,1,0:T(8,128)S(1)} %grad_projection.1.own), channel_id=1, source_target_pairs={{0,3},{1,2},{2,1},{3,0},{4,5},{5,4},{6,7},{7,6},{8,10},{9,11},{10,... | collective-permute-start | bytes 98312 | tf_op jit(solution)/shard_map/ppermute | solution.py:736
  89.8 4.8 %collective-permute-start.16 = (f32[2,32,128]{2,1,0:T(8,128)S(1)}, f32[2,32,128]{2,1,0:T(8,128)S(1)}, u32[]{:S(2)}, u32[]{:S(2)}) collective-permute-start(f32[2,32,128]{2,1,0:T(8,128)S(1)} %grad_projection.1.own), channel_id=1, source_target_pairs={{0,2},{1,3},{2,0},{3,1},{4,7},{5,6},{6,5},{7,4},{8,9},{9,8},{10,11... | collective-permute-start | bytes 98312 | tf_op jit(solution)/shard_map/ppermute | solution.py:736
  89.8 4.8 %collective-permute-start.15 = (f32[2,32,128]{2,1,0:T(8,128)S(1)}, f32[2,32,128]{2,1,0:T(8,128)S(1)}, u32[]{:S(2)}, u32[]{:S(2)}) collective-permute-start(f32[2,32,128]{2,1,0:T(8,128)S(1)} %grad_projection.1.own), channel_id=1, source_target_pairs={{0,1},{1,0},{2,3},{3,2},{4,6},{5,7},{6,4},{7,5},{8,11},{9,10},{10,... | collective-permute-start | bytes 98312 | tf_op jit(solution)/shard_map/ppermute | solution.py:736
  100.0 2.2 %collective-permute-start.20 = (f32[1344,128]{1,0:T(8,128)S(1)}, f32[1344,128]{1,0:T(8,128)S(1)}, u32[]{:S(2)}, u32[]{:S(2)}) collective-permute-start(f32[1344,128]{1,0:T(8,128)S(1)} %get-tuple-element.76), channel_id=1, source_target_pairs={{0,4},{4,0},{8,12},{12,8},{16,20},{20,16},{24,28},{28,24},{1,5},{5... | collective-permute-start | bytes 2064392 | tf_op jit(solution)/shard_map/ppermute | solution.py:726
  102.9 11.3 %collective-permute-start.21 = (f32[336,128]{1,0:T(8,128)S(1)}, f32[336,128]{1,0:T(8,128)S(1)}, u32[]{:S(2)}, u32[]{:S(2)}) collective-permute-start(f32[336,128]{1,0:T(8,128)S(1)} %get-tuple-element.78), channel_id=1, source_target_pairs={{0,8},{4,20},{8,0},{12,28},{16,24},{20,4},{24,16},{28,12},{1,9},{5... | collective-permute-start | bytes 516104 | tf_op jit(solution)/shard_map/ppermute | solution.py:743
  103.8 10.4 %collective-permute-start.22 = (f32[336,128]{1,0:T(8,128)S(1)}, f32[336,128]{1,0:T(8,128)S(1)}, u32[]{:S(2)}, u32[]{:S(2)}) collective-permute-start(f32[336,128]{1,0:T(8,128)S(1)} %get-tuple-element.79), channel_id=1, source_target_pairs={{0,16},{4,28},{8,24},{12,20},{16,0},{20,12},{24,8},{28,4},{1,17},{... | collective-permute-start | bytes 516104 | tf_op jit(solution)/shard_map/ppermute | solution.py:743
  105.0 9.2 %collective-permute-start.23 = (f32[336,128]{1,0:T(8,128)S(1)}, f32[336,128]{1,0:T(8,128)S(1)}, u32[]{:S(2)}, u32[]{:S(2)}) collective-permute-start(f32[336,128]{1,0:T(8,128)S(1)} %get-tuple-element.80), channel_id=1, source_target_pairs={{0,24},{4,12},{8,16},{12,4},{16,8},{20,28},{24,0},{28,20},{1,25},{... | collective-permute-start | bytes 516104 | tf_op jit(solution)/shard_map/ppermute | solution.py:743
  106.4 2.6 %collective-permute-start.18 = (f32[8,768]{1,0:T(8,128)S(1)}, f32[8,768]{1,0:T(8,128)S(1)}, u32[]{:S(2)}, u32[]{:S(2)}) collective-permute-start(f32[8,768]{1,0:T(8,128)S(1)} %get-tuple-element.72), channel_id=1, source_target_pairs={{0,4},{4,8},{8,12},{12,16},{16,20},{20,24},{24,28},{1,5},{5,9},{9,... | collective-permute-start | bytes 73736 | tf_op jit(solution)/shard_map/ppermute | solution.py:716
  107.7 4.1 %collective-permute-start.19 = (f32[8,768]{1,0:T(8,128)S(1)}, f32[8,768]{1,0:T(8,128)S(1)}, u32[]{:S(2)}, u32[]{:S(2)}) collective-permute-start(f32[8,768]{1,0:T(8,128)S(1)} %get-tuple-element.73), channel_id=1, source_target_pairs={{4,0},{8,4},{12,8},{16,12},{20,16},{24,20},{28,24},{5,1},{9,5},{13... | collective-permute-start | bytes 73736 | tf_op jit(solution)/shard_map/ppermute | solution.py:721
  114.2 8.5 %collective-permute-start.26 = (f32[336,128]{1,0:T(8,128)S(1)}, f32[336,128]{1,0:T(8,128)S(1)}, u32[]{:S(2)}, u32[]{:S(2)}) collective-permute-start(f32[336,128]{1,0:T(8,128)S(1)} %share_sum.1.after_this.mine), channel_id=1, source_target_pairs={{0,24},{4,12},{8,16},{12,4},{16,8},{20,28},{24,0},{28,20},{1,25},{... | collective-permute-start | bytes 516104 | tf_op jit(solution)/shard_map/ppermute | solution.py:743
  118.1 9.6 %collective-permute-start.25 = (f32[336,128]{1,0:T(8,128)S(1)}, f32[336,128]{1,0:T(8,128)S(1)}, u32[]{:S(2)}, u32[]{:S(2)}) collective-permute-start(f32[336,128]{1,0:T(8,128)S(1)} %share_sum.1.after_this.mine), channel_id=1, source_target_pairs={{0,16},{4,28},{8,24},{12,20},{16,0},{20,12},{24,8},{28,4},{1,17},{... | collective-permute-start | bytes 516104 | tf_op jit(solution)/shard_map/ppermute | solution.py:743
  118.9 8.9 %collective-permute-start.24 = (f32[336,128]{1,0:T(8,128)S(1)}, f32[336,128]{1,0:T(8,128)S(1)}, u32[]{:S(2)}, u32[]{:S(2)}) collective-permute-start(f32[336,128]{1,0:T(8,128)S(1)} %share_sum.1.after_this.mine), channel_id=1, source_target_pairs={{0,8},{4,20},{8,0},{12,28},{16,24},{20,4},{24,16},{28,12},{1,9},{5... | collective-permute-start | bytes 516104 | tf_op jit(solution)/shard_map/ppermute | solution.py:743
  128.3 2.2 %collective-permute-start.27 = (f32[4,336,128]{2,1,0:T(8,128)S(1)}, f32[4,336,128]{2,1,0:T(8,128)S(1)}, u32[]{:S(2)}, u32[]{:S(2)}) collective-permute-start(f32[4,336,128]{2,1,0:T(8,128)S(1)} %joined.1.mine), channel_id=1, source_target_pairs={{0,4},{4,0},{8,12},{12,8},{16,20},{20,16},{24,28},{28,24},{1,5},{5... | collective-permute-start | bytes 2064392 | tf_op jit(solution)/shard_map/ppermute | solution.py:726

commit v4 on v3

--- a/solution.py
+++ b/solution.py
@@ -80,11 +80,11 @@
 
 
 def entry_kernel(
-    place, before, after, tokens, conv_weight_in, conv_bias_in, select_in,
+    place, column, before, after, tokens, conv_weight_in, conv_bias_in, select_in,
     *refs,
 ):
-    outs, refs = refs[:-11], refs[-11:]
-    act_out, pre_out, ext, conv_weight, conv_bias, select, act, pre, plain, rows, sems = refs
+    outs, refs = refs[:-9], refs[-9:]
+    act, pre, ext, conv_weight, conv_bias, select, plain, rows, sems = refs
 
     length, width = tokens.shape
     loads = copies_of(
@@ -103,30 +103,28 @@
             pre[side, t] = conv
             plain[...] = conv * jax.nn.sigmoid(conv)
             to_cells(plain, act.at[side, t])
-    stores = copies_of([(pre, pre_out), (act, act_out)], sems.at[pl.ds(4, 2)])
     loads[3].wait()
     for side in range(2):
         rows[...] = dot(full_width(act, side), select[side], (1, 0))
-        deal(place, outs, side, rows)
-    finish_all(stores)
+        deal(place, column, outs, side, rows)
 
 
 def turned(k, by, count):
     return lax.rem(k - 1 + by, count - 1) + 1
 
 
-def deal(place, outs, side, rows):
+def deal(place, column, outs, side, rows):
     share = outs[0].shape[1]
     for k in range(len(outs)):
-        to = place[1] ^ turned(k, place[0], len(outs)) if k else place[1]
+        to = column[0] ^ turned(k, place[0], len(outs)) if k else column[0]
         at = pl.multiple_of(to * share, share)
         outs[k][side] = rows[pl.ds(at, share), :]
 
 
-def collect(place, parts, out):
+def collect(place, column, parts, out):
     share = parts[0].shape[1]
     for k in range(len(parts)):
-        source = place[1] ^ turned(k, place[0], len(parts)) if k else place[1]
+        source = column[0] ^ turned(k, place[0], len(parts)) if k else column[0]
         at = pl.multiple_of(source * share, share)
         out[:, pl.ds(at, share), :] = parts[k][...]
 
@@ -212,11 +210,10 @@
 
 
 def local_kernel(
-    place, own, first, second, third,
-    step_weight_in, step_bias_in, decay_log_in, act_in, gate_in, cot_in,
-    projection_out, step_out, step_pre_out, grad_gated_out, entering_out, carry, row_rates,
-    projection, act, step, step_pre, grad_gated, entering, step_weight, step_bias, decay_log,
-    gate, cot, plain, rates, basis_b, basis_c, rate_rows, decays, sems,
+    place, column, own, first, second, third, act,
+    step_weight_in, step_bias_in, decay_log_in, gate_in, cot_in,
+    projection, step, step_pre, grad_gated, entering, decays, carry, row_rates,
+    step_weight, step_bias, decay_log, gate, cot, plain, rates, basis_b, basis_c, rate_rows, sems,
 ):
     sides, tiles, length, _ = act.shape
     states = decay_log.shape[1]
@@ -226,11 +223,11 @@
     loads = copies_of(
         [
             (step_weight_in, step_weight), (step_bias_in, step_bias), (decay_log_in, decay_log),
-            (gate_in, gate), (cot_in, cot), (act_in, act),
+            (gate_in, gate), (cot_in, cot),
         ],
         sems,
     )
-    collect(place, (own, first, second, third), projection)
+    collect(place, column, (own, first, second, third), projection)
     finish_all(loads)
     for t in range(tiles):
         lanes = lane_tile(t)
@@ -245,13 +242,6 @@
             part = wide[:, lane_tile(t)]
             step_pre[side, t] = part
             step[side, t] = jnp.maximum(part, 0.0) + jnp.log1p(jnp.exp(-jnp.abs(part)))
-    stores = copies_of(
-        [
-            (projection, projection_out), (step, step_out), (step_pre, step_pre_out),
-            (grad_gated, grad_gated_out),
-        ],
-        sems,
-    )
     zero = jnp.zeros((CHAINS, LANES), jnp.float32)
     carry[...] = jnp.zeros_like(carry)
     for side in range(2):
@@ -274,12 +264,12 @@
                     b = basis_b[at, lanes]
                     for g in range(group):
                         decay = jnp.exp2(steps[g] * rate_rows[g, n])
-                        decays[g, at, lanes] = decay
+                        decays[side, at_tiles[g], at, lanes] = decay
                         new.append(decay * state[n * group + g] + b * drives[g])
                 return (tuple(new), tuple(a + v for a, v in zip(summed, steps)))
 
             start = ((zero,) * (states * group), (zero,) * group)
-            state, summed = unrolled(count, 8, forward, start)
+            state, summed = unrolled(count, 4, forward, start)
 
             def retreat(i, state):
                 j = order(i, count, not up)
@@ -291,10 +281,10 @@
                     c = basis_c[at, lanes]
                     for g in range(group):
                         adjoint = state[n * group + g] + c * grads[g]
-                        new.append(decays[g, at, lanes] * adjoint)
+                        new.append(decays[side, at_tiles[g], at, lanes] * adjoint)
                 return tuple(new)
 
-            sent = unrolled(count, 8, retreat, (zero,) * (states * group))
+            sent = unrolled(count, 4, retreat, (zero,) * (states * group))
             for g, t in enumerate(at_tiles):
                 across = [jnp.exp2(summed[g] * rate_rows[g, n]) for n in range(states)]
                 for kind, ends, upward in ((0, state, up), (1, sent, not up)):
@@ -312,10 +302,8 @@
             return keep
 
         lax.fori_loop(0, tiles // group, some_tiles, 0)
-    stores = stores + copies_of([(entering, entering_out)], sems.at[pl.ds(4, 1)])
     for side in range(2):
         row_rates[:, side * states : (side + 1) * states] = rates[side]
-    finish_all(stores)
 
 
 def tile_decay(part, rates):
@@ -325,28 +313,11 @@
     return jnp.exp2(rates * sums)
 
 
-def prep_kernel(
-    projection_in, act_in, pre_in, after_this, bases_out, turned_act_out, slope_out, done,
-    projection, act, pre, bases, turned_act, sems,
-):
-    sides, tiles, length, _ = act.shape
-    states = bases.shape[3] // LANES
-    loads = copies_of([(projection_in, projection), (act_in, act), (pre_in, pre)], sems)
-    loads[0].wait()
-    stores = []
-    for side in range(sides):
+def prep_kernel(projection, after_this, bases, done):
+    for side in range(bases.shape[0]):
+        states = bases.shape[3] // LANES
         fill_bases(projection, side, states, bases.at[side, 0], bases.at[side, 1])
-        stores += copies_of([(bases.at[side], bases_out.at[side])], sems.at[pl.ds(3 + side, 1)])
-    finish_all(loads[1:])
-    for side in range(sides):
-        for t in range(tiles):
-            turned_act[side, lane_tile(t)] = act[side, t].T
-            pre[side, t] = silu_grad(pre[side, t])
-    stores += copies_of(
-        [(turned_act, turned_act_out), (pre, slope_out)], sems.at[pl.ds(5, 2)]
-    )
     done[...] = jnp.zeros_like(done)
-    finish_all(stores)
 
 
 def pair_kernel(place, mine, other, rates, *refs):
@@ -412,11 +383,10 @@
 
 
 def scan_kernel(
-    place, incoming, bases_in, step_weight_in, decay_log_in, skip_gain_in, act_in, step_in,
-    step_pre_in, grad_gated_in, entering_in,
-    mine, first_out, second_out, third_out, grad_act_out, grad_pre_out, summed_outs,
-    bases, step_weight, decay_log, skip_gain, act, step, step_pre, grad_gated, entering,
-    grad_act, grad_pre, summed_out, rates, rate_rows, decays, history,
+    place, column, incoming, bases, act, step, step_pre, grad_gated, entering, decays,
+    step_weight_in, decay_log_in, skip_gain_in,
+    mine, first_out, second_out, third_out, grad_act, grad_pre, summed_out,
+    step_weight, decay_log, skip_gain, rates, rate_rows, history,
     grad_in, grad_out, weights, packed, skip_rows, sems,
 ):
     sides, tiles, length, _ = act.shape
@@ -426,17 +396,13 @@
     group = tile_group(tiles)
     loads = copies_of(
         [
-            (decay_log_in, decay_log), (skip_gain_in, skip_gain), (step_in, step),
-            (act_in, act), (bases_in.at[0], bases.at[0]), (grad_gated_in, grad_gated),
-            (entering_in, entering), (step_pre_in, step_pre), (bases_in.at[1], bases.at[1]),
-            (step_weight_in, step_weight),
+            (decay_log_in, decay_log), (skip_gain_in, skip_gain), (step_weight_in, step_weight),
         ],
         sems,
     )
-    stores = []
-    finish_all(loads[:2])
+    finish_all(loads)
     fill_rates(decay_log, rates)
-    column = lax.broadcasted_iota(jnp.int32, (CHAINS, LANES), 1)
+    lane = lax.broadcasted_iota(jnp.int32, (CHAINS, LANES), 1)
     for side in range(2):
         up = side == 0
         basis_b, basis_c = bases.at[side, 0], bases.at[side, 1]
@@ -446,9 +412,6 @@
             for k in range(2):
                 for t in range(tiles):
                     skip_rows[k, t] = skip_gain[k : k + 1, lane_tile(t)]
-            finish_all(loads[2:-2])
-        else:
-            loads[-2].wait()
 
         def some_tiles(first, keep):
             at_tiles = [first * group + g for g in range(group)]
@@ -483,10 +446,9 @@
             def forward(i, state):
                 j = order(i, count, up)
                 at = cell_rows(j)
-                steps = [step[side, t, at, :] for t in at_tiles]
                 acts = [act[side, t, at, :] for t in at_tiles]
                 grads = [grad_gated[t, at, :] for t in at_tiles]
-                drives = [v * a for v, a in zip(steps, acts)]
+                drives = [step[side, t, at, :] * a for t, a in zip(at_tiles, acts)]
                 outs = [[v * a, None] for v, a in zip(skips, acts)]
                 new = []
                 for n in range(states):
@@ -495,8 +457,7 @@
                     read = grad_out[at, lanes]
                     for g in range(group):
                         before = state[n * group + g]
-                        decay = jnp.exp2(steps[g] * rate_rows[g, n])
-                        decays[g, at, lanes] = decay
+                        decay = decays[side, at_tiles[g], at, lanes]
                         history[g, at, lanes] = before
                         current = decay * before + b * drives[g]
                         outs[g][n % 2] = plus(outs[g][n % 2], c * current)
@@ -529,7 +490,7 @@
                     put = grad_in[at, lanes]
                     for g in range(group):
                         adjoint = state[n * group + g] + c * grads[g]
-                        carried = decays[g, at, lanes] * adjoint
+                        carried = decays[side, at_tiles[g], at, lanes] * adjoint
                         new.append(carried)
                         term = carried * history[g, at, lanes] * rate_rows[g, n]
                         step_terms[g][n % 2] = plus(step_terms[g][n % 2], term)
@@ -549,16 +510,8 @@
             return keep
 
         lax.fori_loop(0, tiles // group, some_tiles, 0)
-        pairs = [
-            (grad_act.at[side], grad_act_out.at[side]), (grad_pre.at[side], grad_pre_out.at[side]),
-        ]
-        if side == 1:
-            pairs.append((summed_out, summed_outs))
-        stores = stores + copies_of(pairs, sems.at[pl.ds(2 * side, 3)])
         wide = full_width(grad_pre, side)
         weights[...] = jnp.zeros_like(weights)
-        if side == 0:
-            loads[-1].wait()
         weights[:ranks] = step_weight[side]
         packed[...] = dot(wide, weights[...], (1, 1))
 
@@ -568,18 +521,16 @@
             for values, start_at in ((grad_in, ranks), (grad_out, ranks + states)):
                 for n in range(states):
                     total = jnp.sum(values[at, lane_tile(n)], axis=1, keepdims=True)
-                    line = jnp.where(column == start_at + n, total, line)
+                    line = jnp.where(lane == start_at + n, total, line)
             packed[at, :] = line
             return keep
 
         lax.fori_loop(0, count, pack, 0)
-        deal(place, (mine, first_out, second_out, third_out), side, packed)
-    finish_all(stores)
-
-
-def step_kernel(grad_pre_in, projection_in, after_this, step_part, grad_pre, projection, sems):
+        deal(place, column, (mine, first_out, second_out, third_out), side, packed)
+
+
+def step_kernel(grad_pre, projection, after_this, step_part):
     _, tiles, ranks, _ = step_part.shape
-    finish_all(copies_of([(grad_pre_in, grad_pre), (projection_in, projection)], sems))
     for side in range(2):
         wide = dot(projection[side], full_width(grad_pre, side), (0, 0))
         for t in range(tiles):
@@ -587,9 +538,9 @@
 
 
 def gate_kernel(
-    summed_in, gate_in, cot_in, after_this, block_out, gate_grad, summed, gate, cot, plain, sems
+    summed, gate_in, cot_in, after_this, block_out, gate_grad, gate, cot, plain, sems
 ):
-    finish_all(copies_of([(summed_in, summed), (gate_in, gate), (cot_in, cot)], sems))
+    finish_all(copies_of([(gate_in, gate), (cot_in, cot)], sems))
     for t in range(summed.shape[0]):
         lanes = lane_tile(t)
         values = gate[:, lanes]
@@ -600,40 +551,30 @@
 
 
 def weight_kernel(
-    place, own, first, second, third, turned_act_in, slope_in, grad_act_in, select_in, step_part,
-    keep, send, conv_grad_out, head, tail,
-    turned_act, slope, grad_act, select, grad, conv_grad, plain, sems,
+    place, column, own, first, second, third, act, pre, grad_act, step_part, select_in,
+    keep, send, conv_grad, head, tail, select, grad, plain, cells, sems,
 ):
-    sides, tiles, length, _ = slope.shape
-    loads = copies_of(
-        [
-            (turned_act_in, turned_act), (select_in, select), (grad_act_in, grad_act),
-            (slope_in, slope),
-        ],
-        sems,
-    )
-    collect(place, (own, first, second, third), grad)
-    loads[0].wait()
+    sides, tiles, length, _ = act.shape
+    loads = copies_of([(select_in, select)], sems)
+    collect(place, column, (own, first, second, third), grad)
     for side in range(2):
-        part = dot(turned_act[side], grad[side], (1, 0))
+        part = dot(full_width(act, side), grad[side], (0, 0))
         for out, core in ((keep, side), (send, 1 - side)):
 
             @pl.when(lax.rem(place[0], 2) == core)
             def _():
                 out[: tiles * LANES] = part
                 out[tiles * LANES :] = step_part[side].reshape(-1, LANES)
-    finish_all(loads[1:])
+    finish_all(loads)
     for side in range(2):
         wide = dot(grad[side], select[side], (1, 1))
         for t in range(tiles):
             lanes = lane_tile(t)
-            grad_act[side, t] = grad_act[side, t] + wide[:, lanes]
-            to_tokens(grad_act.at[side, t], plain)
-            conv_grad[side, :, lanes] = plain[...] * slope[side, t]
+            cells[...] = grad_act[side, t] + wide[:, lanes]
+            to_tokens(cells, plain)
+            conv_grad[side, :, lanes] = plain[...] * silu_grad(pre[side, t])
     head[...] = conv_grad[0, :HALO]
     tail[...] = conv_grad[1, length - HALO :]
-    stores = copies_of([(conv_grad, conv_grad_out)], sems.at[pl.ds(4, 1)])
-    finish_all(stores)
 
 
 def halves_kernel(place, keep, got, mine, *refs):
@@ -691,14 +632,14 @@
     margin = taps - 1
     loads = copies_of(
         [
-            (conv_grad.at[0], up.at[pl.ds(0, length)]),
-            (conv_grad.at[1], down.at[pl.ds(HALO, length)]),
             (conv_weight_in, conv_weight),
         ],
         sems,
     )
+    up[:length] = conv_grad[0]
     up[length:] = after[...]
     down[:HALO] = before[...]
+    down[HALO:] = conv_grad[1]
     finish_all(loads)
     for t in range(width // LANES):
         lanes = lane_tile(t)
@@ -746,16 +687,18 @@
 def call(kernel, name, out_shape, scratch, mib, args, kinds, outs=None):
     spaces = {
         "v": pl.BlockSpec(memory_space=pltpu.VMEM),
+        "m": pl.BlockSpec(memory_space=pltpu.VMEM),
         "h": pl.BlockSpec(memory_space=pltpu.HBM),
         "s": pl.BlockSpec(memory_space=pltpu.SMEM),
     }
     outs = outs or "v" * len(out_shape)
+    pinned = {"m": pltpu.VMEM, "h": pltpu.HBM}
     args = [
-        pltpu.with_memory_space_constraint(a, pltpu.HBM) if k == "h" else a
+        pltpu.with_memory_space_constraint(a, pinned[k]) if k in pinned else a
         for a, k in zip(args, kinds, strict=True)
     ]
     results = [
-        pltpu.HBM(shape, jnp.float32) if k == "h" else shape_of(*shape)
+        pinned[k](shape, jnp.float32) if k in pinned else shape_of(*shape)
         for shape, k in zip(out_shape, outs, strict=True)
     ]
     return pl.pallas_call(
@@ -799,7 +742,8 @@
     ranks = step_weight.shape[1]
     places = lax.axis_size("ctx")
     columns = lax.axis_size("ch")
-    place = jnp.stack([lax.axis_index("ctx"), lax.axis_index("ch")]).astype(jnp.int32)
+    place = lax.axis_index("ctx").astype(jnp.int32).reshape(1)
+    column = lax.axis_index("ch").astype(jnp.int32).reshape(1)
     group = tile_group(tiles)
     chips = places // 2
     near = places == 8
@@ -825,25 +769,25 @@
         entry_kernel, "entry", (*(shared,) * columns, pair, pair),
         [
             vmem((length + 2 * HALO, width)), vmem(conv_weight.shape), vmem(conv_bias.shape),
-            vmem(select_weight.shape), vmem(pair), vmem(pair), vmem(one[1:]), vmem(one[1:]), dma(6),
+            vmem(select_weight.shape), vmem(one[1:]), vmem(one[1:]), dma(4),
         ],
-        12, (place, before, after, tokens, conv_weight, conv_bias, select_weight), "svvhhhh",
-        "v" * columns + "hh",
-    )
-    projection, step, step_pre, grad_gated, entering, carried, rates = call(
-        local_kernel, "local", (narrow, pair, pair, one, chain_ends, carry, row_rates),
+        12, (place, column, before, after, tokens, conv_weight, conv_bias, select_weight), "ssvvhhhh",
+        "v" * columns + "mm",
+    )
+    projection, step, step_pre, grad_gated, entering, decays, carried, rates = call(
+        local_kernel, "local",
+        (narrow, pair, pair, one, chain_ends, (*pair[:-1], states * LANES), carry, row_rates),
         [
-            vmem(narrow), vmem(pair), vmem(pair), vmem(pair), vmem(one), vmem(chain_ends),
             vmem(step_weight.shape), vmem(step_bias.shape), vmem(decay_log.shape),
             vmem(flat), vmem(flat), vmem(one[1:]),
-            rate_scratch, bases, bases, row_scratch, grouped, dma(6),
+            rate_scratch, bases, bases, row_scratch, dma(5),
         ],
-        24,
+        12,
         (
-            place, *summed_shares(parts, "projection")[0], step_weight, step_bias, decay_log, act,
-            gate_input, cotangent,
+            place, column, *summed_shares(parts, "projection")[0], act, step_weight, step_bias,
+            decay_log, gate_input, cotangent,
         ),
-        "svvvvhhhhhh", "hhhhhvv",
+        "ssvvvvmhhhhh", "mmmmmmvv",
     )
     if near:
         other = swapped(carried, "ctx", 1)
@@ -856,14 +800,9 @@
     else:
         gathered = lax.all_gather(carried, "ctx")
         ahead = rates
-    spread_bases, turned_act, slope, done = call(
-        prep_kernel, "prep",
-        ((2, 2, length, states * LANES), (2, width, length), pair, (HALO, LANES)),
-        [
-            vmem(narrow), vmem(pair), vmem(pair), vmem((2, 2, length, states * LANES)),
-            vmem((2, width, length)), dma(7),
-        ],
-        14, (projection, act, pre, ahead), "hhhv", "hhhv",
+    spread_bases, done = call(
+        prep_kernel, "prep", ((2, 2, length, states * LANES), (HALO, LANES)), [],
+        6, (projection, ahead), "mv", "mv",
     )
     if near:
         (incoming,) = call(
@@ -878,36 +817,32 @@
     *grad_parts, grad_act, grad_pre, summed = call(
         scan_kernel, "scan", (*(shared,) * columns, pair, pair, one),
         [
-            vmem(spread_bases.shape), vmem(step_weight.shape), vmem(decay_log.shape),
-            vmem(skip_gain.shape),
-            vmem(pair), vmem(pair), vmem(pair), vmem(one), vmem(chain_ends),
-            vmem(pair), vmem(pair), vmem(one), rate_scratch, row_scratch, grouped,
-            grouped, bases, bases, vmem((LANES, width)), vmem((length, LANES)),
-            vmem((2, tiles, 1, LANES)), dma(10),
+            vmem(step_weight.shape), vmem(decay_log.shape), vmem(skip_gain.shape),
+            rate_scratch, row_scratch, grouped, bases, bases, vmem((LANES, width)),
+            vmem((length, LANES)), vmem((2, tiles, 1, LANES)), dma(3),
         ],
-        28,
+        12,
         (
-            place, incoming, spread_bases, step_weight, decay_log, skip_gain, act, step, step_pre,
-            grad_gated, entering,
+            place, column, incoming, spread_bases, act, step, step_pre, grad_gated, entering,
+            decays, step_weight, decay_log, skip_gain,
         ),
-        "svhhhhhhhhh", "v" * columns + "hhh",
+        "ssvmmmmmmmhhh", "v" * columns + "mmm",
     )
     grad_shares, arrived = summed_shares(grad_parts, "grad_projection")
     (step_part,) = call(
-        step_kernel, "step_grad", ((2, tiles, ranks, LANES),), [vmem(pair), vmem(narrow), dma(2)],
-        8, (grad_pre, projection, arrived), "hhv",
+        step_kernel, "step_grad", ((2, tiles, ranks, LANES),), [],
+        8, (grad_pre, projection, arrived), "mmv",
     )
     half = width + tiles * ranks
     keep, send, conv_grad, head, tail = call(
         weight_kernel, "weights",
         ((half, LANES), (half, LANES), (2, *flat), (HALO, width), (HALO, width)),
         [
-            vmem((2, width, length)), vmem(pair), vmem(pair), vmem(select_weight.shape),
-            vmem(narrow), vmem((2, *flat)), vmem(one[1:]), dma(5),
+            vmem(select_weight.shape), vmem(narrow), vmem(one[1:]), vmem(one[1:]), dma(1),
         ],
-        16,
-        (place, *grad_shares, turned_act, slope, grad_act, select_weight, step_part),
-        "svvvvhhhhv", "vvhvv",
+        12,
+        (place, column, *grad_shares, act, pre, grad_act, step_part, select_weight),
+        "ssvvvvmmmvh", "vvmvv",
     )
     before = from_before(tail, "ctx")
     after = from_after(head, "ctx")
@@ -920,9 +855,9 @@
         exit_kernel, "exit", (flat,),
         [
             vmem((length + HALO, width)), vmem((length + HALO, width)), vmem(conv_weight.shape),
-            dma(3),
+            dma(1),
         ],
-        8, (before, after, conv_grad, conv_weight, ahead), "vvhhv",
+        8, (before, after, conv_grad, conv_weight, ahead), "vvmhv",
     )
     if near:
         rows = half // chips
@@ -933,8 +868,8 @@
         ahead = mine
     block_out, gate_grad = call(
         gate_kernel, "gate", (flat, flat),
-        [vmem(one), vmem(flat), vmem(flat), vmem(one[1:]), dma(3)],
-        8, (summed, gate_input, cotangent, ahead), "hhhv",
+        [vmem(flat), vmem(flat), vmem(one[1:]), dma(2)],
+        8, (summed, gate_input, cotangent, ahead), "mhhv",
     )
     if near:
         got = [swapped_chips(mine, k) for k in range(1, chips)]

time: 133 us -> 118 us (0.89)
  Pallas kernels: 61.9 us -> 45 us
  waiting for transfers between devices: 27.2 us -> 29.4 us
    pallas_call x16, Pallas kernels: 61.9 us -> 45 us  [call(): pl.pallas_call(kernel, in_specs=[spaces[k] for k in kinds], out_specs=[sp...]
  transfers between devices with their start and end apart: 28 -> 28, of which waited for: 15 -> 17; matrix products, arithmetic and copies ran while one was open for 0% -> 0% of each run, Pallas kernels for 10% -> 8%
where the time goes in v4:
time: 118 us
  Pallas kernels  45 us (38%)
  starting transfers between devices  41.6 us (35%)
  waiting for transfers between devices  29.4 us (25%)
    pallas_call x16, Pallas kernels, call(): pl.pallas_call(kernel, in_specs=[spaces[k] for k in kinds], out_specs=[sp...  45 us
    ppermute x12, starting transfers between devices, swapped_shares(): return lax.ppermute(value, ('ctx', 'ch'), pairs)  19 us
    ppermute x9, starting transfers between devices, swapped_chips(): return lax.ppermute(value, 'ctx', pairs)  15.4 us
    ppermute x12, waiting for transfers between devices, swapped_shares(): return lax.ppermute(value, ('ctx', 'ch'), pairs)  13.3 us
    ppermute x9, waiting for transfers between devices, swapped_chips(): return lax.ppermute(value, 'ctx', pairs)  6.8 us
    ppermute x3, waiting for transfers between devices, swapped(): return lax.ppermute(value, axis, [(i, i ^ by) for i in range(count)])  5.75 us
    ppermute x2, starting transfers between devices, from_before(): return lax.ppermute(value, axis, [(i, i + 1) for i in range(count - 1)])  4.31 us
    ppermute x2, waiting for transfers between devices, from_after(): return lax.ppermute(value, axis, [(i + 1, i) for i in range(count - 1)])  2.77 us
  transfers between devices with their start and end apart: 28, of which 17 were waited for; matrix products, arithmetic and copies ran while one was open for 0% of the time, Pallas kernels for 8%

profile of v4, /device:TPU:0, one launch (start us, length us, event | category | flops | bytes accessed | tf_op | source)
XLA Modules:
  0.0 117.5 jit_solution(4543048555857327682)
XLA Ops:
  0.6 0.8 fusion
  1.4 1.3 %collective-permute-start.1 = (f32[8,768]{1,0:T(8,128)S(1)}, f32[8,768]{1,0:T(8,128)S(1)}, u32[]{:S(2)}, u32[]{:S(2)}) collective-permute-start(f32[8,768]{1,0:T(8,128)S(1)} %get-tuple-element.83), channel_id=1, source_target_pairs={{4,0},{8,4},{12,8},{16,12},{20,16},{24,20},{28,24},{5,1},{9,5},{13... | collective-permute-start | bytes 73736 | tf_op jit(solution)/shard_map/ppermute | solution.py:662
  2.7 3.0 %collective-permute-start = (f32[8,768]{1,0:T(8,128)S(1)}, f32[8,768]{1,0:T(8,128)S(1)}, u32[]{:S(2)}, u32[]{:S(2)}) collective-permute-start(f32[8,768]{1,0:T(8,128)S(1)} %get-tuple-element.84), channel_id=1, source_target_pairs={{0,4},{4,8},{8,12},{12,16},{16,20},{20,24},{24,28},{1,5},{5,9},{9,... | collective-permute-start | bytes 73736 | tf_op jit(solution)/shard_map/ppermute | solution.py:657
  5.7 0.8 collective-permute-done.before
  6.6 2.5 %entry.1 = (f32[2,32,128]{2,1,0:T(8,128)S(1)}, f32[2,32,128]{2,1,0:T(8,128)S(1)}, f32[2,32,128]{2,1,0:T(8,128)S(1)}, f32[2,32,128]{2,1,0:T(8,128)S(1)}, f32[2,6,...) custom-call(s32[1]{0:T(128)} %bitcast.place, s32[1]{0:T(128)} %bitcast.1.column, ...), custom_call_target="tpu_custom_call" | custom-call | flops 268435456 | bytes 4194304 | tf_op jit(solution)/shard_map/entry/pallas_call | solution.py:704
  9.1 3.1 %collective-permute-start.2 = (f32[2,32,128]{2,1,0:T(8,128)S(1)}, f32[2,32,128]{2,1,0:T(8,128)S(1)}, u32[]{:S(2)}, u32[]{:S(2)}) collective-permute-start(f32[2,32,128]{2,1,0:T(8,128)S(1)} %get-tuple-element.45), channel_id=1, source_target_pairs={{0,1},{1,0},{2,3},{3,2},{4,6},{5,7},{6,4},{7,5},{8,11},{9,10},{10,... | collective-permute-start | bytes 98312 | tf_op jit(solution)/shard_map/ppermute | solution.py:677
  12.2 2.6 %collective-permute-start.3 = (f32[2,32,128]{2,1,0:T(8,128)S(1)}, f32[2,32,128]{2,1,0:T(8,128)S(1)}, u32[]{:S(2)}, u32[]{:S(2)}) collective-permute-start(f32[2,32,128]{2,1,0:T(8,128)S(1)} %get-tuple-element.46), channel_id=1, source_target_pairs={{0,2},{1,3},{2,0},{3,1},{4,7},{5,6},{6,5},{7,4},{8,9},{9,8},{10,11... | collective-permute-start | bytes 98312 | tf_op jit(solution)/shard_map/ppermute | solution.py:677
  14.8 2.8 %collective-permute-done.3.refs_2_ = f32[2,32,128]{2,1,0:T(8,128)S(1)} collective-permute-done((f32[2,32,128]{2,1,0:T(8,128)S(1)}, f32[2,32,128]{2,1,0:T(8,128)S(1)}, u32[]{:S(2)}, u32[]{:S(2)}) %collective-permute-start.3) | collective-permute-done | bytes 32800 | tf_op jit(solution)/shard_map/ppermute | solution.py:677
  17.5 3.0 %collective-permute-done.4.refs_3_ = f32[2,32,128]{2,1,0:T(8,128)S(1)} collective-permute-done((f32[2,32,128]{2,1,0:T(8,128)S(1)}, f32[2,32,128]{2,1,0:T(8,128)S(1)}, u32[]{:S(2)}, u32[]{:S(2)}) %collective-permute-start.4) | collective-permute-done | bytes 32800 | tf_op jit(solution)/shard_map/ppermute | solution.py:677
  20.5 0.9 collective-permute-start.7
  21.4 3.6 %collective-permute-start.5 = (f32[2,32,128]{2,1,0:T(8,128)S(1)}, f32[2,32,128]{2,1,0:T(8,128)S(1)}, u32[]{:S(2)}, u32[]{:S(2)}) collective-permute-start(f32[2,32,128]{2,1,0:T(8,128)S(1)} %projection.1.own), channel_id=1, source_target_pairs={{0,1},{1,0},{2,3},{3,2},{4,6},{5,7},{6,4},{7,5},{8,11},{9,10},{10,... | collective-permute-start | bytes 98312 | tf_op jit(solution)/shard_map/ppermute | solution.py:677
  24.9 1.4 %collective-permute-done.7.third = f32[2,32,128]{2,1,0:T(8,128)S(1)} collective-permute-done((f32[2,32,128]{2,1,0:T(8,128)S(1)}, f32[2,32,128]{2,1,0:T(8,128)S(1)}, u32[]{:S(2)}, u32[]{:S(2)}) %collective-permute-start.7) | collective-permute-done | bytes 32800 | tf_op jit(solution)/shard_map/ppermute | solution.py:677
  26.4 0.7 collective-permute-done.6.second
  27.0 12.4 %local.1 = (f32[2,128,128]{2,1,0:T(8,128)S(1)}, f32[2,6,128,128]{3,2,1,0:T(8,128)S(1)}, f32[2,6,128,128]{3,2,1,0:T(8,128)S(1)}, f32[6,128,128]{2,1,0:T(8,128)S(1...) custom-call(s32[1]{0:T(128)} %bitcast.place, ...), custom_call_target="tpu_custom_call" | custom-call | flops 268435456 | bytes 4194304 | tf_op jit(solution)/shard_map/local/pallas_call | solution.py:704
  39.5 1.5 %collective-permute-done.8.other = f32[2,6,40,128]{3,2,1,0:T(8,128)S(1)} collective-permute-done((f32[2,6,40,128]{3,2,1,0:T(8,128)S(1)}, f32[2,6,40,128]{3,2,1,0:T(8,128)S(1)}, u32[]{:S(2)}, u32[]{:S(2)}) %collective-permute-start.8) | collective-permute-done | bytes 245792 | tf_op jit(solution)/shard_map/ppermute | solution.py:667
  41.2 5.0 %collective-permute-start.10 = (f32[208,128]{1,0:T(8,128)S(1)}, f32[208,128]{1,0:T(8,128)S(1)}, u32[]{:S(2)}, u32[]{:S(2)}) collective-permute-start(f32[208,128]{1,0:T(8,128)S(1)} %get-tuple-element.54), channel_id=1, source_target_pairs={{0,16},{4,28},{8,24},{12,20},{16,0},{20,12},{24,8},{28,4},{1,17},{... | collective-permute-start | bytes 319496 | tf_op jit(solution)/shard_map/ppermute | solution.py:684
  46.1 1.5 %collective-permute-start.9 = (f32[208,128]{1,0:T(8,128)S(1)}, f32[208,128]{1,0:T(8,128)S(1)}, u32[]{:S(2)}, u32[]{:S(2)}) collective-permute-start(f32[208,128]{1,0:T(8,128)S(1)} %get-tuple-element.52.after_this), channel_id=1, source_target_pairs={{0,8},{4,20},{8,0},{12,28},{16,24},{20,4},{24,16},{28,12},{1,9},{5... | collective-permute-start | bytes 319496 | tf_op jit(solution)/shard_map/ppermute | solution.py:684
  47.7 3.9 %prep.1 = (f32[2,2,128,2048]{3,2,1,0:T(8,128)S(1)}, f32[8,128]{1,0:T(8,128)S(1)}) custom-call(f32[2,128,128]{2,1,0:T(8,128)S(1)} %get-tuple-element.51.projection, f32[208,128]{1,0:T(8,128)S(1)} %get-tuple-element.52.after_this), custom_call_target="tpu_custom_call" | custom-call | flops 268435456 | bytes 4194304 | tf_op jit(solution)/shard_map/prep/pallas_call | solution.py:704
  51.6 0.2 collective-permute-done.11.refs_2_
  51.8 1.1 collective-permute-done.9.refs_0_
  52.9 0.2 chain.1.incoming
  53.1 16.5 %scan.1 = (f32[2,32,128]{2,1,0:T(8,128)S(1)}, f32[2,32,128]{2,1,0:T(8,128)S(1)}, f32[2,32,128]{2,1,0:T(8,128)S(1)}, f32[2,32,128]{2,1,0:T(8,128)S(1)}, f32[2,6,1...) custom-call(s32[1]{0:T(128)} %bitcast.place, s32[1]{0:T(128)} %bitcast.1.column, ...), custom_call_target="tpu_custom_call" | custom-call | flops 268435456 | bytes 4194304 | tf_op jit(solution)/shard_map/scan/pallas_call | solution.py:704
  69.7 0.3 collective-permute-start.12
  70.0 1.4 %collective-permute-start.13 = (f32[2,32,128]{2,1,0:T(8,128)S(1)}, f32[2,32,128]{2,1,0:T(8,128)S(1)}, u32[]{:S(2)}, u32[]{:S(2)}) collective-permute-start(f32[2,32,128]{2,1,0:T(8,128)S(1)} %get-tuple-element.65), channel_id=1, source_target_pairs={{0,2},{1,3},{2,0},{3,1},{4,7},{5,6},{6,5},{7,4},{8,9},{9,8},{10,11... | collective-permute-start | bytes 98312 | tf_op jit(solution)/shard_map/ppermute | solution.py:677
  71.4 2.8 %collective-permute-start.14 = (f32[2,32,128]{2,1,0:T(8,128)S(1)}, f32[2,32,128]{2,1,0:T(8,128)S(1)}, u32[]{:S(2)}, u32[]{:S(2)}) collective-permute-start(f32[2,32,128]{2,1,0:T(8,128)S(1)} %get-tuple-element.66), channel_id=1, source_target_pairs={{0,3},{1,2},{2,1},{3,0},{4,5},{5,4},{6,7},{7,6},{8,10},{9,11},{10,... | collective-permute-start | bytes 98312 | tf_op jit(solution)/shard_map/ppermute | solution.py:677
  74.1 0.7 collective-permute-done.13.refs_2_
  74.8 2.4 %collective-permute-done.14.refs_3_ = f32[2,32,128]{2,1,0:T(8,128)S(1)} collective-permute-done((f32[2,32,128]{2,1,0:T(8,128)S(1)}, f32[2,32,128]{2,1,0:T(8,128)S(1)}, u32[]{:S(2)}, u32[]{:S(2)}) %collective-permute-start.14) | collective-permute-done | bytes 32800 | tf_op jit(solution)/shard_map/ppermute | solution.py:677
  77.2 2.9 %collective-permute-start.17 = (f32[2,32,128]{2,1,0:T(8,128)S(1)}, f32[2,32,128]{2,1,0:T(8,128)S(1)}, u32[]{:S(2)}, u32[]{:S(2)}) collective-permute-start(f32[2,32,128]{2,1,0:T(8,128)S(1)} %grad_projection.1.own), channel_id=1, source_target_pairs={{0,3},{1,2},{2,1},{3,0},{4,5},{5,4},{6,7},{7,6},{8,10},{9,11},{10,... | collective-permute-start | bytes 98312 | tf_op jit(solution)/shard_map/ppermute | solution.py:677
  80.1 1.5 %collective-permute-start.15 = (f32[2,32,128]{2,1,0:T(8,128)S(1)}, f32[2,32,128]{2,1,0:T(8,128)S(1)}, u32[]{:S(2)}, u32[]{:S(2)}) collective-permute-start(f32[2,32,128]{2,1,0:T(8,128)S(1)} %grad_projection.1.own), channel_id=1, source_target_pairs={{0,1},{1,0},{2,3},{3,2},{4,6},{5,7},{6,4},{7,5},{8,11},{9,10},{10,... | collective-permute-start | bytes 98312 | tf_op jit(solution)/shard_map/ppermute | solution.py:677
  81.6 0.8 step_grad.1.step_part
  82.4 0.5 collective-permute-done.17.third
  82.9 2.0 %collective-permute-done.16.second = f32[2,32,128]{2,1,0:T(8,128)S(1)} collective-permute-done((f32[2,32,128]{2,1,0:T(8,128)S(1)}, f32[2,32,128]{2,1,0:T(8,128)S(1)}, u32[]{:S(2)}, u32[]{:S(2)}) %collective-permute-start.16) | collective-permute-done | bytes 32800 | tf_op jit(solution)/shard_map/ppermute | solution.py:677
  84.9 2.8 %weights.1 = (f32[1344,128]{1,0:T(8,128)S(1)}, f32[1344,128]{1,0:T(8,128)S(1)}, f32[2,128,768]{2,1,0:T(8,128)S(1)}, f32[8,768]{1,0:T(8,128)S(1)}, f32[8,768]{1,0:T(8,128)S(1)}) custom-call(s32[1]{0:T(128)} %bitcast.place, s32[1]{0:T(128)} %bitcast.1.column, f32[2,32,128]{2,1,0:T(8,128)S(1)} %grad_projection.1.own, ...), custom_call_target="tpu_custom_call" | custom-call | flops 268435456 | bytes 4194304 | tf_op jit(solution)/shard_map/weights/pallas_call | solution.py:704
  87.8 2.1 %collective-permute-done.20.got = f32[1344,128]{1,0:T(8,128)S(1)} collective-permute-done((f32[1344,128]{1,0:T(8,128)S(1)}, f32[1344,128]{1,0:T(8,128)S(1)}, u32[]{:S(2)}, u32[]{:S(2)}) %collective-permute-start.20) | collective-permute-done | bytes 688160 | tf_op jit(solution)/shard_map/ppermute | solution.py:667
  90.1 0.8 collective-permute-start.21
  90.9 0.5 collective-permute-start.22
  91.4 2.3 %collective-permute-start.23 = (f32[336,128]{1,0:T(8,128)S(1)}, f32[336,128]{1,0:T(8,128)S(1)}, u32[]{:S(2)}, u32[]{:S(2)}) collective-permute-start(f32[336,128]{1,0:T(8,128)S(1)} %get-tuple-element.78), channel_id=1, source_target_pairs={{0,24},{4,12},{8,16},{12,4},{16,8},{20,28},{24,0},{28,20},{1,25},{... | collective-permute-start | bytes 516104 | tf_op jit(solution)/shard_map/ppermute | solution.py:684
  93.6 1.3 %collective-permute-start.18 = (f32[8,768]{1,0:T(8,128)S(1)}, f32[8,768]{1,0:T(8,128)S(1)}, u32[]{:S(2)}, u32[]{:S(2)}) collective-permute-start(f32[8,768]{1,0:T(8,128)S(1)} %get-tuple-element.70), channel_id=1, source_target_pairs={{0,4},{4,8},{8,12},{12,16},{16,20},{20,24},{24,28},{1,5},{5,9},{9,... | collective-permute-start | bytes 73736 | tf_op jit(solution)/shard_map/ppermute | solution.py:657
  94.9 1.3 %collective-permute-start.19 = (f32[8,768]{1,0:T(8,128)S(1)}, f32[8,768]{1,0:T(8,128)S(1)}, u32[]{:S(2)}, u32[]{:S(2)}) collective-permute-start(f32[8,768]{1,0:T(8,128)S(1)} %get-tuple-element.71), channel_id=1, source_target_pairs={{4,0},{8,4},{12,8},{16,12},{20,16},{24,20},{28,24},{5,1},{9,5},{13... | collective-permute-start | bytes 73736 | tf_op jit(solution)/shard_map/ppermute | solution.py:662
  96.2 2.8 %collective-permute-done.19.after = f32[8,768]{1,0:T(8,128)S(1)} collective-permute-done((f32[8,768]{1,0:T(8,128)S(1)}, f32[8,768]{1,0:T(8,128)S(1)}, u32[]{:S(2)}, u32[]{:S(2)}) %collective-permute-start.19) | collective-permute-done | bytes 24608 | tf_op jit(solution)/shard_map/ppermute | solution.py:662
  99.0 1.9 %exit.1.after_this = f32[128,768]{1,0:T(8,128)} custom-call(f32[8,768]{1,0:T(8,128)S(1)} %collective-permute-done.18.before, f32[8,768]{1,0:T(8,128)S(1)} %collective-permute-done.19.after, f32[2,128,768]{2,1,0:T(8,128)S(1)} %get-tuple-element.72.conv_grad, f32[2,4,768]{2,1,0:T(4,128)} %conv_weight_in.3, f32[336,128]{1,0:T(8,128)S(1)} %get-tuple-element.75.after_this.refs_0_), custom_call_target="tpu_custom_call" | custom-call | flops 268435456 | bytes 4194304 | tf_op jit(solution)/shard_map/exit/pallas_call | solution.py:704
  101.0 3.1 %collective-permute-start.26 = (f32[336,128]{1,0:T(8,128)S(1)}, f32[336,128]{1,0:T(8,128)S(1)}, u32[]{:S(2)}, u32[]{:S(2)}) collective-permute-start(f32[336,128]{1,0:T(8,128)S(1)} %share_sum.1.after_this.mine), channel_id=1, source_target_pairs={{0,24},{4,12},{8,16},{12,4},{16,8},{20,28},{24,0},{28,20},{1,25},{... | collective-permute-start | bytes 516104 | tf_op jit(solution)/shard_map/ppermute | solution.py:684
  104.1 1.5 %collective-permute-start.25 = (f32[336,128]{1,0:T(8,128)S(1)}, f32[336,128]{1,0:T(8,128)S(1)}, u32[]{:S(2)}, u32[]{:S(2)}) collective-permute-start(f32[336,128]{1,0:T(8,128)S(1)} %share_sum.1.after_this.mine), channel_id=1, source_target_pairs={{0,16},{4,28},{8,24},{12,20},{16,0},{20,12},{24,8},{28,4},{1,17},{... | collective-permute-start | bytes 516104 | tf_op jit(solution)/shard_map/ppermute | solution.py:684
  105.6 0.7 collective-permute-start.24
  106.3 2.3 %gate.1 = (f32[128,768]{1,0:T(8,128)}, f32[128,768]{1,0:T(8,128)}) custom-call(f32[6,128,128]{2,1,0:T(8,128)S(1)} %get-tuple-element.62.summed, f32[128,768]{1,0:T(8,128)} %gate_in.3, f32[128,768]{1,0:T(8,128)} %cot_in.3, f32[336,128]{1,0:T(8,128)S(1)} %share_sum.1.after_this.mine), custom_call_target="tpu_custom_call" | custom-call | flops 268435456 | bytes 4194304 | tf_op jit(solution)/shard_map/gate/pallas_call | solution.py:704
  108.7 5.4 %collective-permute-done.25.refs_1_ = f32[336,128]{1,0:T(8,128)S(1)} collective-permute-done((f32[336,128]{1,0:T(8,128)S(1)}, f32[336,128]{1,0:T(8,128)S(1)}, u32[]{:S(2)}, u32[]{:S(2)}) %collective-permute-start.25) | collective-permute-done | bytes 172064 | tf_op jit(solution)/shard_map/ppermute | solution.py:684
  114.2 2.1 %collective-permute-done.27.other = f32[4,336,128]{2,1,0:T(8,128)S(1)} collective-permute-done((f32[4,336,128]{2,1,0:T(8,128)S(1)}, f32[4,336,128]{2,1,0:T(8,128)S(1)}, u32[]{:S(2)}, u32[]{:S(2)}) %collective-permute-start.27) | collective-permute-done | bytes 688160 | tf_op jit(solution)/shard_map/ppermute | solution.py:667
  116.3 1.2 %weight_grads.1 = (f32[2,768,128]{2,1,0:T(8,128)}, f32[2,96,768]{2,1,0:T(8,128)}) custom-call(s32[1]{0:T(128)} %bitcast.place, f32[4,336,128]{2,1,0:T(8,128)S(1)} %joined.1.mine, f32[4,336,128]{2,1,0:T(8,128)S(1)} %collective-permute-done.27.other), custom_call_target="tpu_custom_call" | custom-call | flops 268435456 | bytes 4194304 | tf_op jit(solution)/shard_map/weight_grads/pallas_call | solution.py:704
  (25 shorter events, 0.7 us)
Async XLA Ops:
  1.4 4.3 %collective-permute-start.1 = (f32[8,768]{1,0:T(8,128)S(1)}, f32[8,768]{1,0:T(8,128)S(1)}, u32[]{:S(2)}, u32[]{:S(2)}) collective-permute-start(f32[8,768]{1,0:T(8,128)S(1)} %get-tuple-element.83), channel_id=1, source_target_pairs={{4,0},{8,4},{12,8},{16,12},{20,16},{24,20},{28,24},{5,1},{9,5},{13... | collective-permute-start | bytes 73736 | tf_op jit(solution)/shard_map/ppermute | solution.py:662
  2.7 3.9 %collective-permute-start = (f32[8,768]{1,0:T(8,128)S(1)}, f32[8,768]{1,0:T(8,128)S(1)}, u32[]{:S(2)}, u32[]{:S(2)}) collective-permute-start(f32[8,768]{1,0:T(8,128)S(1)} %get-tuple-element.84), channel_id=1, source_target_pairs={{0,4},{4,8},{8,12},{12,16},{16,20},{20,24},{24,28},{1,5},{5,9},{9,... | collective-permute-start | bytes 73736 | tf_op jit(solution)/shard_map/ppermute | solution.py:657
  9.1 5.7 %collective-permute-start.2 = (f32[2,32,128]{2,1,0:T(8,128)S(1)}, f32[2,32,128]{2,1,0:T(8,128)S(1)}, u32[]{:S(2)}, u32[]{:S(2)}) collective-permute-start(f32[2,32,128]{2,1,0:T(8,128)S(1)} %get-tuple-element.45), channel_id=1, source_target_pairs={{0,1},{1,0},{2,3},{3,2},{4,6},{5,7},{6,4},{7,5},{8,11},{9,10},{10,... | collective-permute-start | bytes 98312 | tf_op jit(solution)/shard_map/ppermute | solution.py:677
  12.2 5.4 %collective-permute-start.3 = (f32[2,32,128]{2,1,0:T(8,128)S(1)}, f32[2,32,128]{2,1,0:T(8,128)S(1)}, u32[]{:S(2)}, u32[]{:S(2)}) collective-permute-start(f32[2,32,128]{2,1,0:T(8,128)S(1)} %get-tuple-element.46), channel_id=1, source_target_pairs={{0,2},{1,3},{2,0},{3,1},{4,7},{5,6},{6,5},{7,4},{8,9},{9,8},{10,11... | collective-permute-start | bytes 98312 | tf_op jit(solution)/shard_map/ppermute | solution.py:677
  14.8 5.7 %collective-permute-start.4 = (f32[2,32,128]{2,1,0:T(8,128)S(1)}, f32[2,32,128]{2,1,0:T(8,128)S(1)}, u32[]{:S(2)}, u32[]{:S(2)}) collective-permute-start(f32[2,32,128]{2,1,0:T(8,128)S(1)} %get-tuple-element.47), channel_id=1, source_target_pairs={{0,3},{1,2},{2,1},{3,0},{4,5},{5,4},{6,7},{7,6},{8,10},{9,11},{10,... | collective-permute-start | bytes 98312 | tf_op jit(solution)/shard_map/ppermute | solution.py:677
  20.5 5.9 %collective-permute-start.7 = (f32[2,32,128]{2,1,0:T(8,128)S(1)}, f32[2,32,128]{2,1,0:T(8,128)S(1)}, u32[]{:S(2)}, u32[]{:S(2)}) collective-permute-start(f32[2,32,128]{2,1,0:T(8,128)S(1)} %projection.1.own), channel_id=1, source_target_pairs={{0,3},{1,2},{2,1},{3,0},{4,5},{5,4},{6,7},{7,6},{8,10},{9,11},{10,... | collective-permute-start | bytes 98312 | tf_op jit(solution)/shard_map/ppermute | solution.py:677
  21.4 5.7 %collective-permute-start.6 = (f32[2,32,128]{2,1,0:T(8,128)S(1)}, f32[2,32,128]{2,1,0:T(8,128)S(1)}, u32[]{:S(2)}, u32[]{:S(2)}) collective-permute-start(f32[2,32,128]{2,1,0:T(8,128)S(1)} %projection.1.own), channel_id=1, source_target_pairs={{0,2},{1,3},{2,0},{3,1},{4,7},{5,6},{6,5},{7,4},{8,9},{9,8},{10,11... | collective-permute-start | bytes 98312 | tf_op jit(solution)/shard_map/ppermute | solution.py:677
  21.4 5.7 %collective-permute-start.5 = (f32[2,32,128]{2,1,0:T(8,128)S(1)}, f32[2,32,128]{2,1,0:T(8,128)S(1)}, u32[]{:S(2)}, u32[]{:S(2)}) collective-permute-start(f32[2,32,128]{2,1,0:T(8,128)S(1)} %projection.1.own), channel_id=1, source_target_pairs={{0,1},{1,0},{2,3},{3,2},{4,6},{5,7},{6,4},{7,5},{8,11},{9,10},{10,... | collective-permute-start | bytes 98312 | tf_op jit(solution)/shard_map/ppermute | solution.py:677
  39.4 1.6 %collective-permute-start.8 = (f32[2,6,40,128]{3,2,1,0:T(8,128)S(1)}, f32[2,6,40,128]{3,2,1,0:T(8,128)S(1)}, u32[]{:S(2)}, u32[]{:S(2)}) collective-permute-start(f32[2,6,40,128]{3,2,1,0:T(8,128)S(1)} %get-tuple-element.49.mine), channel_id=1, source_target_pairs={{0,4},{4,0},{8,12},{12,8},{16,20},{20,16},{24,28},{28,24},{1,5},{5... | collective-permute-start | bytes 737288 | tf_op jit(solution)/shard_map/ppermute | solution.py:667
  41.2 10.4 %collective-permute-start.10 = (f32[208,128]{1,0:T(8,128)S(1)}, f32[208,128]{1,0:T(8,128)S(1)}, u32[]{:S(2)}, u32[]{:S(2)}) collective-permute-start(f32[208,128]{1,0:T(8,128)S(1)} %get-tuple-element.54), channel_id=1, source_target_pairs={{0,16},{4,28},{8,24},{12,20},{16,0},{20,12},{24,8},{28,4},{1,17},{... | collective-permute-start | bytes 319496 | tf_op jit(solution)/shard_map/ppermute | solution.py:684
  46.1 5.7 %collective-permute-start.11 = (f32[208,128]{1,0:T(8,128)S(1)}, f32[208,128]{1,0:T(8,128)S(1)}, u32[]{:S(2)}, u32[]{:S(2)}) collective-permute-start(f32[208,128]{1,0:T(8,128)S(1)} %get-tuple-element.55), channel_id=1, source_target_pairs={{0,24},{4,12},{8,16},{12,4},{16,8},{20,28},{24,0},{28,20},{1,25},{... | collective-permute-start | bytes 319496 | tf_op jit(solution)/shard_map/ppermute | solution.py:684
  46.1 6.8 %collective-permute-start.9 = (f32[208,128]{1,0:T(8,128)S(1)}, f32[208,128]{1,0:T(8,128)S(1)}, u32[]{:S(2)}, u32[]{:S(2)}) collective-permute-start(f32[208,128]{1,0:T(8,128)S(1)} %get-tuple-element.52.after_this), channel_id=1, source_target_pairs={{0,8},{4,20},{8,0},{12,28},{16,24},{20,4},{24,16},{28,12},{1,9},{5... | collective-permute-start | bytes 319496 | tf_op jit(solution)/shard_map/ppermute | solution.py:684
  69.7 4.5 %collective-permute-start.12 = (f32[2,32,128]{2,1,0:T(8,128)S(1)}, f32[2,32,128]{2,1,0:T(8,128)S(1)}, u32[]{:S(2)}, u32[]{:S(2)}) collective-permute-start(f32[2,32,128]{2,1,0:T(8,128)S(1)} %get-tuple-element.64), channel_id=1, source_target_pairs={{0,1},{1,0},{2,3},{3,2},{4,6},{5,7},{6,4},{7,5},{8,11},{9,10},{10,... | collective-permute-start | bytes 98312 | tf_op jit(solution)/shard_map/ppermute | solution.py:677
  70.0 4.8 %collective-permute-start.13 = (f32[2,32,128]{2,1,0:T(8,128)S(1)}, f32[2,32,128]{2,1,0:T(8,128)S(1)}, u32[]{:S(2)}, u32[]{:S(2)}) collective-permute-start(f32[2,32,128]{2,1,0:T(8,128)S(1)} %get-tuple-element.65), channel_id=1, source_target_pairs={{0,2},{1,3},{2,0},{3,1},{4,7},{5,6},{6,5},{7,4},{8,9},{9,8},{10,11... | collective-permute-start | bytes 98312 | tf_op jit(solution)/shard_map/ppermute | solution.py:677
  71.4 5.8 %collective-permute-start.14 = (f32[2,32,128]{2,1,0:T(8,128)S(1)}, f32[2,32,128]{2,1,0:T(8,128)S(1)}, u32[]{:S(2)}, u32[]{:S(2)}) collective-permute-start(f32[2,32,128]{2,1,0:T(8,128)S(1)} %get-tuple-element.66), channel_id=1, source_target_pairs={{0,3},{1,2},{2,1},{3,0},{4,5},{5,4},{6,7},{7,6},{8,10},{9,11},{10,... | collective-permute-start | bytes 98312 | tf_op jit(solution)/shard_map/ppermute | solution.py:677
  77.2 5.8 %collective-permute-start.17 = (f32[2,32,128]{2,1,0:T(8,128)S(1)}, f32[2,32,128]{2,1,0:T(8,128)S(1)}, u32[]{:S(2)}, u32[]{:S(2)}) collective-permute-start(f32[2,32,128]{2,1,0:T(8,128)S(1)} %grad_projection.1.own), channel_id=1, source_target_pairs={{0,3},{1,2},{2,1},{3,0},{4,5},{5,4},{6,7},{7,6},{8,10},{9,11},{10,... | collective-permute-start | bytes 98312 | tf_op jit(solution)/shard_map/ppermute | solution.py:677
  80.1 4.8 %collective-permute-start.16 = (f32[2,32,128]{2,1,0:T(8,128)S(1)}, f32[2,32,128]{2,1,0:T(8,128)S(1)}, u32[]{:S(2)}, u32[]{:S(2)}) collective-permute-start(f32[2,32,128]{2,1,0:T(8,128)S(1)} %grad_projection.1.own), channel_id=1, source_target_pairs={{0,2},{1,3},{2,0},{3,1},{4,7},{5,6},{6,5},{7,4},{8,9},{9,8},{10,11... | collective-permute-start | bytes 98312 | tf_op jit(solution)/shard_map/ppermute | solution.py:677
  80.1 4.8 %collective-permute-start.15 = (f32[2,32,128]{2,1,0:T(8,128)S(1)}, f32[2,32,128]{2,1,0:T(8,128)S(1)}, u32[]{:S(2)}, u32[]{:S(2)}) collective-permute-start(f32[2,32,128]{2,1,0:T(8,128)S(1)} %grad_projection.1.own), channel_id=1, source_target_pairs={{0,1},{1,0},{2,3},{3,2},{4,6},{5,7},{6,4},{7,5},{8,11},{9,10},{10,... | collective-permute-start | bytes 98312 | tf_op jit(solution)/shard_map/ppermute | solution.py:677
  87.8 2.2 %collective-permute-start.20 = (f32[1344,128]{1,0:T(8,128)S(1)}, f32[1344,128]{1,0:T(8,128)S(1)}, u32[]{:S(2)}, u32[]{:S(2)}) collective-permute-start(f32[1344,128]{1,0:T(8,128)S(1)} %get-tuple-element.74), channel_id=1, source_target_pairs={{0,4},{4,0},{8,12},{12,8},{16,20},{20,16},{24,28},{28,24},{1,5},{5... | collective-permute-start | bytes 2064392 | tf_op jit(solution)/shard_map/ppermute | solution.py:667
  90.1 10.8 %collective-permute-start.21 = (f32[336,128]{1,0:T(8,128)S(1)}, f32[336,128]{1,0:T(8,128)S(1)}, u32[]{:S(2)}, u32[]{:S(2)}) collective-permute-start(f32[336,128]{1,0:T(8,128)S(1)} %get-tuple-element.76), channel_id=1, source_target_pairs={{0,8},{4,20},{8,0},{12,28},{16,24},{20,4},{24,16},{28,12},{1,9},{5... | collective-permute-start | bytes 516104 | tf_op jit(solution)/shard_map/ppermute | solution.py:684
  90.9 10.0 %collective-permute-start.22 = (f32[336,128]{1,0:T(8,128)S(1)}, f32[336,128]{1,0:T(8,128)S(1)}, u32[]{:S(2)}, u32[]{:S(2)}) collective-permute-start(f32[336,128]{1,0:T(8,128)S(1)} %get-tuple-element.77), channel_id=1, source_target_pairs={{0,16},{4,28},{8,24},{12,20},{16,0},{20,12},{24,8},{28,4},{1,17},{... | collective-permute-start | bytes 516104 | tf_op jit(solution)/shard_map/ppermute | solution.py:684
  91.4 9.6 %collective-permute-start.23 = (f32[336,128]{1,0:T(8,128)S(1)}, f32[336,128]{1,0:T(8,128)S(1)}, u32[]{:S(2)}, u32[]{:S(2)}) collective-permute-start(f32[336,128]{1,0:T(8,128)S(1)} %get-tuple-element.78), channel_id=1, source_target_pairs={{0,24},{4,12},{8,16},{12,4},{16,8},{20,28},{24,0},{28,20},{1,25},{... | collective-permute-start | bytes 516104 | tf_op jit(solution)/shard_map/ppermute | solution.py:684
  93.6 2.6 %collective-permute-start.18 = (f32[8,768]{1,0:T(8,128)S(1)}, f32[8,768]{1,0:T(8,128)S(1)}, u32[]{:S(2)}, u32[]{:S(2)}) collective-permute-start(f32[8,768]{1,0:T(8,128)S(1)} %get-tuple-element.70), channel_id=1, source_target_pairs={{0,4},{4,8},{8,12},{12,16},{16,20},{20,24},{24,28},{1,5},{5,9},{9,... | collective-permute-start | bytes 73736 | tf_op jit(solution)/shard_map/ppermute | solution.py:657
  94.9 4.1 %collective-permute-start.19 = (f32[8,768]{1,0:T(8,128)S(1)}, f32[8,768]{1,0:T(8,128)S(1)}, u32[]{:S(2)}, u32[]{:S(2)}) collective-permute-start(f32[8,768]{1,0:T(8,128)S(1)} %get-tuple-element.71), channel_id=1, source_target_pairs={{4,0},{8,4},{12,8},{16,12},{20,16},{24,20},{28,24},{5,1},{9,5},{13... | collective-permute-start | bytes 73736 | tf_op jit(solution)/shard_map/ppermute | solution.py:662
  101.0 7.7 %collective-permute-start.26 = (f32[336,128]{1,0:T(8,128)S(1)}, f32[336,128]{1,0:T(8,128)S(1)}, u32[]{:S(2)}, u32[]{:S(2)}) collective-permute-start(f32[336,128]{1,0:T(8,128)S(1)} %share_sum.1.after_this.mine), channel_id=1, source_target_pairs={{0,24},{4,12},{8,16},{12,4},{16,8},{20,28},{24,0},{28,20},{1,25},{... | collective-permute-start | bytes 516104 | tf_op jit(solution)/shard_map/ppermute | solution.py:684
  104.1 10.0 %collective-permute-start.25 = (f32[336,128]{1,0:T(8,128)S(1)}, f32[336,128]{1,0:T(8,128)S(1)}, u32[]{:S(2)}, u32[]{:S(2)}) collective-permute-start(f32[336,128]{1,0:T(8,128)S(1)} %share_sum.1.after_this.mine), channel_id=1, source_target_pairs={{0,16},{4,28},{8,24},{12,20},{16,0},{20,12},{24,8},{28,4},{1,17},{... | collective-permute-start | bytes 516104 | tf_op jit(solution)/shard_map/ppermute | solution.py:684
  105.6 8.4 %collective-permute-start.24 = (f32[336,128]{1,0:T(8,128)S(1)}, f32[336,128]{1,0:T(8,128)S(1)}, u32[]{:S(2)}, u32[]{:S(2)}) collective-permute-start(f32[336,128]{1,0:T(8,128)S(1)} %share_sum.1.after_this.mine), channel_id=1, source_target_pairs={{0,8},{4,20},{8,0},{12,28},{16,24},{20,4},{24,16},{28,12},{1,9},{5... | collective-permute-start | bytes 516104 | tf_op jit(solution)/shard_map/ppermute | solution.py:684
  114.1 2.2 %collective-permute-start.27 = (f32[4,336,128]{2,1,0:T(8,128)S(1)}, f32[4,336,128]{2,1,0:T(8,128)S(1)}, u32[]{:S(2)}, u32[]{:S(2)}) collective-permute-start(f32[4,336,128]{2,1,0:T(8,128)S(1)} %joined.1.mine), channel_id=1, source_target_pairs={{0,4},{4,0},{8,12},{12,8},{16,20},{20,16},{24,28},{28,24},{1,5},{5... | collective-permute-start | bytes 2064392 | tf_op jit(solution)/shard_map/ppermute | solution.py:667

commit v5 on v4

v5 whole, which is shorter than its diff:
```python
import functools

import jax
import jax.numpy as jnp
from jax import lax
from jax.experimental import pallas as pl
from jax.experimental.pallas import tpu as pltpu
from jax.sharding import PartitionSpec as P

FULL_PRECISION = lax.Precision.HIGHEST
LANES = 128
CHAINS = 8
HALO = 8
LOG2E = 1.4426950408889634
LN2 = 0.6931471805599453
MIB = 1024 * 1024


def params(mib):
    return pltpu.CompilerParams(vmem_limit_bytes=mib * MIB)


def shape_of(*dims):
    return jax.ShapeDtypeStruct(dims, jnp.float32)


def dot(a, b, contract):
    return lax.dot_general(
        a, b, ((contract[:1], contract[1:]), ((), ())), precision=FULL_PRECISION,
        preferred_element_type=jnp.float32,
    )


def silu_grad(values):
    sigmoid_values = jax.nn.sigmoid(values)
    return sigmoid_values * (1.0 + values * (1.0 - sigmoid_values))


def lane_tile(t):
    return slice(t * LANES, (t + 1) * LANES)


def full_width(ref, *lead):
    tiles = ref.shape[len(lead)]
    return jnp.concatenate([ref[(*lead, t)] for t in range(tiles)], axis=1)


def convolved(ext, at_row, side, lanes, rows, conv_weight, conv_bias):
    taps = conv_weight.shape[1]
    margin = taps - 1
    conv = jnp.broadcast_to(conv_bias[side : side + 1, lanes], (rows, LANES))
    for k in range(taps):
        at = at_row + (k - margin if side == 0 else margin - k)
        conv = conv + conv_weight[side, k : k + 1, lanes] * ext[at : at + rows, lanes]
    return conv


def copies_of(pairs, sems):
    copies = [pltpu.make_async_copy(a, b, sems.at[i]) for i, (a, b) in enumerate(pairs)]
    for copy in copies:
        copy.start()
    return copies


def to_cells(tokens, cells):
    count = tokens.shape[0] // CHAINS
    for j in range(count):
        cells[j * CHAINS : (j + 1) * CHAINS] = tokens[pl.ds(j, CHAINS, stride=count), :]


def to_tokens(cells, tokens):
    count = tokens.shape[0] // CHAINS
    for j in range(count):
        tokens[pl.ds(j, CHAINS, stride=count), :] = cells[j * CHAINS : (j + 1) * CHAINS]


def finish_all(copies):
    for copy in copies:
        copy.wait()


def entry_kernel(
    place, near, far, tokens, conv_weight_in, conv_bias_in, select_in,
    partial, act, pre, ext, conv_weight, conv_bias, select, plain, sems,
):
    length, width = tokens.shape
    loads = copies_of(
        [
            (tokens, ext.at[pl.ds(HALO, length)]), (conv_weight_in, conv_weight),
            (conv_bias_in, conv_bias), (select_in.at[0], select),
        ],
        sems,
    )
    core = lax.rem(place[0], 2)
    ext[:HALO] = jnp.where(core == 0, far[...], near[...])
    ext[HALO + length :] = jnp.where(core == 0, near[...], far[...])
    finish_all(loads[:3])
    enter(0, ext, conv_weight, conv_bias, select, loads[3], partial, act, pre, plain)


def second_entry_kernel(
    ext, conv_weight_in, conv_bias_in, select_in, gate_in, cot_in,
    partial, act, pre, grad_gated, spreader,
    conv_weight, conv_bias, select, plain, gate, cot, sems,
):
    loads = copies_of(
        [
            (conv_weight_in, conv_weight), (conv_bias_in, conv_bias), (select_in.at[1], select),
            (gate_in, gate), (cot_in, cot),
        ],
        sems,
    )
    fill_spreader(spreader)
    finish_all(loads[:2])
    enter(1, ext, conv_weight, conv_bias, select, loads[2], partial, act, pre, plain)
    finish_all(loads[3:])
    for t in range(grad_gated.shape[0]):
        lanes = lane_tile(t)
        values = gate[:, lanes]
        plain[...] = cot[:, lanes] * values * jax.nn.sigmoid(values)
        to_cells(plain, grad_gated.at[t])


def enter(side, ext, conv_weight, conv_bias, select, load, partial, act, pre, plain):
    tiles, length, _ = act.shape
    for t in range(tiles):
        conv = convolved(ext, HALO, side, lane_tile(t), length, conv_weight, conv_bias)
        pre[t] = conv
        plain[...] = conv * jax.nn.sigmoid(conv)
        to_cells(plain, act.at[t])
    load.wait()
    partial[...] = dot(full_width(act), select[...], (1, 0))


def turned(k, by, count):
    return lax.rem(k - 1 + by, count - 1) + 1


def fill_spreader(spreader):
    rows, columns = spreader.shape
    bases = columns // LANES
    row = lax.broadcasted_iota(jnp.int32, (rows, LANES), 0)
    kind = jnp.where(row >= rows - 3 * bases, lax.rem(row + bases - rows % bases, bases), -1)
    for n in range(bases):
        spreader[:, lane_tile(n)] = jnp.where(kind == n, 1.0, 0.0).astype(jnp.bfloat16)


def fill_bases(projection, spreader, bases):
    states = bases.shape[2] // LANES
    first = LANES - 2 * states
    lane = lax.broadcasted_iota(jnp.int32, projection.shape, 1)
    rest = jnp.where(lane >= first, projection[...], 0.0)
    joined = jnp.zeros_like(rest)
    for k in range(3):
        part = rest.astype(jnp.bfloat16).astype(jnp.float32)
        rest = rest - part
        joined = joined + (pltpu.roll(part, LANES - 2 * states * k, 1) if k else part)
    joined = joined.astype(jnp.bfloat16)
    width = 4 * LANES
    for at in range(0, 2 * states * LANES, width):
        value = jnp.dot(
            joined, spreader[:, at : at + width], preferred_element_type=jnp.float32
        )
        kind, lanes = at // (states * LANES), at % (states * LANES)
        bases[kind, :, lanes : lanes + width] = value


def fill_rates(decay_log, rates):
    for t in range(rates.shape[0]):
        rates[t] = -LOG2E * jnp.exp(decay_log[:, lane_tile(t)])


def sublane():
    return lax.broadcasted_iota(jnp.int32, (CHAINS, LANES), 0)


def shifted(value, by, up):
    rolled = pltpu.roll(value, by if up else CHAINS - by, 0)
    place = sublane()
    keep = place >= by if up else place < CHAINS - by
    return jnp.where(keep, rolled, 0.0)


def over_chains(decays, ends, up):
    by = 1
    while by < CHAINS:
        ends = [d * shifted(f, by, up) + f for d, f in zip(decays, ends)]
        if 2 * by < CHAINS:
            turn = by if up else CHAINS - by
            decays = [d * pltpu.roll(d, turn, 0) for d in decays]
        by *= 2
    return ends


def order(i, count, up):
    return i if up else count - 1 - i


def tile_group(tiles):
    return 2 if tiles % 2 == 0 else 1


def unrolled(count, times, body, start):
    times = times if count % times == 0 else 1

    def several(i, state):
        for k in range(times):
            state = body(i * times + k, state)
        return state

    return lax.fori_loop(0, count // times, several, start)


def plus(total, term):
    return term if total is None else total + term


def fill_rate_rows(rates, tiles, rate_rows):
    for g, t in enumerate(tiles):
        for n in range(rate_rows.shape[1]):
            rate_rows[g, n] = jnp.broadcast_to(rates[t, n : n + 1], (CHAINS, LANES))


def cell_rows(j):
    return pl.ds(pl.multiple_of(j * CHAINS, CHAINS), CHAINS)


def local_kernel(side, *refs):
    own, first, second, third, act, grad_gated, spreader = refs[:7]
    earlier, refs = refs[7 : 7 + 2 * side], refs[7 + 2 * side :]
    step_weight_in, step_bias_in, decay_log_in, *refs = refs
    projection, step, step_pre, entering, decays, bases, carry, row_rates, *refs = refs
    step_weight, step_bias, decay_log, rates, rate_rows, sems = refs
    tiles, length, _ = act.shape
    states = decay_log.shape[0]
    ranks = step_weight.shape[0]
    count = length // CHAINS
    group = tile_group(tiles)
    loads = copies_of(
        [
            (step_weight_in.at[side], step_weight), (decay_log_in.at[side], decay_log),
            (step_bias_in, step_bias),
        ],
        sems,
    )
    projection[...] = (own[...] + first[...]) + (second[...] + third[...])
    fill_bases(projection, spreader, bases)
    finish_all(loads)
    fill_rates(decay_log, rates)
    wide = dot(projection[:, :ranks], step_weight[...], (1, 0)) + step_bias[side : side + 1]
    for t in range(tiles):
        part = wide[:, lane_tile(t)]
        step_pre[t] = part
        step[t] = jnp.maximum(part, 0.0) + jnp.log1p(jnp.exp(-jnp.abs(part)))
    zero = jnp.zeros((CHAINS, LANES), jnp.float32)
    if side:
        carry[...] = earlier[0][...]
        row_rates[...] = earlier[1][...]
    else:
        carry[...] = jnp.zeros_like(carry)
        row_rates[...] = jnp.zeros_like(row_rates)
    up = side == 0
    basis_b, basis_c = bases.at[0], bases.at[1]

    def some_tiles(first, keep):
        at_tiles = [first * group + g for g in range(group)]
        fill_rate_rows(rates, at_tiles, rate_rows)

        def forward(i, current):
            state, summed = current
            j = order(i, count, up)
            at = cell_rows(j)
            steps = [step[t, at, :] for t in at_tiles]
            drives = [v * act[t, at, :] for v, t in zip(steps, at_tiles)]
            new = []
            for n in range(states):
                lanes = lane_tile(n)
                b = basis_b[at, lanes]
                for g in range(group):
                    decay = jnp.exp2(steps[g] * rate_rows[g, n])
                    decays[at_tiles[g], at, lanes] = decay
                    new.append(decay * state[n * group + g] + b * drives[g])
            return (tuple(new), tuple(a + v for a, v in zip(summed, steps)))

        start = ((zero,) * (states * group), (zero,) * group)
        state, summed = unrolled(count, 4, forward, start)

        def retreat(i, state):
            j = order(i, count, not up)
            at = cell_rows(j)
            grads = [grad_gated[t, at, :] for t in at_tiles]
            new = []
            for n in range(states):
                lanes = lane_tile(n)
                c = basis_c[at, lanes]
                for g in range(group):
                    adjoint = state[n * group + g] + c * grads[g]
                    new.append(decays[at_tiles[g], at, lanes] * adjoint)
            return tuple(new)

        sent = unrolled(count, 4, retreat, (zero,) * (states * group))
        for g, t in enumerate(at_tiles):
            across = [jnp.exp2(summed[g] * rate_rows[g, n]) for n in range(states)]
            for kind, ends, upward in ((0, state, up), (1, sent, not up)):
                ends = over_chains(across, list(ends[g::group]), upward)
                last = CHAINS - 1 if upward else 0
                for n in range(states):
                    entering[kind, t, n] = shifted(ends[n], 1, upward)
                    at = side * states + n
                    carry[0 if upward else 1, t, at : at + 1] = ends[n][last : last + 1]
            whole = jnp.sum(summed[g], axis=0, keepdims=True)
            at = 2 * states + side
            for k in range(2):
                carry[k, t, at : at + 1] = whole
        return keep

    lax.fori_loop(0, tiles // group, some_tiles, 0)
    row_rates[:, side * states : (side + 1) * states] = rates[...]


def tile_decay(part, rates):
    rows = rates.shape[1]
    row = lax.broadcasted_iota(jnp.int32, rates.shape, 1)
    sums = jnp.where(row < rows // 2, part[:, rows : rows + 1], part[:, rows + 1 : rows + 2])
    return jnp.exp2(rates * sums)


def pair_kernel(place, mine, other, rates, *refs):
    outs, total = refs[:-1], refs[-1]
    rows = rates.shape[1]
    core, chip = lax.rem(place[0], 2), lax.div(place[0], 2)
    low = jnp.where(core == 0, mine[...], other[...])
    high = jnp.where(core == 0, other[...], mine[...])
    spread_rates = rates[...]
    decay_low = tile_decay(low[0], spread_rates)
    decay_high = tile_decay(high[0], spread_rates)
    total[...] = low + high
    total[0, :, :rows] = decay_high * low[0][:, :rows] + high[0][:, :rows]
    total[1, :, :rows] = decay_low * high[1][:, :rows] + low[1][:, :rows]
    tiles = rates.shape[0]
    for k, out in enumerate(outs, 1):
        to = chip ^ turned(k, core, len(outs) + 1)
        below = lax.convert_element_type(to < chip, jnp.int32)
        for t in range(tiles):
            out[t * rows : (t + 1) * rows] = total[below, t, :rows]
            for side in range(2):
                at = tiles * rows + side * tiles + t
                out[at : at + 1] = total[0, t, rows + side : rows + side + 1]


def chain_kernel(place, other, rates, *refs):
    gathered, (out, parts) = refs[:-2], refs[-2:]
    rows = rates.shape[1]
    chips = parts.shape[0]
    core, chip = lax.rem(place[0], 2), lax.div(place[0], 2)
    parts[chip] = jnp.zeros(parts.shape[1:], jnp.float32)
    tiles = rates.shape[0]
    for k, part in enumerate(gathered, 1):
        source = chip ^ turned(k, core, chips)
        for t in range(tiles):
            parts[source, t, :rows] = part[t * rows : (t + 1) * rows]
            for side in range(2):
                at = tiles * rows + side * tiles + t
                parts[source, t, rows + side : rows + side + 1] = part[at : at + 1]
    spread_rates = rates[...]
    for kind in range(2):
        state = jnp.zeros(rates.shape, jnp.float32)
        for k in range(chips) if kind == 0 else reversed(range(chips)):
            part = parts[k]
            new = tile_decay(part, spread_rates) * state + part[:, :rows]
            state = jnp.where(k < chip if kind == 0 else k > chip, new, state)
        part = other[kind]
        new = tile_decay(part, spread_rates) * state + part[:, :rows]
        out[kind] = jnp.where(core == 1 - kind, new, state)


def long_chain_kernel(place, gathered, rates, out):
    rows = rates.shape[1]
    shards = gathered.shape[0]
    for kind in range(2):

        def turn(i, state):
            part = gathered[order(i, shards, kind == 0), kind]
            return tile_decay(part, rates[...]) * state + part[:, :rows]

        turns = place[0] if kind == 0 else shards - 1 - place[0]
        out[kind] = lax.fori_loop(0, turns, turn, jnp.zeros(rates.shape, jnp.float32))


def scan_kernel(side, *refs):
    incoming, bases, act, step, step_pre, grad_gated, entering, decays, spreader = refs[:9]
    earlier, refs = refs[9 : 9 + side], refs[9 + side :]
    step_weight_in, decay_log_in, skip_gain_in, *refs = refs
    partial, grad_act, grad_pre, summed_out, *refs = refs
    step_weight, decay_log, skip_gain, rates, rate_rows, history, *refs = refs
    grad_in, grad_out, weights, skip_rows, sems = refs
    tiles, length, _ = act.shape
    states = decay_log.shape[0]
    ranks = step_weight.shape[0]
    count = length // CHAINS
    group = tile_group(tiles)
    loads = copies_of(
        [
            (decay_log_in.at[side], decay_log), (skip_gain_in, skip_gain),
            (step_weight_in.at[side], step_weight),
        ],
        sems,
    )
    grad_in[...] = jnp.zeros_like(grad_in)
    grad_out[...] = jnp.zeros_like(grad_out)
    finish_all(loads)
    fill_rates(decay_log, rates)
    for t in range(tiles):
        skip_rows[t] = skip_gain[side : side + 1, lane_tile(t)]
    up = side == 0
    basis_b, basis_c = bases.at[0], bases.at[1]

    def some_tiles(first, keep):
        at_tiles = [first * group + g for g in range(group)]
        fill_rate_rows(rates, at_tiles, rate_rows)
        skips = [skip_rows[t] for t in at_tiles]
        sums = []
        for t in at_tiles:
            summed = step[t, cell_rows(0), :]
            for j in range(1, count):
                summed = summed + step[t, cell_rows(j), :]
            sums.append(summed)

        def start(kind, upward):
            spans = []
            for g in range(group):
                span = shifted(sums[g], 1, upward)
                by = 1
                while by < CHAINS:
                    span = span + shifted(span, by, upward)
                    by *= 2
                spans.append(span)
            first = []
            for n in range(states):
                at = side * states + n
                for g, t in enumerate(at_tiles):
                    decay = jnp.exp2(spans[g] * rate_rows[g, n])
                    value = incoming[0 if upward else 1, t, at : at + 1, :]
                    first.append(entering[kind, t, n] + decay * value)
            return tuple(first)

        def forward(i, state):
            j = order(i, count, up)
            at = cell_rows(j)
            acts = [act[t, at, :] for t in at_tiles]
            grads = [grad_gated[t, at, :] for t in at_tiles]
            drives = [step[t, at, :] * a for t, a in zip(at_tiles, acts)]
            outs = [[v * a, None] for v, a in zip(skips, acts)]
            new = []
            for n in range(states):
                lanes = lane_tile(n)
                b, c = basis_b[at, lanes], basis_c[at, lanes]
                read = grad_out[at, lanes]
                for g in range(group):
                    before = state[n * group + g]
                    decay = decays[at_tiles[g], at, lanes]
                    history[g, at, lanes] = before
                    current = decay * before + b * drives[g]
                    outs[g][n % 2] = plus(outs[g][n % 2], c * current)
                    read = read + current * grads[g]
                    new.append(current)
                grad_out[at, lanes] = read
            for g, t in enumerate(at_tiles):
                out = outs[g][0] + outs[g][1]
                if side == 0:
                    summed_out[t, at, :] = out
                else:
                    summed_out[t, at, :] = earlier[0][t, at, :] + out
            return tuple(new)

        unrolled(count, 4, forward, start(0, up))

        def retreat(i, state):
            j = order(i, count, not up)
            at = cell_rows(j)
            steps = [step[t, at, :] for t in at_tiles]
            acts = [act[t, at, :] for t in at_tiles]
            grads = [grad_gated[t, at, :] for t in at_tiles]
            drives = [v * a for v, a in zip(steps, acts)]
            step_terms = [[None, None] for _ in range(group)]
            drive_grads = [[None, None] for _ in range(group)]
            new = []
            for n in range(states):
                lanes = lane_tile(n)
                b, c = basis_b[at, lanes], basis_c[at, lanes]
                put = grad_in[at, lanes]
                for g in range(group):
                    adjoint = state[n * group + g] + c * grads[g]
                    carried = decays[at_tiles[g], at, lanes] * adjoint
                    new.append(carried)
                    term = carried * history[g, at, lanes] * rate_rows[g, n]
                    step_terms[g][n % 2] = plus(step_terms[g][n % 2], term)
                    drive_grads[g][n % 2] = plus(drive_grads[g][n % 2], adjoint * b)
                    put = put + adjoint * drives[g]
                grad_in[at, lanes] = put
            for g, t in enumerate(at_tiles):
                drive_grad = drive_grads[g][0] + drive_grads[g][1]
                step_term = step_terms[g][0] + step_terms[g][1]
                grad_step = step_term * LN2 + drive_grad * acts[g]
                grad_act[t, at, :] = grads[g] * skips[g] + drive_grad * steps[g]
                pre = step_pre[t, at, :]
                grad_pre[t, at, :] = grad_step * jax.nn.sigmoid(pre)
            return tuple(new)

        unrolled(count, 4, retreat, start(1, not up))
        return keep

    lax.fori_loop(0, tiles // group, some_tiles, 0)
    wide = full_width(grad_pre)
    weights[...] = jnp.zeros_like(weights)
    weights[:ranks] = step_weight[...]
    sums = jnp.zeros((length, LANES), jnp.float32)
    step_lanes = 4 * LANES
    for k, values in enumerate((grad_in, grad_out)):
        for at in range(0, states * LANES, step_lanes):
            rest = values[:, at : at + step_lanes]
            from_lane = k * states * LANES + at
            pick = spreader[:, from_lane : from_lane + step_lanes]
            for _ in range(2):
                piece = rest.astype(jnp.bfloat16)
                rest = rest - piece.astype(jnp.float32)
                sums = sums + lax.dot_general(
                    piece, pick, (((1,), (1,)), ((), ())), preferred_element_type=jnp.float32
                )
    lane = lax.broadcasted_iota(jnp.int32, (length, LANES), 1)
    partial[...] = dot(wide, weights[...], (1, 1)) + jnp.where(lane >= ranks, sums, 0.0)


def step_kernel(first_pre, second_pre, first, second, after_this, step_part):
    _, tiles, ranks, _ = step_part.shape
    for side, (grad_pre, projection) in enumerate(((first_pre, first), (second_pre, second))):
        wide = dot(projection[...], full_width(grad_pre), (0, 0))
        for t in range(tiles):
            step_part[side, t] = wide[:ranks, lane_tile(t)]


def gate_kernel(
    summed, gate_in, cot_in, after_this, block_out, gate_grad, gate, cot, plain, sems
):
    finish_all(copies_of([(gate_in, gate), (cot_in, cot)], sems))
    for t in range(summed.shape[0]):
        lanes = lane_tile(t)
        values = gate[:, lanes]
        to_tokens(summed.at[t], plain)
        both = plain[...]
        block_out[:, lanes] = both * values * jax.nn.sigmoid(values)
        gate_grad[:, lanes] = cot[:, lanes] * both * silu_grad(values)


def weight_kernel(
    total, act, pre, grad_act, select_in, after_this,
    part, conv_grad, select, grad, plain, cells, sems,
):
    weigh(
        0, (total,), act, pre, grad_act, select_in,
        conv_grad, select, grad, plain, cells, sems, part,
    )


def second_weight_kernel(
    place, own, first, second, third, act, pre, grad_act, select_in, part, step_part, other_grad,
    keep, send, conv_grad, near, far, select, grad, plain, cells, mine, sems,
):
    length, width = conv_grad.shape
    weigh(
        1, (own, first, second, third), act, pre, grad_act, select_in,
        conv_grad, select, grad, plain, cells, sems, mine,
    )
    core = lax.rem(place[0], 2)
    for side, value in enumerate((part, mine)):
        for out, whose in ((keep, side), (send, 1 - side)):

            @pl.when(core == whose)
            def _():
                out[:width] = value[...]
                out[width:] = step_part[side].reshape(-1, LANES)
    head, tail = other_grad[:HALO], conv_grad[length - HALO :]
    near[...] = jnp.where(core == 0, tail, head)
    far[...] = jnp.where(core == 0, head, tail)


def weigh(
    side, terms, act, pre, grad_act, select_in, conv_grad, select, grad, plain, cells, sems, part
):
    loads = copies_of([(select_in.at[side], select)], sems)
    total = terms[0][...]
    for term in terms[1:]:
        total = total + term[...]
    grad[...] = total
    part[...] = dot(full_width(act), grad[...], (0, 0))
    finish_all(loads)
    wide = dot(grad[...], select[...], (1, 1))
    for t in range(act.shape[0]):
        lanes = lane_tile(t)
        cells[...] = grad_act[t] + wide[:, lanes]
        to_tokens(cells, plain)
        conv_grad[:, lanes] = plain[...] * silu_grad(pre[t])


def halves_kernel(place, keep, got, mine, *refs):
    outs, (total,) = refs[:-1], refs[-1:]
    share = mine.shape[0]
    chips = len(outs) + 1
    for k in range(chips):
        at = slice(k * share, (k + 1) * share)
        total[k] = keep[at] + got[at]
    core, chip = lax.rem(place[0], 2), lax.div(place[0], 2)
    mine[...] = total[chip]
    for k, out in enumerate(outs, 1):
        out[...] = total[chip ^ turned(k, core, chips)]


def handover_kernel(value, *refs):
    terms, (total, out) = refs[:-2], refs[-2:]
    add_kernel(*terms, total)
    out[...] = value[...]


def add_after_kernel(after_this, *refs):
    add_kernel(*refs)


def add_kernel(*refs):
    total = refs[0][...]
    for ref in refs[1:-1]:
        total = total + ref[...]
    refs[-1][...] = total


def join_kernel(place, after_this, mine, *refs):
    parts, out = refs[:-1], refs[-1]
    core, chip = lax.rem(place[0], 2), lax.div(place[0], 2)
    out[chip] = mine[...]
    for k, part in enumerate(parts, 1):
        out[chip ^ turned(k, core, len(parts) + 1)] = part[...]


def outputs_kernel(place, mine, other, select_grad, step_grad, both):
    sides, width, _ = select_grad.shape
    ranks = step_grad.shape[1]
    chips = mine.shape[0]
    core = lax.rem(place[0], 2)
    size = mine.shape[1]
    for side in range(2):
        for k in range(chips):
            both[side, k * size : (k + 1) * size] = jnp.where(core == side, mine[k], other[k])
        select_grad[side] = both[side, :width]
        for t in range(width // LANES):
            at = width + t * ranks
            step_grad[side, :, lane_tile(t)] = both[side, at : at + ranks]


def exit_kernel(
    place, near, far, first, second, conv_weight_in, after_this, tokens_grad, up, down, conv_weight, sems
):
    length, width = first.shape
    taps = conv_weight.shape[1]
    margin = taps - 1
    loads = copies_of(
        [
            (conv_weight_in, conv_weight),
        ],
        sems,
    )
    core = lax.rem(place[0], 2)
    up[:length] = first[...]
    up[length:] = jnp.where(core == 0, near[...], far[...])
    down[:HALO] = jnp.where(core == 0, far[...], near[...])
    down[HALO:] = second[...]
    finish_all(loads)
    for t in range(width // LANES):
        lanes = lane_tile(t)
        total = jnp.zeros((length, LANES), jnp.float32)
        for k in range(taps):
            at = margin - k
            total = total + conv_weight[0, k : k + 1, lanes] * up[at : at + length, lanes]
            at = HALO - margin + k
            total = total + conv_weight[1, k : k + 1, lanes] * down[at : at + length, lanes]
        tokens_grad[:, lanes] = total


def swapped_edges(near, far, axis):
    count = lax.axis_size(axis)
    pairs = [(i, i + 1) for i in range(1, count - 1, 2)]
    pairs = pairs + [(j, i) for i, j in pairs]
    return swapped(near, axis, 1), lax.ppermute(far, axis, pairs)


def swapped(value, axis, by):
    count = lax.axis_size(axis)
    return lax.ppermute(value, axis, [(i, i ^ by) for i in range(count)])


def swapped_chips(value, k):
    places = lax.axis_size("ctx")
    chips = places // 2
    pairs = [(i, i ^ (2 * ((k - 1 + i % 2) % (chips - 1) + 1))) for i in range(places)]
    return lax.ppermute(value, "ctx", pairs)


def call(kernel, name, out_shape, scratch, mib, args, kinds, outs=None, flops=2**28):
    spaces = {
        "v": pl.BlockSpec(memory_space=pltpu.VMEM),
        "m": pl.BlockSpec(memory_space=pltpu.VMEM),
        "b": pl.BlockSpec(memory_space=pltpu.VMEM),
        "h": pl.BlockSpec(memory_space=pltpu.HBM),
        "s": pl.BlockSpec(memory_space=pltpu.SMEM),
    }
    outs = outs or "v" * len(out_shape)
    pinned = {"m": pltpu.VMEM, "h": pltpu.HBM}
    args = [
        pltpu.with_memory_space_constraint(a, pinned[k]) if k in pinned else a
        for a, k in zip(args, kinds, strict=True)
    ]
    results = [
        pinned[k](shape, jnp.float32) if k in pinned else shape_of(*shape)
        for shape, k in zip(out_shape, outs, strict=True)
        if k != "b"
    ]
    at = outs.find("b")
    if at >= 0:
        results.insert(at, pltpu.VMEM(out_shape[at], jnp.bfloat16))
    return pl.pallas_call(
        kernel,
        in_specs=[spaces[k] for k in kinds],
        out_specs=[spaces[k] for k in outs],
        out_shape=results,
        scratch_shapes=scratch,
        compiler_params=params(mib),
        cost_estimate=pl.CostEstimate(flops=flops, bytes_accessed=flops // 64, transcendentals=0),
        name=name,
    )(*args)


def terms_of(partial):
    count = lax.axis_size("ch")
    if count != 4:
        zero = jnp.zeros_like(partial)
        return (lax.psum(partial, "ch"), zero, zero, zero)
    return (partial, *(swapped(partial, "ch", k) for k in range(1, count)))


def halved(place, keep, send, rows, chips, name):
    got = swapped(send, "ctx", 1)
    share = rows // chips
    mine, *sent = call(
        halves_kernel, name, ((share, LANES),) * chips, [pltpu.VMEM((chips, share, LANES), jnp.float32)],
        8, (place, keep, got), "svv",
    )
    return (mine, *(swapped_chips(part, k) for k, part in enumerate(sent, 1)))


def on_device(
    tokens, gate_input, cotangent, conv_weight, conv_bias, select_weight, step_weight,
    step_bias, decay_log, skip_gain,
):
    length, width = tokens.shape
    tiles = width // LANES
    states = decay_log.shape[1]
    ranks = step_weight.shape[1]
    places = lax.axis_size("ctx")
    place = lax.axis_index("ctx").astype(jnp.int32).reshape(1)
    group = tile_group(tiles)
    chips = places // 2
    near = places == 8
    narrow = (length, LANES)
    one = (tiles, length, LANES)
    flat = (length, width)
    chain_ends = (2, tiles, states, CHAINS, LANES)
    carry = (2, tiles, 2 * states + 8, LANES)
    row_rates = (tiles, 2 * states, LANES)
    packed = (tiles * 2 * states + -(-2 * tiles // 8) * 8, LANES)
    vmem = functools.partial(pltpu.VMEM, dtype=jnp.float32)
    dma = lambda n: pltpu.SemaphoreType.DMA((n,))
    bases = vmem((length, states * LANES))
    grouped = vmem((group, length, states * LANES))
    rate_scratch = vmem((tiles, states, LANES))
    row_scratch = vmem((group, states, CHAINS, LANES))

    core = (place & 1)[:, None] == 0
    head, tail = tokens[:HALO], tokens[length - HALO :]
    edges = swapped_edges(jnp.where(core, tail, head), jnp.where(core, head, tail), "ctx")
    conv_scratch = [
        vmem(conv_weight.shape), vmem(conv_bias.shape), vmem(select_weight.shape[1:]), vmem(narrow),
    ]
    first_partial, first_act, first_pre, extended = call(
        entry_kernel, "entry", (narrow, one, one, (length + 2 * HALO, width)),
        [*conv_scratch, dma(4)],
        8, (place, *edges, tokens, conv_weight, conv_bias, select_weight), "svvhhhh", "vmmm",
    )
    first_terms = terms_of(first_partial)
    partial, act, pre, grad_gated, spreader = call(
        second_entry_kernel, "second_entry",
        (narrow, one, one, one, (LANES, 2 * states * LANES)),
        [*conv_scratch, vmem(flat), vmem(flat), dma(5)],
        10, (extended, conv_weight, conv_bias, select_weight, gate_input, cotangent),
        "mhhhhh", "vmmmb",
    )
    projection_terms = (first_terms, terms_of(partial))
    acts, pres = (first_act, act), (first_pre, pre)
    earlier, locals_ = (), []
    for side in range(2):
        *found, carried, rates = call(
            functools.partial(local_kernel, side), ("first_local", "second_local")[side],
            (
                narrow, one, one, chain_ends, (*one[:-1], states * LANES),
                (2, length, states * LANES), carry, row_rates,
            ),
            [
                vmem(step_weight.shape[1:]), vmem(step_bias.shape), vmem(decay_log.shape[1:]),
                rate_scratch, row_scratch, dma(3),
            ],
            10,
            (
                *projection_terms[side], acts[side], grad_gated, spreader, *earlier, step_weight,
                step_bias, decay_log,
            ),
            "vvvvmmm" + "v" * len(earlier) + "hhh", "mmmmmmvv", 2**32,
        )
        earlier = (carried, rates)
        locals_.append(found)
    if near:
        other = swapped(carried, "ctx", 1)
        sent = call(
            pair_kernel, "pair", (packed,) * (chips - 1),
            [vmem(carry)], 8, (place, carried, other, rates), "svvv",
        )
        got = [swapped_chips(part, k) for k, part in enumerate(sent, 1)]
        (incoming,) = call(
            chain_kernel, "chain", ((2, *row_rates),), [vmem((chips, *carry[1:]))],
            8, (place, other, rates, *got), "svv" + "v" * len(got),
        )
    else:
        gathered = lax.all_gather(carried, "ctx")
        (incoming,) = call(
            long_chain_kernel, "chain", ((2, *row_rates),), [],
            48, (place, gathered, rates), "svv",
        )
    earlier, grad_terms, grad_acts, grad_pres = (), [], [], []
    for side in range(2):
        projection, step, step_pre, entering, decays, spread_bases = locals_[side]
        partial_grad, grad_act, grad_pre, summed = call(
            functools.partial(scan_kernel, side), ("first_scan", "second_scan")[side],
            (narrow, one, one, one),
            [
                vmem(step_weight.shape[1:]), vmem(decay_log.shape[1:]), vmem(skip_gain.shape),
                rate_scratch, row_scratch, grouped, bases, bases, vmem((LANES, width)),
                vmem((tiles, 1, LANES)), dma(3),
            ],
            10,
            (
                incoming, spread_bases, acts[side], step, step_pre, grad_gated, entering, decays,
                spreader, *earlier, step_weight, decay_log, skip_gain,
            ),
            "vmmmmmmmm" + "m" * side + "hhh", "vmmm", 2**33,
        )
        if side == 1:
            first_total, partial_grad = call(
                handover_kernel, "handover", (narrow, narrow), [], 4,
                (partial_grad, *grad_terms[0]), "vvvvv",
            )
        grad_terms.append(terms_of(partial_grad))
        earlier = (summed,)
        grad_acts.append(grad_act)
        grad_pres.append(grad_pre)
    arrived = grad_terms[1][1]
    (step_part,) = call(
        step_kernel, "step_grad", ((2, tiles, ranks, LANES),), [],
        8, (*grad_pres, locals_[0][0], locals_[1][0], arrived), "mmmmv", flops=0,
    )
    weight_scratch = [
        vmem(select_weight.shape[1:]), vmem(narrow), vmem(narrow), vmem(narrow),
    ]
    part, first_grad = call(
        weight_kernel, "first_weights", ((width, LANES), flat), [*weight_scratch, dma(1)],
        8, (first_total, first_act, first_pre, grad_acts[0], select_weight, arrived),
        "vmmmhv", "mm", 0,
    )
    half = width + tiles * ranks
    keep, send, second_grad, *edges = call(
        second_weight_kernel, "weights",
        ((half, LANES), (half, LANES), flat, (HALO, width), (HALO, width)),
        [*weight_scratch, vmem((width, LANES)), dma(1)],
        10,
        (
            place, *grad_terms[1], act, pre, grad_acts[1], select_weight, part, step_part,
            first_grad,
        ),
        "svvvvmmmhmvm", "vvmvv",
    )
    edges = swapped_edges(*edges, "ctx")
    if near:
        shares = halved(place, keep, send, half, chips, "halves")
        ahead = shares[0]
    else:
        ahead = edges[0]
    (tokens_grad,) = call(
        exit_kernel, "exit", (flat,),
        [
            vmem((length + HALO, width)), vmem((length + HALO, width)), vmem(conv_weight.shape),
            dma(1),
        ],
        8, (place, *edges, first_grad, second_grad, conv_weight, ahead), "svvmmhv",
    )
    if near:
        rows = half // chips
        (mine,) = call(
            add_after_kernel, "share_sum", ((rows, LANES),), [], 4, (tokens_grad, *shares),
            "h" + "v" * chips,
        )
        ahead = mine
    block_out, gate_grad = call(
        gate_kernel, "gate", (flat, flat),
        [vmem(flat), vmem(flat), vmem(one[1:]), dma(2)],
        8, (summed, gate_input, cotangent, ahead), "mhhv", flops=0,
    )
    if near:
        got = [swapped_chips(mine, k) for k in range(1, chips)]
        (joined,) = call(
            join_kernel, "joined", ((chips, rows, LANES),), [],
            8, (place, block_out, mine, *got), "sh" + "v" * chips,
        )
        select_grad, step_grad = call(
            outputs_kernel, "weight_grads", ((2, width, LANES), (2, ranks, width)),
            [vmem((2, half, LANES))],
            12, (place, joined, swapped(joined, "ctx", 1)), "svv",
        )
    else:
        first = lax.rem(place[0], 2) == 0
        both = jnp.where(first, jnp.stack([keep, send]), jnp.stack([send, keep]))
        both = lax.psum(both, "ctx")
        select_grad = both[:, :width]
        step_grad = both[:, width:].reshape(2, tiles, ranks, LANES)
        step_grad = step_grad.transpose(0, 2, 1, 3).reshape(2, ranks, width)
    return (block_out, tokens_grad, gate_grad, select_grad, step_grad)


def solution(mesh):
    return jax.shard_map(
        on_device,
        mesh=mesh,
        in_specs=(
            P("ctx", "ch"),
            P("ctx", "ch"),
            P("ctx", "ch"),
            P(None, None, "ch"),
            P(None, "ch"),
            P(None, "ch", None),
            P(None, None, "ch"),
            P(None, "ch"),
            P(None, None, "ch"),
            P(None, "ch"),
        ),
        out_specs=(
            P("ctx", "ch"),
            P("ctx", "ch"),
            P("ctx", "ch"),
            P(None, "ch", None),
            P(None, None, "ch"),
        ),
        check_vma=False,
    )
```

time: 118 us -> 104 us (0.88)
  Pallas kernels: 45 us -> 38.5 us
  starting transfers between devices: 41.6 us -> 37.1 us
  waiting for transfers between devices: 29.4 us -> 25.7 us
    ppermute x16 -> x2, starting transfers between devices: 25.9 us -> 1.3 us  [swapped_edges(): return (swapped(near, axis, 1), lax.ppermute(far, axis, pairs))]
    ppermute x3 -> x17, starting transfers between devices: 0.23 us -> 22.2 us  [swapped(): return lax.ppermute(value, axis, [(i, i ^ by) for i in range(count)])]
    ppermute x16 -> x2, waiting for transfers between devices: 16.9 us -> 0.01 us  [swapped_edges(): return (swapped(near, axis, 1), lax.ppermute(far, axis, pairs))]
    ppermute x9, waiting for transfers between devices: 6.8 us -> 15.6 us  [swapped_chips(): return lax.ppermute(value, 'ctx', pairs)]
    pallas_call x16 -> x18, Pallas kernels: 45 us -> 38.5 us  [call(): pl.pallas_call(kernel, in_specs=[spaces[k] for k in kinds], out_specs=[sp...]
    ppermute x3 -> x17, waiting for transfers between devices: 5.75 us -> 10.1 us  [swapped(): return lax.ppermute(value, axis, [(i, i ^ by) for i in range(count)])]
    ppermute x9, starting transfers between devices: 15.4 us -> 13.6 us  [swapped_chips(): return lax.ppermute(value, 'ctx', pairs)]
  transfers between devices with their start and end apart: 28 -> 28, of which waited for: 17 -> 16; matrix products, arithmetic and copies ran while one was open for 0% -> 0% of each run, Pallas kernels for 8% -> 20%
where the time goes in v5:
time: 104 us; the launch traced here: 103 us
  Pallas kernels  38.5 us (37%)
  starting transfers between devices  37.1 us (36%)
  waiting for transfers between devices  25.7 us (25%)
    pallas_call x18, Pallas kernels, call(): pl.pallas_call(kernel, in_specs=[spaces[k] for k in kinds], out_specs=[sp...  38.5 us
    ppermute x17, starting transfers between devices, swapped(): return lax.ppermute(value, axis, [(i, i ^ by) for i in range(count)])  22.2 us
    ppermute x9, waiting for transfers between devices, swapped_chips(): return lax.ppermute(value, 'ctx', pairs)  15.6 us
    ppermute x9, starting transfers between devices, swapped_chips(): return lax.ppermute(value, 'ctx', pairs)  13.6 us
    ppermute x17, waiting for transfers between devices, swapped(): return lax.ppermute(value, axis, [(i, i ^ by) for i in range(count)])  10.1 us
  transfers between devices with their start and end apart: 28, of which 16 were waited for; matrix products, arithmetic and copies ran while one was open for 0% of the time, Pallas kernels for 20%

profile of v5, /device:TPU:0, one launch (start us, length us, event | category | flops | bytes accessed | tf_op | source)
XLA Modules:
  0.0 103.0 jit_solution(11147195848627055159)
XLA Ops:
  0.6 0.8 slice_select_fusion
  1.4 0.7 collective-permute-start.1
  2.1 4.4 %collective-permute-start = (f32[8,768]{1,0:T(8,128)S(1)}, f32[8,768]{1,0:T(8,128)S(1)}, u32[]{:S(2)}, u32[]{:S(2)}) collective-permute-start(f32[8,768]{1,0:T(8,128)S(1)} %get-tuple-element.112), channel_id=1, source_target_pairs={{0,4},{4,0},{8,12},{12,8},{16,20},{20,16},{24,28},{28,24},{1,5},{5... | collective-permute-start | bytes 73736 | tf_op jit(solution)/shard_map/ppermute | solution.py:696
  6.4 0.8 collective-permute-done.near
  7.3 1.9 %entry.1 = (f32[128,128]{1,0:T(8,128)S(1)}, f32[6,128,128]{2,1,0:T(8,128)S(1)}, f32[6,128,128]{2,1,0:T(8,128)S(1)}, f32[144,768]{1,0:T(8,128)S(1)}) custom-call(s32[1]{0:T(128)} %bitcast.place, f32[8,768]{1,0:T(8,128)S(1)} %collective-permute-done.near, f32[8,768]{1,0:T(8,128)S(1)} %collective-permute-done.1.far, f32[128,768]{1,0:T(8,128)} %tokens.1, ...), custom_call_target="tpu_custom_call" | custom-call | flops 268435456 | bytes 4194304 | tf_op jit(solution)/shard_map/entry/pallas_call | solution.py:728
  9.1 3.7 %collective-permute-start.7 = (f32[128,128]{1,0:T(8,128)S(1)}, f32[128,128]{1,0:T(8,128)S(1)}, u32[]{:S(2)}, u32[]{:S(2)}) collective-permute-start(f32[128,128]{1,0:T(8,128)S(1)} %get-tuple-element.63.refs_0_), channel_id=1, source_target_pairs={{0,3},{1,2},{2,1},{3,0},{4,7},{5,6},{6,5},{7,4},{8,11},{9,10},{10,... | collective-permute-start | bytes 196616 | tf_op jit(solution)/shard_map/ppermute | solution.py:696
  12.8 0.8 collective-permute-start.5
  13.6 1.8 %second_entry.1 = (f32[128,128]{1,0:T(8,128)S(1)}, f32[6,128,128]{2,1,0:T(8,128)S(1)}, f32[6,128,128]{2,1,0:T(8,128)S(1)}, f32[6,128,128]{2,1,0:T(8,128)S(1)}, bf16[128,4096]{1,0:T(8,128)(2,1)S(1)}) custom-call(f32[144,768]{1,0:T(8,128)S(1)} %get-tuple-element.58.ext, f32[2,4,768]{2,1,0:T(4,128)} %conv_weight_in.5, f32[2,768]{1,0:T(2,128)} %conv_bias_in.3, ...), custom_call_target="tpu_custom_call" | custom-call | flops 268435456 | bytes 4194304 | tf_op jit(solution)/shard_map/second_entry/pallas_call | solution.py:728
  15.4 3.7 %collective-permute-start.4 = (f32[128,128]{1,0:T(8,128)S(1)}, f32[128,128]{1,0:T(8,128)S(1)}, u32[]{:S(2)}, u32[]{:S(2)}) collective-permute-start(f32[128,128]{1,0:T(8,128)S(1)} %get-tuple-element.59.refs_0_), channel_id=1, source_target_pairs={{0,3},{1,2},{2,1},{3,0},{4,7},{5,6},{6,5},{7,4},{8,11},{9,10},{10,... | collective-permute-start | bytes 196616 | tf_op jit(solution)/shard_map/ppermute | solution.py:696
  19.1 0.8 collective-permute-start.2
  19.9 4.6 %first_local.1 = (f32[128,128]{1,0:T(8,128)S(1)}, f32[6,128,128]{2,1,0:T(8,128)S(1)}, f32[6,128,128]{2,1,0:T(8,128)S(1)}, f32[2,6,16,8,128]{4,3,2,1,0:T(8,128)S(...) custom-call(f32[128,128]{1,0:T(8,128)S(1)} %get-tuple-element.63.ref, ...), custom_call_target="tpu_custom_call" | custom-call | flops 4294967296 | bytes 67108864 | tf_op jit(solution)/shard_map/first_local/pallas_call | solution.py:728
  24.7 4.7 %second_local.1 = (f32[128,128]{1,0:T(8,128)S(1)}, f32[6,128,128]{2,1,0:T(8,128)S(1)}, f32[6,128,128]{2,1,0:T(8,128)S(1)}, f32[2,6,16,8,128]{4,3,2,1,0:T(8,128)S...) custom-call(f32[128,128]{1,0:T(8,128)S(1)} %get-tuple-element.59.ref, ...), custom_call_target="tpu_custom_call" | custom-call | flops 4294967296 | bytes 67108864 | tf_op jit(solution)/shard_map/second_local/pallas_call | solution.py:728
  29.5 1.5 %collective-permute-done.8.other = f32[2,6,40,128]{3,2,1,0:T(8,128)S(1)} collective-permute-done((f32[2,6,40,128]{3,2,1,0:T(8,128)S(1)}, f32[2,6,40,128]{3,2,1,0:T(8,128)S(1)}, u32[]{:S(2)}, u32[]{:S(2)}) %collective-permute-start.8) | collective-permute-done | bytes 245792 | tf_op jit(solution)/shard_map/ppermute | solution.py:696
  31.2 2.5 %collective-permute-start.9 = (f32[208,128]{1,0:T(8,128)S(1)}, f32[208,128]{1,0:T(8,128)S(1)}, u32[]{:S(2)}, u32[]{:S(2)}) collective-permute-start(f32[208,128]{1,0:T(8,128)S(1)} %get-tuple-element.69), channel_id=1, source_target_pairs={{0,8},{4,20},{8,0},{12,28},{16,24},{20,4},{24,16},{28,12},{1,9},{5... | collective-permute-start | bytes 319496 | tf_op jit(solution)/shard_map/ppermute | solution.py:703
  33.7 1.3 %collective-permute-start.10 = (f32[208,128]{1,0:T(8,128)S(1)}, f32[208,128]{1,0:T(8,128)S(1)}, u32[]{:S(2)}, u32[]{:S(2)}) collective-permute-start(f32[208,128]{1,0:T(8,128)S(1)} %get-tuple-element.70), channel_id=1, source_target_pairs={{0,16},{4,28},{8,24},{12,20},{16,0},{20,12},{24,8},{28,4},{1,17},{... | collective-permute-start | bytes 319496 | tf_op jit(solution)/shard_map/ppermute | solution.py:703
  35.0 0.6 collective-permute-start.11
  35.6 1.2 %collective-permute-done.9.refs_0_ = f32[208,128]{1,0:T(8,128)S(1)} collective-permute-done((f32[208,128]{1,0:T(8,128)S(1)}, f32[208,128]{1,0:T(8,128)S(1)}, u32[]{:S(2)}, u32[]{:S(2)}) %collective-permute-start.9) | collective-permute-done | bytes 106528 | tf_op jit(solution)/shard_map/ppermute | solution.py:703
  36.8 2.7 %collective-permute-done.10.refs_1_ = f32[208,128]{1,0:T(8,128)S(1)} collective-permute-done((f32[208,128]{1,0:T(8,128)S(1)}, f32[208,128]{1,0:T(8,128)S(1)}, u32[]{:S(2)}, u32[]{:S(2)}) %collective-permute-start.10) | collective-permute-done | bytes 106528 | tf_op jit(solution)/shard_map/ppermute | solution.py:703
  39.5 2.2 %collective-permute-done.11.refs_2_ = f32[208,128]{1,0:T(8,128)S(1)} collective-permute-done((f32[208,128]{1,0:T(8,128)S(1)}, f32[208,128]{1,0:T(8,128)S(1)}, u32[]{:S(2)}, u32[]{:S(2)}) %collective-permute-start.11) | collective-permute-done | bytes 106528 | tf_op jit(solution)/shard_map/ppermute | solution.py:703
  41.9 7.5 %first_scan.1 = (f32[128,128]{1,0:T(8,128)S(1)}, f32[6,128,128]{2,1,0:T(8,128)S(1)}, f32[6,128,128]{2,1,0:T(8,128)S(1)}, f32[6,128,128]{2,1,0:T(8,128)S(1)}) custom-call(f32[2,6,32,128]{3,2,1,0:T(8,128)S(1)} %chain.1.refs_0_, f32[2,128,2048]{2,1,0:T(8,128)S(1)} %get-tuple-element.77.refs_1_, f32[6,128,128]{2,1,0:T(8,128)S(1)} %get-tuple-element.64.refs_4_.refs_2_.act, ...), custom_call_target="tpu_custom_call" | custom-call | flops 8589934592 | bytes 134217728 | tf_op jit(solution)/shard_map/first_scan/pallas_call | solution.py:728
  49.4 3.7 %collective-permute-start.14 = (f32[128,128]{1,0:T(8,128)S(1)}, f32[128,128]{1,0:T(8,128)S(1)}, u32[]{:S(2)}, u32[]{:S(2)}) collective-permute-start(f32[128,128]{1,0:T(8,128)S(1)} %get-tuple-element.85.refs_0_), channel_id=1, source_target_pairs={{0,3},{1,2},{2,1},{3,0},{4,7},{5,6},{6,5},{7,4},{8,11},{9,10},{10,... | collective-permute-start | bytes 196616 | tf_op jit(solution)/shard_map/ppermute | solution.py:696
  53.1 0.8 collective-permute-start.12
  53.9 7.4 %second_scan.1 = (f32[128,128]{1,0:T(8,128)S(1)}, f32[6,128,128]{2,1,0:T(8,128)S(1)}, f32[6,128,128]{2,1,0:T(8,128)S(1)}, f32[6,128,128]{2,1,0:T(8,128)S(1)}) custom-call(f32[2,6,32,128]{3,2,1,0:T(8,128)S(1)} %chain.1.refs_0_, f32[2,128,2048]{2,1,0:T(8,128)S(1)} %get-tuple-element.72.refs_1_, f32[6,128,128]{2,1,0:T(8,128)S(1)} %get-tuple-element.60.refs_4_.refs_2_.act, ...), custom_call_target="tpu_custom_call" | custom-call | flops 8589934592 | bytes 134217728 | tf_op jit(solution)/shard_map/second_scan/pallas_call | solution.py:728
  61.3 1.3 %collective-permute-start.15 = (f32[128,128]{1,0:T(8,128)S(1)}, f32[128,128]{1,0:T(8,128)S(1)}, u32[]{:S(2)}, u32[]{:S(2)}) collective-permute-start(f32[128,128]{1,0:T(8,128)S(1)} %get-tuple-element.86.own), channel_id=1, source_target_pairs={{0,1},{1,0},{2,3},{3,2},{4,5},{5,4},{6,7},{7,6},{8,9},{9,8},{10,11... | collective-permute-start | bytes 196616 | tf_op jit(solution)/shard_map/ppermute | solution.py:696
  62.6 2.4 %collective-permute-start.17 = (f32[128,128]{1,0:T(8,128)S(1)}, f32[128,128]{1,0:T(8,128)S(1)}, u32[]{:S(2)}, u32[]{:S(2)}) collective-permute-start(f32[128,128]{1,0:T(8,128)S(1)} %get-tuple-element.86.own), channel_id=1, source_target_pairs={{0,3},{1,2},{2,1},{3,0},{4,7},{5,6},{6,5},{7,4},{8,11},{9,10},{10,... | collective-permute-start | bytes 196616 | tf_op jit(solution)/shard_map/ppermute | solution.py:696
  65.1 0.5 collective-permute-start.16
  65.6 0.4 collective-permute-done.15.after_this.first
  66.0 1.9 %first_weights.1 = (f32[768,128]{1,0:T(8,128)S(1)}, f32[128,768]{1,0:T(8,128)S(1)}) custom-call(f32[128,128]{1,0:T(8,128)S(1)} %get-tuple-element.89.total, f32[6,128,128]{2,1,0:T(8,128)S(1)} %get-tuple-element.64.refs_4_.refs_2_.act, f32[6,128,128]{2,1,0:T(8,128)S(1)} %get-tuple-element.90.pre, f32[6,128,128]{2,1,0:T(8,128)S(1)} %get-tuple-element.91.grad_act, ...), custom_call_target="tpu_custom_call" | custom-call | tf_op jit(solution)/shard_map/first_weights/pallas_call | solution.py:728
  67.8 0.8 step_grad.1.step_part
  68.7 2.2 %collective-permute-done.16.second = f32[128,128]{1,0:T(8,128)S(1)} collective-permute-done((f32[128,128]{1,0:T(8,128)S(1)}, f32[128,128]{1,0:T(8,128)S(1)}, u32[]{:S(2)}, u32[]{:S(2)}) %collective-permute-start.16) | collective-permute-done | bytes 65568 | tf_op jit(solution)/shard_map/ppermute | solution.py:696
  71.0 2.1 %weights.1 = (f32[1344,128]{1,0:T(8,128)S(1)}, f32[1344,128]{1,0:T(8,128)S(1)}, f32[128,768]{1,0:T(8,128)S(1)}, f32[8,768]{1,0:T(8,128)S(1)}, f32[8,768]{1,0:T(8,128)S(1)}) custom-call(s32[1]{0:T(128)} %bitcast.place, f32[128,128]{1,0:T(8,128)S(1)} %get-tuple-element.86.own, f32[128,128]{1,0:T(8,128)S(1)} %collective-permute-done.15.after_this.first, ...), custom_call_target="tpu_custom_call" | custom-call | flops 268435456 | bytes 4194304 | tf_op jit(solution)/shard_map/weights/pallas_call | solution.py:728
  73.1 2.1 %collective-permute-done.20.got = f32[1344,128]{1,0:T(8,128)S(1)} collective-permute-done((f32[1344,128]{1,0:T(8,128)S(1)}, f32[1344,128]{1,0:T(8,128)S(1)}, u32[]{:S(2)}, u32[]{:S(2)}) %collective-permute-start.20) | collective-permute-done | bytes 688160 | tf_op jit(solution)/shard_map/ppermute | solution.py:696
  75.4 0.9 collective-permute-start.21
  76.2 0.7 collective-permute-start.22
  76.9 2.0 %collective-permute-start.23 = (f32[336,128]{1,0:T(8,128)S(1)}, f32[336,128]{1,0:T(8,128)S(1)}, u32[]{:S(2)}, u32[]{:S(2)}) collective-permute-start(f32[336,128]{1,0:T(8,128)S(1)} %get-tuple-element.106), channel_id=1, source_target_pairs={{0,24},{4,12},{8,16},{12,4},{16,8},{20,28},{24,0},{28,20},{1,25},{... | collective-permute-start | bytes 516104 | tf_op jit(solution)/shard_map/ppermute | solution.py:703
  78.9 0.7 collective-permute-start.19
  79.6 0.5 collective-permute-done.18.near
  80.1 1.9 %exit.1.after_this = f32[128,768]{1,0:T(8,128)} custom-call(s32[1]{0:T(128)} %bitcast.place, f32[8,768]{1,0:T(8,128)S(1)} %collective-permute-done.18.near, f32[8,768]{1,0:T(8,128)S(1)} %collective-permute-done.19.far, f32[128,768]{1,0:T(8,128)S(1)} %get-tuple-element.97.other_grad.first, f32[128,768]{1,0:T(8,128)S(1)} %get-tuple-element.100.second, ...), custom_call_target="tpu_custom_call" | custom-call | flops 268435456 | bytes 4194304 | tf_op jit(solution)/shard_map/exit/pallas_call | solution.py:728
  82.4 2.5 %collective-permute-done.22.refs_2_ = f32[336,128]{1,0:T(8,128)S(1)} collective-permute-done((f32[336,128]{1,0:T(8,128)S(1)}, f32[336,128]{1,0:T(8,128)S(1)}, u32[]{:S(2)}, u32[]{:S(2)}) %collective-permute-start.22) | collective-permute-done | bytes 172064 | tf_op jit(solution)/shard_map/ppermute | solution.py:703
  84.9 1.3 %collective-permute-done.23.refs_3_ = f32[336,128]{1,0:T(8,128)S(1)} collective-permute-done((f32[336,128]{1,0:T(8,128)S(1)}, f32[336,128]{1,0:T(8,128)S(1)}, u32[]{:S(2)}, u32[]{:S(2)}) %collective-permute-start.23) | collective-permute-done | bytes 172064 | tf_op jit(solution)/shard_map/ppermute | solution.py:703
  86.2 3.6 %collective-permute-start.26 = (f32[336,128]{1,0:T(8,128)S(1)}, f32[336,128]{1,0:T(8,128)S(1)}, u32[]{:S(2)}, u32[]{:S(2)}) collective-permute-start(f32[336,128]{1,0:T(8,128)S(1)} %share_sum.1.after_this.mine), channel_id=1, source_target_pairs={{0,24},{4,12},{8,16},{12,4},{16,8},{20,28},{24,0},{28,20},{1,25},{... | collective-permute-start | bytes 516104 | tf_op jit(solution)/shard_map/ppermute | solution.py:703
  89.9 1.1 %collective-permute-start.25 = (f32[336,128]{1,0:T(8,128)S(1)}, f32[336,128]{1,0:T(8,128)S(1)}, u32[]{:S(2)}, u32[]{:S(2)}) collective-permute-start(f32[336,128]{1,0:T(8,128)S(1)} %share_sum.1.after_this.mine), channel_id=1, source_target_pairs={{0,16},{4,28},{8,24},{12,20},{16,0},{20,12},{24,8},{28,4},{1,17},{... | collective-permute-start | bytes 516104 | tf_op jit(solution)/shard_map/ppermute | solution.py:703
  90.9 0.9 collective-permute-start.24
  91.9 2.3 %gate.1 = (f32[128,768]{1,0:T(8,128)}, f32[128,768]{1,0:T(8,128)}) custom-call(f32[6,128,128]{2,1,0:T(8,128)S(1)} %get-tuple-element.83.summed, f32[128,768]{1,0:T(8,128)} %gate_in.3, f32[128,768]{1,0:T(8,128)} %cot_in.3, f32[336,128]{1,0:T(8,128)S(1)} %share_sum.1.after_this.mine), custom_call_target="tpu_custom_call" | custom-call | tf_op jit(solution)/shard_map/gate/pallas_call | solution.py:728
  94.1 0.9 collective-permute-done.26.refs_2_
  95.1 4.5 %collective-permute-done.25.refs_1_ = f32[336,128]{1,0:T(8,128)S(1)} collective-permute-done((f32[336,128]{1,0:T(8,128)S(1)}, f32[336,128]{1,0:T(8,128)S(1)}, u32[]{:S(2)}, u32[]{:S(2)}) %collective-permute-start.25) | collective-permute-done | bytes 172064 | tf_op jit(solution)/shard_map/ppermute | solution.py:703
  99.7 2.1 %collective-permute-done.27.other = f32[4,336,128]{2,1,0:T(8,128)S(1)} collective-permute-done((f32[4,336,128]{2,1,0:T(8,128)S(1)}, f32[4,336,128]{2,1,0:T(8,128)S(1)}, u32[]{:S(2)}, u32[]{:S(2)}) %collective-permute-start.27) | collective-permute-done | bytes 688160 | tf_op jit(solution)/shard_map/ppermute | solution.py:696
  101.8 1.2 %weight_grads.1 = (f32[2,768,128]{2,1,0:T(8,128)}, f32[2,96,768]{2,1,0:T(8,128)}) custom-call(s32[1]{0:T(128)} %bitcast.place, f32[4,336,128]{2,1,0:T(8,128)S(1)} %joined.1.mine, f32[4,336,128]{2,1,0:T(8,128)S(1)} %collective-permute-done.27.other), custom_call_target="tpu_custom_call" | custom-call | flops 268435456 | bytes 4194304 | tf_op jit(solution)/shard_map/weight_grads/pallas_call | solution.py:728
  (27 shorter events, 1.5 us)
Async XLA Ops:
  1.4 5.0 %collective-permute-start.1 = (f32[8,768]{1,0:T(8,128)S(1)}, f32[8,768]{1,0:T(8,128)S(1)}, u32[]{:S(2)}, u32[]{:S(2)}) collective-permute-start(f32[8,768]{1,0:T(8,128)S(1)} %get-tuple-element.111), channel_id=1, source_target_pairs={{4,8},{12,16},{20,24},{8,4},{16,12},{24,20},{5,9},{13,17},{21,25},... | collective-permute-start | bytes 73736 | tf_op jit(solution)/shard_map/ppermute | solution.py:691
  2.1 5.2 %collective-permute-start = (f32[8,768]{1,0:T(8,128)S(1)}, f32[8,768]{1,0:T(8,128)S(1)}, u32[]{:S(2)}, u32[]{:S(2)}) collective-permute-start(f32[8,768]{1,0:T(8,128)S(1)} %get-tuple-element.112), channel_id=1, source_target_pairs={{0,4},{4,0},{8,12},{12,8},{16,20},{20,16},{24,28},{28,24},{1,5},{5... | collective-permute-start | bytes 73736 | tf_op jit(solution)/shard_map/ppermute | solution.py:696
  9.1 9.9 %collective-permute-start.7 = (f32[128,128]{1,0:T(8,128)S(1)}, f32[128,128]{1,0:T(8,128)S(1)}, u32[]{:S(2)}, u32[]{:S(2)}) collective-permute-start(f32[128,128]{1,0:T(8,128)S(1)} %get-tuple-element.63.refs_0_), channel_id=1, source_target_pairs={{0,3},{1,2},{2,1},{3,0},{4,7},{5,6},{6,5},{7,4},{8,11},{9,10},{10,... | collective-permute-start | bytes 196616 | tf_op jit(solution)/shard_map/ppermute | solution.py:696
  12.8 7.0 %collective-permute-start.6 = (f32[128,128]{1,0:T(8,128)S(1)}, f32[128,128]{1,0:T(8,128)S(1)}, u32[]{:S(2)}, u32[]{:S(2)}) collective-permute-start(f32[128,128]{1,0:T(8,128)S(1)} %get-tuple-element.63.refs_0_), channel_id=1, source_target_pairs={{0,2},{1,3},{2,0},{3,1},{4,6},{5,7},{6,4},{7,5},{8,10},{9,11},{10,... | collective-permute-start | bytes 196616 | tf_op jit(solution)/shard_map/ppermute | solution.py:696
  12.8 7.0 %collective-permute-start.5 = (f32[128,128]{1,0:T(8,128)S(1)}, f32[128,128]{1,0:T(8,128)S(1)}, u32[]{:S(2)}, u32[]{:S(2)}) collective-permute-start(f32[128,128]{1,0:T(8,128)S(1)} %get-tuple-element.63.refs_0_), channel_id=1, source_target_pairs={{0,1},{1,0},{2,3},{3,2},{4,5},{5,4},{6,7},{7,6},{8,9},{9,8},{10,11... | collective-permute-start | bytes 196616 | tf_op jit(solution)/shard_map/ppermute | solution.py:696
  15.4 9.1 %collective-permute-start.4 = (f32[128,128]{1,0:T(8,128)S(1)}, f32[128,128]{1,0:T(8,128)S(1)}, u32[]{:S(2)}, u32[]{:S(2)}) collective-permute-start(f32[128,128]{1,0:T(8,128)S(1)} %get-tuple-element.59.refs_0_), channel_id=1, source_target_pairs={{0,3},{1,2},{2,1},{3,0},{4,7},{5,6},{6,5},{7,4},{8,11},{9,10},{10,... | collective-permute-start | bytes 196616 | tf_op jit(solution)/shard_map/ppermute | solution.py:696
  19.1 5.7 %collective-permute-start.3 = (f32[128,128]{1,0:T(8,128)S(1)}, f32[128,128]{1,0:T(8,128)S(1)}, u32[]{:S(2)}, u32[]{:S(2)}) collective-permute-start(f32[128,128]{1,0:T(8,128)S(1)} %get-tuple-element.59.refs_0_), channel_id=1, source_target_pairs={{0,2},{1,3},{2,0},{3,1},{4,6},{5,7},{6,4},{7,5},{8,10},{9,11},{10,... | collective-permute-start | bytes 196616 | tf_op jit(solution)/shard_map/ppermute | solution.py:696
  19.1 5.7 %collective-permute-start.2 = (f32[128,128]{1,0:T(8,128)S(1)}, f32[128,128]{1,0:T(8,128)S(1)}, u32[]{:S(2)}, u32[]{:S(2)}) collective-permute-start(f32[128,128]{1,0:T(8,128)S(1)} %get-tuple-element.59.refs_0_), channel_id=1, source_target_pairs={{0,1},{1,0},{2,3},{3,2},{4,5},{5,4},{6,7},{7,6},{8,9},{9,8},{10,11... | collective-permute-start | bytes 196616 | tf_op jit(solution)/shard_map/ppermute | solution.py:696
  29.4 1.6 %collective-permute-start.8 = (f32[2,6,40,128]{3,2,1,0:T(8,128)S(1)}, f32[2,6,40,128]{3,2,1,0:T(8,128)S(1)}, u32[]{:S(2)}, u32[]{:S(2)}) collective-permute-start(f32[2,6,40,128]{3,2,1,0:T(8,128)S(1)} %get-tuple-element.67.mine), channel_id=1, source_target_pairs={{0,4},{4,0},{8,12},{12,8},{16,20},{20,16},{24,28},{28,24},{1,5},{5... | collective-permute-start | bytes 737288 | tf_op jit(solution)/shard_map/ppermute | solution.py:696
  31.2 5.6 %collective-permute-start.9 = (f32[208,128]{1,0:T(8,128)S(1)}, f32[208,128]{1,0:T(8,128)S(1)}, u32[]{:S(2)}, u32[]{:S(2)}) collective-permute-start(f32[208,128]{1,0:T(8,128)S(1)} %get-tuple-element.69), channel_id=1, source_target_pairs={{0,8},{4,20},{8,0},{12,28},{16,24},{20,4},{24,16},{28,12},{1,9},{5... | collective-permute-start | bytes 319496 | tf_op jit(solution)/shard_map/ppermute | solution.py:703
  33.7 5.8 %collective-permute-start.10 = (f32[208,128]{1,0:T(8,128)S(1)}, f32[208,128]{1,0:T(8,128)S(1)}, u32[]{:S(2)}, u32[]{:S(2)}) collective-permute-start(f32[208,128]{1,0:T(8,128)S(1)} %get-tuple-element.70), channel_id=1, source_target_pairs={{0,16},{4,28},{8,24},{12,20},{16,0},{20,12},{24,8},{28,4},{1,17},{... | collective-permute-start | bytes 319496 | tf_op jit(solution)/shard_map/ppermute | solution.py:703
  35.0 6.7 %collective-permute-start.11 = (f32[208,128]{1,0:T(8,128)S(1)}, f32[208,128]{1,0:T(8,128)S(1)}, u32[]{:S(2)}, u32[]{:S(2)}) collective-permute-start(f32[208,128]{1,0:T(8,128)S(1)} %get-tuple-element.71), channel_id=1, source_target_pairs={{0,24},{4,12},{8,16},{12,4},{16,8},{20,28},{24,0},{28,20},{1,25},{... | collective-permute-start | bytes 319496 | tf_op jit(solution)/shard_map/ppermute | solution.py:703
  49.4 11.9 %collective-permute-start.14 = (f32[128,128]{1,0:T(8,128)S(1)}, f32[128,128]{1,0:T(8,128)S(1)}, u32[]{:S(2)}, u32[]{:S(2)}) collective-permute-start(f32[128,128]{1,0:T(8,128)S(1)} %get-tuple-element.85.refs_0_), channel_id=1, source_target_pairs={{0,3},{1,2},{2,1},{3,0},{4,7},{5,6},{6,5},{7,4},{8,11},{9,10},{10,... | collective-permute-start | bytes 196616 | tf_op jit(solution)/shard_map/ppermute | solution.py:696
  53.1 8.2 %collective-permute-start.13 = (f32[128,128]{1,0:T(8,128)S(1)}, f32[128,128]{1,0:T(8,128)S(1)}, u32[]{:S(2)}, u32[]{:S(2)}) collective-permute-start(f32[128,128]{1,0:T(8,128)S(1)} %get-tuple-element.85.refs_0_), channel_id=1, source_target_pairs={{0,2},{1,3},{2,0},{3,1},{4,6},{5,7},{6,4},{7,5},{8,10},{9,11},{10,... | collective-permute-start | bytes 196616 | tf_op jit(solution)/shard_map/ppermute | solution.py:696
  53.1 8.2 %collective-permute-start.12 = (f32[128,128]{1,0:T(8,128)S(1)}, f32[128,128]{1,0:T(8,128)S(1)}, u32[]{:S(2)}, u32[]{:S(2)}) collective-permute-start(f32[128,128]{1,0:T(8,128)S(1)} %get-tuple-element.85.refs_0_), channel_id=1, source_target_pairs={{0,1},{1,0},{2,3},{3,2},{4,5},{5,4},{6,7},{7,6},{8,9},{9,8},{10,11... | collective-permute-start | bytes 196616 | tf_op jit(solution)/shard_map/ppermute | solution.py:696
  61.3 4.6 %collective-permute-start.15 = (f32[128,128]{1,0:T(8,128)S(1)}, f32[128,128]{1,0:T(8,128)S(1)}, u32[]{:S(2)}, u32[]{:S(2)}) collective-permute-start(f32[128,128]{1,0:T(8,128)S(1)} %get-tuple-element.86.own), channel_id=1, source_target_pairs={{0,1},{1,0},{2,3},{3,2},{4,5},{5,4},{6,7},{7,6},{8,9},{9,8},{10,11... | collective-permute-start | bytes 196616 | tf_op jit(solution)/shard_map/ppermute | solution.py:696
  62.6 6.1 %collective-permute-start.17 = (f32[128,128]{1,0:T(8,128)S(1)}, f32[128,128]{1,0:T(8,128)S(1)}, u32[]{:S(2)}, u32[]{:S(2)}) collective-permute-start(f32[128,128]{1,0:T(8,128)S(1)} %get-tuple-element.86.own), channel_id=1, source_target_pairs={{0,3},{1,2},{2,1},{3,0},{4,7},{5,6},{6,5},{7,4},{8,11},{9,10},{10,... | collective-permute-start | bytes 196616 | tf_op jit(solution)/shard_map/ppermute | solution.py:696
  65.1 5.9 %collective-permute-start.16 = (f32[128,128]{1,0:T(8,128)S(1)}, f32[128,128]{1,0:T(8,128)S(1)}, u32[]{:S(2)}, u32[]{:S(2)}) collective-permute-start(f32[128,128]{1,0:T(8,128)S(1)} %get-tuple-element.86.own), channel_id=1, source_target_pairs={{0,2},{1,3},{2,0},{3,1},{4,6},{5,7},{6,4},{7,5},{8,10},{9,11},{10,... | collective-permute-start | bytes 196616 | tf_op jit(solution)/shard_map/ppermute | solution.py:696
  73.0 2.2 %collective-permute-start.20 = (f32[1344,128]{1,0:T(8,128)S(1)}, f32[1344,128]{1,0:T(8,128)S(1)}, u32[]{:S(2)}, u32[]{:S(2)}) collective-permute-start(f32[1344,128]{1,0:T(8,128)S(1)} %get-tuple-element.102), channel_id=1, source_target_pairs={{0,4},{4,0},{8,12},{12,8},{16,20},{20,16},{24,28},{28,24},{1,5},{5... | collective-permute-start | bytes 2064392 | tf_op jit(solution)/shard_map/ppermute | solution.py:696
  75.4 7.1 %collective-permute-start.21 = (f32[336,128]{1,0:T(8,128)S(1)}, f32[336,128]{1,0:T(8,128)S(1)}, u32[]{:S(2)}, u32[]{:S(2)}) collective-permute-start(f32[336,128]{1,0:T(8,128)S(1)} %get-tuple-element.104), channel_id=1, source_target_pairs={{0,8},{4,20},{8,0},{12,28},{16,24},{20,4},{24,16},{28,12},{1,9},{5... | collective-permute-start | bytes 516104 | tf_op jit(solution)/shard_map/ppermute | solution.py:703
  76.2 8.6 %collective-permute-start.22 = (f32[336,128]{1,0:T(8,128)S(1)}, f32[336,128]{1,0:T(8,128)S(1)}, u32[]{:S(2)}, u32[]{:S(2)}) collective-permute-start(f32[336,128]{1,0:T(8,128)S(1)} %get-tuple-element.105), channel_id=1, source_target_pairs={{0,16},{4,28},{8,24},{12,20},{16,0},{20,12},{24,8},{28,4},{1,17},{... | collective-permute-start | bytes 516104 | tf_op jit(solution)/shard_map/ppermute | solution.py:703
  76.9 9.3 %collective-permute-start.23 = (f32[336,128]{1,0:T(8,128)S(1)}, f32[336,128]{1,0:T(8,128)S(1)}, u32[]{:S(2)}, u32[]{:S(2)}) collective-permute-start(f32[336,128]{1,0:T(8,128)S(1)} %get-tuple-element.106), channel_id=1, source_target_pairs={{0,24},{4,12},{8,16},{12,4},{16,8},{20,28},{24,0},{28,20},{1,25},{... | collective-permute-start | bytes 516104 | tf_op jit(solution)/shard_map/ppermute | solution.py:703
  78.9 1.2 %collective-permute-start.18 = (f32[8,768]{1,0:T(8,128)S(1)}, f32[8,768]{1,0:T(8,128)S(1)}, u32[]{:S(2)}, u32[]{:S(2)}) collective-permute-start(f32[8,768]{1,0:T(8,128)S(1)} %get-tuple-element.98), channel_id=1, source_target_pairs={{0,4},{4,0},{8,12},{12,8},{16,20},{20,16},{24,28},{28,24},{1,5},{5... | collective-permute-start | bytes 73736 | tf_op jit(solution)/shard_map/ppermute | solution.py:696
  78.9 1.2 %collective-permute-start.19 = (f32[8,768]{1,0:T(8,128)S(1)}, f32[8,768]{1,0:T(8,128)S(1)}, u32[]{:S(2)}, u32[]{:S(2)}) collective-permute-start(f32[8,768]{1,0:T(8,128)S(1)} %get-tuple-element.99), channel_id=1, source_target_pairs={{4,8},{12,16},{20,24},{8,4},{16,12},{24,20},{5,9},{13,17},{21,25},... | collective-permute-start | bytes 73736 | tf_op jit(solution)/shard_map/ppermute | solution.py:691
  86.2 8.8 %collective-permute-start.26 = (f32[336,128]{1,0:T(8,128)S(1)}, f32[336,128]{1,0:T(8,128)S(1)}, u32[]{:S(2)}, u32[]{:S(2)}) collective-permute-start(f32[336,128]{1,0:T(8,128)S(1)} %share_sum.1.after_this.mine), channel_id=1, source_target_pairs={{0,24},{4,12},{8,16},{12,4},{16,8},{20,28},{24,0},{28,20},{1,25},{... | collective-permute-start | bytes 516104 | tf_op jit(solution)/shard_map/ppermute | solution.py:703
  89.9 9.6 %collective-permute-start.25 = (f32[336,128]{1,0:T(8,128)S(1)}, f32[336,128]{1,0:T(8,128)S(1)}, u32[]{:S(2)}, u32[]{:S(2)}) collective-permute-start(f32[336,128]{1,0:T(8,128)S(1)} %share_sum.1.after_this.mine), channel_id=1, source_target_pairs={{0,16},{4,28},{8,24},{12,20},{16,0},{20,12},{24,8},{28,4},{1,17},{... | collective-permute-start | bytes 516104 | tf_op jit(solution)/shard_map/ppermute | solution.py:703
  90.9 8.6 %collective-permute-start.24 = (f32[336,128]{1,0:T(8,128)S(1)}, f32[336,128]{1,0:T(8,128)S(1)}, u32[]{:S(2)}, u32[]{:S(2)}) collective-permute-start(f32[336,128]{1,0:T(8,128)S(1)} %share_sum.1.after_this.mine), channel_id=1, source_target_pairs={{0,8},{4,20},{8,0},{12,28},{16,24},{20,4},{24,16},{28,12},{1,9},{5... | collective-permute-start | bytes 516104 | tf_op jit(solution)/shard_map/ppermute | solution.py:703
  99.6 2.2 %collective-permute-start.27 = (f32[4,336,128]{2,1,0:T(8,128)S(1)}, f32[4,336,128]{2,1,0:T(8,128)S(1)}, u32[]{:S(2)}, u32[]{:S(2)}) collective-permute-start(f32[4,336,128]{2,1,0:T(8,128)S(1)} %joined.1.mine), channel_id=1, source_target_pairs={{0,4},{4,0},{8,12},{12,8},{16,20},{20,16},{24,28},{28,24},{1,5},{5... | collective-permute-start | bytes 2064392 | tf_op jit(solution)/shard_map/ppermute | solution.py:696

commit v6 on v5

--- a/solution.py
+++ b/solution.py
@@ -79,41 +79,29 @@
         copy.wait()
 
 
+def fetch_kernel(*refs):
+    count = (len(refs) - 1) // 2
+    finish_all(copies_of(list(zip(refs[:count], refs[count : 2 * count])), refs[-1]))
+
+
 def entry_kernel(
-    place, near, far, tokens, conv_weight_in, conv_bias_in, select_in,
-    partial, act, pre, ext, conv_weight, conv_bias, select, plain, sems,
+    place, near, far, tokens, conv_weight, conv_bias, select,
+    partial, act, pre, ext, plain,
 ):
     length, width = tokens.shape
-    loads = copies_of(
-        [
-            (tokens, ext.at[pl.ds(HALO, length)]), (conv_weight_in, conv_weight),
-            (conv_bias_in, conv_bias), (select_in.at[0], select),
-        ],
-        sems,
-    )
     core = lax.rem(place[0], 2)
     ext[:HALO] = jnp.where(core == 0, far[...], near[...])
+    ext[HALO : HALO + length] = tokens[...]
     ext[HALO + length :] = jnp.where(core == 0, near[...], far[...])
-    finish_all(loads[:3])
-    enter(0, ext, conv_weight, conv_bias, select, loads[3], partial, act, pre, plain)
+    enter(0, ext, conv_weight, conv_bias, select, partial, act, pre, plain)
 
 
 def second_entry_kernel(
-    ext, conv_weight_in, conv_bias_in, select_in, gate_in, cot_in,
-    partial, act, pre, grad_gated, spreader,
-    conv_weight, conv_bias, select, plain, gate, cot, sems,
+    ext, conv_weight, conv_bias, select, gate, cot,
+    partial, act, pre, grad_gated, spreader, plain,
 ):
-    loads = copies_of(
-        [
-            (conv_weight_in, conv_weight), (conv_bias_in, conv_bias), (select_in.at[1], select),
-            (gate_in, gate), (cot_in, cot),
-        ],
-        sems,
-    )
     fill_spreader(spreader)
-    finish_all(loads[:2])
-    enter(1, ext, conv_weight, conv_bias, select, loads[2], partial, act, pre, plain)
-    finish_all(loads[3:])
+    enter(1, ext, conv_weight, conv_bias, select, partial, act, pre, plain)
     for t in range(grad_gated.shape[0]):
         lanes = lane_tile(t)
         values = gate[:, lanes]
@@ -121,15 +109,14 @@
         to_cells(plain, grad_gated.at[t])
 
 
-def enter(side, ext, conv_weight, conv_bias, select, load, partial, act, pre, plain):
+def enter(side, ext, conv_weight, conv_bias, select, partial, act, pre, plain):
     tiles, length, _ = act.shape
     for t in range(tiles):
         conv = convolved(ext, HALO, side, lane_tile(t), length, conv_weight, conv_bias)
         pre[t] = conv
         plain[...] = conv * jax.nn.sigmoid(conv)
         to_cells(plain, act.at[t])
-    load.wait()
-    partial[...] = dot(full_width(act), select[...], (1, 0))
+    partial[...] = dot(full_width(act), select[side], (1, 0))
 
 
 def turned(k, by, count):
@@ -228,9 +215,9 @@
 def local_kernel(side, *refs):
     own, first, second, third, act, grad_gated, spreader = refs[:7]
     earlier, refs = refs[7 : 7 + 2 * side], refs[7 + 2 * side :]
-    step_weight_in, step_bias_in, decay_log_in, *refs = refs
-    projection, step, step_pre, entering, decays, bases, carry, row_rates, *refs = refs
-    step_weight, step_bias, decay_log, rates, rate_rows, sems = refs
+    step_weight_in, step_bias_in, decay_log_in, skip_gain_in, *refs = refs
+    projection, step, step_pre, entering, decays, bases, rates, skip_rows, *refs = refs
+    carry, row_rates, step_weight, step_bias, decay_log, skip_gain, rate_rows, sems = refs
     tiles, length, _ = act.shape
     states = decay_log.shape[0]
     ranks = step_weight.shape[0]
@@ -239,7 +226,7 @@
     loads = copies_of(
         [
             (step_weight_in.at[side], step_weight), (decay_log_in.at[side], decay_log),
-            (step_bias_in, step_bias),
+            (step_bias_in, step_bias), (skip_gain_in, skip_gain),
         ],
         sems,
     )
@@ -247,6 +234,8 @@
     fill_bases(projection, spreader, bases)
     finish_all(loads)
     fill_rates(decay_log, rates)
+    for t in range(tiles):
+        skip_rows[t] = skip_gain[side : side + 1, lane_tile(t)]
     wide = dot(projection[:, :ranks], step_weight[...], (1, 0)) + step_bias[side : side + 1]
     for t in range(tiles):
         part = wide[:, lane_tile(t)]
@@ -388,30 +377,20 @@
 
 
 def scan_kernel(side, *refs):
-    incoming, bases, act, step, step_pre, grad_gated, entering, decays, spreader = refs[:9]
-    earlier, refs = refs[9 : 9 + side], refs[9 + side :]
-    step_weight_in, decay_log_in, skip_gain_in, *refs = refs
+    incoming, bases, act, step, step_pre, grad_gated, entering, decays, spreader, *refs = refs
+    rates, skip_rows, *refs = refs
+    earlier, refs = refs[:side], refs[side:]
+    step_weight_in, *refs = refs
     partial, grad_act, grad_pre, summed_out, *refs = refs
-    step_weight, decay_log, skip_gain, rates, rate_rows, history, *refs = refs
-    grad_in, grad_out, weights, skip_rows, sems = refs
+    step_weight, rate_rows, history, grad_in, grad_out, weights, sems = refs
     tiles, length, _ = act.shape
-    states = decay_log.shape[0]
+    states = rates.shape[1]
     ranks = step_weight.shape[0]
     count = length // CHAINS
     group = tile_group(tiles)
-    loads = copies_of(
-        [
-            (decay_log_in.at[side], decay_log), (skip_gain_in, skip_gain),
-            (step_weight_in.at[side], step_weight),
-        ],
-        sems,
-    )
+    loads = copies_of([(step_weight_in.at[side], step_weight)], sems)
     grad_in[...] = jnp.zeros_like(grad_in)
     grad_out[...] = jnp.zeros_like(grad_out)
-    finish_all(loads)
-    fill_rates(decay_log, rates)
-    for t in range(tiles):
-        skip_rows[t] = skip_gain[side : side + 1, lane_tile(t)]
     up = side == 0
     basis_b, basis_c = bases.at[0], bases.at[1]
 
@@ -513,6 +492,7 @@
     lax.fori_loop(0, tiles // group, some_tiles, 0)
     wide = full_width(grad_pre)
     weights[...] = jnp.zeros_like(weights)
+    finish_all(loads)
     weights[:ranks] = step_weight[...]
     sums = jnp.zeros((length, LANES), jnp.float32)
     step_lanes = 4 * LANES
@@ -540,9 +520,8 @@
 
 
 def gate_kernel(
-    summed, gate_in, cot_in, after_this, block_out, gate_grad, gate, cot, plain, sems
+    summed, gate, cot, after_this, block_out, gate_grad, plain
 ):
-    finish_all(copies_of([(gate_in, gate), (cot_in, cot)], sems))
     for t in range(summed.shape[0]):
         lanes = lane_tile(t)
         values = gate[:, lanes]
@@ -553,23 +532,22 @@
 
 
 def weight_kernel(
-    total, act, pre, grad_act, select_in, after_this,
-    part, conv_grad, select, grad, plain, cells, sems,
+    total, act, pre, grad_act, select, after_this, part, conv_grad, grad, plain, cells,
 ):
     weigh(
-        0, (total,), act, pre, grad_act, select_in,
-        conv_grad, select, grad, plain, cells, sems, part,
+        0, (total,), act, pre, grad_act, select, conv_grad, grad, plain, cells, part,
     )
 
 
 def second_weight_kernel(
-    place, own, first, second, third, act, pre, grad_act, select_in, part, step_part, other_grad,
-    keep, send, conv_grad, near, far, select, grad, plain, cells, mine, sems,
+    place, own, first, second, third, act, pre, grad_act, select, after_this,
+    part, step_part, other_grad,
+    keep, send, conv_grad, near, far, grad, plain, cells, mine,
 ):
     length, width = conv_grad.shape
     weigh(
-        1, (own, first, second, third), act, pre, grad_act, select_in,
-        conv_grad, select, grad, plain, cells, sems, mine,
+        1, (own, first, second, third), act, pre, grad_act, select,
+        conv_grad, grad, plain, cells, mine,
     )
     core = lax.rem(place[0], 2)
     for side, value in enumerate((part, mine)):
@@ -584,17 +562,13 @@
     far[...] = jnp.where(core == 0, head, tail)
 
 
-def weigh(
-    side, terms, act, pre, grad_act, select_in, conv_grad, select, grad, plain, cells, sems, part
-):
-    loads = copies_of([(select_in.at[side], select)], sems)
+def weigh(side, terms, act, pre, grad_act, select, conv_grad, grad, plain, cells, part):
     total = terms[0][...]
     for term in terms[1:]:
         total = total + term[...]
     grad[...] = total
     part[...] = dot(full_width(act), grad[...], (0, 0))
-    finish_all(loads)
-    wide = dot(grad[...], select[...], (1, 1))
+    wide = dot(grad[...], select[side], (1, 1))
     for t in range(act.shape[0]):
         lanes = lane_tile(t)
         cells[...] = grad_act[t] + wide[:, lanes]
@@ -619,10 +593,6 @@
     terms, (total, out) = refs[:-2], refs[-2:]
     add_kernel(*terms, total)
     out[...] = value[...]
-
-
-def add_after_kernel(after_this, *refs):
-    add_kernel(*refs)
 
 
 def add_kernel(*refs):
@@ -779,85 +749,84 @@
     dma = lambda n: pltpu.SemaphoreType.DMA((n,))
     bases = vmem((length, states * LANES))
     grouped = vmem((group, length, states * LANES))
-    rate_scratch = vmem((tiles, states, LANES))
     row_scratch = vmem((group, states, CHAINS, LANES))
 
     core = (place & 1)[:, None] == 0
     head, tail = tokens[:HALO], tokens[length - HALO :]
     edges = swapped_edges(jnp.where(core, tail, head), jnp.where(core, head, tail), "ctx")
-    conv_scratch = [
-        vmem(conv_weight.shape), vmem(conv_bias.shape), vmem(select_weight.shape[1:]), vmem(narrow),
-    ]
+    fetched = (tokens, conv_weight, conv_bias, select_weight, gate_input, cotangent)
+    held, conv_weight_held, conv_bias_held, select, gate, cot = call(
+        fetch_kernel, "fetch", tuple(a.shape for a in fetched), [dma(6)], 4, fetched,
+        "hhhhhh", "mmmmmm",
+    )
     first_partial, first_act, first_pre, extended = call(
-        entry_kernel, "entry", (narrow, one, one, (length + 2 * HALO, width)),
-        [*conv_scratch, dma(4)],
-        8, (place, *edges, tokens, conv_weight, conv_bias, select_weight), "svvhhhh", "vmmm",
+        entry_kernel, "entry", (narrow, one, one, (length + 2 * HALO, width)), [vmem(narrow)],
+        6, (place, *edges, held, conv_weight_held, conv_bias_held, select), "svvmmmm", "vmmm",
     )
     first_terms = terms_of(first_partial)
     partial, act, pre, grad_gated, spreader = call(
         second_entry_kernel, "second_entry",
         (narrow, one, one, one, (LANES, 2 * states * LANES)),
-        [*conv_scratch, vmem(flat), vmem(flat), dma(5)],
-        10, (extended, conv_weight, conv_bias, select_weight, gate_input, cotangent),
-        "mhhhhh", "vmmmb",
+        [vmem(narrow)],
+        6, (extended, conv_weight_held, conv_bias_held, select, gate, cot), "mmmmmm", "vmmmb",
     )
     projection_terms = (first_terms, terms_of(partial))
     acts, pres = (first_act, act), (first_pre, pre)
     earlier, locals_ = (), []
     for side in range(2):
-        *found, carried, rates = call(
+        *found, carried, every_rate = call(
             functools.partial(local_kernel, side), ("first_local", "second_local")[side],
             (
                 narrow, one, one, chain_ends, (*one[:-1], states * LANES),
-                (2, length, states * LANES), carry, row_rates,
+                (2, length, states * LANES), (tiles, states, LANES), (tiles, 1, LANES),
+                carry, row_rates,
             ),
             [
                 vmem(step_weight.shape[1:]), vmem(step_bias.shape), vmem(decay_log.shape[1:]),
-                rate_scratch, row_scratch, dma(3),
+                vmem(skip_gain.shape), row_scratch, dma(4),
             ],
             10,
             (
                 *projection_terms[side], acts[side], grad_gated, spreader, *earlier, step_weight,
-                step_bias, decay_log,
+                step_bias, decay_log, skip_gain,
             ),
-            "vvvvmmm" + "v" * len(earlier) + "hhh", "mmmmmmvv", 2**32,
+            "vvvvmmm" + "v" * len(earlier) + "hhhh", "mmmmmmmmvv", 2**32,
         )
-        earlier = (carried, rates)
+        earlier = (carried, every_rate)
         locals_.append(found)
     if near:
         other = swapped(carried, "ctx", 1)
         sent = call(
             pair_kernel, "pair", (packed,) * (chips - 1),
-            [vmem(carry)], 8, (place, carried, other, rates), "svvv",
+            [vmem(carry)], 8, (place, carried, other, every_rate), "svvv",
         )
         got = [swapped_chips(part, k) for k, part in enumerate(sent, 1)]
         (incoming,) = call(
             chain_kernel, "chain", ((2, *row_rates),), [vmem((chips, *carry[1:]))],
-            8, (place, other, rates, *got), "svv" + "v" * len(got),
+            8, (place, other, every_rate, *got), "svv" + "v" * len(got),
         )
     else:
         gathered = lax.all_gather(carried, "ctx")
         (incoming,) = call(
             long_chain_kernel, "chain", ((2, *row_rates),), [],
-            48, (place, gathered, rates), "svv",
+            48, (place, gathered, every_rate), "svv",
         )
     earlier, grad_terms, grad_acts, grad_pres = (), [], [], []
     for side in range(2):
-        projection, step, step_pre, entering, decays, spread_bases = locals_[side]
+        _, step, step_pre, entering, decays, spread_bases, rates, skip_rows = locals_[side]
         partial_grad, grad_act, grad_pre, summed = call(
             functools.partial(scan_kernel, side), ("first_scan", "second_scan")[side],
             (narrow, one, one, one),
             [
-                vmem(step_weight.shape[1:]), vmem(decay_log.shape[1:]), vmem(skip_gain.shape),
-                rate_scratch, row_scratch, grouped, bases, bases, vmem((LANES, width)),
-                vmem((tiles, 1, LANES)), dma(3),
+                vmem(step_weight.shape[1:]), row_scratch, grouped, bases, bases,
+                vmem((LANES, width)), dma(1),
             ],
             10,
             (
                 incoming, spread_bases, acts[side], step, step_pre, grad_gated, entering, decays,
-                spreader, *earlier, step_weight, decay_log, skip_gain,
+                spreader, rates, skip_rows, *earlier, step_weight,
             ),
-            "vmmmmmmmm" + "m" * side + "hhh", "vmmm", 2**33,
+            "vmmmmmmmmmm" + "m" * side + "h", "vmmm", 2**33,
         )
         if side == 1:
             first_total, partial_grad = call(
@@ -873,30 +842,36 @@
         step_kernel, "step_grad", ((2, tiles, ranks, LANES),), [],
         8, (*grad_pres, locals_[0][0], locals_[1][0], arrived), "mmmmv", flops=0,
     )
-    weight_scratch = [
-        vmem(select_weight.shape[1:]), vmem(narrow), vmem(narrow), vmem(narrow),
-    ]
+    weight_scratch = [vmem(narrow), vmem(narrow), vmem(narrow)]
     part, first_grad = call(
-        weight_kernel, "first_weights", ((width, LANES), flat), [*weight_scratch, dma(1)],
-        8, (first_total, first_act, first_pre, grad_acts[0], select_weight, arrived),
-        "vmmmhv", "mm", 0,
+        weight_kernel, "first_weights", ((width, LANES), flat), weight_scratch,
+        8, (first_total, first_act, first_pre, grad_acts[0], select, arrived),
+        "vmmmmv", "mm", 0,
+    )
+    block_out, gate_grad = call(
+        gate_kernel, "gate", (flat, flat), [vmem(one[1:])],
+        6, (summed, gate, cot, arrived), "mmmv", flops=0,
     )
     half = width + tiles * ranks
     keep, send, second_grad, *edges = call(
         second_weight_kernel, "weights",
         ((half, LANES), (half, LANES), flat, (HALO, width), (HALO, width)),
-        [*weight_scratch, vmem((width, LANES)), dma(1)],
+        [*weight_scratch, vmem((width, LANES))],
         10,
         (
-            place, *grad_terms[1], act, pre, grad_acts[1], select_weight, part, step_part,
+            place, *grad_terms[1], act, pre, grad_acts[1], select, block_out, part, step_part,
             first_grad,
         ),
-        "svvvvmmmhmvm", "vvmvv",
+        "svvvvmmmmhmvm", "vvmvv",
     )
     edges = swapped_edges(*edges, "ctx")
     if near:
         shares = halved(place, keep, send, half, chips, "halves")
-        ahead = shares[0]
+        rows = half // chips
+        (mine,) = call(
+            add_kernel, "share_sum", ((rows, LANES),), [], 4, shares, "v" * chips
+        )
+        ahead = mine
     else:
         ahead = edges[0]
     (tokens_grad,) = call(
@@ -908,22 +883,10 @@
         8, (place, *edges, first_grad, second_grad, conv_weight, ahead), "svvmmhv",
     )
     if near:
-        rows = half // chips
-        (mine,) = call(
-            add_after_kernel, "share_sum", ((rows, LANES),), [], 4, (tokens_grad, *shares),
-            "h" + "v" * chips,
-        )
-        ahead = mine
-    block_out, gate_grad = call(
-        gate_kernel, "gate", (flat, flat),
-        [vmem(flat), vmem(flat), vmem(one[1:]), dma(2)],
-        8, (summed, gate_input, cotangent, ahead), "mhhv", flops=0,
-    )
-    if near:
         got = [swapped_chips(mine, k) for k in range(1, chips)]
         (joined,) = call(
             join_kernel, "joined", ((chips, rows, LANES),), [],
-            8, (place, block_out, mine, *got), "sh" + "v" * chips,
+            8, (place, tokens_grad, mine, *got), "sh" + "v" * chips,
         )
         select_grad, step_grad = call(
             outputs_kernel, "weight_grads", ((2, width, LANES), (2, ranks, width)),

time: 104 us -> 96.6 us (0.929)
  Pallas kernels: 38.5 us -> 32.3 us
  starting transfers between devices: 37.1 us -> 35.1 us
  waiting for transfers between devices: 25.7 us -> 27.3 us
    pallas_call x18 -> x19, Pallas kernels: 38.5 us -> 32.3 us  [call(): pl.pallas_call(kernel, in_specs=[spaces[k] for k in kinds], out_specs=[sp...]
    ppermute x9, waiting for transfers between devices: 15.6 us -> 18.6 us  [swapped_chips(): return lax.ppermute(value, 'ctx', pairs)]
    ppermute x9, starting transfers between devices: 13.6 us -> 11.4 us  [swapped_chips(): return lax.ppermute(value, 'ctx', pairs)]
    ppermute x17, waiting for transfers between devices: 10.1 us -> 8.74 us  [swapped(): return lax.ppermute(value, axis, [(i, i ^ by) for i in range(count)])]
  transfers between devices with their start and end apart: 28 -> 28, of which waited for: 16 -> 15; matrix products, arithmetic and copies ran while one was open for 0% -> 0% of each run, Pallas kernels for 20% -> 19%
where the time goes in v6:
time: 96.6 us; the launch traced here: 96.3 us
  starting transfers between devices  35.1 us (36%)
  Pallas kernels  32.3 us (33%)
  waiting for transfers between devices  27.3 us (28%)
    pallas_call x19, Pallas kernels, call(): pl.pallas_call(kernel, in_specs=[spaces[k] for k in kinds], out_specs=[sp...  32.3 us
    ppermute x17, starting transfers between devices, swapped(): return lax.ppermute(value, axis, [(i, i ^ by) for i in range(count)])  22.4 us
    ppermute x9, waiting for transfers between devices, swapped_chips(): return lax.ppermute(value, 'ctx', pairs)  18.6 us
    ppermute x9, starting transfers between devices, swapped_chips(): return lax.ppermute(value, 'ctx', pairs)  11.4 us
    ppermute x17, waiting for transfers between devices, swapped(): return lax.ppermute(value, axis, [(i, i ^ by) for i in range(count)])  8.74 us
  transfers between devices with their start and end apart: 28, of which 15 were waited for; matrix products, arithmetic and copies ran while one was open for 0% of the time, Pallas kernels for 19%

profile of v6, /device:TPU:0, one launch (start us, length us, event | category | flops | bytes accessed | tf_op | source)
XLA Modules:
  0.0 96.3 jit_solution(6230097487987353155)
XLA Ops:
  0.6 0.8 slice_select_fusion
  1.4 0.7 collective-permute-start.1
  2.1 4.4 %collective-permute-start = (f32[8,768]{1,0:T(8,128)S(1)}, f32[8,768]{1,0:T(8,128)S(1)}, u32[]{:S(2)}, u32[]{:S(2)}) collective-permute-start(f32[8,768]{1,0:T(8,128)S(1)} %get-tuple-element.132), channel_id=1, source_target_pairs={{0,4},{4,0},{8,12},{12,8},{16,20},{20,16},{24,28},{28,24},{1,5},{5... | collective-permute-start | bytes 73736 | tf_op jit(solution)/shard_map/ppermute | solution.py:666
  6.4 1.6 %fetch.1 = (f32[128,768]{1,0:T(8,128)S(1)}, f32[2,4,768]{2,1,0:T(4,128)S(1)}, f32[2,768]{1,0:T(2,128)S(1)}, f32[2,768,128]{2,1,0:T(8,128)S(1)}, f32[128,768]{1,0:T(8,128)S(1)}, /*index=5*/f32[128,768]{1,0:T(8,128)S(1)}) custom-call(f32[128,768]{1,0:T(8,128)} %refs_0_.1, f32[2,4,768]{2,1,0:T(4,128)} %conv_weight_in.1, f32[2,768]{1,0:T(2,128)} %refs_2_.1, ...), custom_call_target="tpu_custom_call" | custom-call | flops 268435456 | bytes 4194304 | tf_op jit(solution)/shard_map/fetch/pallas_call | solution.py:698
  8.0 0.8 entry.1
  8.8 3.7 %collective-permute-start.7 = (f32[128,128]{1,0:T(8,128)S(1)}, f32[128,128]{1,0:T(8,128)S(1)}, u32[]{:S(2)}, u32[]{:S(2)}) collective-permute-start(f32[128,128]{1,0:T(8,128)S(1)} %get-tuple-element.79.refs_0_), channel_id=1, source_target_pairs={{0,3},{1,2},{2,1},{3,0},{4,7},{5,6},{6,5},{7,4},{8,11},{9,10},{10,... | collective-permute-start | bytes 196616 | tf_op jit(solution)/shard_map/ppermute | solution.py:666
  12.5 0.8 collective-permute-start.5
  13.3 1.2 %second_entry.1 = (f32[128,128]{1,0:T(8,128)S(1)}, f32[6,128,128]{2,1,0:T(8,128)S(1)}, f32[6,128,128]{2,1,0:T(8,128)S(1)}, f32[6,128,128]{2,1,0:T(8,128)S(1)}, bf16[128,4096]{1,0:T(8,128)(2,1)S(1)}) custom-call(f32[144,768]{1,0:T(8,128)S(1)} %get-tuple-element.72.ext, f32[2,4,768]{2,1,0:T(4,128)S(1)} %get-tuple-element.69.conv_weight, ...), custom_call_target="tpu_custom_call" | custom-call | flops 268435456 | bytes 4194304 | tf_op jit(solution)/shard_map/second_entry/pallas_call | solution.py:698
  14.5 3.7 %collective-permute-start.4 = (f32[128,128]{1,0:T(8,128)S(1)}, f32[128,128]{1,0:T(8,128)S(1)}, u32[]{:S(2)}, u32[]{:S(2)}) collective-permute-start(f32[128,128]{1,0:T(8,128)S(1)} %get-tuple-element.75.refs_0_), channel_id=1, source_target_pairs={{0,3},{1,2},{2,1},{3,0},{4,7},{5,6},{6,5},{7,4},{8,11},{9,10},{10,... | collective-permute-start | bytes 196616 | tf_op jit(solution)/shard_map/ppermute | solution.py:666
  18.2 0.8 collective-permute-start.2
  19.4 4.7 %first_local.1 = (f32[128,128]{1,0:T(8,128)S(1)}, f32[6,128,128]{2,1,0:T(8,128)S(1)}, f32[6,128,128]{2,1,0:T(8,128)S(1)}, f32[2,6,16,8,128]{4,3,2,1,0:T(8,128)S(...) custom-call(f32[128,128]{1,0:T(8,128)S(1)} %get-tuple-element.79.ref, ...), custom_call_target="tpu_custom_call" | custom-call | flops 4294967296 | bytes 67108864 | tf_op jit(solution)/shard_map/first_local/pallas_call | solution.py:698
  24.1 4.9 %second_local.1 = (f32[128,128]{1,0:T(8,128)S(1)}, f32[6,128,128]{2,1,0:T(8,128)S(1)}, f32[6,128,128]{2,1,0:T(8,128)S(1)}, f32[2,6,16,8,128]{4,3,2,1,0:T(8,128)S...) custom-call(f32[128,128]{1,0:T(8,128)S(1)} %get-tuple-element.75.ref, ...), custom_call_target="tpu_custom_call" | custom-call | flops 4294967296 | bytes 67108864 | tf_op jit(solution)/shard_map/second_local/pallas_call | solution.py:698
  29.1 1.5 %collective-permute-done.8.other = f32[2,6,40,128]{3,2,1,0:T(8,128)S(1)} collective-permute-done((f32[2,6,40,128]{3,2,1,0:T(8,128)S(1)}, f32[2,6,40,128]{3,2,1,0:T(8,128)S(1)}, u32[]{:S(2)}, u32[]{:S(2)}) %collective-permute-start.8) | collective-permute-done | bytes 245792 | tf_op jit(solution)/shard_map/ppermute | solution.py:666
  30.7 2.1 %collective-permute-start.9 = (f32[208,128]{1,0:T(8,128)S(1)}, f32[208,128]{1,0:T(8,128)S(1)}, u32[]{:S(2)}, u32[]{:S(2)}) collective-permute-start(f32[208,128]{1,0:T(8,128)S(1)} %get-tuple-element.85), channel_id=1, source_target_pairs={{0,8},{4,20},{8,0},{12,28},{16,24},{20,4},{24,16},{28,12},{1,9},{5... | collective-permute-start | bytes 319496 | tf_op jit(solution)/shard_map/ppermute | solution.py:673
  32.8 1.8 %collective-permute-start.10 = (f32[208,128]{1,0:T(8,128)S(1)}, f32[208,128]{1,0:T(8,128)S(1)}, u32[]{:S(2)}, u32[]{:S(2)}) collective-permute-start(f32[208,128]{1,0:T(8,128)S(1)} %get-tuple-element.86), channel_id=1, source_target_pairs={{0,16},{4,28},{8,24},{12,20},{16,0},{20,12},{24,8},{28,4},{1,17},{... | collective-permute-start | bytes 319496 | tf_op jit(solution)/shard_map/ppermute | solution.py:673
  35.0 0.8 collective-permute-done.9.refs_0_
  35.8 2.5 %collective-permute-done.10.refs_1_ = f32[208,128]{1,0:T(8,128)S(1)} collective-permute-done((f32[208,128]{1,0:T(8,128)S(1)}, f32[208,128]{1,0:T(8,128)S(1)}, u32[]{:S(2)}, u32[]{:S(2)}) %collective-permute-start.10) | collective-permute-done | bytes 106528 | tf_op jit(solution)/shard_map/ppermute | solution.py:673
  38.3 2.7 %collective-permute-done.11.refs_2_ = f32[208,128]{1,0:T(8,128)S(1)} collective-permute-done((f32[208,128]{1,0:T(8,128)S(1)}, f32[208,128]{1,0:T(8,128)S(1)}, u32[]{:S(2)}, u32[]{:S(2)}) %collective-permute-start.11) | collective-permute-done | bytes 106528 | tf_op jit(solution)/shard_map/ppermute | solution.py:673
  41.3 5.7 %first_scan.1 = (f32[128,128]{1,0:T(8,128)S(1)}, f32[6,128,128]{2,1,0:T(8,128)S(1)}, f32[6,128,128]{2,1,0:T(8,128)S(1)}, f32[6,128,128]{2,1,0:T(8,128)S(1)}) custom-call(f32[2,6,32,128]{3,2,1,0:T(8,128)S(1)} %chain.1.refs_0_, f32[2,128,2048]{2,1,0:T(8,128)S(1)} %get-tuple-element.95.refs_1_, f32[6,128,128]{2,1,0:T(8,128)S(1)} %get-tuple-element.80.refs_4_.refs_2_.act, ...), custom_call_target="tpu_custom_call" | custom-call | flops 8589934592 | bytes 134217728 | tf_op jit(solution)/shard_map/first_scan/pallas_call | solution.py:698
  47.0 3.0 %collective-permute-start.14 = (f32[128,128]{1,0:T(8,128)S(1)}, f32[128,128]{1,0:T(8,128)S(1)}, u32[]{:S(2)}, u32[]{:S(2)}) collective-permute-start(f32[128,128]{1,0:T(8,128)S(1)} %get-tuple-element.105.refs_0_), channel_id=1, source_target_pairs={{0,3},{1,2},{2,1},{3,0},{4,7},{5,6},{6,5},{7,4},{8,11},{9,10},{10,... | collective-permute-start | bytes 196616 | tf_op jit(solution)/shard_map/ppermute | solution.py:666
  50.0 1.5 %collective-permute-start.12 = (f32[128,128]{1,0:T(8,128)S(1)}, f32[128,128]{1,0:T(8,128)S(1)}, u32[]{:S(2)}, u32[]{:S(2)}) collective-permute-start(f32[128,128]{1,0:T(8,128)S(1)} %get-tuple-element.105.refs_0_), channel_id=1, source_target_pairs={{0,1},{1,0},{2,3},{3,2},{4,5},{5,4},{6,7},{7,6},{8,9},{9,8},{10,11... | collective-permute-start | bytes 196616 | tf_op jit(solution)/shard_map/ppermute | solution.py:666
  51.4 5.7 %second_scan.1 = (f32[128,128]{1,0:T(8,128)S(1)}, f32[6,128,128]{2,1,0:T(8,128)S(1)}, f32[6,128,128]{2,1,0:T(8,128)S(1)}, f32[6,128,128]{2,1,0:T(8,128)S(1)}) custom-call(f32[2,6,32,128]{3,2,1,0:T(8,128)S(1)} %chain.1.refs_0_, f32[2,128,2048]{2,1,0:T(8,128)S(1)} %get-tuple-element.88.refs_1_, f32[6,128,128]{2,1,0:T(8,128)S(1)} %get-tuple-element.76.refs_4_.refs_2_.act, ...), custom_call_target="tpu_custom_call" | custom-call | flops 8589934592 | bytes 134217728 | tf_op jit(solution)/shard_map/second_scan/pallas_call | solution.py:698
  57.2 0.6 collective-permute-start.15
  57.8 2.4 %collective-permute-start.17 = (f32[128,128]{1,0:T(8,128)S(1)}, f32[128,128]{1,0:T(8,128)S(1)}, u32[]{:S(2)}, u32[]{:S(2)}) collective-permute-start(f32[128,128]{1,0:T(8,128)S(1)} %get-tuple-element.106.own), channel_id=1, source_target_pairs={{0,3},{1,2},{2,1},{3,0},{4,7},{5,6},{6,5},{7,4},{8,11},{9,10},{10,... | collective-permute-start | bytes 196616 | tf_op jit(solution)/shard_map/ppermute | solution.py:666
  60.8 1.2 %collective-permute-done.15.after_this.first = f32[128,128]{1,0:T(8,128)S(1)} collective-permute-done((f32[128,128]{1,0:T(8,128)S(1)}, f32[128,128]{1,0:T(8,128)S(1)}, u32[]{:S(2)}, u32[]{:S(2)}) %collective-permute-start.15) | collective-permute-done | bytes 65568 | tf_op jit(solution)/shard_map/ppermute | solution.py:666
  61.9 1.2 %gate.1 = (f32[128,768]{1,0:T(8,128)}, f32[128,768]{1,0:T(8,128)}) custom-call(f32[6,128,128]{2,1,0:T(8,128)S(1)} %get-tuple-element.103.summed, f32[128,768]{1,0:T(8,128)S(1)} %get-tuple-element.73.gate, f32[128,768]{1,0:T(8,128)S(1)} %get-tuple-element.74.cot, f32[128,128]{1,0:T(8,128)S(1)} %collective-permute-done.15.after_this.first), custom_call_target="tpu_custom_call" | custom-call | tf_op jit(solution)/shard_map/gate/pallas_call | solution.py:698
  63.1 0.9 first_weights.1
  64.1 0.8 step_grad.1.step_part
  64.9 1.2 %collective-permute-done.16.second = f32[128,128]{1,0:T(8,128)S(1)} collective-permute-done((f32[128,128]{1,0:T(8,128)S(1)}, f32[128,128]{1,0:T(8,128)S(1)}, u32[]{:S(2)}, u32[]{:S(2)}) %collective-permute-start.16) | collective-permute-done | bytes 65568 | tf_op jit(solution)/shard_map/ppermute | solution.py:666
  66.1 1.0 %weights.1 = (f32[1344,128]{1,0:T(8,128)S(1)}, f32[1344,128]{1,0:T(8,128)S(1)}, f32[128,768]{1,0:T(8,128)S(1)}, f32[8,768]{1,0:T(8,128)S(1)}, f32[8,768]{1,0:T(8,128)S(1)}) custom-call(s32[1]{0:T(128)} %bitcast.place, f32[128,128]{1,0:T(8,128)S(1)} %get-tuple-element.106.own, f32[128,128]{1,0:T(8,128)S(1)} %collective-permute-done.15.after_this.first, ...), custom_call_target="tpu_custom_call" | custom-call | flops 268435456 | bytes 4194304 | tf_op jit(solution)/shard_map/weights/pallas_call | solution.py:698
  67.3 2.1 %collective-permute-done.20.got = f32[1344,128]{1,0:T(8,128)S(1)} collective-permute-done((f32[1344,128]{1,0:T(8,128)S(1)}, f32[1344,128]{1,0:T(8,128)S(1)}, u32[]{:S(2)}, u32[]{:S(2)}) %collective-permute-start.20) | collective-permute-done | bytes 688160 | tf_op jit(solution)/shard_map/ppermute | solution.py:666
  69.5 0.9 collective-permute-start.21
  70.4 0.9 collective-permute-start.22
  71.2 1.8 %collective-permute-start.23 = (f32[336,128]{1,0:T(8,128)S(1)}, f32[336,128]{1,0:T(8,128)S(1)}, u32[]{:S(2)}, u32[]{:S(2)}) collective-permute-start(f32[336,128]{1,0:T(8,128)S(1)} %get-tuple-element.127), channel_id=1, source_target_pairs={{0,24},{4,12},{8,16},{12,4},{16,8},{20,28},{24,0},{28,20},{1,25},{... | collective-permute-start | bytes 516104 | tf_op jit(solution)/shard_map/ppermute | solution.py:673
  73.1 3.5 %collective-permute-done.21.refs_1_ = f32[336,128]{1,0:T(8,128)S(1)} collective-permute-done((f32[336,128]{1,0:T(8,128)S(1)}, f32[336,128]{1,0:T(8,128)S(1)}, u32[]{:S(2)}, u32[]{:S(2)}) %collective-permute-start.21) | collective-permute-done | bytes 172064 | tf_op jit(solution)/shard_map/ppermute | solution.py:673
  76.6 2.4 %collective-permute-done.22.refs_2_ = f32[336,128]{1,0:T(8,128)S(1)} collective-permute-done((f32[336,128]{1,0:T(8,128)S(1)}, f32[336,128]{1,0:T(8,128)S(1)}, u32[]{:S(2)}, u32[]{:S(2)}) %collective-permute-start.22) | collective-permute-done | bytes 172064 | tf_op jit(solution)/shard_map/ppermute | solution.py:673
  79.0 1.3 %collective-permute-done.23.refs_3_ = f32[336,128]{1,0:T(8,128)S(1)} collective-permute-done((f32[336,128]{1,0:T(8,128)S(1)}, f32[336,128]{1,0:T(8,128)S(1)}, u32[]{:S(2)}, u32[]{:S(2)}) %collective-permute-start.23) | collective-permute-done | bytes 172064 | tf_op jit(solution)/shard_map/ppermute | solution.py:673
  80.4 1.7 %collective-permute-start.26 = (f32[336,128]{1,0:T(8,128)S(1)}, f32[336,128]{1,0:T(8,128)S(1)}, u32[]{:S(2)}, u32[]{:S(2)}) collective-permute-start(f32[336,128]{1,0:T(8,128)S(1)} %share_sum.1.after_this.mine), channel_id=1, source_target_pairs={{0,24},{4,12},{8,16},{12,4},{16,8},{20,28},{24,0},{28,20},{1,25},{... | collective-permute-start | bytes 516104 | tf_op jit(solution)/shard_map/ppermute | solution.py:673
  82.1 0.9 collective-permute-start.25
  82.9 1.0 %collective-permute-start.24 = (f32[336,128]{1,0:T(8,128)S(1)}, f32[336,128]{1,0:T(8,128)S(1)}, u32[]{:S(2)}, u32[]{:S(2)}) collective-permute-start(f32[336,128]{1,0:T(8,128)S(1)} %share_sum.1.after_this.mine), channel_id=1, source_target_pairs={{0,8},{4,20},{8,0},{12,28},{16,24},{20,4},{24,16},{28,12},{1,9},{5... | collective-permute-start | bytes 516104 | tf_op jit(solution)/shard_map/ppermute | solution.py:673
  84.0 0.7 collective-permute-start.19
  84.6 0.5 collective-permute-done.18.near
  85.1 1.9 %exit.1.after_this = f32[128,768]{1,0:T(8,128)} custom-call(s32[1]{0:T(128)} %bitcast.place, f32[8,768]{1,0:T(8,128)S(1)} %collective-permute-done.18.near, f32[8,768]{1,0:T(8,128)S(1)} %collective-permute-done.19.far, f32[128,768]{1,0:T(8,128)S(1)} %get-tuple-element.118.other_grad.first, f32[128,768]{1,0:T(8,128)S(1)} %get-tuple-element.121.second, ...), custom_call_target="tpu_custom_call" | custom-call | flops 268435456 | bytes 4194304 | tf_op jit(solution)/shard_map/exit/pallas_call | solution.py:698
  87.1 1.7 %collective-permute-done.26.refs_2_ = f32[336,128]{1,0:T(8,128)S(1)} collective-permute-done((f32[336,128]{1,0:T(8,128)S(1)}, f32[336,128]{1,0:T(8,128)S(1)}, u32[]{:S(2)}, u32[]{:S(2)}) %collective-permute-start.26) | collective-permute-done | bytes 172064 | tf_op jit(solution)/shard_map/ppermute | solution.py:673
  88.8 3.5 %collective-permute-done.25.refs_1_ = f32[336,128]{1,0:T(8,128)S(1)} collective-permute-done((f32[336,128]{1,0:T(8,128)S(1)}, f32[336,128]{1,0:T(8,128)S(1)}, u32[]{:S(2)}, u32[]{:S(2)}) %collective-permute-start.25) | collective-permute-done | bytes 172064 | tf_op jit(solution)/shard_map/ppermute | solution.py:673
  92.3 1.0 %collective-permute-start.27 = (f32[4,336,128]{2,1,0:T(8,128)S(1)}, f32[4,336,128]{2,1,0:T(8,128)S(1)}, u32[]{:S(2)}, u32[]{:S(2)}) collective-permute-start(f32[4,336,128]{2,1,0:T(8,128)S(1)} %joined.1.mine), channel_id=1, source_target_pairs={{0,4},{4,0},{8,12},{12,8},{16,20},{20,16},{24,28},{28,24},{1,5},{5... | collective-permute-start | bytes 2064392 | tf_op jit(solution)/shard_map/ppermute | solution.py:666
  93.3 1.8 %collective-permute-done.27.other = f32[4,336,128]{2,1,0:T(8,128)S(1)} collective-permute-done((f32[4,336,128]{2,1,0:T(8,128)S(1)}, f32[4,336,128]{2,1,0:T(8,128)S(1)}, u32[]{:S(2)}, u32[]{:S(2)}) %collective-permute-start.27) | collective-permute-done | bytes 688160 | tf_op jit(solution)/shard_map/ppermute | solution.py:666
  95.1 1.2 %weight_grads.1 = (f32[2,768,128]{2,1,0:T(8,128)}, f32[2,96,768]{2,1,0:T(8,128)}) custom-call(s32[1]{0:T(128)} %bitcast.place, f32[4,336,128]{2,1,0:T(8,128)S(1)} %joined.1.mine, f32[4,336,128]{2,1,0:T(8,128)S(1)} %collective-permute-done.27.other), custom_call_target="tpu_custom_call" | custom-call | flops 268435456 | bytes 4194304 | tf_op jit(solution)/shard_map/weight_grads/pallas_call | solution.py:698
  (28 shorter events, 2.0 us)
Async XLA Ops:
  1.4 6.6 %collective-permute-start.1 = (f32[8,768]{1,0:T(8,128)S(1)}, f32[8,768]{1,0:T(8,128)S(1)}, u32[]{:S(2)}, u32[]{:S(2)}) collective-permute-start(f32[8,768]{1,0:T(8,128)S(1)} %get-tuple-element.131), channel_id=1, source_target_pairs={{4,8},{12,16},{20,24},{8,4},{16,12},{24,20},{5,9},{13,17},{21,25},... | collective-permute-start | bytes 73736 | tf_op jit(solution)/shard_map/ppermute | solution.py:661
  2.1 5.9 %collective-permute-start = (f32[8,768]{1,0:T(8,128)S(1)}, f32[8,768]{1,0:T(8,128)S(1)}, u32[]{:S(2)}, u32[]{:S(2)}) collective-permute-start(f32[8,768]{1,0:T(8,128)S(1)} %get-tuple-element.132), channel_id=1, source_target_pairs={{0,4},{4,0},{8,12},{12,8},{16,20},{20,16},{24,28},{28,24},{1,5},{5... | collective-permute-start | bytes 73736 | tf_op jit(solution)/shard_map/ppermute | solution.py:666
  8.8 9.3 %collective-permute-start.7 = (f32[128,128]{1,0:T(8,128)S(1)}, f32[128,128]{1,0:T(8,128)S(1)}, u32[]{:S(2)}, u32[]{:S(2)}) collective-permute-start(f32[128,128]{1,0:T(8,128)S(1)} %get-tuple-element.79.refs_0_), channel_id=1, source_target_pairs={{0,3},{1,2},{2,1},{3,0},{4,7},{5,6},{6,5},{7,4},{8,11},{9,10},{10,... | collective-permute-start | bytes 196616 | tf_op jit(solution)/shard_map/ppermute | solution.py:666
  12.5 6.8 %collective-permute-start.6 = (f32[128,128]{1,0:T(8,128)S(1)}, f32[128,128]{1,0:T(8,128)S(1)}, u32[]{:S(2)}, u32[]{:S(2)}) collective-permute-start(f32[128,128]{1,0:T(8,128)S(1)} %get-tuple-element.79.refs_0_), channel_id=1, source_target_pairs={{0,2},{1,3},{2,0},{3,1},{4,6},{5,7},{6,4},{7,5},{8,10},{9,11},{10,... | collective-permute-start | bytes 196616 | tf_op jit(solution)/shard_map/ppermute | solution.py:666
  12.5 6.8 %collective-permute-start.5 = (f32[128,128]{1,0:T(8,128)S(1)}, f32[128,128]{1,0:T(8,128)S(1)}, u32[]{:S(2)}, u32[]{:S(2)}) collective-permute-start(f32[128,128]{1,0:T(8,128)S(1)} %get-tuple-element.79.refs_0_), channel_id=1, source_target_pairs={{0,1},{1,0},{2,3},{3,2},{4,5},{5,4},{6,7},{7,6},{8,9},{9,8},{10,11... | collective-permute-start | bytes 196616 | tf_op jit(solution)/shard_map/ppermute | solution.py:666
  14.5 9.5 %collective-permute-start.4 = (f32[128,128]{1,0:T(8,128)S(1)}, f32[128,128]{1,0:T(8,128)S(1)}, u32[]{:S(2)}, u32[]{:S(2)}) collective-permute-start(f32[128,128]{1,0:T(8,128)S(1)} %get-tuple-element.75.refs_0_), channel_id=1, source_target_pairs={{0,3},{1,2},{2,1},{3,0},{4,7},{5,6},{6,5},{7,4},{8,11},{9,10},{10,... | collective-permute-start | bytes 196616 | tf_op jit(solution)/shard_map/ppermute | solution.py:666
  18.2 5.9 %collective-permute-start.3 = (f32[128,128]{1,0:T(8,128)S(1)}, f32[128,128]{1,0:T(8,128)S(1)}, u32[]{:S(2)}, u32[]{:S(2)}) collective-permute-start(f32[128,128]{1,0:T(8,128)S(1)} %get-tuple-element.75.refs_0_), channel_id=1, source_target_pairs={{0,2},{1,3},{2,0},{3,1},{4,6},{5,7},{6,4},{7,5},{8,10},{9,11},{10,... | collective-permute-start | bytes 196616 | tf_op jit(solution)/shard_map/ppermute | solution.py:666
  18.2 5.9 %collective-permute-start.2 = (f32[128,128]{1,0:T(8,128)S(1)}, f32[128,128]{1,0:T(8,128)S(1)}, u32[]{:S(2)}, u32[]{:S(2)}) collective-permute-start(f32[128,128]{1,0:T(8,128)S(1)} %get-tuple-element.75.refs_0_), channel_id=1, source_target_pairs={{0,1},{1,0},{2,3},{3,2},{4,5},{5,4},{6,7},{7,6},{8,9},{9,8},{10,11... | collective-permute-start | bytes 196616 | tf_op jit(solution)/shard_map/ppermute | solution.py:666
  29.0 1.6 %collective-permute-start.8 = (f32[2,6,40,128]{3,2,1,0:T(8,128)S(1)}, f32[2,6,40,128]{3,2,1,0:T(8,128)S(1)}, u32[]{:S(2)}, u32[]{:S(2)}) collective-permute-start(f32[2,6,40,128]{3,2,1,0:T(8,128)S(1)} %get-tuple-element.83.mine), channel_id=1, source_target_pairs={{0,4},{4,0},{8,12},{12,8},{16,20},{20,16},{24,28},{28,24},{1,5},{5... | collective-permute-start | bytes 737288 | tf_op jit(solution)/shard_map/ppermute | solution.py:666
  30.7 5.1 %collective-permute-start.9 = (f32[208,128]{1,0:T(8,128)S(1)}, f32[208,128]{1,0:T(8,128)S(1)}, u32[]{:S(2)}, u32[]{:S(2)}) collective-permute-start(f32[208,128]{1,0:T(8,128)S(1)} %get-tuple-element.85), channel_id=1, source_target_pairs={{0,8},{4,20},{8,0},{12,28},{16,24},{20,4},{24,16},{28,12},{1,9},{5... | collective-permute-start | bytes 319496 | tf_op jit(solution)/shard_map/ppermute | solution.py:673
  32.8 5.5 %collective-permute-start.10 = (f32[208,128]{1,0:T(8,128)S(1)}, f32[208,128]{1,0:T(8,128)S(1)}, u32[]{:S(2)}, u32[]{:S(2)}) collective-permute-start(f32[208,128]{1,0:T(8,128)S(1)} %get-tuple-element.86), channel_id=1, source_target_pairs={{0,16},{4,28},{8,24},{12,20},{16,0},{20,12},{24,8},{28,4},{1,17},{... | collective-permute-start | bytes 319496 | tf_op jit(solution)/shard_map/ppermute | solution.py:673
  34.6 6.4 %collective-permute-start.11 = (f32[208,128]{1,0:T(8,128)S(1)}, f32[208,128]{1,0:T(8,128)S(1)}, u32[]{:S(2)}, u32[]{:S(2)}) collective-permute-start(f32[208,128]{1,0:T(8,128)S(1)} %get-tuple-element.87), channel_id=1, source_target_pairs={{0,24},{4,12},{8,16},{12,4},{16,8},{20,28},{24,0},{28,20},{1,25},{... | collective-permute-start | bytes 319496 | tf_op jit(solution)/shard_map/ppermute | solution.py:673
  47.0 10.2 %collective-permute-start.14 = (f32[128,128]{1,0:T(8,128)S(1)}, f32[128,128]{1,0:T(8,128)S(1)}, u32[]{:S(2)}, u32[]{:S(2)}) collective-permute-start(f32[128,128]{1,0:T(8,128)S(1)} %get-tuple-element.105.refs_0_), channel_id=1, source_target_pairs={{0,3},{1,2},{2,1},{3,0},{4,7},{5,6},{6,5},{7,4},{8,11},{9,10},{10,... | collective-permute-start | bytes 196616 | tf_op jit(solution)/shard_map/ppermute | solution.py:666
  50.0 7.2 %collective-permute-start.13 = (f32[128,128]{1,0:T(8,128)S(1)}, f32[128,128]{1,0:T(8,128)S(1)}, u32[]{:S(2)}, u32[]{:S(2)}) collective-permute-start(f32[128,128]{1,0:T(8,128)S(1)} %get-tuple-element.105.refs_0_), channel_id=1, source_target_pairs={{0,2},{1,3},{2,0},{3,1},{4,6},{5,7},{6,4},{7,5},{8,10},{9,11},{10,... | collective-permute-start | bytes 196616 | tf_op jit(solution)/shard_map/ppermute | solution.py:666
  50.0 7.2 %collective-permute-start.12 = (f32[128,128]{1,0:T(8,128)S(1)}, f32[128,128]{1,0:T(8,128)S(1)}, u32[]{:S(2)}, u32[]{:S(2)}) collective-permute-start(f32[128,128]{1,0:T(8,128)S(1)} %get-tuple-element.105.refs_0_), channel_id=1, source_target_pairs={{0,1},{1,0},{2,3},{3,2},{4,5},{5,4},{6,7},{7,6},{8,9},{9,8},{10,11... | collective-permute-start | bytes 196616 | tf_op jit(solution)/shard_map/ppermute | solution.py:666
  57.2 4.7 %collective-permute-start.15 = (f32[128,128]{1,0:T(8,128)S(1)}, f32[128,128]{1,0:T(8,128)S(1)}, u32[]{:S(2)}, u32[]{:S(2)}) collective-permute-start(f32[128,128]{1,0:T(8,128)S(1)} %get-tuple-element.106.own), channel_id=1, source_target_pairs={{0,1},{1,0},{2,3},{3,2},{4,5},{5,4},{6,7},{7,6},{8,9},{9,8},{10,11... | collective-permute-start | bytes 196616 | tf_op jit(solution)/shard_map/ppermute | solution.py:666
  57.8 7.1 %collective-permute-start.17 = (f32[128,128]{1,0:T(8,128)S(1)}, f32[128,128]{1,0:T(8,128)S(1)}, u32[]{:S(2)}, u32[]{:S(2)}) collective-permute-start(f32[128,128]{1,0:T(8,128)S(1)} %get-tuple-element.106.own), channel_id=1, source_target_pairs={{0,3},{1,2},{2,1},{3,0},{4,7},{5,6},{6,5},{7,4},{8,11},{9,10},{10,... | collective-permute-start | bytes 196616 | tf_op jit(solution)/shard_map/ppermute | solution.py:666
  60.3 5.9 %collective-permute-start.16 = (f32[128,128]{1,0:T(8,128)S(1)}, f32[128,128]{1,0:T(8,128)S(1)}, u32[]{:S(2)}, u32[]{:S(2)}) collective-permute-start(f32[128,128]{1,0:T(8,128)S(1)} %get-tuple-element.106.own), channel_id=1, source_target_pairs={{0,2},{1,3},{2,0},{3,1},{4,6},{5,7},{6,4},{7,5},{8,10},{9,11},{10,... | collective-permute-start | bytes 196616 | tf_op jit(solution)/shard_map/ppermute | solution.py:666
  67.2 2.2 %collective-permute-start.20 = (f32[1344,128]{1,0:T(8,128)S(1)}, f32[1344,128]{1,0:T(8,128)S(1)}, u32[]{:S(2)}, u32[]{:S(2)}) collective-permute-start(f32[1344,128]{1,0:T(8,128)S(1)} %get-tuple-element.123), channel_id=1, source_target_pairs={{0,4},{4,0},{8,12},{12,8},{16,20},{20,16},{24,28},{28,24},{1,5},{5... | collective-permute-start | bytes 2064392 | tf_op jit(solution)/shard_map/ppermute | solution.py:666
  69.5 7.1 %collective-permute-start.21 = (f32[336,128]{1,0:T(8,128)S(1)}, f32[336,128]{1,0:T(8,128)S(1)}, u32[]{:S(2)}, u32[]{:S(2)}) collective-permute-start(f32[336,128]{1,0:T(8,128)S(1)} %get-tuple-element.125), channel_id=1, source_target_pairs={{0,8},{4,20},{8,0},{12,28},{16,24},{20,4},{24,16},{28,12},{1,9},{5... | collective-permute-start | bytes 516104 | tf_op jit(solution)/shard_map/ppermute | solution.py:673
  70.4 8.6 %collective-permute-start.22 = (f32[336,128]{1,0:T(8,128)S(1)}, f32[336,128]{1,0:T(8,128)S(1)}, u32[]{:S(2)}, u32[]{:S(2)}) collective-permute-start(f32[336,128]{1,0:T(8,128)S(1)} %get-tuple-element.126), channel_id=1, source_target_pairs={{0,16},{4,28},{8,24},{12,20},{16,0},{20,12},{24,8},{28,4},{1,17},{... | collective-permute-start | bytes 516104 | tf_op jit(solution)/shard_map/ppermute | solution.py:673
  71.2 9.1 %collective-permute-start.23 = (f32[336,128]{1,0:T(8,128)S(1)}, f32[336,128]{1,0:T(8,128)S(1)}, u32[]{:S(2)}, u32[]{:S(2)}) collective-permute-start(f32[336,128]{1,0:T(8,128)S(1)} %get-tuple-element.127), channel_id=1, source_target_pairs={{0,24},{4,12},{8,16},{12,4},{16,8},{20,28},{24,0},{28,20},{1,25},{... | collective-permute-start | bytes 516104 | tf_op jit(solution)/shard_map/ppermute | solution.py:673
  80.4 8.4 %collective-permute-start.26 = (f32[336,128]{1,0:T(8,128)S(1)}, f32[336,128]{1,0:T(8,128)S(1)}, u32[]{:S(2)}, u32[]{:S(2)}) collective-permute-start(f32[336,128]{1,0:T(8,128)S(1)} %share_sum.1.after_this.mine), channel_id=1, source_target_pairs={{0,24},{4,12},{8,16},{12,4},{16,8},{20,28},{24,0},{28,20},{1,25},{... | collective-permute-start | bytes 516104 | tf_op jit(solution)/shard_map/ppermute | solution.py:673
  82.1 10.2 %collective-permute-start.25 = (f32[336,128]{1,0:T(8,128)S(1)}, f32[336,128]{1,0:T(8,128)S(1)}, u32[]{:S(2)}, u32[]{:S(2)}) collective-permute-start(f32[336,128]{1,0:T(8,128)S(1)} %share_sum.1.after_this.mine), channel_id=1, source_target_pairs={{0,16},{4,28},{8,24},{12,20},{16,0},{20,12},{24,8},{28,4},{1,17},{... | collective-permute-start | bytes 516104 | tf_op jit(solution)/shard_map/ppermute | solution.py:673
  82.9 9.3 %collective-permute-start.24 = (f32[336,128]{1,0:T(8,128)S(1)}, f32[336,128]{1,0:T(8,128)S(1)}, u32[]{:S(2)}, u32[]{:S(2)}) collective-permute-start(f32[336,128]{1,0:T(8,128)S(1)} %share_sum.1.after_this.mine), channel_id=1, source_target_pairs={{0,8},{4,20},{8,0},{12,28},{16,24},{20,4},{24,16},{28,12},{1,9},{5... | collective-permute-start | bytes 516104 | tf_op jit(solution)/shard_map/ppermute | solution.py:673
  83.9 1.2 %collective-permute-start.18 = (f32[8,768]{1,0:T(8,128)S(1)}, f32[8,768]{1,0:T(8,128)S(1)}, u32[]{:S(2)}, u32[]{:S(2)}) collective-permute-start(f32[8,768]{1,0:T(8,128)S(1)} %get-tuple-element.119), channel_id=1, source_target_pairs={{0,4},{4,0},{8,12},{12,8},{16,20},{20,16},{24,28},{28,24},{1,5},{5... | collective-permute-start | bytes 73736 | tf_op jit(solution)/shard_map/ppermute | solution.py:666
  84.0 1.2 %collective-permute-start.19 = (f32[8,768]{1,0:T(8,128)S(1)}, f32[8,768]{1,0:T(8,128)S(1)}, u32[]{:S(2)}, u32[]{:S(2)}) collective-permute-start(f32[8,768]{1,0:T(8,128)S(1)} %get-tuple-element.120), channel_id=1, source_target_pairs={{4,8},{12,16},{20,24},{8,4},{16,12},{24,20},{5,9},{13,17},{21,25},... | collective-permute-start | bytes 73736 | tf_op jit(solution)/shard_map/ppermute | solution.py:661
  92.3 2.7 %collective-permute-start.27 = (f32[4,336,128]{2,1,0:T(8,128)S(1)}, f32[4,336,128]{2,1,0:T(8,128)S(1)}, u32[]{:S(2)}, u32[]{:S(2)}) collective-permute-start(f32[4,336,128]{2,1,0:T(8,128)S(1)} %joined.1.mine), channel_id=1, source_target_pairs={{0,4},{4,0},{8,12},{12,8},{16,20},{20,16},{24,28},{28,24},{1,5},{5... | collective-permute-start | bytes 2064392 | tf_op jit(solution)/shard_map/ppermute | solution.py:666

commit v7 on v6

--- a/solution.py
+++ b/solution.py
@@ -215,28 +215,20 @@
 def local_kernel(side, *refs):
     own, first, second, third, act, grad_gated, spreader = refs[:7]
     earlier, refs = refs[7 : 7 + 2 * side], refs[7 + 2 * side :]
-    step_weight_in, step_bias_in, decay_log_in, skip_gain_in, *refs = refs
+    step_weight, decay_log, step_bias, skip_gain, *refs = refs
     projection, step, step_pre, entering, decays, bases, rates, skip_rows, *refs = refs
-    carry, row_rates, step_weight, step_bias, decay_log, skip_gain, rate_rows, sems = refs
+    carry, row_rates, rate_rows = refs
     tiles, length, _ = act.shape
-    states = decay_log.shape[0]
-    ranks = step_weight.shape[0]
+    states = decay_log.shape[1]
+    ranks = step_weight.shape[1]
     count = length // CHAINS
     group = tile_group(tiles)
-    loads = copies_of(
-        [
-            (step_weight_in.at[side], step_weight), (decay_log_in.at[side], decay_log),
-            (step_bias_in, step_bias), (skip_gain_in, skip_gain),
-        ],
-        sems,
-    )
     projection[...] = (own[...] + first[...]) + (second[...] + third[...])
     fill_bases(projection, spreader, bases)
-    finish_all(loads)
-    fill_rates(decay_log, rates)
+    fill_rates(decay_log.at[side], rates)
     for t in range(tiles):
         skip_rows[t] = skip_gain[side : side + 1, lane_tile(t)]
-    wide = dot(projection[:, :ranks], step_weight[...], (1, 0)) + step_bias[side : side + 1]
+    wide = dot(projection[:, :ranks], step_weight[side], (1, 0)) + step_bias[side : side + 1]
     for t in range(tiles):
         part = wide[:, lane_tile(t)]
         step_pre[t] = part
@@ -380,15 +372,14 @@
     incoming, bases, act, step, step_pre, grad_gated, entering, decays, spreader, *refs = refs
     rates, skip_rows, *refs = refs
     earlier, refs = refs[:side], refs[side:]
-    step_weight_in, *refs = refs
+    step_weight, *refs = refs
     partial, grad_act, grad_pre, summed_out, *refs = refs
-    step_weight, rate_rows, history, grad_in, grad_out, weights, sems = refs
+    rate_rows, history, grad_in, grad_out, weights = refs
     tiles, length, _ = act.shape
     states = rates.shape[1]
-    ranks = step_weight.shape[0]
+    ranks = step_weight.shape[1]
     count = length // CHAINS
     group = tile_group(tiles)
-    loads = copies_of([(step_weight_in.at[side], step_weight)], sems)
     grad_in[...] = jnp.zeros_like(grad_in)
     grad_out[...] = jnp.zeros_like(grad_out)
     up = side == 0
@@ -492,8 +483,7 @@
     lax.fori_loop(0, tiles // group, some_tiles, 0)
     wide = full_width(grad_pre)
     weights[...] = jnp.zeros_like(weights)
-    finish_all(loads)
-    weights[:ranks] = step_weight[...]
+    weights[:ranks] = step_weight[side]
     sums = jnp.zeros((length, LANES), jnp.float32)
     step_lanes = 4 * LANES
     for k, values in enumerate((grad_in, grad_out)):
@@ -626,23 +616,16 @@
 
 
 def exit_kernel(
-    place, near, far, first, second, conv_weight_in, after_this, tokens_grad, up, down, conv_weight, sems
+    place, near, far, first, second, conv_weight, after_this, tokens_grad, up, down
 ):
     length, width = first.shape
     taps = conv_weight.shape[1]
     margin = taps - 1
-    loads = copies_of(
-        [
-            (conv_weight_in, conv_weight),
-        ],
-        sems,
-    )
     core = lax.rem(place[0], 2)
     up[:length] = first[...]
     up[length:] = jnp.where(core == 0, near[...], far[...])
     down[:HALO] = jnp.where(core == 0, far[...], near[...])
     down[HALO:] = second[...]
-    finish_all(loads)
     for t in range(width // LANES):
         lanes = lane_tile(t)
         total = jnp.zeros((length, LANES), jnp.float32)
@@ -754,21 +737,24 @@
     core = (place & 1)[:, None] == 0
     head, tail = tokens[:HALO], tokens[length - HALO :]
     edges = swapped_edges(jnp.where(core, tail, head), jnp.where(core, head, tail), "ctx")
-    fetched = (tokens, conv_weight, conv_bias, select_weight, gate_input, cotangent)
-    held, conv_weight_held, conv_bias_held, select, gate, cot = call(
-        fetch_kernel, "fetch", tuple(a.shape for a in fetched), [dma(6)], 4, fetched,
-        "hhhhhh", "mmmmmm",
+    fetched = (
+        tokens, select_weight, conv_weight, conv_bias, gate_input, cotangent, step_weight,
+        decay_log, step_bias, skip_gain,
+    )
+    held, select, taps, taps_bias, gate, cot, *step_held = call(
+        fetch_kernel, "fetch", tuple(a.shape for a in fetched), [dma(len(fetched))], 4, fetched,
+        "h" * len(fetched), "m" * len(fetched),
     )
     first_partial, first_act, first_pre, extended = call(
         entry_kernel, "entry", (narrow, one, one, (length + 2 * HALO, width)), [vmem(narrow)],
-        6, (place, *edges, held, conv_weight_held, conv_bias_held, select), "svvmmmm", "vmmm",
+        6, (place, *edges, held, taps, taps_bias, select), "svvmmmm", "vmmm",
     )
     first_terms = terms_of(first_partial)
     partial, act, pre, grad_gated, spreader = call(
         second_entry_kernel, "second_entry",
         (narrow, one, one, one, (LANES, 2 * states * LANES)),
         [vmem(narrow)],
-        6, (extended, conv_weight_held, conv_bias_held, select, gate, cot), "mmmmmm", "vmmmb",
+        6, (extended, taps, taps_bias, select, gate, cot), "mmmmmm", "vmmmb",
     )
     projection_terms = (first_terms, terms_of(partial))
     acts, pres = (first_act, act), (first_pre, pre)
@@ -781,16 +767,12 @@
                 (2, length, states * LANES), (tiles, states, LANES), (tiles, 1, LANES),
                 carry, row_rates,
             ),
-            [
-                vmem(step_weight.shape[1:]), vmem(step_bias.shape), vmem(decay_log.shape[1:]),
-                vmem(skip_gain.shape), row_scratch, dma(4),
-            ],
+            [row_scratch],
             10,
             (
-                *projection_terms[side], acts[side], grad_gated, spreader, *earlier, step_weight,
-                step_bias, decay_log, skip_gain,
+                *projection_terms[side], acts[side], grad_gated, spreader, *earlier, *step_held,
             ),
-            "vvvvmmm" + "v" * len(earlier) + "hhhh", "mmmmmmmmvv", 2**32,
+            "vvvvmmm" + "v" * len(earlier) + "mmmm", "mmmmmmmmvv", 2**32,
         )
         earlier = (carried, every_rate)
         locals_.append(found)
@@ -818,15 +800,14 @@
             functools.partial(scan_kernel, side), ("first_scan", "second_scan")[side],
             (narrow, one, one, one),
             [
-                vmem(step_weight.shape[1:]), row_scratch, grouped, bases, bases,
-                vmem((LANES, width)), dma(1),
+                row_scratch, grouped, bases, bases, vmem((LANES, width)),
             ],
             10,
             (
                 incoming, spread_bases, acts[side], step, step_pre, grad_gated, entering, decays,
-                spreader, rates, skip_rows, *earlier, step_weight,
+                spreader, rates, skip_rows, *earlier, step_held[0],
             ),
-            "vmmmmmmmmmm" + "m" * side + "h", "vmmm", 2**33,
+            "vmmmmmmmmmm" + "m" * side + "m", "vmmm", 2**33,
         )
         if side == 1:
             first_total, partial_grad = call(
@@ -877,10 +858,9 @@
     (tokens_grad,) = call(
         exit_kernel, "exit", (flat,),
         [
-            vmem((length + HALO, width)), vmem((length + HALO, width)), vmem(conv_weight.shape),
-            dma(1),
+            vmem((length + HALO, width)), vmem((length + HALO, width)),
         ],
-        8, (place, *edges, first_grad, second_grad, conv_weight, ahead), "svvmmhv",
+        6, (place, *edges, first_grad, second_grad, taps, ahead), "svvmmmv",
     )
     if near:
         got = [swapped_chips(mine, k) for k in range(1, chips)]

time: 96.6 us -> 95.2 us (0.986)
  waiting for transfers between devices: 27.3 us -> 29.1 us
  Pallas kernels: 32.3 us -> 30.7 us
  starting transfers between devices: 35.1 us -> 33.6 us
    pallas_call x19, Pallas kernels: 32.3 us -> 30.7 us  [call(): pl.pallas_call(kernel, in_specs=[spaces[k] for k in kinds], out_specs=[sp...]
    ppermute x17, waiting for transfers between devices: 8.74 us -> 9.87 us  [swapped(): return lax.ppermute(value, axis, [(i, i ^ by) for i in range(count)])]
  transfers between devices with their start and end apart: 28 -> 28, of which waited for: 15 -> 16; matrix products, arithmetic and copies ran while one was open for 0% -> 0% of each run, Pallas kernels for 19% -> 18%
where the time goes in v7:
time: 95.2 us; the launch traced here: 94.9 us
  starting transfers between devices  33.6 us (35%)
  Pallas kernels  30.7 us (32%)
  waiting for transfers between devices  29.1 us (31%)
    pallas_call x19, Pallas kernels, call(): pl.pallas_call(kernel, in_specs=[spaces[k] for k in kinds], out_specs=[sp...  30.7 us
    ppermute x17, starting transfers between devices, swapped(): return lax.ppermute(value, axis, [(i, i ^ by) for i in range(count)])  21.5 us
    ppermute x9, waiting for transfers between devices, swapped_chips(): return lax.ppermute(value, 'ctx', pairs)  19.2 us
    ppermute x9, starting transfers between devices, swapped_chips(): return lax.ppermute(value, 'ctx', pairs)  10.7 us
    ppermute x17, waiting for transfers between devices, swapped(): return lax.ppermute(value, axis, [(i, i ^ by) for i in range(count)])  9.87 us
  transfers between devices with their start and end apart: 28, of which 16 were waited for; matrix products, arithmetic and copies ran while one was open for 0% of the time, Pallas kernels for 18%

profile of v7, /device:TPU:0, one launch (start us, length us, event | category | flops | bytes accessed | tf_op | source)
XLA Modules:
  0.0 94.9 jit_solution(2740416642960867870)
XLA Ops:
  0.6 0.8 slice_select_fusion
  1.4 0.7 collective-permute-start.1
  2.1 4.4 %collective-permute-start = (f32[8,768]{1,0:T(8,128)S(1)}, f32[8,768]{1,0:T(8,128)S(1)}, u32[]{:S(2)}, u32[]{:S(2)}) collective-permute-start(f32[8,768]{1,0:T(8,128)S(1)} %get-tuple-element.140), channel_id=1, source_target_pairs={{0,4},{4,0},{8,12},{12,8},{16,20},{20,16},{24,28},{28,24},{1,5},{5... | collective-permute-start | bytes 73736 | tf_op jit(solution)/shard_map/ppermute | solution.py:649
  6.4 1.8 %fetch.1 = (f32[128,768]{1,0:T(8,128)S(1)}, f32[2,768,128]{2,1,0:T(8,128)S(1)}, f32[2,4,768]{2,1,0:T(4,128)S(1)}, f32[2,768]{1,0:T(2,128)S(1)}, f32[128,768]{1,0...) custom-call(f32[128,768]{1,0:T(8,128)} %refs_0_.1, ...), custom_call_target="tpu_custom_call" | custom-call | flops 268435456 | bytes 4194304 | tf_op jit(solution)/shard_map/fetch/pallas_call | solution.py:681
  8.2 0.8 entry.1
  9.1 3.7 %collective-permute-start.7 = (f32[128,128]{1,0:T(8,128)S(1)}, f32[128,128]{1,0:T(8,128)S(1)}, u32[]{:S(2)}, u32[]{:S(2)}) collective-permute-start(f32[128,128]{1,0:T(8,128)S(1)} %get-tuple-element.83.refs_0_), channel_id=1, source_target_pairs={{0,3},{1,2},{2,1},{3,0},{4,7},{5,6},{6,5},{7,4},{8,11},{9,10},{10,... | collective-permute-start | bytes 196616 | tf_op jit(solution)/shard_map/ppermute | solution.py:649
  12.8 0.8 collective-permute-start.5
  13.5 1.2 %second_entry.1 = (f32[128,128]{1,0:T(8,128)S(1)}, f32[6,128,128]{2,1,0:T(8,128)S(1)}, f32[6,128,128]{2,1,0:T(8,128)S(1)}, f32[6,128,128]{2,1,0:T(8,128)S(1)}, bf16[128,4096]{1,0:T(8,128)(2,1)S(1)}) custom-call(f32[144,768]{1,0:T(8,128)S(1)} %get-tuple-element.76.ext, f32[2,4,768]{2,1,0:T(4,128)S(1)} %get-tuple-element.73.conv_weight, ...), custom_call_target="tpu_custom_call" | custom-call | flops 268435456 | bytes 4194304 | tf_op jit(solution)/shard_map/second_entry/pallas_call | solution.py:681
  14.8 3.7 %collective-permute-start.4 = (f32[128,128]{1,0:T(8,128)S(1)}, f32[128,128]{1,0:T(8,128)S(1)}, u32[]{:S(2)}, u32[]{:S(2)}) collective-permute-start(f32[128,128]{1,0:T(8,128)S(1)} %get-tuple-element.79.refs_0_), channel_id=1, source_target_pairs={{0,3},{1,2},{2,1},{3,0},{4,7},{5,6},{6,5},{7,4},{8,11},{9,10},{10,... | collective-permute-start | bytes 196616 | tf_op jit(solution)/shard_map/ppermute | solution.py:649
  18.4 0.8 collective-permute-start.2
  19.6 3.8 %first_local.1 = (f32[128,128]{1,0:T(8,128)S(1)}, f32[6,128,128]{2,1,0:T(8,128)S(1)}, f32[6,128,128]{2,1,0:T(8,128)S(1)}, f32[2,6,16,8,128]{4,3,2,1,0:T(8,128)S(...) custom-call(f32[128,128]{1,0:T(8,128)S(1)} %get-tuple-element.83.ref, ...), custom_call_target="tpu_custom_call" | custom-call | flops 4294967296 | bytes 67108864 | tf_op jit(solution)/shard_map/first_local/pallas_call | solution.py:681
  23.4 0.8 collective-permute-done.3.refs_2_
  24.2 3.8 %second_local.1 = (f32[128,128]{1,0:T(8,128)S(1)}, f32[6,128,128]{2,1,0:T(8,128)S(1)}, f32[6,128,128]{2,1,0:T(8,128)S(1)}, f32[2,6,16,8,128]{4,3,2,1,0:T(8,128)S...) custom-call(f32[128,128]{1,0:T(8,128)S(1)} %get-tuple-element.79.ref, ...), custom_call_target="tpu_custom_call" | custom-call | flops 4294967296 | bytes 67108864 | tf_op jit(solution)/shard_map/second_local/pallas_call | solution.py:681
  28.0 1.5 %collective-permute-done.8.other = f32[2,6,40,128]{3,2,1,0:T(8,128)S(1)} collective-permute-done((f32[2,6,40,128]{3,2,1,0:T(8,128)S(1)}, f32[2,6,40,128]{3,2,1,0:T(8,128)S(1)}, u32[]{:S(2)}, u32[]{:S(2)}) %collective-permute-start.8) | collective-permute-done | bytes 245792 | tf_op jit(solution)/shard_map/ppermute | solution.py:649
  29.7 2.1 %collective-permute-start.9 = (f32[208,128]{1,0:T(8,128)S(1)}, f32[208,128]{1,0:T(8,128)S(1)}, u32[]{:S(2)}, u32[]{:S(2)}) collective-permute-start(f32[208,128]{1,0:T(8,128)S(1)} %get-tuple-element.93), channel_id=1, source_target_pairs={{0,8},{4,20},{8,0},{12,28},{16,24},{20,4},{24,16},{28,12},{1,9},{5... | collective-permute-start | bytes 319496 | tf_op jit(solution)/shard_map/ppermute | solution.py:656
  31.7 1.5 %collective-permute-start.10 = (f32[208,128]{1,0:T(8,128)S(1)}, f32[208,128]{1,0:T(8,128)S(1)}, u32[]{:S(2)}, u32[]{:S(2)}) collective-permute-start(f32[208,128]{1,0:T(8,128)S(1)} %get-tuple-element.94), channel_id=1, source_target_pairs={{0,16},{4,28},{8,24},{12,20},{16,0},{20,12},{24,8},{28,4},{1,17},{... | collective-permute-start | bytes 319496 | tf_op jit(solution)/shard_map/ppermute | solution.py:656
  33.3 1.7 %collective-permute-done.9.refs_0_ = f32[208,128]{1,0:T(8,128)S(1)} collective-permute-done((f32[208,128]{1,0:T(8,128)S(1)}, f32[208,128]{1,0:T(8,128)S(1)}, u32[]{:S(2)}, u32[]{:S(2)}) %collective-permute-start.9) | collective-permute-done | bytes 106528 | tf_op jit(solution)/shard_map/ppermute | solution.py:656
  34.9 2.3 %collective-permute-done.10.refs_1_ = f32[208,128]{1,0:T(8,128)S(1)} collective-permute-done((f32[208,128]{1,0:T(8,128)S(1)}, f32[208,128]{1,0:T(8,128)S(1)}, u32[]{:S(2)}, u32[]{:S(2)}) %collective-permute-start.10) | collective-permute-done | bytes 106528 | tf_op jit(solution)/shard_map/ppermute | solution.py:656
  37.3 1.7 %collective-permute-done.11.refs_2_ = f32[208,128]{1,0:T(8,128)S(1)} collective-permute-done((f32[208,128]{1,0:T(8,128)S(1)}, f32[208,128]{1,0:T(8,128)S(1)}, u32[]{:S(2)}, u32[]{:S(2)}) %collective-permute-start.11) | collective-permute-done | bytes 106528 | tf_op jit(solution)/shard_map/ppermute | solution.py:656
  39.2 6.2 %first_scan.1 = (f32[128,128]{1,0:T(8,128)S(1)}, f32[6,128,128]{2,1,0:T(8,128)S(1)}, f32[6,128,128]{2,1,0:T(8,128)S(1)}, f32[6,128,128]{2,1,0:T(8,128)S(1)}) custom-call(f32[2,6,32,128]{3,2,1,0:T(8,128)S(1)} %chain.1.refs_0_, f32[2,128,2048]{2,1,0:T(8,128)S(1)} %get-tuple-element.103.refs_1_, f32[6,128,128]{2,1,0:T(8,128)S(1)} %get-tuple-element.84.refs_4_.refs_2_.act, ...), custom_call_target="tpu_custom_call" | custom-call | flops 8589934592 | bytes 134217728 | tf_op jit(solution)/shard_map/first_scan/pallas_call | solution.py:681
  45.4 3.0 %collective-permute-start.14 = (f32[128,128]{1,0:T(8,128)S(1)}, f32[128,128]{1,0:T(8,128)S(1)}, u32[]{:S(2)}, u32[]{:S(2)}) collective-permute-start(f32[128,128]{1,0:T(8,128)S(1)} %get-tuple-element.113.refs_0_), channel_id=1, source_target_pairs={{0,3},{1,2},{2,1},{3,0},{4,7},{5,6},{6,5},{7,4},{8,11},{9,10},{10,... | collective-permute-start | bytes 196616 | tf_op jit(solution)/shard_map/ppermute | solution.py:649
  48.4 1.5 %collective-permute-start.12 = (f32[128,128]{1,0:T(8,128)S(1)}, f32[128,128]{1,0:T(8,128)S(1)}, u32[]{:S(2)}, u32[]{:S(2)}) collective-permute-start(f32[128,128]{1,0:T(8,128)S(1)} %get-tuple-element.113.refs_0_), channel_id=1, source_target_pairs={{0,1},{1,0},{2,3},{3,2},{4,5},{5,4},{6,7},{7,6},{8,9},{9,8},{10,11... | collective-permute-start | bytes 196616 | tf_op jit(solution)/shard_map/ppermute | solution.py:649
  49.8 6.2 %second_scan.1 = (f32[128,128]{1,0:T(8,128)S(1)}, f32[6,128,128]{2,1,0:T(8,128)S(1)}, f32[6,128,128]{2,1,0:T(8,128)S(1)}, f32[6,128,128]{2,1,0:T(8,128)S(1)}) custom-call(f32[2,6,32,128]{3,2,1,0:T(8,128)S(1)} %chain.1.refs_0_, f32[2,128,2048]{2,1,0:T(8,128)S(1)} %get-tuple-element.96.refs_1_, f32[6,128,128]{2,1,0:T(8,128)S(1)} %get-tuple-element.80.refs_4_.refs_2_.act, ...), custom_call_target="tpu_custom_call" | custom-call | flops 8589934592 | bytes 134217728 | tf_op jit(solution)/shard_map/second_scan/pallas_call | solution.py:681
  56.1 0.6 collective-permute-start.15
  56.7 2.4 %collective-permute-start.17 = (f32[128,128]{1,0:T(8,128)S(1)}, f32[128,128]{1,0:T(8,128)S(1)}, u32[]{:S(2)}, u32[]{:S(2)}) collective-permute-start(f32[128,128]{1,0:T(8,128)S(1)} %get-tuple-element.114.own), channel_id=1, source_target_pairs={{0,3},{1,2},{2,1},{3,0},{4,7},{5,6},{6,5},{7,4},{8,11},{9,10},{10,... | collective-permute-start | bytes 196616 | tf_op jit(solution)/shard_map/ppermute | solution.py:649
  59.6 0.9 collective-permute-done.15.after_this.first
  60.6 1.2 %gate.1 = (f32[128,768]{1,0:T(8,128)}, f32[128,768]{1,0:T(8,128)}) custom-call(f32[6,128,128]{2,1,0:T(8,128)S(1)} %get-tuple-element.111.summed, f32[128,768]{1,0:T(8,128)S(1)} %get-tuple-element.77.gate, f32[128,768]{1,0:T(8,128)S(1)} %get-tuple-element.78.cot, f32[128,128]{1,0:T(8,128)S(1)} %collective-permute-done.15.after_this.first), custom_call_target="tpu_custom_call" | custom-call | tf_op jit(solution)/shard_map/gate/pallas_call | solution.py:681
  61.7 0.9 first_weights.1
  62.7 0.8 step_grad.1.step_part
  63.5 1.5 %collective-permute-done.16.second = f32[128,128]{1,0:T(8,128)S(1)} collective-permute-done((f32[128,128]{1,0:T(8,128)S(1)}, f32[128,128]{1,0:T(8,128)S(1)}, u32[]{:S(2)}, u32[]{:S(2)}) %collective-permute-start.16) | collective-permute-done | bytes 65568 | tf_op jit(solution)/shard_map/ppermute | solution.py:649
  65.0 1.0 %weights.1 = (f32[1344,128]{1,0:T(8,128)S(1)}, f32[1344,128]{1,0:T(8,128)S(1)}, f32[128,768]{1,0:T(8,128)S(1)}, f32[8,768]{1,0:T(8,128)S(1)}, f32[8,768]{1,0:T(8,128)S(1)}) custom-call(s32[1]{0:T(128)} %bitcast.place, f32[128,128]{1,0:T(8,128)S(1)} %get-tuple-element.114.own, f32[128,128]{1,0:T(8,128)S(1)} %collective-permute-done.15.after_this.first, ...), custom_call_target="tpu_custom_call" | custom-call | flops 268435456 | bytes 4194304 | tf_op jit(solution)/shard_map/weights/pallas_call | solution.py:681
  66.1 2.1 %collective-permute-done.20.got = f32[1344,128]{1,0:T(8,128)S(1)} collective-permute-done((f32[1344,128]{1,0:T(8,128)S(1)}, f32[1344,128]{1,0:T(8,128)S(1)}, u32[]{:S(2)}, u32[]{:S(2)}) %collective-permute-start.20) | collective-permute-done | bytes 688160 | tf_op jit(solution)/shard_map/ppermute | solution.py:649
  68.4 1.3 %collective-permute-start.21 = (f32[336,128]{1,0:T(8,128)S(1)}, f32[336,128]{1,0:T(8,128)S(1)}, u32[]{:S(2)}, u32[]{:S(2)}) collective-permute-start(f32[336,128]{1,0:T(8,128)S(1)} %get-tuple-element.133), channel_id=1, source_target_pairs={{0,8},{4,20},{8,0},{12,28},{16,24},{20,4},{24,16},{28,12},{1,9},{5... | collective-permute-start | bytes 516104 | tf_op jit(solution)/shard_map/ppermute | solution.py:656
  69.7 0.8 collective-permute-start.22
  70.5 1.5 %collective-permute-start.23 = (f32[336,128]{1,0:T(8,128)S(1)}, f32[336,128]{1,0:T(8,128)S(1)}, u32[]{:S(2)}, u32[]{:S(2)}) collective-permute-start(f32[336,128]{1,0:T(8,128)S(1)} %get-tuple-element.135), channel_id=1, source_target_pairs={{0,24},{4,12},{8,16},{12,4},{16,8},{20,28},{24,0},{28,20},{1,25},{... | collective-permute-start | bytes 516104 | tf_op jit(solution)/shard_map/ppermute | solution.py:656
  71.9 3.5 %collective-permute-done.21.refs_1_ = f32[336,128]{1,0:T(8,128)S(1)} collective-permute-done((f32[336,128]{1,0:T(8,128)S(1)}, f32[336,128]{1,0:T(8,128)S(1)}, u32[]{:S(2)}, u32[]{:S(2)}) %collective-permute-start.21) | collective-permute-done | bytes 172064 | tf_op jit(solution)/shard_map/ppermute | solution.py:656
  75.4 2.1 %collective-permute-done.22.refs_2_ = f32[336,128]{1,0:T(8,128)S(1)} collective-permute-done((f32[336,128]{1,0:T(8,128)S(1)}, f32[336,128]{1,0:T(8,128)S(1)}, u32[]{:S(2)}, u32[]{:S(2)}) %collective-permute-start.22) | collective-permute-done | bytes 172064 | tf_op jit(solution)/shard_map/ppermute | solution.py:656
  77.5 2.0 %collective-permute-done.23.refs_3_ = f32[336,128]{1,0:T(8,128)S(1)} collective-permute-done((f32[336,128]{1,0:T(8,128)S(1)}, f32[336,128]{1,0:T(8,128)S(1)}, u32[]{:S(2)}, u32[]{:S(2)}) %collective-permute-start.23) | collective-permute-done | bytes 172064 | tf_op jit(solution)/shard_map/ppermute | solution.py:656
  79.6 1.8 %collective-permute-start.26 = (f32[336,128]{1,0:T(8,128)S(1)}, f32[336,128]{1,0:T(8,128)S(1)}, u32[]{:S(2)}, u32[]{:S(2)}) collective-permute-start(f32[336,128]{1,0:T(8,128)S(1)} %share_sum.1.after_this.mine), channel_id=1, source_target_pairs={{0,24},{4,12},{8,16},{12,4},{16,8},{20,28},{24,0},{28,20},{1,25},{... | collective-permute-start | bytes 516104 | tf_op jit(solution)/shard_map/ppermute | solution.py:656
  81.4 0.8 collective-permute-start.25
  82.2 1.0 %collective-permute-start.24 = (f32[336,128]{1,0:T(8,128)S(1)}, f32[336,128]{1,0:T(8,128)S(1)}, u32[]{:S(2)}, u32[]{:S(2)}) collective-permute-start(f32[336,128]{1,0:T(8,128)S(1)} %share_sum.1.after_this.mine), channel_id=1, source_target_pairs={{0,8},{4,20},{8,0},{12,28},{16,24},{20,4},{24,16},{28,12},{1,9},{5... | collective-permute-start | bytes 516104 | tf_op jit(solution)/shard_map/ppermute | solution.py:656
  83.1 0.7 collective-permute-start.19
  83.8 0.5 collective-permute-done.18.near
  84.3 1.2 %exit.1.after_this = f32[128,768]{1,0:T(8,128)} custom-call(s32[1]{0:T(128)} %bitcast.place, f32[8,768]{1,0:T(8,128)S(1)} %collective-permute-done.18.near, f32[8,768]{1,0:T(8,128)S(1)} %collective-permute-done.19.far, f32[128,768]{1,0:T(8,128)S(1)} %get-tuple-element.126.other_grad.first, f32[128,768]{1,0:T(8,128)S(1)} %get-tuple-element.129.second, ...), custom_call_target="tpu_custom_call" | custom-call | flops 268435456 | bytes 4194304 | tf_op jit(solution)/shard_map/exit/pallas_call | solution.py:681
  85.5 2.4 %collective-permute-done.26.refs_2_ = f32[336,128]{1,0:T(8,128)S(1)} collective-permute-done((f32[336,128]{1,0:T(8,128)S(1)}, f32[336,128]{1,0:T(8,128)S(1)}, u32[]{:S(2)}, u32[]{:S(2)}) %collective-permute-start.26) | collective-permute-done | bytes 172064 | tf_op jit(solution)/shard_map/ppermute | solution.py:656
  88.0 3.5 %collective-permute-done.25.refs_1_ = f32[336,128]{1,0:T(8,128)S(1)} collective-permute-done((f32[336,128]{1,0:T(8,128)S(1)}, f32[336,128]{1,0:T(8,128)S(1)}, u32[]{:S(2)}, u32[]{:S(2)}) %collective-permute-start.25) | collective-permute-done | bytes 172064 | tf_op jit(solution)/shard_map/ppermute | solution.py:656
  91.6 2.1 %collective-permute-done.27.other = f32[4,336,128]{2,1,0:T(8,128)S(1)} collective-permute-done((f32[4,336,128]{2,1,0:T(8,128)S(1)}, f32[4,336,128]{2,1,0:T(8,128)S(1)}, u32[]{:S(2)}, u32[]{:S(2)}) %collective-permute-start.27) | collective-permute-done | bytes 688160 | tf_op jit(solution)/shard_map/ppermute | solution.py:649
  93.7 1.2 %weight_grads.1 = (f32[2,768,128]{2,1,0:T(8,128)}, f32[2,96,768]{2,1,0:T(8,128)}) custom-call(s32[1]{0:T(128)} %bitcast.place, f32[4,336,128]{2,1,0:T(8,128)S(1)} %joined.1.mine, f32[4,336,128]{2,1,0:T(8,128)S(1)} %collective-permute-done.27.other), custom_call_target="tpu_custom_call" | custom-call | flops 268435456 | bytes 4194304 | tf_op jit(solution)/shard_map/weight_grads/pallas_call | solution.py:681
  (28 shorter events, 1.8 us)
Async XLA Ops:
  1.4 6.8 %collective-permute-start.1 = (f32[8,768]{1,0:T(8,128)S(1)}, f32[8,768]{1,0:T(8,128)S(1)}, u32[]{:S(2)}, u32[]{:S(2)}) collective-permute-start(f32[8,768]{1,0:T(8,128)S(1)} %get-tuple-element.139), channel_id=1, source_target_pairs={{4,8},{12,16},{20,24},{8,4},{16,12},{24,20},{5,9},{13,17},{21,25},... | collective-permute-start | bytes 73736 | tf_op jit(solution)/shard_map/ppermute | solution.py:644
  2.1 6.2 %collective-permute-start = (f32[8,768]{1,0:T(8,128)S(1)}, f32[8,768]{1,0:T(8,128)S(1)}, u32[]{:S(2)}, u32[]{:S(2)}) collective-permute-start(f32[8,768]{1,0:T(8,128)S(1)} %get-tuple-element.140), channel_id=1, source_target_pairs={{0,4},{4,0},{8,12},{12,8},{16,20},{20,16},{24,28},{28,24},{1,5},{5... | collective-permute-start | bytes 73736 | tf_op jit(solution)/shard_map/ppermute | solution.py:649
  9.1 9.3 %collective-permute-start.7 = (f32[128,128]{1,0:T(8,128)S(1)}, f32[128,128]{1,0:T(8,128)S(1)}, u32[]{:S(2)}, u32[]{:S(2)}) collective-permute-start(f32[128,128]{1,0:T(8,128)S(1)} %get-tuple-element.83.refs_0_), channel_id=1, source_target_pairs={{0,3},{1,2},{2,1},{3,0},{4,7},{5,6},{6,5},{7,4},{8,11},{9,10},{10,... | collective-permute-start | bytes 196616 | tf_op jit(solution)/shard_map/ppermute | solution.py:649
  12.7 6.8 %collective-permute-start.6 = (f32[128,128]{1,0:T(8,128)S(1)}, f32[128,128]{1,0:T(8,128)S(1)}, u32[]{:S(2)}, u32[]{:S(2)}) collective-permute-start(f32[128,128]{1,0:T(8,128)S(1)} %get-tuple-element.83.refs_0_), channel_id=1, source_target_pairs={{0,2},{1,3},{2,0},{3,1},{4,6},{5,7},{6,4},{7,5},{8,10},{9,11},{10,... | collective-permute-start | bytes 196616 | tf_op jit(solution)/shard_map/ppermute | solution.py:649
  12.8 6.8 %collective-permute-start.5 = (f32[128,128]{1,0:T(8,128)S(1)}, f32[128,128]{1,0:T(8,128)S(1)}, u32[]{:S(2)}, u32[]{:S(2)}) collective-permute-start(f32[128,128]{1,0:T(8,128)S(1)} %get-tuple-element.83.refs_0_), channel_id=1, source_target_pairs={{0,1},{1,0},{2,3},{3,2},{4,5},{5,4},{6,7},{7,6},{8,9},{9,8},{10,11... | collective-permute-start | bytes 196616 | tf_op jit(solution)/shard_map/ppermute | solution.py:649
  14.8 8.6 %collective-permute-start.4 = (f32[128,128]{1,0:T(8,128)S(1)}, f32[128,128]{1,0:T(8,128)S(1)}, u32[]{:S(2)}, u32[]{:S(2)}) collective-permute-start(f32[128,128]{1,0:T(8,128)S(1)} %get-tuple-element.79.refs_0_), channel_id=1, source_target_pairs={{0,3},{1,2},{2,1},{3,0},{4,7},{5,6},{6,5},{7,4},{8,11},{9,10},{10,... | collective-permute-start | bytes 196616 | tf_op jit(solution)/shard_map/ppermute | solution.py:649
  18.4 5.7 %collective-permute-start.3 = (f32[128,128]{1,0:T(8,128)S(1)}, f32[128,128]{1,0:T(8,128)S(1)}, u32[]{:S(2)}, u32[]{:S(2)}) collective-permute-start(f32[128,128]{1,0:T(8,128)S(1)} %get-tuple-element.79.refs_0_), channel_id=1, source_target_pairs={{0,2},{1,3},{2,0},{3,1},{4,6},{5,7},{6,4},{7,5},{8,10},{9,11},{10,... | collective-permute-start | bytes 196616 | tf_op jit(solution)/shard_map/ppermute | solution.py:649
  18.4 5.7 %collective-permute-start.2 = (f32[128,128]{1,0:T(8,128)S(1)}, f32[128,128]{1,0:T(8,128)S(1)}, u32[]{:S(2)}, u32[]{:S(2)}) collective-permute-start(f32[128,128]{1,0:T(8,128)S(1)} %get-tuple-element.79.refs_0_), channel_id=1, source_target_pairs={{0,1},{1,0},{2,3},{3,2},{4,5},{5,4},{6,7},{7,6},{8,9},{9,8},{10,11... | collective-permute-start | bytes 196616 | tf_op jit(solution)/shard_map/ppermute | solution.py:649
  27.9 1.6 %collective-permute-start.8 = (f32[2,6,40,128]{3,2,1,0:T(8,128)S(1)}, f32[2,6,40,128]{3,2,1,0:T(8,128)S(1)}, u32[]{:S(2)}, u32[]{:S(2)}) collective-permute-start(f32[2,6,40,128]{3,2,1,0:T(8,128)S(1)} %get-tuple-element.91.mine), channel_id=1, source_target_pairs={{0,4},{4,0},{8,12},{12,8},{16,20},{20,16},{24,28},{28,24},{1,5},{5... | collective-permute-start | bytes 737288 | tf_op jit(solution)/shard_map/ppermute | solution.py:649
  29.7 5.3 %collective-permute-start.9 = (f32[208,128]{1,0:T(8,128)S(1)}, f32[208,128]{1,0:T(8,128)S(1)}, u32[]{:S(2)}, u32[]{:S(2)}) collective-permute-start(f32[208,128]{1,0:T(8,128)S(1)} %get-tuple-element.93), channel_id=1, source_target_pairs={{0,8},{4,20},{8,0},{12,28},{16,24},{20,4},{24,16},{28,12},{1,9},{5... | collective-permute-start | bytes 319496 | tf_op jit(solution)/shard_map/ppermute | solution.py:656
  31.7 5.5 %collective-permute-start.10 = (f32[208,128]{1,0:T(8,128)S(1)}, f32[208,128]{1,0:T(8,128)S(1)}, u32[]{:S(2)}, u32[]{:S(2)}) collective-permute-start(f32[208,128]{1,0:T(8,128)S(1)} %get-tuple-element.94), channel_id=1, source_target_pairs={{0,16},{4,28},{8,24},{12,20},{16,0},{20,12},{24,8},{28,4},{1,17},{... | collective-permute-start | bytes 319496 | tf_op jit(solution)/shard_map/ppermute | solution.py:656
  33.2 5.8 %collective-permute-start.11 = (f32[208,128]{1,0:T(8,128)S(1)}, f32[208,128]{1,0:T(8,128)S(1)}, u32[]{:S(2)}, u32[]{:S(2)}) collective-permute-start(f32[208,128]{1,0:T(8,128)S(1)} %get-tuple-element.95), channel_id=1, source_target_pairs={{0,24},{4,12},{8,16},{12,4},{16,8},{20,28},{24,0},{28,20},{1,25},{... | collective-permute-start | bytes 319496 | tf_op jit(solution)/shard_map/ppermute | solution.py:656
  45.4 10.6 %collective-permute-start.14 = (f32[128,128]{1,0:T(8,128)S(1)}, f32[128,128]{1,0:T(8,128)S(1)}, u32[]{:S(2)}, u32[]{:S(2)}) collective-permute-start(f32[128,128]{1,0:T(8,128)S(1)} %get-tuple-element.113.refs_0_), channel_id=1, source_target_pairs={{0,3},{1,2},{2,1},{3,0},{4,7},{5,6},{6,5},{7,4},{8,11},{9,10},{10,... | collective-permute-start | bytes 196616 | tf_op jit(solution)/shard_map/ppermute | solution.py:649
  48.4 7.7 %collective-permute-start.13 = (f32[128,128]{1,0:T(8,128)S(1)}, f32[128,128]{1,0:T(8,128)S(1)}, u32[]{:S(2)}, u32[]{:S(2)}) collective-permute-start(f32[128,128]{1,0:T(8,128)S(1)} %get-tuple-element.113.refs_0_), channel_id=1, source_target_pairs={{0,2},{1,3},{2,0},{3,1},{4,6},{5,7},{6,4},{7,5},{8,10},{9,11},{10,... | collective-permute-start | bytes 196616 | tf_op jit(solution)/shard_map/ppermute | solution.py:649
  48.4 7.7 %collective-permute-start.12 = (f32[128,128]{1,0:T(8,128)S(1)}, f32[128,128]{1,0:T(8,128)S(1)}, u32[]{:S(2)}, u32[]{:S(2)}) collective-permute-start(f32[128,128]{1,0:T(8,128)S(1)} %get-tuple-element.113.refs_0_), channel_id=1, source_target_pairs={{0,1},{1,0},{2,3},{3,2},{4,5},{5,4},{6,7},{7,6},{8,9},{9,8},{10,11... | collective-permute-start | bytes 196616 | tf_op jit(solution)/shard_map/ppermute | solution.py:649
  56.1 4.5 %collective-permute-start.15 = (f32[128,128]{1,0:T(8,128)S(1)}, f32[128,128]{1,0:T(8,128)S(1)}, u32[]{:S(2)}, u32[]{:S(2)}) collective-permute-start(f32[128,128]{1,0:T(8,128)S(1)} %get-tuple-element.114.own), channel_id=1, source_target_pairs={{0,1},{1,0},{2,3},{3,2},{4,5},{5,4},{6,7},{7,6},{8,9},{9,8},{10,11... | collective-permute-start | bytes 196616 | tf_op jit(solution)/shard_map/ppermute | solution.py:649
  56.7 6.8 %collective-permute-start.17 = (f32[128,128]{1,0:T(8,128)S(1)}, f32[128,128]{1,0:T(8,128)S(1)}, u32[]{:S(2)}, u32[]{:S(2)}) collective-permute-start(f32[128,128]{1,0:T(8,128)S(1)} %get-tuple-element.114.own), channel_id=1, source_target_pairs={{0,3},{1,2},{2,1},{3,0},{4,7},{5,6},{6,5},{7,4},{8,11},{9,10},{10,... | collective-permute-start | bytes 196616 | tf_op jit(solution)/shard_map/ppermute | solution.py:649
  59.1 5.9 %collective-permute-start.16 = (f32[128,128]{1,0:T(8,128)S(1)}, f32[128,128]{1,0:T(8,128)S(1)}, u32[]{:S(2)}, u32[]{:S(2)}) collective-permute-start(f32[128,128]{1,0:T(8,128)S(1)} %get-tuple-element.114.own), channel_id=1, source_target_pairs={{0,2},{1,3},{2,0},{3,1},{4,6},{5,7},{6,4},{7,5},{8,10},{9,11},{10,... | collective-permute-start | bytes 196616 | tf_op jit(solution)/shard_map/ppermute | solution.py:649
  66.0 2.2 %collective-permute-start.20 = (f32[1344,128]{1,0:T(8,128)S(1)}, f32[1344,128]{1,0:T(8,128)S(1)}, u32[]{:S(2)}, u32[]{:S(2)}) collective-permute-start(f32[1344,128]{1,0:T(8,128)S(1)} %get-tuple-element.131), channel_id=1, source_target_pairs={{0,4},{4,0},{8,12},{12,8},{16,20},{20,16},{24,28},{28,24},{1,5},{5... | collective-permute-start | bytes 2064392 | tf_op jit(solution)/shard_map/ppermute | solution.py:649
  68.4 7.1 %collective-permute-start.21 = (f32[336,128]{1,0:T(8,128)S(1)}, f32[336,128]{1,0:T(8,128)S(1)}, u32[]{:S(2)}, u32[]{:S(2)}) collective-permute-start(f32[336,128]{1,0:T(8,128)S(1)} %get-tuple-element.133), channel_id=1, source_target_pairs={{0,8},{4,20},{8,0},{12,28},{16,24},{20,4},{24,16},{28,12},{1,9},{5... | collective-permute-start | bytes 516104 | tf_op jit(solution)/shard_map/ppermute | solution.py:656
  69.7 7.8 %collective-permute-start.22 = (f32[336,128]{1,0:T(8,128)S(1)}, f32[336,128]{1,0:T(8,128)S(1)}, u32[]{:S(2)}, u32[]{:S(2)}) collective-permute-start(f32[336,128]{1,0:T(8,128)S(1)} %get-tuple-element.134), channel_id=1, source_target_pairs={{0,16},{4,28},{8,24},{12,20},{16,0},{20,12},{24,8},{28,4},{1,17},{... | collective-permute-start | bytes 516104 | tf_op jit(solution)/shard_map/ppermute | solution.py:656
  70.5 9.1 %collective-permute-start.23 = (f32[336,128]{1,0:T(8,128)S(1)}, f32[336,128]{1,0:T(8,128)S(1)}, u32[]{:S(2)}, u32[]{:S(2)}) collective-permute-start(f32[336,128]{1,0:T(8,128)S(1)} %get-tuple-element.135), channel_id=1, source_target_pairs={{0,24},{4,12},{8,16},{12,4},{16,8},{20,28},{24,0},{28,20},{1,25},{... | collective-permute-start | bytes 516104 | tf_op jit(solution)/shard_map/ppermute | solution.py:656
  79.6 8.4 %collective-permute-start.26 = (f32[336,128]{1,0:T(8,128)S(1)}, f32[336,128]{1,0:T(8,128)S(1)}, u32[]{:S(2)}, u32[]{:S(2)}) collective-permute-start(f32[336,128]{1,0:T(8,128)S(1)} %share_sum.1.after_this.mine), channel_id=1, source_target_pairs={{0,24},{4,12},{8,16},{12,4},{16,8},{20,28},{24,0},{28,20},{1,25},{... | collective-permute-start | bytes 516104 | tf_op jit(solution)/shard_map/ppermute | solution.py:656
  81.4 10.0 %collective-permute-start.25 = (f32[336,128]{1,0:T(8,128)S(1)}, f32[336,128]{1,0:T(8,128)S(1)}, u32[]{:S(2)}, u32[]{:S(2)}) collective-permute-start(f32[336,128]{1,0:T(8,128)S(1)} %share_sum.1.after_this.mine), channel_id=1, source_target_pairs={{0,16},{4,28},{8,24},{12,20},{16,0},{20,12},{24,8},{28,4},{1,17},{... | collective-permute-start | bytes 516104 | tf_op jit(solution)/shard_map/ppermute | solution.py:656
  82.2 9.3 %collective-permute-start.24 = (f32[336,128]{1,0:T(8,128)S(1)}, f32[336,128]{1,0:T(8,128)S(1)}, u32[]{:S(2)}, u32[]{:S(2)}) collective-permute-start(f32[336,128]{1,0:T(8,128)S(1)} %share_sum.1.after_this.mine), channel_id=1, source_target_pairs={{0,8},{4,20},{8,0},{12,28},{16,24},{20,4},{24,16},{28,12},{1,9},{5... | collective-permute-start | bytes 516104 | tf_op jit(solution)/shard_map/ppermute | solution.py:656
  83.1 1.2 %collective-permute-start.18 = (f32[8,768]{1,0:T(8,128)S(1)}, f32[8,768]{1,0:T(8,128)S(1)}, u32[]{:S(2)}, u32[]{:S(2)}) collective-permute-start(f32[8,768]{1,0:T(8,128)S(1)} %get-tuple-element.127), channel_id=1, source_target_pairs={{0,4},{4,0},{8,12},{12,8},{16,20},{20,16},{24,28},{28,24},{1,5},{5... | collective-permute-start | bytes 73736 | tf_op jit(solution)/shard_map/ppermute | solution.py:649
  83.1 1.2 %collective-permute-start.19 = (f32[8,768]{1,0:T(8,128)S(1)}, f32[8,768]{1,0:T(8,128)S(1)}, u32[]{:S(2)}, u32[]{:S(2)}) collective-permute-start(f32[8,768]{1,0:T(8,128)S(1)} %get-tuple-element.128), channel_id=1, source_target_pairs={{4,8},{12,16},{20,24},{8,4},{16,12},{24,20},{5,9},{13,17},{21,25},... | collective-permute-start | bytes 73736 | tf_op jit(solution)/shard_map/ppermute | solution.py:644
  91.5 2.2 %collective-permute-start.27 = (f32[4,336,128]{2,1,0:T(8,128)S(1)}, f32[4,336,128]{2,1,0:T(8,128)S(1)}, u32[]{:S(2)}, u32[]{:S(2)}) collective-permute-start(f32[4,336,128]{2,1,0:T(8,128)S(1)} %joined.1.mine), channel_id=1, source_target_pairs={{0,4},{4,0},{8,12},{12,8},{16,20},{20,16},{24,28},{28,24},{1,5},{5... | collective-permute-start | bytes 2064392 | tf_op jit(solution)/shard_map/ppermute | solution.py:649

commit v8 on v7

--- a/solution.py
+++ b/solution.py
@@ -372,14 +372,15 @@
     incoming, bases, act, step, step_pre, grad_gated, entering, decays, spreader, *refs = refs
     rates, skip_rows, *refs = refs
     earlier, refs = refs[:side], refs[side:]
-    step_weight, *refs = refs
+    step_weight_in, *refs = refs
     partial, grad_act, grad_pre, summed_out, *refs = refs
-    rate_rows, history, grad_in, grad_out, weights = refs
+    step_weight, rate_rows, history, grad_in, grad_out, weights, sems = refs
     tiles, length, _ = act.shape
     states = rates.shape[1]
-    ranks = step_weight.shape[1]
+    ranks = step_weight.shape[0]
     count = length // CHAINS
     group = tile_group(tiles)
+    loads = copies_of([(step_weight_in.at[side], step_weight)], sems)
     grad_in[...] = jnp.zeros_like(grad_in)
     grad_out[...] = jnp.zeros_like(grad_out)
     up = side == 0
@@ -483,7 +484,8 @@
     lax.fori_loop(0, tiles // group, some_tiles, 0)
     wide = full_width(grad_pre)
     weights[...] = jnp.zeros_like(weights)
-    weights[:ranks] = step_weight[side]
+    finish_all(loads)
+    weights[:ranks] = step_weight[...]
     sums = jnp.zeros((length, LANES), jnp.float32)
     step_lanes = 4 * LANES
     for k, values in enumerate((grad_in, grad_out)):
@@ -583,6 +585,10 @@
     terms, (total, out) = refs[:-2], refs[-2:]
     add_kernel(*terms, total)
     out[...] = value[...]
+
+
+def add_after_kernel(near, far, *refs):
+    add_kernel(*refs)
 
 
 def add_kernel(*refs):
@@ -800,14 +806,15 @@
             functools.partial(scan_kernel, side), ("first_scan", "second_scan")[side],
             (narrow, one, one, one),
             [
-                row_scratch, grouped, bases, bases, vmem((LANES, width)),
+                vmem(step_weight.shape[1:]), row_scratch, grouped, bases, bases,
+                vmem((LANES, width)), dma(1),
             ],
             10,
             (
                 incoming, spread_bases, acts[side], step, step_pre, grad_gated, entering, decays,
-                spreader, rates, skip_rows, *earlier, step_held[0],
+                spreader, rates, skip_rows, *earlier, step_weight,
             ),
-            "vmmmmmmmmmm" + "m" * side + "m", "vmmm", 2**33,
+            "vmmmmmmmmmm" + "m" * side + "h", "vmmm", 2**33,
         )
         if side == 1:
             first_total, partial_grad = call(
@@ -850,7 +857,8 @@
         shares = halved(place, keep, send, half, chips, "halves")
         rows = half // chips
         (mine,) = call(
-            add_kernel, "share_sum", ((rows, LANES),), [], 4, shares, "v" * chips
+            add_after_kernel, "share_sum", ((rows, LANES),), [], 4, (*edges, *shares),
+            "v" * (2 + chips),
         )
         ahead = mine
     else:

time: 95.2 us -> 95.4 us (level)
  no operation moved by 1% of the time
where the time goes in v8:
time: 95.4 us; the launch traced here: 95.1 us
  starting transfers between devices  33.5 us (35%)
  Pallas kernels  30.7 us (32%)
  waiting for transfers between devices  29.3 us (31%)
    pallas_call x19, Pallas kernels, call(): pl.pallas_call(kernel, in_specs=[spaces[k] for k in kinds], out_specs=[sp...  30.7 us
    ppermute x17, starting transfers between devices, swapped(): return lax.ppermute(value, axis, [(i, i ^ by) for i in range(count)])  21.5 us
    ppermute x9, waiting for transfers between devices, swapped_chips(): return lax.ppermute(value, 'ctx', pairs)  19.4 us
    ppermute x9, starting transfers between devices, swapped_chips(): return lax.ppermute(value, 'ctx', pairs)  10.7 us
    ppermute x17, waiting for transfers between devices, swapped(): return lax.ppermute(value, axis, [(i, i ^ by) for i in range(count)])  9.9 us
  transfers between devices with their start and end apart: 28, of which 16 were waited for; matrix products, arithmetic and copies ran while one was open for 0% of the time, Pallas kernels for 18%

profile of v8, /device:TPU:0, one launch (start us, length us, event | category | flops | bytes accessed | tf_op | source)
XLA Modules:
  0.0 95.1 jit_solution(2509754500066975671)
XLA Ops:
  0.6 0.8 slice_select_fusion
  1.4 0.7 collective-permute-start.1
  2.1 4.4 %collective-permute-start = (f32[8,768]{1,0:T(8,128)S(1)}, f32[8,768]{1,0:T(8,128)S(1)}, u32[]{:S(2)}, u32[]{:S(2)}) collective-permute-start(f32[8,768]{1,0:T(8,128)S(1)} %get-tuple-element.140), channel_id=1, source_target_pairs={{0,4},{4,0},{8,12},{12,8},{16,20},{20,16},{24,28},{28,24},{1,5},{5... | collective-permute-start | bytes 73736 | tf_op jit(solution)/shard_map/ppermute | solution.py:655
  6.4 1.8 %fetch.1 = (f32[128,768]{1,0:T(8,128)S(1)}, f32[2,768,128]{2,1,0:T(8,128)S(1)}, f32[2,4,768]{2,1,0:T(4,128)S(1)}, f32[2,768]{1,0:T(2,128)S(1)}, f32[128,768]{1,0...) custom-call(f32[128,768]{1,0:T(8,128)} %refs_0_.1, ...), custom_call_target="tpu_custom_call" | custom-call | flops 268435456 | bytes 4194304 | tf_op jit(solution)/shard_map/fetch/pallas_call | solution.py:687
  8.2 0.8 entry.1
  9.1 3.7 %collective-permute-start.7 = (f32[128,128]{1,0:T(8,128)S(1)}, f32[128,128]{1,0:T(8,128)S(1)}, u32[]{:S(2)}, u32[]{:S(2)}) collective-permute-start(f32[128,128]{1,0:T(8,128)S(1)} %get-tuple-element.83.refs_0_), channel_id=1, source_target_pairs={{0,3},{1,2},{2,1},{3,0},{4,7},{5,6},{6,5},{7,4},{8,11},{9,10},{10,... | collective-permute-start | bytes 196616 | tf_op jit(solution)/shard_map/ppermute | solution.py:655
  12.8 0.8 collective-permute-start.5
  13.5 1.2 %second_entry.1 = (f32[128,128]{1,0:T(8,128)S(1)}, f32[6,128,128]{2,1,0:T(8,128)S(1)}, f32[6,128,128]{2,1,0:T(8,128)S(1)}, f32[6,128,128]{2,1,0:T(8,128)S(1)}, bf16[128,4096]{1,0:T(8,128)(2,1)S(1)}) custom-call(f32[144,768]{1,0:T(8,128)S(1)} %get-tuple-element.76.ext, f32[2,4,768]{2,1,0:T(4,128)S(1)} %get-tuple-element.73.conv_weight, ...), custom_call_target="tpu_custom_call" | custom-call | flops 268435456 | bytes 4194304 | tf_op jit(solution)/shard_map/second_entry/pallas_call | solution.py:687
  14.8 3.7 %collective-permute-start.4 = (f32[128,128]{1,0:T(8,128)S(1)}, f32[128,128]{1,0:T(8,128)S(1)}, u32[]{:S(2)}, u32[]{:S(2)}) collective-permute-start(f32[128,128]{1,0:T(8,128)S(1)} %get-tuple-element.79.refs_0_), channel_id=1, source_target_pairs={{0,3},{1,2},{2,1},{3,0},{4,7},{5,6},{6,5},{7,4},{8,11},{9,10},{10,... | collective-permute-start | bytes 196616 | tf_op jit(solution)/shard_map/ppermute | solution.py:655
  18.4 0.8 collective-permute-start.2
  19.6 3.8 %first_local.1 = (f32[128,128]{1,0:T(8,128)S(1)}, f32[6,128,128]{2,1,0:T(8,128)S(1)}, f32[6,128,128]{2,1,0:T(8,128)S(1)}, f32[2,6,16,8,128]{4,3,2,1,0:T(8,128)S(...) custom-call(f32[128,128]{1,0:T(8,128)S(1)} %get-tuple-element.83.ref, ...), custom_call_target="tpu_custom_call" | custom-call | flops 4294967296 | bytes 67108864 | tf_op jit(solution)/shard_map/first_local/pallas_call | solution.py:687
  23.3 0.8 collective-permute-done.3.refs_2_
  24.2 3.8 %second_local.1 = (f32[128,128]{1,0:T(8,128)S(1)}, f32[6,128,128]{2,1,0:T(8,128)S(1)}, f32[6,128,128]{2,1,0:T(8,128)S(1)}, f32[2,6,16,8,128]{4,3,2,1,0:T(8,128)S...) custom-call(f32[128,128]{1,0:T(8,128)S(1)} %get-tuple-element.79.ref, ...), custom_call_target="tpu_custom_call" | custom-call | flops 4294967296 | bytes 67108864 | tf_op jit(solution)/shard_map/second_local/pallas_call | solution.py:687
  28.0 1.5 %collective-permute-done.8.other = f32[2,6,40,128]{3,2,1,0:T(8,128)S(1)} collective-permute-done((f32[2,6,40,128]{3,2,1,0:T(8,128)S(1)}, f32[2,6,40,128]{3,2,1,0:T(8,128)S(1)}, u32[]{:S(2)}, u32[]{:S(2)}) %collective-permute-start.8) | collective-permute-done | bytes 245792 | tf_op jit(solution)/shard_map/ppermute | solution.py:655
  29.6 2.1 %collective-permute-start.9 = (f32[208,128]{1,0:T(8,128)S(1)}, f32[208,128]{1,0:T(8,128)S(1)}, u32[]{:S(2)}, u32[]{:S(2)}) collective-permute-start(f32[208,128]{1,0:T(8,128)S(1)} %get-tuple-element.93), channel_id=1, source_target_pairs={{0,8},{4,20},{8,0},{12,28},{16,24},{20,4},{24,16},{28,12},{1,9},{5... | collective-permute-start | bytes 319496 | tf_op jit(solution)/shard_map/ppermute | solution.py:662
  31.7 1.5 %collective-permute-start.10 = (f32[208,128]{1,0:T(8,128)S(1)}, f32[208,128]{1,0:T(8,128)S(1)}, u32[]{:S(2)}, u32[]{:S(2)}) collective-permute-start(f32[208,128]{1,0:T(8,128)S(1)} %get-tuple-element.94), channel_id=1, source_target_pairs={{0,16},{4,28},{8,24},{12,20},{16,0},{20,12},{24,8},{28,4},{1,17},{... | collective-permute-start | bytes 319496 | tf_op jit(solution)/shard_map/ppermute | solution.py:662
  33.3 1.6 %collective-permute-done.9.refs_0_ = f32[208,128]{1,0:T(8,128)S(1)} collective-permute-done((f32[208,128]{1,0:T(8,128)S(1)}, f32[208,128]{1,0:T(8,128)S(1)}, u32[]{:S(2)}, u32[]{:S(2)}) %collective-permute-start.9) | collective-permute-done | bytes 106528 | tf_op jit(solution)/shard_map/ppermute | solution.py:662
  34.9 2.4 %collective-permute-done.10.refs_1_ = f32[208,128]{1,0:T(8,128)S(1)} collective-permute-done((f32[208,128]{1,0:T(8,128)S(1)}, f32[208,128]{1,0:T(8,128)S(1)}, u32[]{:S(2)}, u32[]{:S(2)}) %collective-permute-start.10) | collective-permute-done | bytes 106528 | tf_op jit(solution)/shard_map/ppermute | solution.py:662
  37.3 1.7 %collective-permute-done.11.refs_2_ = f32[208,128]{1,0:T(8,128)S(1)} collective-permute-done((f32[208,128]{1,0:T(8,128)S(1)}, f32[208,128]{1,0:T(8,128)S(1)}, u32[]{:S(2)}, u32[]{:S(2)}) %collective-permute-start.11) | collective-permute-done | bytes 106528 | tf_op jit(solution)/shard_map/ppermute | solution.py:662
  39.2 6.2 %first_scan.1 = (f32[128,128]{1,0:T(8,128)S(1)}, f32[6,128,128]{2,1,0:T(8,128)S(1)}, f32[6,128,128]{2,1,0:T(8,128)S(1)}, f32[6,128,128]{2,1,0:T(8,128)S(1)}) custom-call(f32[2,6,32,128]{3,2,1,0:T(8,128)S(1)} %chain.1.refs_0_, f32[2,128,2048]{2,1,0:T(8,128)S(1)} %get-tuple-element.103.refs_1_, f32[6,128,128]{2,1,0:T(8,128)S(1)} %get-tuple-element.84.refs_4_.refs_2_.act, ...), custom_call_target="tpu_custom_call" | custom-call | flops 8589934592 | bytes 134217728 | tf_op jit(solution)/shard_map/first_scan/pallas_call | solution.py:687
  45.4 3.0 %collective-permute-start.14 = (f32[128,128]{1,0:T(8,128)S(1)}, f32[128,128]{1,0:T(8,128)S(1)}, u32[]{:S(2)}, u32[]{:S(2)}) collective-permute-start(f32[128,128]{1,0:T(8,128)S(1)} %get-tuple-element.113.refs_0_), channel_id=1, source_target_pairs={{0,3},{1,2},{2,1},{3,0},{4,7},{5,6},{6,5},{7,4},{8,11},{9,10},{10,... | collective-permute-start | bytes 196616 | tf_op jit(solution)/shard_map/ppermute | solution.py:655
  48.4 1.5 %collective-permute-start.12 = (f32[128,128]{1,0:T(8,128)S(1)}, f32[128,128]{1,0:T(8,128)S(1)}, u32[]{:S(2)}, u32[]{:S(2)}) collective-permute-start(f32[128,128]{1,0:T(8,128)S(1)} %get-tuple-element.113.refs_0_), channel_id=1, source_target_pairs={{0,1},{1,0},{2,3},{3,2},{4,5},{5,4},{6,7},{7,6},{8,9},{9,8},{10,11... | collective-permute-start | bytes 196616 | tf_op jit(solution)/shard_map/ppermute | solution.py:655
  49.9 6.2 %second_scan.1 = (f32[128,128]{1,0:T(8,128)S(1)}, f32[6,128,128]{2,1,0:T(8,128)S(1)}, f32[6,128,128]{2,1,0:T(8,128)S(1)}, f32[6,128,128]{2,1,0:T(8,128)S(1)}) custom-call(f32[2,6,32,128]{3,2,1,0:T(8,128)S(1)} %chain.1.refs_0_, f32[2,128,2048]{2,1,0:T(8,128)S(1)} %get-tuple-element.96.refs_1_, f32[6,128,128]{2,1,0:T(8,128)S(1)} %get-tuple-element.80.refs_4_.refs_2_.act, ...), custom_call_target="tpu_custom_call" | custom-call | flops 8589934592 | bytes 134217728 | tf_op jit(solution)/shard_map/second_scan/pallas_call | solution.py:687
  56.1 0.6 collective-permute-start.15
  56.7 2.4 %collective-permute-start.17 = (f32[128,128]{1,0:T(8,128)S(1)}, f32[128,128]{1,0:T(8,128)S(1)}, u32[]{:S(2)}, u32[]{:S(2)}) collective-permute-start(f32[128,128]{1,0:T(8,128)S(1)} %get-tuple-element.114.own), channel_id=1, source_target_pairs={{0,3},{1,2},{2,1},{3,0},{4,7},{5,6},{6,5},{7,4},{8,11},{9,10},{10,... | collective-permute-start | bytes 196616 | tf_op jit(solution)/shard_map/ppermute | solution.py:655
  59.7 0.9 collective-permute-done.15.after_this.first
  60.6 1.2 %gate.1 = (f32[128,768]{1,0:T(8,128)}, f32[128,768]{1,0:T(8,128)}) custom-call(f32[6,128,128]{2,1,0:T(8,128)S(1)} %get-tuple-element.111.summed, f32[128,768]{1,0:T(8,128)S(1)} %get-tuple-element.77.gate, f32[128,768]{1,0:T(8,128)S(1)} %get-tuple-element.78.cot, f32[128,128]{1,0:T(8,128)S(1)} %collective-permute-done.15.after_this.first), custom_call_target="tpu_custom_call" | custom-call | tf_op jit(solution)/shard_map/gate/pallas_call | solution.py:687
  61.8 0.9 first_weights.1
  62.7 0.8 step_grad.1.step_part
  63.6 1.5 %collective-permute-done.16.second = f32[128,128]{1,0:T(8,128)S(1)} collective-permute-done((f32[128,128]{1,0:T(8,128)S(1)}, f32[128,128]{1,0:T(8,128)S(1)}, u32[]{:S(2)}, u32[]{:S(2)}) %collective-permute-start.16) | collective-permute-done | bytes 65568 | tf_op jit(solution)/shard_map/ppermute | solution.py:655
  65.0 1.1 %weights.1 = (f32[1344,128]{1,0:T(8,128)S(1)}, f32[1344,128]{1,0:T(8,128)S(1)}, f32[128,768]{1,0:T(8,128)S(1)}, f32[8,768]{1,0:T(8,128)S(1)}, f32[8,768]{1,0:T(8,128)S(1)}) custom-call(s32[1]{0:T(128)} %bitcast.place, f32[128,128]{1,0:T(8,128)S(1)} %get-tuple-element.114.own, f32[128,128]{1,0:T(8,128)S(1)} %collective-permute-done.15.after_this.first, ...), custom_call_target="tpu_custom_call" | custom-call | flops 268435456 | bytes 4194304 | tf_op jit(solution)/shard_map/weights/pallas_call | solution.py:687
  66.2 2.1 %collective-permute-done.20.got = f32[1344,128]{1,0:T(8,128)S(1)} collective-permute-done((f32[1344,128]{1,0:T(8,128)S(1)}, f32[1344,128]{1,0:T(8,128)S(1)}, u32[]{:S(2)}, u32[]{:S(2)}) %collective-permute-start.20) | collective-permute-done | bytes 688160 | tf_op jit(solution)/shard_map/ppermute | solution.py:655
  68.4 1.3 %collective-permute-start.21 = (f32[336,128]{1,0:T(8,128)S(1)}, f32[336,128]{1,0:T(8,128)S(1)}, u32[]{:S(2)}, u32[]{:S(2)}) collective-permute-start(f32[336,128]{1,0:T(8,128)S(1)} %get-tuple-element.133), channel_id=1, source_target_pairs={{0,8},{4,20},{8,0},{12,28},{16,24},{20,4},{24,16},{28,12},{1,9},{5... | collective-permute-start | bytes 516104 | tf_op jit(solution)/shard_map/ppermute | solution.py:662
  69.8 0.8 collective-permute-start.22
  70.5 1.4 %collective-permute-start.23 = (f32[336,128]{1,0:T(8,128)S(1)}, f32[336,128]{1,0:T(8,128)S(1)}, u32[]{:S(2)}, u32[]{:S(2)}) collective-permute-start(f32[336,128]{1,0:T(8,128)S(1)} %get-tuple-element.135), channel_id=1, source_target_pairs={{0,24},{4,12},{8,16},{12,4},{16,8},{20,28},{24,0},{28,20},{1,25},{... | collective-permute-start | bytes 516104 | tf_op jit(solution)/shard_map/ppermute | solution.py:662
  72.0 0.7 collective-permute-start.19
  72.6 0.5 collective-permute-done.18.near
  73.2 2.3 %collective-permute-done.21.refs_1_ = f32[336,128]{1,0:T(8,128)S(1)} collective-permute-done((f32[336,128]{1,0:T(8,128)S(1)}, f32[336,128]{1,0:T(8,128)S(1)}, u32[]{:S(2)}, u32[]{:S(2)}) %collective-permute-start.21) | collective-permute-done | bytes 172064 | tf_op jit(solution)/shard_map/ppermute | solution.py:662
  75.5 2.1 %collective-permute-done.22.refs_2_ = f32[336,128]{1,0:T(8,128)S(1)} collective-permute-done((f32[336,128]{1,0:T(8,128)S(1)}, f32[336,128]{1,0:T(8,128)S(1)}, u32[]{:S(2)}, u32[]{:S(2)}) %collective-permute-start.22) | collective-permute-done | bytes 172064 | tf_op jit(solution)/shard_map/ppermute | solution.py:662
  77.6 2.0 %collective-permute-done.23.refs_3_ = f32[336,128]{1,0:T(8,128)S(1)} collective-permute-done((f32[336,128]{1,0:T(8,128)S(1)}, f32[336,128]{1,0:T(8,128)S(1)}, u32[]{:S(2)}, u32[]{:S(2)}) %collective-permute-start.23) | collective-permute-done | bytes 172064 | tf_op jit(solution)/shard_map/ppermute | solution.py:662
  79.6 1.9 %collective-permute-start.26 = (f32[336,128]{1,0:T(8,128)S(1)}, f32[336,128]{1,0:T(8,128)S(1)}, u32[]{:S(2)}, u32[]{:S(2)}) collective-permute-start(f32[336,128]{1,0:T(8,128)S(1)} %share_sum.1.after_this.mine), channel_id=1, source_target_pairs={{0,24},{4,12},{8,16},{12,4},{16,8},{20,28},{24,0},{28,20},{1,25},{... | collective-permute-start | bytes 516104 | tf_op jit(solution)/shard_map/ppermute | solution.py:662
  81.6 1.0 %collective-permute-start.25 = (f32[336,128]{1,0:T(8,128)S(1)}, f32[336,128]{1,0:T(8,128)S(1)}, u32[]{:S(2)}, u32[]{:S(2)}) collective-permute-start(f32[336,128]{1,0:T(8,128)S(1)} %share_sum.1.after_this.mine), channel_id=1, source_target_pairs={{0,16},{4,28},{8,24},{12,20},{16,0},{20,12},{24,8},{28,4},{1,17},{... | collective-permute-start | bytes 516104 | tf_op jit(solution)/shard_map/ppermute | solution.py:662
  82.5 0.6 collective-permute-start.24
  83.2 1.2 %exit.1.after_this = f32[128,768]{1,0:T(8,128)} custom-call(s32[1]{0:T(128)} %bitcast.place, f32[8,768]{1,0:T(8,128)S(1)} %collective-permute-done.18.near, f32[8,768]{1,0:T(8,128)S(1)} %collective-permute-done.19.far, f32[128,768]{1,0:T(8,128)S(1)} %get-tuple-element.126.other_grad.first, f32[128,768]{1,0:T(8,128)S(1)} %get-tuple-element.129.second, ...), custom_call_target="tpu_custom_call" | custom-call | flops 268435456 | bytes 4194304 | tf_op jit(solution)/shard_map/exit/pallas_call | solution.py:687
  84.4 3.6 %collective-permute-done.26.refs_2_ = f32[336,128]{1,0:T(8,128)S(1)} collective-permute-done((f32[336,128]{1,0:T(8,128)S(1)}, f32[336,128]{1,0:T(8,128)S(1)}, u32[]{:S(2)}, u32[]{:S(2)}) %collective-permute-start.26) | collective-permute-done | bytes 172064 | tf_op jit(solution)/shard_map/ppermute | solution.py:662
  88.0 3.7 %collective-permute-done.25.refs_1_ = f32[336,128]{1,0:T(8,128)S(1)} collective-permute-done((f32[336,128]{1,0:T(8,128)S(1)}, f32[336,128]{1,0:T(8,128)S(1)}, u32[]{:S(2)}, u32[]{:S(2)}) %collective-permute-start.25) | collective-permute-done | bytes 172064 | tf_op jit(solution)/shard_map/ppermute | solution.py:662
  91.8 2.1 %collective-permute-done.27.other = f32[4,336,128]{2,1,0:T(8,128)S(1)} collective-permute-done((f32[4,336,128]{2,1,0:T(8,128)S(1)}, f32[4,336,128]{2,1,0:T(8,128)S(1)}, u32[]{:S(2)}, u32[]{:S(2)}) %collective-permute-start.27) | collective-permute-done | bytes 688160 | tf_op jit(solution)/shard_map/ppermute | solution.py:655
  93.9 1.2 %weight_grads.1 = (f32[2,768,128]{2,1,0:T(8,128)}, f32[2,96,768]{2,1,0:T(8,128)}) custom-call(s32[1]{0:T(128)} %bitcast.place, f32[4,336,128]{2,1,0:T(8,128)S(1)} %joined.1.mine, f32[4,336,128]{2,1,0:T(8,128)S(1)} %collective-permute-done.27.other), custom_call_target="tpu_custom_call" | custom-call | flops 268435456 | bytes 4194304 | tf_op jit(solution)/shard_map/weight_grads/pallas_call | solution.py:687
  (28 shorter events, 1.7 us)
Async XLA Ops:
  1.4 6.8 %collective-permute-start.1 = (f32[8,768]{1,0:T(8,128)S(1)}, f32[8,768]{1,0:T(8,128)S(1)}, u32[]{:S(2)}, u32[]{:S(2)}) collective-permute-start(f32[8,768]{1,0:T(8,128)S(1)} %get-tuple-element.139), channel_id=1, source_target_pairs={{4,8},{12,16},{20,24},{8,4},{16,12},{24,20},{5,9},{13,17},{21,25},... | collective-permute-start | bytes 73736 | tf_op jit(solution)/shard_map/ppermute | solution.py:650
  2.1 6.2 %collective-permute-start = (f32[8,768]{1,0:T(8,128)S(1)}, f32[8,768]{1,0:T(8,128)S(1)}, u32[]{:S(2)}, u32[]{:S(2)}) collective-permute-start(f32[8,768]{1,0:T(8,128)S(1)} %get-tuple-element.140), channel_id=1, source_target_pairs={{0,4},{4,0},{8,12},{12,8},{16,20},{20,16},{24,28},{28,24},{1,5},{5... | collective-permute-start | bytes 73736 | tf_op jit(solution)/shard_map/ppermute | solution.py:655
  9.1 9.3 %collective-permute-start.7 = (f32[128,128]{1,0:T(8,128)S(1)}, f32[128,128]{1,0:T(8,128)S(1)}, u32[]{:S(2)}, u32[]{:S(2)}) collective-permute-start(f32[128,128]{1,0:T(8,128)S(1)} %get-tuple-element.83.refs_0_), channel_id=1, source_target_pairs={{0,3},{1,2},{2,1},{3,0},{4,7},{5,6},{6,5},{7,4},{8,11},{9,10},{10,... | collective-permute-start | bytes 196616 | tf_op jit(solution)/shard_map/ppermute | solution.py:655
  12.7 6.8 %collective-permute-start.6 = (f32[128,128]{1,0:T(8,128)S(1)}, f32[128,128]{1,0:T(8,128)S(1)}, u32[]{:S(2)}, u32[]{:S(2)}) collective-permute-start(f32[128,128]{1,0:T(8,128)S(1)} %get-tuple-element.83.refs_0_), channel_id=1, source_target_pairs={{0,2},{1,3},{2,0},{3,1},{4,6},{5,7},{6,4},{7,5},{8,10},{9,11},{10,... | collective-permute-start | bytes 196616 | tf_op jit(solution)/shard_map/ppermute | solution.py:655
  12.8 6.8 %collective-permute-start.5 = (f32[128,128]{1,0:T(8,128)S(1)}, f32[128,128]{1,0:T(8,128)S(1)}, u32[]{:S(2)}, u32[]{:S(2)}) collective-permute-start(f32[128,128]{1,0:T(8,128)S(1)} %get-tuple-element.83.refs_0_), channel_id=1, source_target_pairs={{0,1},{1,0},{2,3},{3,2},{4,5},{5,4},{6,7},{7,6},{8,9},{9,8},{10,11... | collective-permute-start | bytes 196616 | tf_op jit(solution)/shard_map/ppermute | solution.py:655
  14.8 8.6 %collective-permute-start.4 = (f32[128,128]{1,0:T(8,128)S(1)}, f32[128,128]{1,0:T(8,128)S(1)}, u32[]{:S(2)}, u32[]{:S(2)}) collective-permute-start(f32[128,128]{1,0:T(8,128)S(1)} %get-tuple-element.79.refs_0_), channel_id=1, source_target_pairs={{0,3},{1,2},{2,1},{3,0},{4,7},{5,6},{6,5},{7,4},{8,11},{9,10},{10,... | collective-permute-start | bytes 196616 | tf_op jit(solution)/shard_map/ppermute | solution.py:655
  18.4 5.7 %collective-permute-start.3 = (f32[128,128]{1,0:T(8,128)S(1)}, f32[128,128]{1,0:T(8,128)S(1)}, u32[]{:S(2)}, u32[]{:S(2)}) collective-permute-start(f32[128,128]{1,0:T(8,128)S(1)} %get-tuple-element.79.refs_0_), channel_id=1, source_target_pairs={{0,2},{1,3},{2,0},{3,1},{4,6},{5,7},{6,4},{7,5},{8,10},{9,11},{10,... | collective-permute-start | bytes 196616 | tf_op jit(solution)/shard_map/ppermute | solution.py:655
  18.4 5.7 %collective-permute-start.2 = (f32[128,128]{1,0:T(8,128)S(1)}, f32[128,128]{1,0:T(8,128)S(1)}, u32[]{:S(2)}, u32[]{:S(2)}) collective-permute-start(f32[128,128]{1,0:T(8,128)S(1)} %get-tuple-element.79.refs_0_), channel_id=1, source_target_pairs={{0,1},{1,0},{2,3},{3,2},{4,5},{5,4},{6,7},{7,6},{8,9},{9,8},{10,11... | collective-permute-start | bytes 196616 | tf_op jit(solution)/shard_map/ppermute | solution.py:655
  27.9 1.6 %collective-permute-start.8 = (f32[2,6,40,128]{3,2,1,0:T(8,128)S(1)}, f32[2,6,40,128]{3,2,1,0:T(8,128)S(1)}, u32[]{:S(2)}, u32[]{:S(2)}) collective-permute-start(f32[2,6,40,128]{3,2,1,0:T(8,128)S(1)} %get-tuple-element.91.mine), channel_id=1, source_target_pairs={{0,4},{4,0},{8,12},{12,8},{16,20},{20,16},{24,28},{28,24},{1,5},{5... | collective-permute-start | bytes 737288 | tf_op jit(solution)/shard_map/ppermute | solution.py:655
  29.6 5.3 %collective-permute-start.9 = (f32[208,128]{1,0:T(8,128)S(1)}, f32[208,128]{1,0:T(8,128)S(1)}, u32[]{:S(2)}, u32[]{:S(2)}) collective-permute-start(f32[208,128]{1,0:T(8,128)S(1)} %get-tuple-element.93), channel_id=1, source_target_pairs={{0,8},{4,20},{8,0},{12,28},{16,24},{20,4},{24,16},{28,12},{1,9},{5... | collective-permute-start | bytes 319496 | tf_op jit(solution)/shard_map/ppermute | solution.py:662
  31.7 5.5 %collective-permute-start.10 = (f32[208,128]{1,0:T(8,128)S(1)}, f32[208,128]{1,0:T(8,128)S(1)}, u32[]{:S(2)}, u32[]{:S(2)}) collective-permute-start(f32[208,128]{1,0:T(8,128)S(1)} %get-tuple-element.94), channel_id=1, source_target_pairs={{0,16},{4,28},{8,24},{12,20},{16,0},{20,12},{24,8},{28,4},{1,17},{... | collective-permute-start | bytes 319496 | tf_op jit(solution)/shard_map/ppermute | solution.py:662
  33.3 5.7 %collective-permute-start.11 = (f32[208,128]{1,0:T(8,128)S(1)}, f32[208,128]{1,0:T(8,128)S(1)}, u32[]{:S(2)}, u32[]{:S(2)}) collective-permute-start(f32[208,128]{1,0:T(8,128)S(1)} %get-tuple-element.95), channel_id=1, source_target_pairs={{0,24},{4,12},{8,16},{12,4},{16,8},{20,28},{24,0},{28,20},{1,25},{... | collective-permute-start | bytes 319496 | tf_op jit(solution)/shard_map/ppermute | solution.py:662
  45.4 10.6 %collective-permute-start.14 = (f32[128,128]{1,0:T(8,128)S(1)}, f32[128,128]{1,0:T(8,128)S(1)}, u32[]{:S(2)}, u32[]{:S(2)}) collective-permute-start(f32[128,128]{1,0:T(8,128)S(1)} %get-tuple-element.113.refs_0_), channel_id=1, source_target_pairs={{0,3},{1,2},{2,1},{3,0},{4,7},{5,6},{6,5},{7,4},{8,11},{9,10},{10,... | collective-permute-start | bytes 196616 | tf_op jit(solution)/shard_map/ppermute | solution.py:655
  48.4 7.7 %collective-permute-start.13 = (f32[128,128]{1,0:T(8,128)S(1)}, f32[128,128]{1,0:T(8,128)S(1)}, u32[]{:S(2)}, u32[]{:S(2)}) collective-permute-start(f32[128,128]{1,0:T(8,128)S(1)} %get-tuple-element.113.refs_0_), channel_id=1, source_target_pairs={{0,2},{1,3},{2,0},{3,1},{4,6},{5,7},{6,4},{7,5},{8,10},{9,11},{10,... | collective-permute-start | bytes 196616 | tf_op jit(solution)/shard_map/ppermute | solution.py:655
  48.4 7.7 %collective-permute-start.12 = (f32[128,128]{1,0:T(8,128)S(1)}, f32[128,128]{1,0:T(8,128)S(1)}, u32[]{:S(2)}, u32[]{:S(2)}) collective-permute-start(f32[128,128]{1,0:T(8,128)S(1)} %get-tuple-element.113.refs_0_), channel_id=1, source_target_pairs={{0,1},{1,0},{2,3},{3,2},{4,5},{5,4},{6,7},{7,6},{8,9},{9,8},{10,11... | collective-permute-start | bytes 196616 | tf_op jit(solution)/shard_map/ppermute | solution.py:655
  56.1 4.5 %collective-permute-start.15 = (f32[128,128]{1,0:T(8,128)S(1)}, f32[128,128]{1,0:T(8,128)S(1)}, u32[]{:S(2)}, u32[]{:S(2)}) collective-permute-start(f32[128,128]{1,0:T(8,128)S(1)} %get-tuple-element.114.own), channel_id=1, source_target_pairs={{0,1},{1,0},{2,3},{3,2},{4,5},{5,4},{6,7},{7,6},{8,9},{9,8},{10,11... | collective-permute-start | bytes 196616 | tf_op jit(solution)/shard_map/ppermute | solution.py:655
  56.7 6.8 %collective-permute-start.17 = (f32[128,128]{1,0:T(8,128)S(1)}, f32[128,128]{1,0:T(8,128)S(1)}, u32[]{:S(2)}, u32[]{:S(2)}) collective-permute-start(f32[128,128]{1,0:T(8,128)S(1)} %get-tuple-element.114.own), channel_id=1, source_target_pairs={{0,3},{1,2},{2,1},{3,0},{4,7},{5,6},{6,5},{7,4},{8,11},{9,10},{10,... | collective-permute-start | bytes 196616 | tf_op jit(solution)/shard_map/ppermute | solution.py:655
  59.2 5.9 %collective-permute-start.16 = (f32[128,128]{1,0:T(8,128)S(1)}, f32[128,128]{1,0:T(8,128)S(1)}, u32[]{:S(2)}, u32[]{:S(2)}) collective-permute-start(f32[128,128]{1,0:T(8,128)S(1)} %get-tuple-element.114.own), channel_id=1, source_target_pairs={{0,2},{1,3},{2,0},{3,1},{4,6},{5,7},{6,4},{7,5},{8,10},{9,11},{10,... | collective-permute-start | bytes 196616 | tf_op jit(solution)/shard_map/ppermute | solution.py:655
  66.1 2.2 %collective-permute-start.20 = (f32[1344,128]{1,0:T(8,128)S(1)}, f32[1344,128]{1,0:T(8,128)S(1)}, u32[]{:S(2)}, u32[]{:S(2)}) collective-permute-start(f32[1344,128]{1,0:T(8,128)S(1)} %get-tuple-element.131), channel_id=1, source_target_pairs={{0,4},{4,0},{8,12},{12,8},{16,20},{20,16},{24,28},{28,24},{1,5},{5... | collective-permute-start | bytes 2064392 | tf_op jit(solution)/shard_map/ppermute | solution.py:655
  68.4 7.1 %collective-permute-start.21 = (f32[336,128]{1,0:T(8,128)S(1)}, f32[336,128]{1,0:T(8,128)S(1)}, u32[]{:S(2)}, u32[]{:S(2)}) collective-permute-start(f32[336,128]{1,0:T(8,128)S(1)} %get-tuple-element.133), channel_id=1, source_target_pairs={{0,8},{4,20},{8,0},{12,28},{16,24},{20,4},{24,16},{28,12},{1,9},{5... | collective-permute-start | bytes 516104 | tf_op jit(solution)/shard_map/ppermute | solution.py:662
  69.8 7.9 %collective-permute-start.22 = (f32[336,128]{1,0:T(8,128)S(1)}, f32[336,128]{1,0:T(8,128)S(1)}, u32[]{:S(2)}, u32[]{:S(2)}) collective-permute-start(f32[336,128]{1,0:T(8,128)S(1)} %get-tuple-element.134), channel_id=1, source_target_pairs={{0,16},{4,28},{8,24},{12,20},{16,0},{20,12},{24,8},{28,4},{1,17},{... | collective-permute-start | bytes 516104 | tf_op jit(solution)/shard_map/ppermute | solution.py:662
  70.5 9.0 %collective-permute-start.23 = (f32[336,128]{1,0:T(8,128)S(1)}, f32[336,128]{1,0:T(8,128)S(1)}, u32[]{:S(2)}, u32[]{:S(2)}) collective-permute-start(f32[336,128]{1,0:T(8,128)S(1)} %get-tuple-element.135), channel_id=1, source_target_pairs={{0,24},{4,12},{8,16},{12,4},{16,8},{20,28},{24,0},{28,20},{1,25},{... | collective-permute-start | bytes 516104 | tf_op jit(solution)/shard_map/ppermute | solution.py:662
  72.0 1.2 %collective-permute-start.18 = (f32[8,768]{1,0:T(8,128)S(1)}, f32[8,768]{1,0:T(8,128)S(1)}, u32[]{:S(2)}, u32[]{:S(2)}) collective-permute-start(f32[8,768]{1,0:T(8,128)S(1)} %get-tuple-element.127), channel_id=1, source_target_pairs={{0,4},{4,0},{8,12},{12,8},{16,20},{20,16},{24,28},{28,24},{1,5},{5... | collective-permute-start | bytes 73736 | tf_op jit(solution)/shard_map/ppermute | solution.py:655
  72.0 1.2 %collective-permute-start.19 = (f32[8,768]{1,0:T(8,128)S(1)}, f32[8,768]{1,0:T(8,128)S(1)}, u32[]{:S(2)}, u32[]{:S(2)}) collective-permute-start(f32[8,768]{1,0:T(8,128)S(1)} %get-tuple-element.128), channel_id=1, source_target_pairs={{4,8},{12,16},{20,24},{8,4},{16,12},{24,20},{5,9},{13,17},{21,25},... | collective-permute-start | bytes 73736 | tf_op jit(solution)/shard_map/ppermute | solution.py:650
  79.6 8.3 %collective-permute-start.26 = (f32[336,128]{1,0:T(8,128)S(1)}, f32[336,128]{1,0:T(8,128)S(1)}, u32[]{:S(2)}, u32[]{:S(2)}) collective-permute-start(f32[336,128]{1,0:T(8,128)S(1)} %share_sum.1.after_this.mine), channel_id=1, source_target_pairs={{0,24},{4,12},{8,16},{12,4},{16,8},{20,28},{24,0},{28,20},{1,25},{... | collective-permute-start | bytes 516104 | tf_op jit(solution)/shard_map/ppermute | solution.py:662
  81.6 10.1 %collective-permute-start.25 = (f32[336,128]{1,0:T(8,128)S(1)}, f32[336,128]{1,0:T(8,128)S(1)}, u32[]{:S(2)}, u32[]{:S(2)}) collective-permute-start(f32[336,128]{1,0:T(8,128)S(1)} %share_sum.1.after_this.mine), channel_id=1, source_target_pairs={{0,16},{4,28},{8,24},{12,20},{16,0},{20,12},{24,8},{28,4},{1,17},{... | collective-permute-start | bytes 516104 | tf_op jit(solution)/shard_map/ppermute | solution.py:662
  82.5 9.1 %collective-permute-start.24 = (f32[336,128]{1,0:T(8,128)S(1)}, f32[336,128]{1,0:T(8,128)S(1)}, u32[]{:S(2)}, u32[]{:S(2)}) collective-permute-start(f32[336,128]{1,0:T(8,128)S(1)} %share_sum.1.after_this.mine), channel_id=1, source_target_pairs={{0,8},{4,20},{8,0},{12,28},{16,24},{20,4},{24,16},{28,12},{1,9},{5... | collective-permute-start | bytes 516104 | tf_op jit(solution)/shard_map/ppermute | solution.py:662
  91.7 2.2 %collective-permute-start.27 = (f32[4,336,128]{2,1,0:T(8,128)S(1)}, f32[4,336,128]{2,1,0:T(8,128)S(1)}, u32[]{:S(2)}, u32[]{:S(2)}) collective-permute-start(f32[4,336,128]{2,1,0:T(8,128)S(1)} %joined.1.mine), channel_id=1, source_target_pairs={{0,4},{4,0},{8,12},{12,8},{16,20},{20,16},{24,28},{28,24},{1,5},{5... | collective-permute-start | bytes 2064392 | tf_op jit(solution)/shard_map/ppermute | solution.py:655

commit v9 on v7

--- a/solution.py
+++ b/solution.py
@@ -443,7 +443,7 @@
                     summed_out[t, at, :] = earlier[0][t, at, :] + out
             return tuple(new)
 
-        unrolled(count, 4, forward, start(0, up))
+        unrolled(count, 2, forward, start(0, up))
 
         def retreat(i, state):
             j = order(i, count, not up)
@@ -477,7 +477,7 @@
                 grad_pre[t, at, :] = grad_step * jax.nn.sigmoid(pre)
             return tuple(new)
 
-        unrolled(count, 4, retreat, start(1, not up))
+        unrolled(count, 2, retreat, start(1, not up))
         return keep
 
     lax.fori_loop(0, tiles // group, some_tiles, 0)

time: 95.2 us -> 95.7 us (level)
  no operation moved by 1% of the time
where the time goes in v9:
time: 95.7 us; the launch traced here: 95.5 us
  starting transfers between devices  33.6 us (35%)
  Pallas kernels  31.3 us (33%)
  waiting for transfers between devices  29.1 us (30%)
    pallas_call x19, Pallas kernels, call(): pl.pallas_call(kernel, in_specs=[spaces[k] for k in kinds], out_specs=[sp...  31.3 us
    ppermute x17, starting transfers between devices, swapped(): return lax.ppermute(value, axis, [(i, i ^ by) for i in range(count)])  21.6 us
    ppermute x9, waiting for transfers between devices, swapped_chips(): return lax.ppermute(value, 'ctx', pairs)  19.2 us
    ppermute x9, starting transfers between devices, swapped_chips(): return lax.ppermute(value, 'ctx', pairs)  10.7 us
    ppermute x17, waiting for transfers between devices, swapped(): return lax.ppermute(value, axis, [(i, i ^ by) for i in range(count)])  9.86 us
  transfers between devices with their start and end apart: 28, of which 16 were waited for; matrix products, arithmetic and copies ran while one was open for 0% of the time, Pallas kernels for 18%

profile of v9, /device:TPU:0, one launch (start us, length us, event | category | flops | bytes accessed | tf_op | source)
XLA Modules:
  0.0 95.5 jit_solution(83992575723546768)
XLA Ops:
  0.6 0.8 slice_select_fusion
  1.4 0.7 collective-permute-start.1
  2.1 4.4 %collective-permute-start = (f32[8,768]{1,0:T(8,128)S(1)}, f32[8,768]{1,0:T(8,128)S(1)}, u32[]{:S(2)}, u32[]{:S(2)}) collective-permute-start(f32[8,768]{1,0:T(8,128)S(1)} %get-tuple-element.140), channel_id=1, source_target_pairs={{0,4},{4,0},{8,12},{12,8},{16,20},{20,16},{24,28},{28,24},{1,5},{5... | collective-permute-start | bytes 73736 | tf_op jit(solution)/shard_map/ppermute | solution.py:649
  6.4 1.8 %fetch.1 = (f32[128,768]{1,0:T(8,128)S(1)}, f32[2,768,128]{2,1,0:T(8,128)S(1)}, f32[2,4,768]{2,1,0:T(4,128)S(1)}, f32[2,768]{1,0:T(2,128)S(1)}, f32[128,768]{1,0...) custom-call(f32[128,768]{1,0:T(8,128)} %refs_0_.1, ...), custom_call_target="tpu_custom_call" | custom-call | flops 268435456 | bytes 4194304 | tf_op jit(solution)/shard_map/fetch/pallas_call | solution.py:681
  8.2 0.8 entry.1
  9.1 3.7 %collective-permute-start.7 = (f32[128,128]{1,0:T(8,128)S(1)}, f32[128,128]{1,0:T(8,128)S(1)}, u32[]{:S(2)}, u32[]{:S(2)}) collective-permute-start(f32[128,128]{1,0:T(8,128)S(1)} %get-tuple-element.83.refs_0_), channel_id=1, source_target_pairs={{0,3},{1,2},{2,1},{3,0},{4,7},{5,6},{6,5},{7,4},{8,11},{9,10},{10,... | collective-permute-start | bytes 196616 | tf_op jit(solution)/shard_map/ppermute | solution.py:649
  12.8 0.8 collective-permute-start.5
  13.5 1.2 %second_entry.1 = (f32[128,128]{1,0:T(8,128)S(1)}, f32[6,128,128]{2,1,0:T(8,128)S(1)}, f32[6,128,128]{2,1,0:T(8,128)S(1)}, f32[6,128,128]{2,1,0:T(8,128)S(1)}, bf16[128,4096]{1,0:T(8,128)(2,1)S(1)}) custom-call(f32[144,768]{1,0:T(8,128)S(1)} %get-tuple-element.76.ext, f32[2,4,768]{2,1,0:T(4,128)S(1)} %get-tuple-element.73.conv_weight, ...), custom_call_target="tpu_custom_call" | custom-call | flops 268435456 | bytes 4194304 | tf_op jit(solution)/shard_map/second_entry/pallas_call | solution.py:681
  14.8 3.7 %collective-permute-start.4 = (f32[128,128]{1,0:T(8,128)S(1)}, f32[128,128]{1,0:T(8,128)S(1)}, u32[]{:S(2)}, u32[]{:S(2)}) collective-permute-start(f32[128,128]{1,0:T(8,128)S(1)} %get-tuple-element.79.refs_0_), channel_id=1, source_target_pairs={{0,3},{1,2},{2,1},{3,0},{4,7},{5,6},{6,5},{7,4},{8,11},{9,10},{10,... | collective-permute-start | bytes 196616 | tf_op jit(solution)/shard_map/ppermute | solution.py:649
  18.4 0.8 collective-permute-start.2
  19.6 3.8 %first_local.1 = (f32[128,128]{1,0:T(8,128)S(1)}, f32[6,128,128]{2,1,0:T(8,128)S(1)}, f32[6,128,128]{2,1,0:T(8,128)S(1)}, f32[2,6,16,8,128]{4,3,2,1,0:T(8,128)S(...) custom-call(f32[128,128]{1,0:T(8,128)S(1)} %get-tuple-element.83.ref, ...), custom_call_target="tpu_custom_call" | custom-call | flops 4294967296 | bytes 67108864 | tf_op jit(solution)/shard_map/first_local/pallas_call | solution.py:681
  23.4 0.8 collective-permute-done.3.refs_2_
  24.2 3.8 %second_local.1 = (f32[128,128]{1,0:T(8,128)S(1)}, f32[6,128,128]{2,1,0:T(8,128)S(1)}, f32[6,128,128]{2,1,0:T(8,128)S(1)}, f32[2,6,16,8,128]{4,3,2,1,0:T(8,128)S...) custom-call(f32[128,128]{1,0:T(8,128)S(1)} %get-tuple-element.79.ref, ...), custom_call_target="tpu_custom_call" | custom-call | flops 4294967296 | bytes 67108864 | tf_op jit(solution)/shard_map/second_local/pallas_call | solution.py:681
  28.0 1.5 %collective-permute-done.8.other = f32[2,6,40,128]{3,2,1,0:T(8,128)S(1)} collective-permute-done((f32[2,6,40,128]{3,2,1,0:T(8,128)S(1)}, f32[2,6,40,128]{3,2,1,0:T(8,128)S(1)}, u32[]{:S(2)}, u32[]{:S(2)}) %collective-permute-start.8) | collective-permute-done | bytes 245792 | tf_op jit(solution)/shard_map/ppermute | solution.py:649
  29.7 2.1 %collective-permute-start.9 = (f32[208,128]{1,0:T(8,128)S(1)}, f32[208,128]{1,0:T(8,128)S(1)}, u32[]{:S(2)}, u32[]{:S(2)}) collective-permute-start(f32[208,128]{1,0:T(8,128)S(1)} %get-tuple-element.93), channel_id=1, source_target_pairs={{0,8},{4,20},{8,0},{12,28},{16,24},{20,4},{24,16},{28,12},{1,9},{5... | collective-permute-start | bytes 319496 | tf_op jit(solution)/shard_map/ppermute | solution.py:656
  31.7 1.5 %collective-permute-start.10 = (f32[208,128]{1,0:T(8,128)S(1)}, f32[208,128]{1,0:T(8,128)S(1)}, u32[]{:S(2)}, u32[]{:S(2)}) collective-permute-start(f32[208,128]{1,0:T(8,128)S(1)} %get-tuple-element.94), channel_id=1, source_target_pairs={{0,16},{4,28},{8,24},{12,20},{16,0},{20,12},{24,8},{28,4},{1,17},{... | collective-permute-start | bytes 319496 | tf_op jit(solution)/shard_map/ppermute | solution.py:656
  33.3 1.7 %collective-permute-done.9.refs_0_ = f32[208,128]{1,0:T(8,128)S(1)} collective-permute-done((f32[208,128]{1,0:T(8,128)S(1)}, f32[208,128]{1,0:T(8,128)S(1)}, u32[]{:S(2)}, u32[]{:S(2)}) %collective-permute-start.9) | collective-permute-done | bytes 106528 | tf_op jit(solution)/shard_map/ppermute | solution.py:656
  34.9 2.3 %collective-permute-done.10.refs_1_ = f32[208,128]{1,0:T(8,128)S(1)} collective-permute-done((f32[208,128]{1,0:T(8,128)S(1)}, f32[208,128]{1,0:T(8,128)S(1)}, u32[]{:S(2)}, u32[]{:S(2)}) %collective-permute-start.10) | collective-permute-done | bytes 106528 | tf_op jit(solution)/shard_map/ppermute | solution.py:656
  37.3 1.7 %collective-permute-done.11.refs_2_ = f32[208,128]{1,0:T(8,128)S(1)} collective-permute-done((f32[208,128]{1,0:T(8,128)S(1)}, f32[208,128]{1,0:T(8,128)S(1)}, u32[]{:S(2)}, u32[]{:S(2)}) %collective-permute-start.11) | collective-permute-done | bytes 106528 | tf_op jit(solution)/shard_map/ppermute | solution.py:656
  39.2 6.4 %first_scan.1 = (f32[128,128]{1,0:T(8,128)S(1)}, f32[6,128,128]{2,1,0:T(8,128)S(1)}, f32[6,128,128]{2,1,0:T(8,128)S(1)}, f32[6,128,128]{2,1,0:T(8,128)S(1)}) custom-call(f32[2,6,32,128]{3,2,1,0:T(8,128)S(1)} %chain.1.refs_0_, f32[2,128,2048]{2,1,0:T(8,128)S(1)} %get-tuple-element.103.refs_1_, f32[6,128,128]{2,1,0:T(8,128)S(1)} %get-tuple-element.84.refs_4_.refs_2_.act, ...), custom_call_target="tpu_custom_call" | custom-call | flops 8589934592 | bytes 134217728 | tf_op jit(solution)/shard_map/first_scan/pallas_call | solution.py:681
  45.7 3.0 %collective-permute-start.14 = (f32[128,128]{1,0:T(8,128)S(1)}, f32[128,128]{1,0:T(8,128)S(1)}, u32[]{:S(2)}, u32[]{:S(2)}) collective-permute-start(f32[128,128]{1,0:T(8,128)S(1)} %get-tuple-element.113.refs_0_), channel_id=1, source_target_pairs={{0,3},{1,2},{2,1},{3,0},{4,7},{5,6},{6,5},{7,4},{8,11},{9,10},{10,... | collective-permute-start | bytes 196616 | tf_op jit(solution)/shard_map/ppermute | solution.py:649
  48.7 1.5 %collective-permute-start.12 = (f32[128,128]{1,0:T(8,128)S(1)}, f32[128,128]{1,0:T(8,128)S(1)}, u32[]{:S(2)}, u32[]{:S(2)}) collective-permute-start(f32[128,128]{1,0:T(8,128)S(1)} %get-tuple-element.113.refs_0_), channel_id=1, source_target_pairs={{0,1},{1,0},{2,3},{3,2},{4,5},{5,4},{6,7},{7,6},{8,9},{9,8},{10,11... | collective-permute-start | bytes 196616 | tf_op jit(solution)/shard_map/ppermute | solution.py:649
  50.1 6.5 %second_scan.1 = (f32[128,128]{1,0:T(8,128)S(1)}, f32[6,128,128]{2,1,0:T(8,128)S(1)}, f32[6,128,128]{2,1,0:T(8,128)S(1)}, f32[6,128,128]{2,1,0:T(8,128)S(1)}) custom-call(f32[2,6,32,128]{3,2,1,0:T(8,128)S(1)} %chain.1.refs_0_, f32[2,128,2048]{2,1,0:T(8,128)S(1)} %get-tuple-element.96.refs_1_, f32[6,128,128]{2,1,0:T(8,128)S(1)} %get-tuple-element.80.refs_4_.refs_2_.act, ...), custom_call_target="tpu_custom_call" | custom-call | flops 8589934592 | bytes 134217728 | tf_op jit(solution)/shard_map/second_scan/pallas_call | solution.py:681
  56.7 0.6 collective-permute-start.15
  57.3 2.4 %collective-permute-start.17 = (f32[128,128]{1,0:T(8,128)S(1)}, f32[128,128]{1,0:T(8,128)S(1)}, u32[]{:S(2)}, u32[]{:S(2)}) collective-permute-start(f32[128,128]{1,0:T(8,128)S(1)} %get-tuple-element.114.own), channel_id=1, source_target_pairs={{0,3},{1,2},{2,1},{3,0},{4,7},{5,6},{6,5},{7,4},{8,11},{9,10},{10,... | collective-permute-start | bytes 196616 | tf_op jit(solution)/shard_map/ppermute | solution.py:649
  60.2 0.9 collective-permute-done.15.after_this.first
  61.1 1.2 %gate.1 = (f32[128,768]{1,0:T(8,128)}, f32[128,768]{1,0:T(8,128)}) custom-call(f32[6,128,128]{2,1,0:T(8,128)S(1)} %get-tuple-element.111.summed, f32[128,768]{1,0:T(8,128)S(1)} %get-tuple-element.77.gate, f32[128,768]{1,0:T(8,128)S(1)} %get-tuple-element.78.cot, f32[128,128]{1,0:T(8,128)S(1)} %collective-permute-done.15.after_this.first), custom_call_target="tpu_custom_call" | custom-call | tf_op jit(solution)/shard_map/gate/pallas_call | solution.py:681
  62.3 0.9 first_weights.1
  63.3 0.8 step_grad.1.step_part
  64.1 1.5 %collective-permute-done.16.second = f32[128,128]{1,0:T(8,128)S(1)} collective-permute-done((f32[128,128]{1,0:T(8,128)S(1)}, f32[128,128]{1,0:T(8,128)S(1)}, u32[]{:S(2)}, u32[]{:S(2)}) %collective-permute-start.16) | collective-permute-done | bytes 65568 | tf_op jit(solution)/shard_map/ppermute | solution.py:649
  65.6 1.0 %weights.1 = (f32[1344,128]{1,0:T(8,128)S(1)}, f32[1344,128]{1,0:T(8,128)S(1)}, f32[128,768]{1,0:T(8,128)S(1)}, f32[8,768]{1,0:T(8,128)S(1)}, f32[8,768]{1,0:T(8,128)S(1)}) custom-call(s32[1]{0:T(128)} %bitcast.place, f32[128,128]{1,0:T(8,128)S(1)} %get-tuple-element.114.own, f32[128,128]{1,0:T(8,128)S(1)} %collective-permute-done.15.after_this.first, ...), custom_call_target="tpu_custom_call" | custom-call | flops 268435456 | bytes 4194304 | tf_op jit(solution)/shard_map/weights/pallas_call | solution.py:681
  66.7 2.1 %collective-permute-done.20.got = f32[1344,128]{1,0:T(8,128)S(1)} collective-permute-done((f32[1344,128]{1,0:T(8,128)S(1)}, f32[1344,128]{1,0:T(8,128)S(1)}, u32[]{:S(2)}, u32[]{:S(2)}) %collective-permute-start.20) | collective-permute-done | bytes 688160 | tf_op jit(solution)/shard_map/ppermute | solution.py:649
  69.0 1.3 %collective-permute-start.21 = (f32[336,128]{1,0:T(8,128)S(1)}, f32[336,128]{1,0:T(8,128)S(1)}, u32[]{:S(2)}, u32[]{:S(2)}) collective-permute-start(f32[336,128]{1,0:T(8,128)S(1)} %get-tuple-element.133), channel_id=1, source_target_pairs={{0,8},{4,20},{8,0},{12,28},{16,24},{20,4},{24,16},{28,12},{1,9},{5... | collective-permute-start | bytes 516104 | tf_op jit(solution)/shard_map/ppermute | solution.py:656
  70.3 0.8 collective-permute-start.22
  71.1 1.5 %collective-permute-start.23 = (f32[336,128]{1,0:T(8,128)S(1)}, f32[336,128]{1,0:T(8,128)S(1)}, u32[]{:S(2)}, u32[]{:S(2)}) collective-permute-start(f32[336,128]{1,0:T(8,128)S(1)} %get-tuple-element.135), channel_id=1, source_target_pairs={{0,24},{4,12},{8,16},{12,4},{16,8},{20,28},{24,0},{28,20},{1,25},{... | collective-permute-start | bytes 516104 | tf_op jit(solution)/shard_map/ppermute | solution.py:656
  72.5 3.5 %collective-permute-done.21.refs_1_ = f32[336,128]{1,0:T(8,128)S(1)} collective-permute-done((f32[336,128]{1,0:T(8,128)S(1)}, f32[336,128]{1,0:T(8,128)S(1)}, u32[]{:S(2)}, u32[]{:S(2)}) %collective-permute-start.21) | collective-permute-done | bytes 172064 | tf_op jit(solution)/shard_map/ppermute | solution.py:656
  76.0 2.1 %collective-permute-done.22.refs_2_ = f32[336,128]{1,0:T(8,128)S(1)} collective-permute-done((f32[336,128]{1,0:T(8,128)S(1)}, f32[336,128]{1,0:T(8,128)S(1)}, u32[]{:S(2)}, u32[]{:S(2)}) %collective-permute-start.22) | collective-permute-done | bytes 172064 | tf_op jit(solution)/shard_map/ppermute | solution.py:656
  78.2 1.9 %collective-permute-done.23.refs_3_ = f32[336,128]{1,0:T(8,128)S(1)} collective-permute-done((f32[336,128]{1,0:T(8,128)S(1)}, f32[336,128]{1,0:T(8,128)S(1)}, u32[]{:S(2)}, u32[]{:S(2)}) %collective-permute-start.23) | collective-permute-done | bytes 172064 | tf_op jit(solution)/shard_map/ppermute | solution.py:656
  80.2 1.8 %collective-permute-start.26 = (f32[336,128]{1,0:T(8,128)S(1)}, f32[336,128]{1,0:T(8,128)S(1)}, u32[]{:S(2)}, u32[]{:S(2)}) collective-permute-start(f32[336,128]{1,0:T(8,128)S(1)} %share_sum.1.after_this.mine), channel_id=1, source_target_pairs={{0,24},{4,12},{8,16},{12,4},{16,8},{20,28},{24,0},{28,20},{1,25},{... | collective-permute-start | bytes 516104 | tf_op jit(solution)/shard_map/ppermute | solution.py:656
  82.0 0.8 collective-permute-start.25
  82.8 0.9 collective-permute-start.24
  83.7 0.7 collective-permute-start.19
  84.4 0.5 collective-permute-done.18.near
  84.9 1.2 %exit.1.after_this = f32[128,768]{1,0:T(8,128)} custom-call(s32[1]{0:T(128)} %bitcast.place, f32[8,768]{1,0:T(8,128)S(1)} %collective-permute-done.18.near, f32[8,768]{1,0:T(8,128)S(1)} %collective-permute-done.19.far, f32[128,768]{1,0:T(8,128)S(1)} %get-tuple-element.126.other_grad.first, f32[128,768]{1,0:T(8,128)S(1)} %get-tuple-element.129.second, ...), custom_call_target="tpu_custom_call" | custom-call | flops 268435456 | bytes 4194304 | tf_op jit(solution)/shard_map/exit/pallas_call | solution.py:681
  86.1 2.4 %collective-permute-done.26.refs_2_ = f32[336,128]{1,0:T(8,128)S(1)} collective-permute-done((f32[336,128]{1,0:T(8,128)S(1)}, f32[336,128]{1,0:T(8,128)S(1)}, u32[]{:S(2)}, u32[]{:S(2)}) %collective-permute-start.26) | collective-permute-done | bytes 172064 | tf_op jit(solution)/shard_map/ppermute | solution.py:656
  88.5 3.5 %collective-permute-done.25.refs_1_ = f32[336,128]{1,0:T(8,128)S(1)} collective-permute-done((f32[336,128]{1,0:T(8,128)S(1)}, f32[336,128]{1,0:T(8,128)S(1)}, u32[]{:S(2)}, u32[]{:S(2)}) %collective-permute-start.25) | collective-permute-done | bytes 172064 | tf_op jit(solution)/shard_map/ppermute | solution.py:656
  92.2 2.1 %collective-permute-done.27.other = f32[4,336,128]{2,1,0:T(8,128)S(1)} collective-permute-done((f32[4,336,128]{2,1,0:T(8,128)S(1)}, f32[4,336,128]{2,1,0:T(8,128)S(1)}, u32[]{:S(2)}, u32[]{:S(2)}) %collective-permute-start.27) | collective-permute-done | bytes 688160 | tf_op jit(solution)/shard_map/ppermute | solution.py:649
  94.3 1.2 %weight_grads.1 = (f32[2,768,128]{2,1,0:T(8,128)}, f32[2,96,768]{2,1,0:T(8,128)}) custom-call(s32[1]{0:T(128)} %bitcast.place, f32[4,336,128]{2,1,0:T(8,128)S(1)} %joined.1.mine, f32[4,336,128]{2,1,0:T(8,128)S(1)} %collective-permute-done.27.other), custom_call_target="tpu_custom_call" | custom-call | flops 268435456 | bytes 4194304 | tf_op jit(solution)/shard_map/weight_grads/pallas_call | solution.py:681
  (28 shorter events, 1.8 us)
Async XLA Ops:
  1.4 6.8 %collective-permute-start.1 = (f32[8,768]{1,0:T(8,128)S(1)}, f32[8,768]{1,0:T(8,128)S(1)}, u32[]{:S(2)}, u32[]{:S(2)}) collective-permute-start(f32[8,768]{1,0:T(8,128)S(1)} %get-tuple-element.139), channel_id=1, source_target_pairs={{4,8},{12,16},{20,24},{8,4},{16,12},{24,20},{5,9},{13,17},{21,25},... | collective-permute-start | bytes 73736 | tf_op jit(solution)/shard_map/ppermute | solution.py:644
  2.1 6.2 %collective-permute-start = (f32[8,768]{1,0:T(8,128)S(1)}, f32[8,768]{1,0:T(8,128)S(1)}, u32[]{:S(2)}, u32[]{:S(2)}) collective-permute-start(f32[8,768]{1,0:T(8,128)S(1)} %get-tuple-element.140), channel_id=1, source_target_pairs={{0,4},{4,0},{8,12},{12,8},{16,20},{20,16},{24,28},{28,24},{1,5},{5... | collective-permute-start | bytes 73736 | tf_op jit(solution)/shard_map/ppermute | solution.py:649
  9.1 9.3 %collective-permute-start.7 = (f32[128,128]{1,0:T(8,128)S(1)}, f32[128,128]{1,0:T(8,128)S(1)}, u32[]{:S(2)}, u32[]{:S(2)}) collective-permute-start(f32[128,128]{1,0:T(8,128)S(1)} %get-tuple-element.83.refs_0_), channel_id=1, source_target_pairs={{0,3},{1,2},{2,1},{3,0},{4,7},{5,6},{6,5},{7,4},{8,11},{9,10},{10,... | collective-permute-start | bytes 196616 | tf_op jit(solution)/shard_map/ppermute | solution.py:649
  12.7 6.8 %collective-permute-start.6 = (f32[128,128]{1,0:T(8,128)S(1)}, f32[128,128]{1,0:T(8,128)S(1)}, u32[]{:S(2)}, u32[]{:S(2)}) collective-permute-start(f32[128,128]{1,0:T(8,128)S(1)} %get-tuple-element.83.refs_0_), channel_id=1, source_target_pairs={{0,2},{1,3},{2,0},{3,1},{4,6},{5,7},{6,4},{7,5},{8,10},{9,11},{10,... | collective-permute-start | bytes 196616 | tf_op jit(solution)/shard_map/ppermute | solution.py:649
  12.8 6.8 %collective-permute-start.5 = (f32[128,128]{1,0:T(8,128)S(1)}, f32[128,128]{1,0:T(8,128)S(1)}, u32[]{:S(2)}, u32[]{:S(2)}) collective-permute-start(f32[128,128]{1,0:T(8,128)S(1)} %get-tuple-element.83.refs_0_), channel_id=1, source_target_pairs={{0,1},{1,0},{2,3},{3,2},{4,5},{5,4},{6,7},{7,6},{8,9},{9,8},{10,11... | collective-permute-start | bytes 196616 | tf_op jit(solution)/shard_map/ppermute | solution.py:649
  14.8 8.6 %collective-permute-start.4 = (f32[128,128]{1,0:T(8,128)S(1)}, f32[128,128]{1,0:T(8,128)S(1)}, u32[]{:S(2)}, u32[]{:S(2)}) collective-permute-start(f32[128,128]{1,0:T(8,128)S(1)} %get-tuple-element.79.refs_0_), channel_id=1, source_target_pairs={{0,3},{1,2},{2,1},{3,0},{4,7},{5,6},{6,5},{7,4},{8,11},{9,10},{10,... | collective-permute-start | bytes 196616 | tf_op jit(solution)/shard_map/ppermute | solution.py:649
  18.4 5.7 %collective-permute-start.3 = (f32[128,128]{1,0:T(8,128)S(1)}, f32[128,128]{1,0:T(8,128)S(1)}, u32[]{:S(2)}, u32[]{:S(2)}) collective-permute-start(f32[128,128]{1,0:T(8,128)S(1)} %get-tuple-element.79.refs_0_), channel_id=1, source_target_pairs={{0,2},{1,3},{2,0},{3,1},{4,6},{5,7},{6,4},{7,5},{8,10},{9,11},{10,... | collective-permute-start | bytes 196616 | tf_op jit(solution)/shard_map/ppermute | solution.py:649
  18.4 5.7 %collective-permute-start.2 = (f32[128,128]{1,0:T(8,128)S(1)}, f32[128,128]{1,0:T(8,128)S(1)}, u32[]{:S(2)}, u32[]{:S(2)}) collective-permute-start(f32[128,128]{1,0:T(8,128)S(1)} %get-tuple-element.79.refs_0_), channel_id=1, source_target_pairs={{0,1},{1,0},{2,3},{3,2},{4,5},{5,4},{6,7},{7,6},{8,9},{9,8},{10,11... | collective-permute-start | bytes 196616 | tf_op jit(solution)/shard_map/ppermute | solution.py:649
  27.9 1.6 %collective-permute-start.8 = (f32[2,6,40,128]{3,2,1,0:T(8,128)S(1)}, f32[2,6,40,128]{3,2,1,0:T(8,128)S(1)}, u32[]{:S(2)}, u32[]{:S(2)}) collective-permute-start(f32[2,6,40,128]{3,2,1,0:T(8,128)S(1)} %get-tuple-element.91.mine), channel_id=1, source_target_pairs={{0,4},{4,0},{8,12},{12,8},{16,20},{20,16},{24,28},{28,24},{1,5},{5... | collective-permute-start | bytes 737288 | tf_op jit(solution)/shard_map/ppermute | solution.py:649
  29.7 5.3 %collective-permute-start.9 = (f32[208,128]{1,0:T(8,128)S(1)}, f32[208,128]{1,0:T(8,128)S(1)}, u32[]{:S(2)}, u32[]{:S(2)}) collective-permute-start(f32[208,128]{1,0:T(8,128)S(1)} %get-tuple-element.93), channel_id=1, source_target_pairs={{0,8},{4,20},{8,0},{12,28},{16,24},{20,4},{24,16},{28,12},{1,9},{5... | collective-permute-start | bytes 319496 | tf_op jit(solution)/shard_map/ppermute | solution.py:656
  31.7 5.5 %collective-permute-start.10 = (f32[208,128]{1,0:T(8,128)S(1)}, f32[208,128]{1,0:T(8,128)S(1)}, u32[]{:S(2)}, u32[]{:S(2)}) collective-permute-start(f32[208,128]{1,0:T(8,128)S(1)} %get-tuple-element.94), channel_id=1, source_target_pairs={{0,16},{4,28},{8,24},{12,20},{16,0},{20,12},{24,8},{28,4},{1,17},{... | collective-permute-start | bytes 319496 | tf_op jit(solution)/shard_map/ppermute | solution.py:656
  33.2 5.8 %collective-permute-start.11 = (f32[208,128]{1,0:T(8,128)S(1)}, f32[208,128]{1,0:T(8,128)S(1)}, u32[]{:S(2)}, u32[]{:S(2)}) collective-permute-start(f32[208,128]{1,0:T(8,128)S(1)} %get-tuple-element.95), channel_id=1, source_target_pairs={{0,24},{4,12},{8,16},{12,4},{16,8},{20,28},{24,0},{28,20},{1,25},{... | collective-permute-start | bytes 319496 | tf_op jit(solution)/shard_map/ppermute | solution.py:656
  45.7 10.9 %collective-permute-start.14 = (f32[128,128]{1,0:T(8,128)S(1)}, f32[128,128]{1,0:T(8,128)S(1)}, u32[]{:S(2)}, u32[]{:S(2)}) collective-permute-start(f32[128,128]{1,0:T(8,128)S(1)} %get-tuple-element.113.refs_0_), channel_id=1, source_target_pairs={{0,3},{1,2},{2,1},{3,0},{4,7},{5,6},{6,5},{7,4},{8,11},{9,10},{10,... | collective-permute-start | bytes 196616 | tf_op jit(solution)/shard_map/ppermute | solution.py:649
  48.7 7.9 %collective-permute-start.13 = (f32[128,128]{1,0:T(8,128)S(1)}, f32[128,128]{1,0:T(8,128)S(1)}, u32[]{:S(2)}, u32[]{:S(2)}) collective-permute-start(f32[128,128]{1,0:T(8,128)S(1)} %get-tuple-element.113.refs_0_), channel_id=1, source_target_pairs={{0,2},{1,3},{2,0},{3,1},{4,6},{5,7},{6,4},{7,5},{8,10},{9,11},{10,... | collective-permute-start | bytes 196616 | tf_op jit(solution)/shard_map/ppermute | solution.py:649
  48.7 8.0 %collective-permute-start.12 = (f32[128,128]{1,0:T(8,128)S(1)}, f32[128,128]{1,0:T(8,128)S(1)}, u32[]{:S(2)}, u32[]{:S(2)}) collective-permute-start(f32[128,128]{1,0:T(8,128)S(1)} %get-tuple-element.113.refs_0_), channel_id=1, source_target_pairs={{0,1},{1,0},{2,3},{3,2},{4,5},{5,4},{6,7},{7,6},{8,9},{9,8},{10,11... | collective-permute-start | bytes 196616 | tf_op jit(solution)/shard_map/ppermute | solution.py:649
  56.7 4.5 %collective-permute-start.15 = (f32[128,128]{1,0:T(8,128)S(1)}, f32[128,128]{1,0:T(8,128)S(1)}, u32[]{:S(2)}, u32[]{:S(2)}) collective-permute-start(f32[128,128]{1,0:T(8,128)S(1)} %get-tuple-element.114.own), channel_id=1, source_target_pairs={{0,1},{1,0},{2,3},{3,2},{4,5},{5,4},{6,7},{7,6},{8,9},{9,8},{10,11... | collective-permute-start | bytes 196616 | tf_op jit(solution)/shard_map/ppermute | solution.py:649
  57.3 6.8 %collective-permute-start.17 = (f32[128,128]{1,0:T(8,128)S(1)}, f32[128,128]{1,0:T(8,128)S(1)}, u32[]{:S(2)}, u32[]{:S(2)}) collective-permute-start(f32[128,128]{1,0:T(8,128)S(1)} %get-tuple-element.114.own), channel_id=1, source_target_pairs={{0,3},{1,2},{2,1},{3,0},{4,7},{5,6},{6,5},{7,4},{8,11},{9,10},{10,... | collective-permute-start | bytes 196616 | tf_op jit(solution)/shard_map/ppermute | solution.py:649
  59.7 5.9 %collective-permute-start.16 = (f32[128,128]{1,0:T(8,128)S(1)}, f32[128,128]{1,0:T(8,128)S(1)}, u32[]{:S(2)}, u32[]{:S(2)}) collective-permute-start(f32[128,128]{1,0:T(8,128)S(1)} %get-tuple-element.114.own), channel_id=1, source_target_pairs={{0,2},{1,3},{2,0},{3,1},{4,6},{5,7},{6,4},{7,5},{8,10},{9,11},{10,... | collective-permute-start | bytes 196616 | tf_op jit(solution)/shard_map/ppermute | solution.py:649
  66.6 2.2 %collective-permute-start.20 = (f32[1344,128]{1,0:T(8,128)S(1)}, f32[1344,128]{1,0:T(8,128)S(1)}, u32[]{:S(2)}, u32[]{:S(2)}) collective-permute-start(f32[1344,128]{1,0:T(8,128)S(1)} %get-tuple-element.131), channel_id=1, source_target_pairs={{0,4},{4,0},{8,12},{12,8},{16,20},{20,16},{24,28},{28,24},{1,5},{5... | collective-permute-start | bytes 2064392 | tf_op jit(solution)/shard_map/ppermute | solution.py:649
  69.0 7.1 %collective-permute-start.21 = (f32[336,128]{1,0:T(8,128)S(1)}, f32[336,128]{1,0:T(8,128)S(1)}, u32[]{:S(2)}, u32[]{:S(2)}) collective-permute-start(f32[336,128]{1,0:T(8,128)S(1)} %get-tuple-element.133), channel_id=1, source_target_pairs={{0,8},{4,20},{8,0},{12,28},{16,24},{20,4},{24,16},{28,12},{1,9},{5... | collective-permute-start | bytes 516104 | tf_op jit(solution)/shard_map/ppermute | solution.py:656
  70.3 7.9 %collective-permute-start.22 = (f32[336,128]{1,0:T(8,128)S(1)}, f32[336,128]{1,0:T(8,128)S(1)}, u32[]{:S(2)}, u32[]{:S(2)}) collective-permute-start(f32[336,128]{1,0:T(8,128)S(1)} %get-tuple-element.134), channel_id=1, source_target_pairs={{0,16},{4,28},{8,24},{12,20},{16,0},{20,12},{24,8},{28,4},{1,17},{... | collective-permute-start | bytes 516104 | tf_op jit(solution)/shard_map/ppermute | solution.py:656
  71.1 9.0 %collective-permute-start.23 = (f32[336,128]{1,0:T(8,128)S(1)}, f32[336,128]{1,0:T(8,128)S(1)}, u32[]{:S(2)}, u32[]{:S(2)}) collective-permute-start(f32[336,128]{1,0:T(8,128)S(1)} %get-tuple-element.135), channel_id=1, source_target_pairs={{0,24},{4,12},{8,16},{12,4},{16,8},{20,28},{24,0},{28,20},{1,25},{... | collective-permute-start | bytes 516104 | tf_op jit(solution)/shard_map/ppermute | solution.py:656
  80.2 8.4 %collective-permute-start.26 = (f32[336,128]{1,0:T(8,128)S(1)}, f32[336,128]{1,0:T(8,128)S(1)}, u32[]{:S(2)}, u32[]{:S(2)}) collective-permute-start(f32[336,128]{1,0:T(8,128)S(1)} %share_sum.1.after_this.mine), channel_id=1, source_target_pairs={{0,24},{4,12},{8,16},{12,4},{16,8},{20,28},{24,0},{28,20},{1,25},{... | collective-permute-start | bytes 516104 | tf_op jit(solution)/shard_map/ppermute | solution.py:656
  82.0 10.0 %collective-permute-start.25 = (f32[336,128]{1,0:T(8,128)S(1)}, f32[336,128]{1,0:T(8,128)S(1)}, u32[]{:S(2)}, u32[]{:S(2)}) collective-permute-start(f32[336,128]{1,0:T(8,128)S(1)} %share_sum.1.after_this.mine), channel_id=1, source_target_pairs={{0,16},{4,28},{8,24},{12,20},{16,0},{20,12},{24,8},{28,4},{1,17},{... | collective-permute-start | bytes 516104 | tf_op jit(solution)/shard_map/ppermute | solution.py:656
  82.8 9.3 %collective-permute-start.24 = (f32[336,128]{1,0:T(8,128)S(1)}, f32[336,128]{1,0:T(8,128)S(1)}, u32[]{:S(2)}, u32[]{:S(2)}) collective-permute-start(f32[336,128]{1,0:T(8,128)S(1)} %share_sum.1.after_this.mine), channel_id=1, source_target_pairs={{0,8},{4,20},{8,0},{12,28},{16,24},{20,4},{24,16},{28,12},{1,9},{5... | collective-permute-start | bytes 516104 | tf_op jit(solution)/shard_map/ppermute | solution.py:656
  83.7 1.2 %collective-permute-start.18 = (f32[8,768]{1,0:T(8,128)S(1)}, f32[8,768]{1,0:T(8,128)S(1)}, u32[]{:S(2)}, u32[]{:S(2)}) collective-permute-start(f32[8,768]{1,0:T(8,128)S(1)} %get-tuple-element.127), channel_id=1, source_target_pairs={{0,4},{4,0},{8,12},{12,8},{16,20},{20,16},{24,28},{28,24},{1,5},{5... | collective-permute-start | bytes 73736 | tf_op jit(solution)/shard_map/ppermute | solution.py:649
  83.7 1.2 %collective-permute-start.19 = (f32[8,768]{1,0:T(8,128)S(1)}, f32[8,768]{1,0:T(8,128)S(1)}, u32[]{:S(2)}, u32[]{:S(2)}) collective-permute-start(f32[8,768]{1,0:T(8,128)S(1)} %get-tuple-element.128), channel_id=1, source_target_pairs={{4,8},{12,16},{20,24},{8,4},{16,12},{24,20},{5,9},{13,17},{21,25},... | collective-permute-start | bytes 73736 | tf_op jit(solution)/shard_map/ppermute | solution.py:644
  92.1 2.2 %collective-permute-start.27 = (f32[4,336,128]{2,1,0:T(8,128)S(1)}, f32[4,336,128]{2,1,0:T(8,128)S(1)}, u32[]{:S(2)}, u32[]{:S(2)}) collective-permute-start(f32[4,336,128]{2,1,0:T(8,128)S(1)} %joined.1.mine), channel_id=1, source_target_pairs={{0,4},{4,0},{8,12},{12,8},{16,20},{20,16},{24,28},{28,24},{1,5},{5... | collective-permute-start | bytes 2064392 | tf_op jit(solution)/shard_map/ppermute | solution.py:649
